TPU v7x, 128 devices: a whole 4x4x4 slice. The times are simulated.
128 devices in a mesh: ctx: 32 (over x, z, y_hi), dp: 4 (over y_lo, core).
Axes of the slice: x: 4, y: 4 (y_hi: 2, y_lo: 2; y = y_hi * 2 + y_lo), z: 4, core: 2. Of those that a mesh axis runs over, the one named last changes fastest.
Arguments:
- hidden_states: bfloat16 [4, 8192, 5120], P('dp', 'ctx'), may hold values from -6 to 6
- block_order: int32 [64], replicated, may hold values from 0 to 63, as said below
- w_query: bfloat16 [5120, 512], P(('ctx', 'dp')), may hold values from -0.2 to 0.2
- w_key: bfloat16 [5120, 128], P(('ctx', 'dp')), may hold values from -0.2 to 0.2
- w_value: bfloat16 [5120, 128], P(('ctx', 'dp')), may hold values from -0.078125 to 0.078125
- gain_query: float32 [128], replicated, may hold values from 0.5 to 4.5
- gain_key: float32 [128], replicated, may hold values from 0.5 to 4.5
- cotangent: bfloat16 [4, 8192, 512], P('dp', 'ctx'), may hold values from -6 to 6
Outputs:
- context: bfloat16 [4, 8192, 512], P('dp', 'ctx')
- grad_states: bfloat16 [4, 8192, 5120], P('dp', 'ctx')
- grad_query: float32 [5120, 512], P(('ctx', 'dp'))
- grad_key: float32 [5120, 128], P(('ctx', 'dp'))
- grad_value: float32 [5120, 128], P(('ctx', 'dp'))
- grad_gain_query: float32 [128], replicated
- grad_gain_key: float32 [128], replicated
Inputs may be any that keep to these rules, and one draw needn't show every extreme that they name: `block_order`: a permutation of the 64 sequence blocks; the stored slots 2 c and 2 c + 1 belong to index c of ctx and hold blocks b and 63 - b for some b, in either order.
All inputs are finite; a program needn't handle non-finite values.
Results may differ from a plain program's by a relative error of at most 0.04.
Values may be sent and summed in bfloat16 or wider, within the bound.
No kernel may reach another device: no remote copies, remote signals or barrier semaphores. Data moves between devices by JAX's collectives and lax.ppermute only.
A program may use at most 128 MiB of HBM per device.

v0:
```python
import math

import jax
import jax.numpy as jnp
from jax import lax
from jax.sharding import PartitionSpec as P

theta = 1000000.0
floor_score = -1e30


def rotation(positions, head_width):
    steps_half = jnp.arange(head_width // 2, dtype=jnp.float32)
    inverse = jnp.power(jnp.float32(theta), -2.0 * steps_half / head_width)
    angles = positions.astype(jnp.float32)[:, None] * inverse[None, :]
    cosine = jnp.cos(angles)
    sine = jnp.sin(angles)
    return (jnp.concatenate([cosine, cosine], 1), jnp.concatenate([sine, sine], 1))


def shape_heads(raw_rows, gain, cosine, sine):
    inverse_norm = lax.rsqrt(jnp.mean(raw_rows * raw_rows, axis=-1, keepdims=True) + 1e-06)
    normed = raw_rows * inverse_norm * gain
    half_width = normed.shape[-1] // 2
    turned = jnp.concatenate([-normed[..., half_width:], normed[..., :half_width]], axis=-1)
    return normed * cosine[:, None, :] + turned * sine[:, None, :]


def attend(query16, query_pos, grad_out, key_blocks, value_blocks, pos_blocks):
    rows_here, head_count, head_width = query16.shape
    score_scale = head_width ** (-0.5)

    def block_scores(key_part, pos_part):
        raw_scores = (
            jnp.einsum("qhd,kd->hqk", query16, key_part, preferred_element_type=jnp.float32)
            * score_scale
        )
        allowed = pos_part[None, :] <= query_pos[:, None]
        return jnp.where(allowed[None], raw_scores, floor_score)

    def first_pass(state_pair, pieces):
        key_part, pos_part = pieces
        running_max, running_sum = state_pair
        scores = block_scores(key_part, pos_part)
        new_max = jnp.maximum(running_max, jnp.max(scores, axis=2))
        new_sum = running_sum * jnp.exp(running_max - new_max) + jnp.sum(
            jnp.exp(scores - new_max[..., None]), axis=2
        )
        return ((new_max, new_sum), None)

    start_pair = (
        jnp.full((head_count, rows_here), floor_score, jnp.float32),
        jnp.zeros((head_count, rows_here), jnp.float32),
    )
    (row_max, row_sum), _ = lax.scan(first_pass, start_pair, (key_blocks, pos_blocks))
    log_total = row_max + jnp.log(row_sum)

    def second_pass(running, pieces):
        key_part, value_part, pos_part = pieces
        probs16 = jnp.exp(block_scores(key_part, pos_part) - log_total[..., None]).astype(
            jnp.bfloat16
        )
        return (
            running
            + jnp.einsum("hqk,kd->qhd", probs16, value_part, preferred_element_type=jnp.float32),
            None,
        )

    context_sum, _ = lax.scan(
        second_pass,
        jnp.zeros((rows_here, head_count, head_width), jnp.float32),
        (key_blocks, value_blocks, pos_blocks),
    )
    context16 = context_sum.astype(jnp.bfloat16)
    row_delta = jnp.sum(grad_out.astype(jnp.float32) * context16.astype(jnp.float32), axis=2).T

    def third_pass(grad_q, pieces):
        key_part, value_part, pos_part = pieces
        probs = jnp.exp(block_scores(key_part, pos_part) - log_total[..., None])
        probs16 = probs.astype(jnp.bfloat16)
        grad_probs = jnp.einsum(
            "qhd,kd->hqk", grad_out, value_part, preferred_element_type=jnp.float32
        )
        grad_scores = (probs * (grad_probs - row_delta[..., None]) * score_scale).astype(
            jnp.bfloat16
        )
        new_grad_q = grad_q + jnp.einsum(
            "hqk,kd->qhd", grad_scores, key_part, preferred_element_type=jnp.float32
        )
        grad_k = jnp.einsum("hqk,qhd->kd", grad_scores, query16, preferred_element_type=jnp.float32)
        grad_v = jnp.einsum("hqk,qhd->kd", probs16, grad_out, preferred_element_type=jnp.float32)
        return (new_grad_q, jnp.concatenate([grad_k, grad_v], axis=1))

    grad_q, key_terms = lax.scan(
        third_pass,
        jnp.zeros((rows_here, head_count, head_width), jnp.float32),
        (key_blocks, value_blocks, pos_blocks),
    )
    return (context16, grad_q, key_terms.reshape(-1, 2 * head_width))


def local(hidden_states, block_order, w_query, w_key, w_value, gain_query, gain_key, cotangent):
    tokens = hidden_states[0]
    tok_rows = tokens.shape[0]
    half_rows = tok_rows // 2
    head_width = gain_query.shape[0]
    head_count = w_query.shape[1] // head_width
    q_cols = head_count * head_width
    ctx_index = lax.axis_index("ctx")
    own_slots = lax.dynamic_slice_in_dim(block_order, 2 * ctx_index, 2)
    offsets = jnp.arange(half_rows, dtype=jnp.int32)
    query_pos = (own_slots[:, None] * half_rows + offsets[None, :]).reshape(tok_rows)
    key_pos_all = (block_order[:, None] * half_rows + offsets[None, :]).reshape(-1)
    full_query, full_key, full_value = (
        lax.all_gather(w_query, ("ctx", "dp"), axis=0, tiled=True),
        lax.all_gather(w_key, ("ctx", "dp"), axis=0, tiled=True),
        lax.all_gather(w_value, ("ctx", "dp"), axis=0, tiled=True),
    )
    raw_q = jnp.dot(tokens, full_query, preferred_element_type=jnp.float32).reshape(
        tok_rows, head_count, head_width
    )
    raw_k = jnp.dot(tokens, full_key, preferred_element_type=jnp.float32)[:, None, :]
    raw_v = jnp.dot(tokens, full_value, preferred_element_type=jnp.float32)
    cosine, sine = rotation(query_pos, head_width)

    def local_heads(rq, rk, gq, gk):
        return (shape_heads(rq, gq, cosine, sine), shape_heads(rk, gk, cosine, sine))

    (shaped_q, shaped_k), pullback = jax.vjp(local_heads, raw_q, raw_k, gain_query, gain_key)
    query16 = shaped_q.astype(jnp.bfloat16)
    key16 = shaped_k[:, 0, :].astype(jnp.bfloat16)
    value16 = raw_v.astype(jnp.bfloat16)
    all_keys, all_values = (
        lax.all_gather(key16, "ctx", axis=0, tiled=True),
        lax.all_gather(value16, "ctx", axis=0, tiled=True),
    )
    keys_len = all_keys.shape[0]
    key_block = math.gcd(keys_len, 512)
    blocks = keys_len // key_block
    grad_out = cotangent[0].reshape(tok_rows, head_count, head_width)
    context16, grad_q, key_terms = attend(
        query16,
        query_pos,
        grad_out,
        all_keys.reshape(blocks, key_block, head_width),
        all_values.reshape(blocks, key_block, head_width),
        key_pos_all.reshape(blocks, key_block),
    )
    own_kv = lax.psum_scatter(
        key_terms.astype(jnp.bfloat16), "ctx", scatter_dimension=0, tiled=True
    ).astype(jnp.float32)
    grad_raw_q, grad_raw_k, grad_gq, grad_gk = pullback((grad_q, own_kv[:, None, :head_width]))
    grad_rows = jnp.concatenate(
        [grad_raw_q.reshape(tok_rows, q_cols), grad_raw_k[:, 0, :], own_kv[:, head_width:]], axis=1
    ).astype(jnp.bfloat16)
    contract = (((1,), (1,)), ((), ()))
    grad_tokens = lax.dot_general(
        grad_rows[:, :q_cols], full_query, contract, preferred_element_type=jnp.float32
    )
    grad_tokens = grad_tokens + lax.dot_general(
        grad_rows[:, q_cols : q_cols + head_width],
        full_key,
        contract,
        preferred_element_type=jnp.float32,
    )
    grad_tokens = grad_tokens + lax.dot_general(
        grad_rows[:, q_cols + head_width :],
        full_value,
        contract,
        preferred_element_type=jnp.float32,
    )
    grad_states = grad_tokens.astype(jnp.bfloat16)
    own_grads = lax.psum_scatter(
        lax.dot_general(
            tokens, grad_rows, (((0,), (0,)), ((), ())), preferred_element_type=jnp.float32
        ),
        ("ctx", "dp"),
        scatter_dimension=0,
        tiled=True,
    )
    gain_sums = lax.psum((grad_gq, grad_gk), ("ctx", "dp"))
    return (
        context16.reshape(1, tok_rows, q_cols),
        grad_states[None],
        own_grads[:, :q_cols],
        own_grads[:, q_cols : q_cols + head_width],
        own_grads[:, q_cols + head_width :],
        gain_sums[0],
        gain_sums[1],
    )


def solution(mesh):
    in_specs = (
        P("dp", "ctx", None),
        P(),
        P(("ctx", "dp"), None),
        P(("ctx", "dp"), None),
        P(("ctx", "dp"), None),
        P(),
        P(),
        P("dp", "ctx", None),
    )
    out_specs = (
        P("dp", "ctx", None),
        P("dp", "ctx", None),
        P(("ctx", "dp"), None),
        P(("ctx", "dp"), None),
        P(("ctx", "dp"), None),
        P(),
        P(),
    )
    return jax.shard_map(local, mesh=mesh, in_specs=in_specs, out_specs=out_specs, check_vma=False)
```

profile of v0, /device:TPU:39, one launch (start us, length us, event | category | flops | bytes accessed | tf_op | source)
XLA Modules:
  0.0 1013.5 jit_solution(1392421694397586980)
XLA Ops:
  10.4 64.6 %all-gather.10.cloned.1.call-done = bf16[5120,128]{1,0:T(8,128)(2,1)} async-done(((bf16[40,128]{1,0:T(8,128)(2,1)}), bf16[5120,128]{1,0:T(8,128)(2,1)}) %all-gather.10.cloned.1.call-update) | async-done | bytes 1310736 | tf_op jit(solution)/shard_map/all_gather | solution.py:116
  81.3 57.9 %all-gather.6.cloned.1.call-done = bf16[5120,128]{1,0:T(8,128)(2,1)} async-done(((bf16[40,128]{1,0:T(8,128)(2,1)}), bf16[5120,128]{1,0:T(8,128)(2,1)}) %all-gather.6.cloned.1.call-update) | async-done | bytes 1310736 | tf_op jit(solution)/shard_map/all_gather | solution.py:117
  142.1 66.0 %all-gather.12.cloned.1.call-done = bf16[8192,128]{0,1:T(8,128)(2,1)} async-done(((bf16[256,128]{0,1:T(8,128)(2,1)}), bf16[8192,128]{0,1:T(8,128)(2,1)}) %all-gather.12.cloned.1.call-update) | async-done | bytes 2097168 | tf_op jit(solution)/shard_map/all_gather | solution.py:134
  208.1 4.1 copy.84
  212.1 66.9 %all-gather.14.cloned.1.call-done = bf16[5120,512]{1,0:T(8,128)(2,1)} async-done(((bf16[40,512]{1,0:T(8,128)(2,1)}), bf16[5120,512]{1,0:T(8,128)(2,1)}) %all-gather.14.cloned.1.call-update) | async-done | bytes 5242896 | tf_op jit(solution)/shard_map/all_gather | solution.py:115
  279.0 7.8 copy.60
  286.9 4.1 multiply_reduce_fusion.3
  294.7 58.3 %while.37 = (s32[]{:T(128)}, f32[4,256]{1,0:T(4,128)S(1)}, f32[4,256]{1,0:T(4,128)S(1)}, s32[16,512]{1,0:T(8,128)}, bf16[16,512,128]{2,1,0:T(8,128)(2,1)}, /*ind...) while((s32[]{:T(128)}, f32[4,256]{1,0:T(4,128)S(1)}, f32[4,256]{1,0:T(4,128)S(1)}, ...), condition=%wide.region_5.6_spmd.clone, body=%wide.region_2.5_spmd.clone.sunk | while | flops 138024192 | bytes 5042304 | solution.py:55
  353.6 83.1 %while.38 = (s32[]{:T(128)}, f32[256,4,128]{0,2,1:T(8,128)}, bf16[16,512,128]{2,1,0:T(8,128)(2,1)}, s32[16,512]{1,0:T(8,128)}, bf16[16,512,128]{2,1,0:T(8,128)(2...) while((s32[]{:T(128)}, f32[256,4,128]{0,2,1:T(8,128)}, ...), condition=%wide.region_7.8_spmd.clone, body=%wide.region_6.7_spmd.clone.sunk | while | flops 270926080 | bytes 1848962 | solution.py:69
  360.9 3.0 fusion.131
  366.1 3.0 fusion.131
  371.3 3.0 fusion.131
  376.5 3.0 fusion.131
  381.7 3.0 fusion.131
  386.9 3.0 fusion.131
  392.1 3.0 fusion.131
  397.3 3.0 fusion.131
  402.5 3.0 fusion.131
  407.7 3.0 fusion.131
  412.9 3.0 fusion.131
  418.2 3.0 fusion.131
  423.4 3.0 fusion.131
  433.8 3.0 fusion.131
  438.5 121.9 %while.39 = (s32[]{:T(128)}, f32[256,4,128]{0,2,1:T(8,128)S(1)}, bf16[16,512,256]{1,2,0:T(8,128)(2,1)}, bf16[16,512,128]{2,1,0:T(8,128)(2,1)}, s32[16,512]{1,0:T...) while((s32[]{:T(128)}, f32[256,4,128]{0,2,1:T(8,128)S(1)}, ...), condition=%wide.region_10.11_spmd.clone, body=%wide.region_9.10_spmd.clone.sunk | while | flops 676200704 | bytes 14041287 | solution.py:94
  560.5 4.7 copy.89
  567.4 157.9 %reduce-scatter.5.cloned.1.call-done = bf16[256,256]{0,1:T(8,128)(2,1)} async-done(((bf16[8192,256]{0,1:T(8,128)(2,1)}), bf16[256,256]{0,1:T(8,128)(2,1)}) %reduce-scatter.5.cloned.1.call-update) | async-done | bytes 131088 | tf_op jit(solution)/shard_map/reduce_scatter | solution.py:149
  728.9 7.7 convolution_bitcast_fusion.3
  736.7 15.6 %copy.82 = f32[5120,768]{1,0:T(8,128)} copy(f32[5120,768]{0,1:T(8,128)} %convolution_bitcast_fusion.3) | data formatting | bytes 31457280
  754.1 6.3 fusion.87
  760.4 91.9 %all-reduce.4 = (f32[128]{0:T(128)}, f32[128]{0:T(128)}) all-reduce(f32[128]{0:T(128)S(1)} %copy-done.23, f32[128]{0:T(128)S(1)} %get-tuple-element.347), channel_id=1, replica_groups=mesh['ctx'=32,'dp'=4] {'ctx','dp'}, use_global_device_ids=true, to_apply=%region_16.17 | all-reduce | flops 256 | bytes 2048 | tf_op jit(solution)/shard_map/psum | solution.py:181
  852.3 4.0 convolution_add_fusion.1
  858.7 145.0 %reduce-scatter.7.cloned.1.call-done = f32[40,768]{1,0:T(8,128)} async-done(((f32[5120,768]{1,0:T(8,128)}), f32[40,768]{1,0:T(8,128)}) %reduce-scatter.7.cloned.1.call-update) | async-done | bytes 122896
  (462 shorter events, 251.2 us)
Async XLA Ops:
  7.2 67.8 %copy-start = (bf16[1,256,5120]{2,1,0:T(8,128)(2,1)S(1)}, bf16[1,256,5120]{2,1,0:T(8,128)(2,1)}, u32[]{:S(2)}) copy-start(bf16[1,256,5120]{2,1,0:T(8,128)(2,1)} %param.14) | copy-start | bytes 7864324
  7.2 67.8 %all-gather.10.cloned.1.call-start = ((), (), s32[]{:S(2)}) async-start(), calls=%async_computation.4 | async-start | bytes 1320960 | tf_op jit(solution)/shard_map/all_gather | solution.py:116
  7.9 131.3 %all-gather.6.cloned.1.call-start = ((), (), s32[]{:S(2)}) async-start(), calls=%async_computation.2 | async-start | bytes 1320960 | tf_op jit(solution)/shard_map/all_gather | solution.py:117
  8.7 199.4 %all-gather.12.cloned.1.call-start = ((), (), s32[]{:S(2)}) async-start(), calls=%async_computation.5 | async-start | bytes 2162688 | tf_op jit(solution)/shard_map/all_gather | solution.py:134
  10.0 67.8 %copy-start.19 = (f32[128]{0:T(128)S(1)}, f32[128]{0:T(128)}, u32[]{:S(2)}) copy-start(f32[128]{0:T(128)} %param.20) | copy-start | bytes 1540
  10.4 67.6 %copy-start.9 = (f32[256,64]{0,1:T(8,128)}, f32[256,64]{0,1:T(8,128)S(1)}, u32[]{:S(2)}) copy-start(f32[256,64]{0,1:T(8,128)S(1)} %get-tuple-element.421) | copy-start | bytes 196612
  10.4 67.6 %copy-start.13 = (f32[256,64]{0,1:T(8,128)}, f32[256,64]{0,1:T(8,128)S(1)}, u32[]{:S(2)}) copy-start(f32[256,64]{0,1:T(8,128)S(1)} %get-tuple-element.422) | copy-start | bytes 196612
  10.4 69.0 %copy-start.24 = (s32[64]{0:T(128)S(1)}, s32[64]{0:T(128)}, u32[]{:S(2)}) copy-start(s32[64]{0:T(128)} %param.15) | copy-start | bytes 772
  77.8 1.6 copy-start.15
  78.7 200.3 %all-gather.14.cloned.1.call-start = ((), (), s32[]{:S(2)}) async-start(), calls=%async_computation.6 | async-start | bytes 5283840 | tf_op jit(solution)/shard_map/all_gather | solution.py:115
  79.3 274.3 %all-gather.8.cloned.1.call-start = ((), (), s32[]{:S(2)}) async-start(), calls=%async_computation.3 | async-start | bytes 2162688 | tf_op jit(solution)/shard_map/all_gather | solution.py:135
  142.0 583.2 %reduce-scatter.5.cloned.1.call-start = ((), (), s32[]{:S(2)}) async-start(), calls=%async_computation.7 | async-start | bytes 4325376 | tf_op jit(solution)/shard_map/reduce_scatter | solution.py:149
  286.9 4.1 copy-start.21
  449.9 1.4 copy-start.1
  465.1 1.4 copy-start.1
  472.7 1.4 copy-start.1
  480.3 1.4 copy-start.1
  487.9 1.4 copy-start.1
  495.5 1.4 copy-start.1
  518.4 1.4 copy-start.1
  526.0 1.4 copy-start.1
  541.3 1.4 copy-start.1
  556.6 1.4 copy-start.1
  565.2 438.6 %reduce-scatter.7.cloned.1.call-start = ((), (), s32[]{:S(2)}) async-start(), calls=%async_computation.8 | async-start | bytes 15851520
  566.1 159.1 %copy-start.14 = (f32[256,64]{0,1:T(8,128)S(1)}, f32[256,64]{0,1:T(8,128)}, u32[]{:S(2)}) copy-start(f32[256,64]{0,1:T(8,128)} %copy-done.13) | copy-start | bytes 196612
  566.2 160.0 %copy-start.10 = (f32[256,64]{0,1:T(8,128)S(1)}, f32[256,64]{0,1:T(8,128)}, u32[]{:S(2)}) copy-start(f32[256,64]{0,1:T(8,128)} %copy-done.9) | copy-start | bytes 196612
  566.2 160.0 %copy-start.16 = (f32[256]{0:T(256)S(1)}, f32[256]{0:T(256)}, u32[]{:S(2)}) copy-start(f32[256]{0:T(256)} %copy-done.15) | copy-start | bytes 3076
  567.2 159.9 %copy-start.18 = (f32[256]{0:T(256)S(1)}, f32[256]{0:T(256)}, u32[]{:S(2)}) copy-start(f32[256]{0:T(256)} %copy-done.17) | copy-start | bytes 3076
  567.2 160.8 %copy-start.20 = (f32[128]{0:T(128)S(1)}, f32[128]{0:T(128)}, u32[]{:S(2)}) copy-start(f32[128]{0:T(128)} %param.20) | copy-start | bytes 1540
  754.1 6.3 copy-start.23
  852.3 4.0 copy-start.4
  852.3 4.0 copy-start.12
  (16 other events, 17.5 us)
Sparse Core Ops, SparseCore 0:
  10.8 64.0 all-gather.9
  77.7 61.4 all-gather.5
  142.6 65.4 all-gather.11
  210.9 68.0 all-gather.13
  282.4 66.4 all-gather.7
  565.3 159.8 reduce-scatter.4
  752.4 251.2 reduce-scatter.6
where the time goes:
time: 1020 us; the launch traced here: 1010 us
  waiting for transfers between devices  560 us (55%)
  matrix products  185 us (18%)
  blocking collectives  91.9 us (9%)
  other arithmetic  81.5 us (8%)
  local copies, waits for them, and re-layouts  78.5 us (8%)
  between operations  14.5 us (1%)
    reduce_scatter x1, waiting for transfers between devices, local(): lax.psum_scatter(key_terms.astype(jnp.bfloat16), 'ctx', scatter_dimension...  158 us
    unnamed x8, waiting for transfers between devices  147 us
    psum x1, blocking collectives, local(): gain_sums = lax.psum((grad_gq, grad_gk), ('ctx', 'dp'))  91.9 us
    all_gather x1, waiting for transfers between devices, local(): lax.all_gather(w_query, ('ctx', 'dp'), axis=0, tiled=True)  66.9 us
    all_gather x1, waiting for transfers between devices, local(): lax.all_gather(key16, 'ctx', axis=0, tiled=True)  66 us
    all_gather x1, waiting for transfers between devices, local(): lax.all_gather(w_key, ('ctx', 'dp'), axis=0, tiled=True)  64.6 us
    all_gather x1, waiting for transfers between devices, local(): lax.all_gather(w_value, ('ctx', 'dp'), axis=0, tiled=True)  57.9 us
    le x96, other arithmetic, block_scores(): allowed = pos_part[None, :] <= query_pos[:, None]  52.2 us
  transfers between devices with their start and end apart: 7, of which 6 were waited for; matrix products, arithmetic and copies ran while one was open for 10% of the time, Pallas kernels for 0%

commit v1 on v0

v1 whole, which is shorter than its diff:
```python
import math

import jax
import jax.numpy as jnp
from jax import lax
from jax.experimental import pallas as pl
from jax.experimental.pallas import tpu as pltpu
from jax.sharding import Mesh
from jax.sharding import PartitionSpec as P

bf16, f32 = jnp.bfloat16, jnp.float32
theta = 1000000.0
floor_score = -1e30
span = 128
chunk = 512
per_chunk = chunk // span
mib = 2**20
smem = pl.BlockSpec(memory_space=pltpu.SMEM)
vmem = pl.BlockSpec(memory_space=pltpu.VMEM)


def mm(a, b):
    return jnp.dot(a, b, preferred_element_type=f32)


def rotation(positions, head_width):
    steps_half = jnp.arange(head_width // 2, dtype=f32)
    inverse = jnp.power(f32(theta), -2.0 * steps_half / head_width)
    angles = positions.astype(f32)[:, None] * inverse[None, :]
    cosine = jnp.cos(angles)
    sine = jnp.sin(angles)
    return jnp.concatenate([cosine, cosine], 1), jnp.concatenate([-sine, sine], 1)


def inverse_norm(raw):
    return lax.rsqrt(jnp.mean(raw * raw, axis=-1, keepdims=True) + 1e-06)


def shape_head(raw, gain, cosine, sine):
    normed = raw * inverse_norm(raw) * gain
    return normed * cosine + pltpu.roll(normed, span // 2, 1) * sine


def shape_head_grad(raw, gain, cosine, sine, grad):
    inverse = inverse_norm(raw)
    grad_normed = grad * cosine + pltpu.roll(grad * sine, span // 2, 1)
    grad_unit = grad_normed * gain
    unit = raw * inverse
    shrink = jnp.mean(grad_unit * unit, axis=-1, keepdims=True)
    return inverse * (grad_unit - unit * shrink), grad_normed * unit


def key_value_kernel(tok_ref, w_ref, gain_ref, cos_ref, sin_ref, kv_ref):
    raw = mm(tok_ref[...], w_ref[...])
    kv_ref[:, :span] = shape_head(raw[:, :span], gain_ref[...], cos_ref[...], sin_ref[...]).astype(bf16)
    kv_ref[:, span:] = raw[:, span:].astype(bf16)


def query_kernel(tok_ref, wq_ref, wkv_ref, gain_ref, cos_ref, sin_ref, q_ref, raw_ref):
    cols = wq_ref.shape[1]
    raw_ref[:, :cols] = mm(tok_ref[...], wq_ref[...])
    raw_ref[:, cols:] = mm(tok_ref[...], wkv_ref[...])[:, :span]
    gain = gain_ref[...] * (span**-0.5 / math.log(2.0))
    for h in range(cols // span):
        part = slice(h * span, (h + 1) * span)
        q_ref[:, part] = shape_head(raw_ref[:, part], gain, cos_ref[...], sin_ref[...]).astype(bf16)


def attention_kernel(
    order, own, q_ref, g_ref, kv_ref, kv_other_ref, ctx_ref, dq_ref, dkv_ref, dkv_other_ref,
    slot_of, ks, vs, kt, vt, acc_kv, qs, gs, qt, gt, acc_o, row_max, row_sum, row_delta, acc_q,
):
    spans, heads = order.shape[0], q_ref.shape[1] // span
    chunks = spans // per_chunk
    rows = heads * span
    core = own[2]

    def place(slot, carry):
        slot_of[order[slot]] = slot
        return carry

    lax.fori_loop(0, spans, place, 0)

    def arrange(c, carry):
        for j in range(per_chunk):
            slot = slot_of[c * per_chunk + j]
            pair, rows_at = slot // 4, pl.multiple_of(slot % 2 * span, span)
            mine = (slot // 2) % 2 == core
            both = jnp.where(
                mine, kv_ref[pair, pl.ds(rows_at, span), :], kv_other_ref[pair, pl.ds(rows_at, span), :]
            )
            part = slice(j * span, (j + 1) * span)
            ks[c, part, :] = both[:, :span]
            vs[c, part, :] = both[:, span:]
            kt[c, :, part] = both[:, :span].T
            vt[c, :, part] = both[:, span:].T
        acc_kv[c] = jnp.zeros_like(acc_kv[c])
        return carry

    lax.fori_loop(0, chunks, arrange, 0)

    first_upper = own[0] > own[1]
    for upper in (True, False):
        which = jnp.where(first_upper, 0, 1) if upper else jnp.where(first_upper, 1, 0)
        block = own[which]
        row0 = pl.multiple_of(which * span, span)
        last = block // per_chunk
        for h in range(heads):
            part = slice(h * span, (h + 1) * span)
            qh = q_ref[pl.ds(row0, span), part]
            gh = g_ref[pl.ds(row0, span), part]
            qs[part, :] = qh
            gs[part, :] = gh
            qt[:, part] = qh.T
            gt[:, part] = gh.T

        def allowed(c):
            key_pos = c * chunk + lax.broadcasted_iota(jnp.int32, (chunk, rows), 0)
            row = lax.broadcasted_iota(jnp.int32, (chunk, rows), 1)
            return key_pos <= block * span + jnp.bitwise_and(row, span - 1)

        row_max[...] = jnp.full_like(row_max, floor_score)
        row_sum[...] = jnp.zeros_like(row_sum)
        acc_o[...] = jnp.zeros_like(acc_o)

        def forward(c, masked):
            s = mm(ks[c], qt[...])
            if masked:
                s = jnp.where(allowed(c), s, floor_score)
            old = row_max[...]
            new = jnp.maximum(old, jnp.max(s, axis=0, keepdims=True))
            p = jnp.exp2(s - new)
            alpha = jnp.exp2(old - new)
            row_max[...] = new
            row_sum[...] = row_sum[...] * alpha + jnp.sum(p, axis=0, keepdims=True)
            acc_o[...] = acc_o[...] * alpha + mm(vt[c], p.astype(bf16))

        def forward_step(c, carry):
            forward(c, False)
            return carry

        lax.fori_loop(0, last, forward_step, 0)
        forward(last, True)

        total = row_sum[...]
        ctx_t = (acc_o[...] / total).astype(bf16)
        row_max[...] = row_max[...] + jnp.log2(total)
        row_delta[...] = jnp.sum(ctx_t.astype(f32) * gt[...].astype(f32), axis=0, keepdims=True)
        for h in range(heads):
            part = slice(h * span, (h + 1) * span)
            ctx_ref[pl.ds(row0, span), part] = ctx_t[:, part].T
        acc_q[...] = jnp.zeros_like(acc_q)

        def backward(c, masked):
            s = mm(ks[c], qt[...])
            p = jnp.exp2(s - row_max[...])
            if masked:
                p = jnp.where(allowed(c), p, 0.0)
            dp = mm(vs[c], gt[...])
            ds = (p * (dp - row_delta[...])).astype(bf16)
            acc_kv[c, :, span:] += mm(p.astype(bf16), gs[...])
            acc_kv[c, :, :span] += mm(ds, qs[...])
            acc_q[...] += mm(kt[c], ds)

        def backward_step(c, carry):
            backward(c, False)
            return carry

        lax.fori_loop(0, last, backward_step, 0)
        backward(last, True)
        for h in range(heads):
            part = slice(h * span, (h + 1) * span)
            dq_ref[pl.ds(row0, span), part] = acc_q[:, part].T * (span**-0.5)

    def give(c, carry):
        for j in range(per_chunk):
            part = slice(j * span, (j + 1) * span)
            slot = slot_of[c * per_chunk + j]
            pair, rows_at = slot // 4, pl.multiple_of(slot % 2 * span, span)
            mine = (slot // 2) % 2 == core
            dk = (acc_kv[c, part, :span] * math.log(2.0)).astype(bf16)
            dv = acc_kv[c, part, span:].astype(bf16)

            @pl.when(mine)
            def _():
                dkv_ref[pair, pl.ds(rows_at, span), :span] = dk
                dkv_ref[pair, pl.ds(rows_at, span), span:] = dv

            @pl.when(jnp.logical_not(mine))
            def _():
                dkv_other_ref[pair, pl.ds(rows_at, span), :span] = dk
                dkv_other_ref[pair, pl.ds(rows_at, span), span:] = dv

        return carry

    lax.fori_loop(0, chunks, give, 0)


def attention(order, own, q16, g16, kv, kv_other):
    rows_here, cols = q16.shape
    spans = order.shape[0]
    chunks = spans // per_chunk
    rows = cols
    share = jax.ShapeDtypeStruct(kv.shape, bf16)
    return pl.pallas_call(
        attention_kernel,
        out_shape=(
            jax.ShapeDtypeStruct((rows_here, cols), bf16),
            jax.ShapeDtypeStruct((rows_here, cols), f32),
            share,
            share,
        ),
        in_specs=[smem, smem] + [vmem] * 4,
        out_specs=(vmem,) * 4,
        scratch_shapes=[
            pltpu.SMEM((spans,), jnp.int32),
            pltpu.VMEM((chunks, chunk, span), bf16),
            pltpu.VMEM((chunks, chunk, span), bf16),
            pltpu.VMEM((chunks, span, chunk), bf16),
            pltpu.VMEM((chunks, span, chunk), bf16),
            pltpu.VMEM((chunks, chunk, 2 * span), f32),
            pltpu.VMEM((rows, span), bf16),
            pltpu.VMEM((rows, span), bf16),
            pltpu.VMEM((span, rows), bf16),
            pltpu.VMEM((span, rows), bf16),
            pltpu.VMEM((span, rows), f32),
            pltpu.VMEM((1, rows), f32),
            pltpu.VMEM((1, rows), f32),
            pltpu.VMEM((1, rows), f32),
            pltpu.VMEM((span, rows), f32),
        ],
        compiler_params=pltpu.CompilerParams(vmem_limit_bytes=48 * mib),
        cost_estimate=pl.CostEstimate(
            flops=8 * 10**9, bytes_accessed=10 * 10**6, transcendentals=9 * 10**6
        ),
        name="attention",
    )(order, own, q16, g16, kv, kv_other)


def grad_rows_kernel(raw_ref, dq_ref, dkv_ref, gq_ref, gk_ref, cos_ref, sin_ref, g_ref, gain_ref):
    cols = dq_ref.shape[1]
    cosine, sine = cos_ref[...], sin_ref[...]
    gain_q = jnp.zeros((1, span), f32)
    for h in range(cols // span):
        part = slice(h * span, (h + 1) * span)
        grad, terms = shape_head_grad(raw_ref[:, part], gq_ref[...], cosine, sine, dq_ref[:, part])
        g_ref[:, part] = grad.astype(bf16)
        gain_q = gain_q + jnp.sum(terms, axis=0, keepdims=True)
    dkv = jnp.sum(dkv_ref[...].astype(f32), axis=0)
    grad, terms = shape_head_grad(raw_ref[:, cols:], gk_ref[...], cosine, sine, dkv[:, :span])
    g_ref[:, cols : cols + span] = grad.astype(bf16)
    g_ref[:, cols + span :] = dkv[:, span:].astype(bf16)
    gain_k = jnp.sum(terms, axis=0, keepdims=True)
    pieces = []
    for gain in (gain_q, gain_k):
        high = gain.astype(bf16).astype(f32)
        pieces += [high, gain - high]
    row = jnp.concatenate(pieces + [jnp.zeros((1, 2 * span), f32)], axis=1)
    gain_ref[...] = jnp.where(lax.broadcasted_iota(jnp.int32, gain_ref.shape, 0) == 0, row, 0.0)


def weight_grad_kernel(mine_ref, other_ref, g_ref, g_other_ref, gain_ref, out_ref):
    total = mm(mine_ref[...], g_ref[...]) + mm(other_ref[...], g_other_ref[...])
    owners, padded = out_ref.shape[0], out_ref.shape[1]
    own_rows = padded - gain_ref.shape[0]
    for i in range(owners):
        part = total[i * own_rows : (i + 1) * own_rows]
        out_ref[i] = jnp.concatenate([part, gain_ref[...]], axis=0).astype(bf16)


def weight_grad(mine, other, g, g_other, gains, owners):
    rows, cols = mine.shape[0] // owners, g.shape[1]
    padded = rows + gains.shape[0]
    step = math.gcd(owners, 16)
    toks = mine.shape[1]
    whole = lambda shape: pl.BlockSpec(shape, lambda i: (0,) * len(shape))
    return pl.pallas_call(
        weight_grad_kernel,
        grid=(owners // step,),
        out_shape=jax.ShapeDtypeStruct((owners, padded, cols), bf16),
        in_specs=[
            pl.BlockSpec((step * rows, toks), lambda i: (i, 0)),
            pl.BlockSpec((step * rows, toks), lambda i: (i, 0)),
            whole(g.shape),
            whole(g.shape),
            whole(gains.shape),
        ],
        out_specs=pl.BlockSpec((step, padded, cols), lambda i: (i, 0, 0)),
        compiler_params=pltpu.CompilerParams(vmem_limit_bytes=40 * mib),
        name="weight_grad",
    )(mine, other, g, g_other, gains)


def call(kernel, shapes, *args, name):
    return pl.pallas_call(
        kernel,
        out_shape=shapes,
        in_specs=[vmem] * len(args),
        out_specs=jax.tree.map(lambda _: vmem, shapes),
        compiler_params=pltpu.CompilerParams(vmem_limit_bytes=48 * mib),
        name=name,
    )(*args)


plane = ("x", "z")
chips = ("x", "z", "y_hi", "y_lo")
swapped = [(0, 0), (1, 2), (2, 1), (3, 3)]
flipped = [(0, 1), (1, 0)]


def swap(array):
    return lax.ppermute(array, ("y_hi", "core"), swapped)


def flip(array):
    return lax.ppermute(array, "core", flipped)


def to_all(array, axes, count):
    return lax.all_to_all(jnp.broadcast_to(array[None], (count,) + array.shape), axes, 0, 0)


def pick(array, index, axis):
    return lax.dynamic_index_in_dim(array, index, axis, keepdims=False)


def local(hidden_states, block_order, w_query, w_key, w_value, gain_query, gain_key, cotangent):
    tokens = hidden_states[0]
    tok_rows, width = tokens.shape
    q_cols = w_query.shape[1]
    own_rows = w_query.shape[0]
    chip_count = width // own_rows // 2
    pairs = 16
    at_x, at_z = lax.axis_index("x"), lax.axis_index("z")
    y_hi, core = lax.axis_index("y_hi"), lax.axis_index("core")
    offsets = jnp.arange(span, dtype=jnp.int32)

    def slots_of(half):
        place = (at_x * 4 + at_z) * 2 + half
        blocks = lax.dynamic_slice_in_dim(block_order, 2 * place, 2)
        positions = (blocks[:, None] * span + offsets[None, :]).reshape(tok_rows)
        return blocks, rotation(positions, span)

    _, (cos_kv, sin_kv) = slots_of(y_hi)
    own_blocks, (cosine, sine) = slots_of(core)
    own = jnp.concatenate([own_blocks, core[None].astype(jnp.int32)])
    gain_q, gain_k = gain_query[None, :], gain_key[None, :]

    w_kv = jnp.concatenate([w_key, w_value], axis=1)
    kv_mine = to_all(w_kv, chips, chip_count)
    kv_theirs = flip(kv_mine)
    full_query = lax.all_gather(
        w_query, ("x", "z", "y_hi", "y_lo", "core"), axis=0, tiled=True
    )
    lower = jnp.where(core == 0, kv_mine, kv_theirs)
    upper = jnp.where(core == 0, kv_theirs, kv_mine)
    full_kv = jnp.stack([lower, upper], axis=1).reshape(width, 2 * span)

    toks = swap(tokens)
    grad_out = swap(cotangent[0])

    kv16 = call(
        key_value_kernel,
        jax.ShapeDtypeStruct((tok_rows, 2 * span), bf16),
        tokens, full_kv, gain_k, cos_kv, sin_kv,
        name="key_value",
    )
    kv_own = to_all(swap(kv16), plane, pairs)
    kv_other = flip(kv_own)

    q16, raw = call(
        query_kernel,
        (
            jax.ShapeDtypeStruct((tok_rows, q_cols), bf16),
            jax.ShapeDtypeStruct((tok_rows, q_cols + span), f32),
        ),
        toks, full_query, full_kv, gain_q, cosine, sine,
        name="query",
    )
    turned = toks.T.reshape(chip_count, 2, own_rows, tok_rows)
    turned_mine = pick(turned, core, 1).reshape(-1, tok_rows)
    turned_other = flip(pick(turned, 1 - core, 1).reshape(-1, tok_rows))

    ctx, dq, dkv_mine, dkv_theirs = attention(block_order, own, q16, grad_out, kv_own, kv_other)
    context = swap(ctx)
    dkv = (dkv_mine.astype(f32) + flip(dkv_theirs).astype(f32)).astype(bf16)
    dkv = lax.all_to_all(dkv, plane, 0, 0)

    grad_rows, gains = call(
        grad_rows_kernel,
        (
            jax.ShapeDtypeStruct((tok_rows, q_cols + 2 * span), bf16),
            jax.ShapeDtypeStruct((8, q_cols + 2 * span), f32),
        ),
        raw, dq, dkv, gain_q, gain_k, cosine, sine,
        name="grad_rows",
    )
    partial = weight_grad(turned_mine, turned_other, grad_rows, flip(grad_rows), gains, chip_count)
    parts = lax.all_to_all(partial, chips, 0, 0)
    sums = jnp.sum(parts.astype(f32), axis=0)
    own_grads = sums[:own_rows]
    gain_row = sums[own_rows, : 4 * span].reshape(2, 2, span).sum(axis=1)
    gain_sums = gain_row + flip(gain_row)

    own_grad_rows = swap(grad_rows)
    contract = (((1,), (1,)), ((), ()))
    grad_tokens = lax.dot_general(
        own_grad_rows[:, :q_cols], full_query, contract, preferred_element_type=f32
    ) + lax.dot_general(own_grad_rows[:, q_cols:], full_kv, contract, preferred_element_type=f32)
    return (
        context[None],
        grad_tokens.astype(bf16)[None],
        own_grads[:, :q_cols],
        own_grads[:, q_cols : q_cols + span],
        own_grads[:, q_cols + span :],
        gain_sums[0],
        gain_sums[1],
    )


def solution(mesh):
    fine = Mesh(mesh.devices.reshape(4, 4, 2, 2, 2), ("x", "z", "y_hi", "y_lo", "core"))
    ctx, dp = ("x", "z", "y_hi"), ("y_lo", "core")
    rows = P(ctx + dp, None)
    tokens = P(dp, ctx, None)
    in_specs = (tokens, P(), rows, rows, rows, P(), P(), tokens)
    out_specs = (tokens, tokens, rows, rows, rows, P(), P())
    return jax.shard_map(local, mesh=fine, in_specs=in_specs, out_specs=out_specs, check_vma=False)
```

time: 1020 us -> 305 us (0.30)
  waiting for transfers between devices: 560 us -> 135 us
  matrix products: 185 us -> 6.47 us
  other arithmetic: 81.5 us -> 7.81 us
  blocking collectives: 91.9 us -> 28.2 us
  local copies, waits for them, and re-layouts: 78.5 us -> 17.7 us
  starting transfers between devices: 0.46 us -> 49 us
  Pallas kernels: 0 us -> 45.1 us
    all_gather x5 -> x1, waiting for transfers between devices: 255 us -> 0.01 us  [local(): lax.all_gather(w_query, ('x', 'z', 'y_hi', 'y_lo', 'core'), axis=0, tiled...]
    dot_general x119 -> x2, matrix products: 185 us -> 6.47 us  [the longest x1 5.6 us: local(): lax.dot_general(own_grad_rows[:, :q_cols], full_query, contract, preferre...]
    reduce_scatter x1 -> x0, waiting for transfers between devices: 158 us -> none  [local(): lax.psum_scatter(key_terms.astype(jnp.bfloat16), 'ctx', scatter_dimension...]
    unnamed x8 -> x1, waiting for transfers between devices: 147 us -> 0.68 us
    ppermute x0 -> x11, waiting for transfers between devices: none -> 95.6 us  [the longest x5 89.2 us: swap(): return lax.ppermute(array, ('y_hi', 'core'), swapped)]
    psum x1 -> x0, blocking collectives: 91.9 us -> none  [local(): gain_sums = lax.psum((grad_gq, grad_gk), ('ctx', 'dp'))]
    le x96 -> x0, other arithmetic: 52.2 us -> none  [block_scores(): allowed = pos_part[None, :] <= query_pos[:, None]]
    pallas_call x0 -> x5, Pallas kernels: none -> 45.1 us  [the longest x1 32.9 us: attention(): pl.pallas_call(attention_kernel, out_shape=(jax.ShapeDtypeStruct((rows_he...]
  transfers between devices with their start and end apart: 7 -> 15, of which waited for: 6 -> 8; matrix products, arithmetic and copies ran while one was open for 10% -> 6% of each run, Pallas kernels for 0% -> 3%
where the time goes in v1:
time: 305 us; the launch traced here: 304 us
  waiting for transfers between devices  135 us (44%)
  starting transfers between devices  49 us (16%)
  Pallas kernels  45.1 us (15%)
  blocking collectives  28.2 us (9%)
  local copies, waits for them, and re-layouts  17.7 us (6%)
  between operations  14.3 us (5%)
  other arithmetic  7.81 us (3%)
  matrix products  6.47 us (2%)
    ppermute x5, waiting for transfers between devices, swap(): return lax.ppermute(array, ('y_hi', 'core'), swapped)  89.2 us
    pallas_call x1, Pallas kernels, attention(): pl.pallas_call(attention_kernel, out_shape=(jax.ShapeDtypeStruct((rows_he...  32.9 us
    all_to_all x1, blocking collectives, to_all(): lax.all_to_all(jnp.broadcast_to(array[None], (count,) + array.shape), axe...  28.2 us
    all_to_all x1, waiting for transfers between devices, local(): dkv = lax.all_to_all(dkv, plane, 0, 0)  21.3 us
    all_to_all x1, waiting for transfers between devices, to_all(): lax.all_to_all(jnp.broadcast_to(array[None], (count,) + array.shape), axe...  17.5 us
    ppermute x5, starting transfers between devices, swap(): return lax.ppermute(array, ('y_hi', 'core'), swapped)  16.4 us
    all_to_all x1, starting transfers between devices, local(): parts = lax.all_to_all(partial, chips, 0, 0)  10.8 us
    pallas_call x3, Pallas kernels, call(): pl.pallas_call(kernel, out_shape=shapes, in_specs=[vmem] * len(args), out...  9.47 us
  transfers between devices with their start and end apart: 15, of which 8 were waited for; matrix products, arithmetic and copies ran while one was open for 6% of the time, Pallas kernels for 3%

profile of v1, /device:TPU:39, one launch (start us, length us, event | category | flops | bytes accessed | tf_op | source)
XLA Modules:
  0.0 303.7 jit_solution(10200328657818629377)
XLA Ops:
  8.7 28.2 %all_to_all.20 = bf16[64,40,256]{2,1,0:T(8,128)(2,1)S(1)} all-to-all(bf16[64,40,256]{2,1,0:T(8,128)(2,1)S(1)} %broadcast_in_dim.15), channel_id=1, replica_groups=mesh['x'=4,'z'=4,'y_hi'=2,'y_lo'=2,'core'=2] {'x','z','y_hi','y_lo'}, dimensions={0} | all-to-all | bytes 2621440 | tf_op jit(solution)/shard_map/all_to_all | solution.py:320
  36.9 2.3 collective-permute-start.1
  40.6 1.3 collective-permute-done.1
  42.3 2.4 copy-done.3
  45.7 2.4 collective-permute-start.3
  48.2 5.3 %collective-permute-done.3 = bf16[256,256]{1,0:T(8,128)(2,1)S(1)} collective-permute-done((bf16[256,256]{1,0:T(8,128)(2,1)S(1)}, bf16[256,256]{1,0:T(8,128)(2,1)S(1)}, u32[]{:S(2)}, u32[]{:S(2)}) %collective-permute-start.3) | collective-permute-done | bytes 131104 | tf_op jit(solution)/shard_map/ppermute | solution.py:312
  53.5 1.6 broadcast_in_dim.18
  55.1 7.8 %all-to-all-start.1 = ((bf16[16,256,256]{2,1,0:T(8,128)(2,1)}), bf16[16,256,256]{2,1,0:T(8,128)(2,1)}, u32[]{:S(2)}, u32[]{:S(2)}) async-start(bf16[16,256,256]{2,1,0:T(8,128)(2,1)} %broadcast_in_dim.18), calls=%async_computation.1 | async-start | bytes 4194304 | tf_op jit(solution)/shard_map/all_to_all | solution.py:320
  62.9 3.2 %collective-permute-start = (bf16[256,5120]{1,0:T(8,128)(2,1)}, bf16[256,5120]{1,0:T(8,128)(2,1)S(1)}, u32[]{:S(2)}, u32[]{:S(2)}) collective-permute-start(bf16[256,5120]{1,0:T(8,128)(2,1)} %bitcast.35), channel_id=1, source_target_pairs={{0,0},{1,4},{4,1},{5,5},{2,2},{3,6},{6,3},{7,7},{8,8},{9,12},{12,9... | collective-permute-start | bytes 7864328 | tf_op jit(solution)/shard_map/ppermute | solution.py:312
  66.1 17.5 %all-to-all-done.1.kv_ref = bf16[16,256,256]{2,1,0:T(8,128)(2,1)} async-done(((bf16[16,256,256]{2,1,0:T(8,128)(2,1)}), bf16[16,256,256]{2,1,0:T(8,128)(2,1)}, u32[]{:S(2)}, u32[]{:S(2)}) %all-to-all-start.1) | async-done | bytes 2097184 | tf_op jit(solution)/shard_map/all_to_all | solution.py:320
  83.6 3.4 %collective-permute-start.2 = (bf16[256,512]{1,0:T(8,128)(2,1)}, bf16[256,512]{1,0:T(8,128)(2,1)}, u32[]{:S(2)}, u32[]{:S(2)}) collective-permute-start(bf16[256,512]{1,0:T(8,128)(2,1)} %bitcast.8), channel_id=1, source_target_pairs={{0,0},{1,4},{4,1},{5,5},{2,2},{3,6},{6,3},{7,7},{8,8},{9,12},{12,9... | collective-permute-start | bytes 786440 | tf_op jit(solution)/shard_map/ppermute | solution.py:312
  87.3 17.3 %collective-permute-done.tok_ref = bf16[256,5120]{1,0:T(8,128)(2,1)S(1)} collective-permute-done((bf16[256,5120]{1,0:T(8,128)(2,1)}, bf16[256,5120]{1,0:T(8,128)(2,1)S(1)}, u32[]{:S(2)}, u32[]{:S(2)}) %collective-permute-start) | collective-permute-done | bytes 2621472 | tf_op jit(solution)/shard_map/ppermute | solution.py:312
  104.6 5.8 %query.1 = (bf16[256,512]{1,0:T(8,128)(2,1)S(1)}, f32[256,640]{1,0:T(8,128)S(1)}) custom-call(bf16[256,5120]{1,0:T(8,128)(2,1)S(1)} %collective-permute-done.tok_ref, bf16[5120,512]{1,0:T(8,128)(2,1)} %all-gather.2.cloned.1.call-done.wq_ref, bf16[5120,256]{1,0:T(8,128)(2,1)} %bitcast.31, f32[1,128]{1,0:T(1,128)S(1)} %bitcast.37, ...), custom_call_target="tpu_custom_call" | custom-call | tf_op jit(solution)/shard_map/query/pallas_call | solution.py:295
  110.5 32.9 %attention.1 = (bf16[256,512]{1,0:T(8,128)(2,1)S(1)}, f32[256,512]{1,0:T(8,128)S(1)}, bf16[16,256,256]{2,1,0:T(8,128)(2,1)S(1)}, bf16[16,256,256]{2,1,0:T(8,128)(2,1)S(1)}) custom-call(s32[64]{0:T(128)S(1)} %copy-done.9, s32[3]{0:T(128)S(1)} %pad_add_fusion.own, bf16[256,512]{1,0:T(8,128)(2,1)S(1)} %get-tuple-element.15.q_ref, ...), custom_call_target="tpu_custom_call" | custom-call | flops 8000000000 | bytes 10000000 | tf_op jit(solution)/shard_map/attention/pallas_call | solution.py:205
  145.9 3.8 %collective-permute-done.6 = bf16[16,256,256]{2,1,0:T(8,128)(2,1)S(1)} collective-permute-done((bf16[16,256,256]{2,1,0:T(8,128)(2,1)S(1)}, bf16[16,256,256]{2,1,0:T(8,128)(2,1)S(1)}, u32[]{:S(2)}, u32[]{:S(2)}) %collective-permute-start.6) | collective-permute-done | bytes 2097184 | tf_op jit(solution)/shard_map/ppermute | solution.py:316
  149.7 2.0 add_convert_fusion
  151.7 8.6 %all-to-all-start.2 = ((bf16[16,256,256]{2,1,0:T(8,128)(2,1)}), bf16[16,256,256]{2,1,0:T(8,128)(2,1)}, u32[]{:S(2)}, u32[]{:S(2)}) async-start(bf16[16,256,256]{2,1,0:T(8,128)(2,1)} %add_convert_fusion), calls=%async_computation.2 | async-start | bytes 4194304 | tf_op jit(solution)/shard_map/all_to_all | solution.py:387
  160.2 2.6 copy.19
  162.8 3.0 constant_dynamic-slice_fusion
  166.4 21.3 %all-to-all-done.2.dkv_ref = bf16[16,256,256]{2,1,0:T(8,128)(2,1)} async-done(((bf16[16,256,256]{2,1,0:T(8,128)(2,1)}), bf16[16,256,256]{2,1,0:T(8,128)(2,1)}, u32[]{:S(2)}, u32[]{:S(2)}) %all-to-all-start.2) | async-done | bytes 2097184 | tf_op jit(solution)/shard_map/all_to_all | solution.py:387
  187.7 1.0 copy-done.5
  188.8 2.7 grad_rows.1
  191.4 1.5 collective-permute-start.9
  192.9 1.3 collective-permute-done.9.g_other_ref
  194.2 2.7 weight_grad.1
  197.0 2.2 copy-done.2
  199.9 10.8 %all-to-all-start.3 = ((bf16[64,48,768]{2,1,0:T(8,128)(2,1)}), bf16[64,48,768]{2,1,0:T(8,128)(2,1)}, u32[]{:S(2)}, u32[]{:S(2)}) async-start(bf16[64,48,768]{2,1,0:T(8,128)(2,1)} %copy-done.2), calls=%async_computation.3 | async-start | bytes 9437184 | tf_op jit(solution)/shard_map/all_to_all | solution.py:399
  210.8 5.4 %collective-permute-start.7 = (bf16[256,768]{1,0:T(8,128)(2,1)}, bf16[256,768]{1,0:T(8,128)(2,1)S(1)}, u32[]{:S(2)}, u32[]{:S(2)}) collective-permute-start(bf16[256,768]{1,0:T(8,128)(2,1)} %copy-done.6), channel_id=1, source_target_pairs={{0,0},{1,4},{4,1},{5,5},{2,2},{3,6},{6,3},{7,7},{8,8},{9,12},{12,9... | collective-permute-start | bytes 1179656 | tf_op jit(solution)/shard_map/ppermute | solution.py:312
  216.2 1.9 collective-permute-start.5
  218.2 66.6 %collective-permute-done.5 = bf16[256,512]{1,0:T(8,128)(2,1)S(1)} collective-permute-done((bf16[256,512]{1,0:T(8,128)(2,1)S(1)}, bf16[256,512]{1,0:T(8,128)(2,1)S(1)}, u32[]{:S(2)}, u32[]{:S(2)}) %collective-permute-start.5) | collective-permute-done | bytes 262176 | tf_op jit(solution)/shard_map/ppermute | solution.py:312
  285.6 5.6 %fusion.1 = bf16[1,256,5120]{2,1,0:T(8,128)(2,1)} fusion(f32[256,5120]{1,0:T(8,128)S(1)} %fusion.3, bf16[5120,512]{1,0:T(8,128)(2,1)} %all-gather.2.cloned.1.call-done.wq_ref, bf16[256,768]{1,0:T(8,128)(2,1)S(1)} %collective-permute-done.7), kind=kOutput, calls=%fused_computation.3 | convolution fusion | flops 1344798720 | bytes 13369344 | tf_op jit(solution)/shard_map/dot_general | solution.py:407
  291.2 3.0 convert_reduce_fusion
  (56 shorter events, 11.9 us)
Async XLA Ops:
  7.2 32.0 %copy-start.9 = (s32[64]{0:T(128)S(1)}, s32[64]{0:T(128)}, u32[]{:S(2)}) copy-start(s32[64]{0:T(128)} %order.1) | copy-start | bytes 772
  7.2 97.5 %all-gather.2.cloned.1.call-start = ((), (), s32[]{:S(2)}) async-start(), calls=%async_computation.4 | async-start | bytes 5283840 | tf_op jit(solution)/shard_map/all_gather | solution.py:352
  36.9 4.9 %collective-permute-start.1 = (bf16[64,40,256]{2,1,0:T(8,128)(2,1)S(1)}, bf16[64,40,256]{2,1,0:T(8,128)(2,1)S(1)}, u32[]{:S(2)}, u32[]{:S(2)}) collective-permute-start(bf16[64,40,256]{2,1,0:T(8,128)(2,1)S(1)} %all_to_all.20), channel_id=1, source_target_pairs={{0,1},{1,0},{2,3},{3,2},{4,5},{5,4},{6,7},{7,6},{8,9},{9,8},{10,11... | collective-permute-start | bytes 3932168 | tf_op jit(solution)/shard_map/ppermute | solution.py:316
  42.0 2.7 copy-start.3
  42.0 2.7 copy-start.8
  42.3 3.4 %copy-start = (bf16[64,2,40,256]{3,2,1,0:T(8,128)(2,1)}, bf16[64,2,40,256]{3,2,1,0:T(8,128)(2,1)S(1)}, u32[]{:S(2)}) copy-start(bf16[64,2,40,256]{3,2,1,0:T(8,128)(2,1)S(1)} %pad_maximum_fusion) | copy-start | bytes 7864324
  45.7 7.8 %collective-permute-start.3 = (bf16[256,256]{1,0:T(8,128)(2,1)S(1)}, bf16[256,256]{1,0:T(8,128)(2,1)S(1)}, u32[]{:S(2)}, u32[]{:S(2)}) collective-permute-start(bf16[256,256]{1,0:T(8,128)(2,1)S(1)} %key_value.1), channel_id=1, source_target_pairs={{0,0},{1,4},{4,1},{5,5},{2,2},{3,6},{6,3},{7,7},{8,8},{9,12},{12,9... | collective-permute-start | bytes 393224 | tf_op jit(solution)/shard_map/ppermute | solution.py:312
  55.1 49.5 %copy-start.7 = (f32[128]{0:T(128)S(1)}, f32[128]{0:T(128)}, u32[]{:S(2)}) copy-start(f32[128]{0:T(128)} %param.13) | copy-start | bytes 1540
  55.1 28.5 %all-to-all-start.1 = ((bf16[16,256,256]{2,1,0:T(8,128)(2,1)}), bf16[16,256,256]{2,1,0:T(8,128)(2,1)}, u32[]{:S(2)}, u32[]{:S(2)}) async-start(bf16[16,256,256]{2,1,0:T(8,128)(2,1)} %broadcast_in_dim.18), calls=%async_computation.1 | async-start | bytes 4194304 | tf_op jit(solution)/shard_map/all_to_all | solution.py:320
  62.9 41.7 %collective-permute-start = (bf16[256,5120]{1,0:T(8,128)(2,1)}, bf16[256,5120]{1,0:T(8,128)(2,1)S(1)}, u32[]{:S(2)}, u32[]{:S(2)}) collective-permute-start(bf16[256,5120]{1,0:T(8,128)(2,1)} %bitcast.35), channel_id=1, source_target_pairs={{0,0},{1,4},{4,1},{5,5},{2,2},{3,6},{6,3},{7,7},{8,8},{9,12},{12,9... | collective-permute-start | bytes 7864328 | tf_op jit(solution)/shard_map/ppermute | solution.py:312
  83.6 26.9 %collective-permute-start.4 = (bf16[16,256,256]{2,1,0:T(8,128)(2,1)}, bf16[16,256,256]{2,1,0:T(8,128)(2,1)}, u32[]{:S(2)}, u32[]{:S(2)}) collective-permute-start(bf16[16,256,256]{2,1,0:T(8,128)(2,1)} %all-to-all-done.1.kv_ref), channel_id=1, source_target_pairs={{0,1},{1,0},{2,3},{3,2},{4,5},{5,4},{6,7},{7,6},{8,9},{9,8},{10,11... | collective-permute-start | bytes 6291464 | tf_op jit(solution)/shard_map/ppermute | solution.py:316
  83.6 26.8 %collective-permute-start.2 = (bf16[256,512]{1,0:T(8,128)(2,1)}, bf16[256,512]{1,0:T(8,128)(2,1)}, u32[]{:S(2)}, u32[]{:S(2)}) collective-permute-start(bf16[256,512]{1,0:T(8,128)(2,1)} %bitcast.8), channel_id=1, source_target_pairs={{0,0},{1,4},{4,1},{5,5},{2,2},{3,6},{6,3},{7,7},{8,8},{9,12},{12,9... | collective-permute-start | bytes 786440 | tf_op jit(solution)/shard_map/ppermute | solution.py:312
  143.4 0.8 copy-start.4
  144.2 0.7 copy-start.10
  144.9 4.8 %collective-permute-start.6 = (bf16[16,256,256]{2,1,0:T(8,128)(2,1)S(1)}, bf16[16,256,256]{2,1,0:T(8,128)(2,1)S(1)}, u32[]{:S(2)}, u32[]{:S(2)}) collective-permute-start(bf16[16,256,256]{2,1,0:T(8,128)(2,1)S(1)} %get-tuple-element.20), channel_id=1, source_target_pairs={{0,1},{1,0},{2,3},{3,2},{4,5},{5,4},{6,7},{7,6},{8,9},{9,8},{10,11... | collective-permute-start | bytes 6291464 | tf_op jit(solution)/shard_map/ppermute | solution.py:316
  151.7 36.1 %all-to-all-start.2 = ((bf16[16,256,256]{2,1,0:T(8,128)(2,1)}), bf16[16,256,256]{2,1,0:T(8,128)(2,1)}, u32[]{:S(2)}, u32[]{:S(2)}) async-start(bf16[16,256,256]{2,1,0:T(8,128)(2,1)} %add_convert_fusion), calls=%async_computation.2 | async-start | bytes 4194304 | tf_op jit(solution)/shard_map/all_to_all | solution.py:387
  165.8 27.1 %collective-permute-start.8 = (bf16[2560,256]{1,0:T(8,128)(2,1)}, bf16[2560,256]{1,0:T(8,128)(2,1)S(1)}, u32[]{:S(2)}, u32[]{:S(2)}) collective-permute-start(bf16[2560,256]{1,0:T(8,128)(2,1)} %bitcast.16), channel_id=1, source_target_pairs={{0,1},{1,0},{2,3},{3,2},{4,5},{5,4},{6,7},{7,6},{8,9},{9,8},{10,11... | collective-permute-start | bytes 3932168 | tf_op jit(solution)/shard_map/ppermute | solution.py:316
  187.7 1.0 copy-start.5
  191.4 2.8 collective-permute-start.9
  197.0 2.2 copy-start.2
  199.2 0.8 copy-start.6
  199.9 16.3 %copy-start.11 = (bf16[256,512]{1,0:T(8,128)(2,1)S(1)}, bf16[256,512]{1,0:T(8,128)(2,1)}, u32[]{:S(2)}) copy-start(bf16[256,512]{1,0:T(8,128)(2,1)} %copy-done.10) | copy-start | bytes 786436
  199.9 84.8 %copy-start.1 = (bf16[64,2,40,256]{3,2,1,0:T(8,128)(2,1)S(1)}, bf16[64,2,40,256]{3,2,1,0:T(8,128)(2,1)}, u32[]{:S(2)}) copy-start(bf16[64,2,40,256]{3,2,1,0:T(8,128)(2,1)} %copy-done) | copy-start | bytes 7864324
  199.9 91.3 %all-to-all-start.3 = ((bf16[64,48,768]{2,1,0:T(8,128)(2,1)}), bf16[64,48,768]{2,1,0:T(8,128)(2,1)}, u32[]{:S(2)}, u32[]{:S(2)}) async-start(bf16[64,48,768]{2,1,0:T(8,128)(2,1)} %copy-done.2), calls=%async_computation.3 | async-start | bytes 9437184 | tf_op jit(solution)/shard_map/all_to_all | solution.py:399
  210.8 73.9 %collective-permute-start.7 = (bf16[256,768]{1,0:T(8,128)(2,1)}, bf16[256,768]{1,0:T(8,128)(2,1)S(1)}, u32[]{:S(2)}, u32[]{:S(2)}) collective-permute-start(bf16[256,768]{1,0:T(8,128)(2,1)} %copy-done.6), channel_id=1, source_target_pairs={{0,0},{1,4},{4,1},{5,5},{2,2},{3,6},{6,3},{7,7},{8,8},{9,12},{12,9... | collective-permute-start | bytes 1179656 | tf_op jit(solution)/shard_map/ppermute | solution.py:312
  216.2 68.5 %collective-permute-start.5 = (bf16[256,512]{1,0:T(8,128)(2,1)S(1)}, bf16[256,512]{1,0:T(8,128)(2,1)S(1)}, u32[]{:S(2)}, u32[]{:S(2)}) collective-permute-start(bf16[256,512]{1,0:T(8,128)(2,1)S(1)} %copy-done.11), channel_id=1, source_target_pairs={{0,0},{1,4},{4,1},{5,5},{2,2},{3,6},{6,3},{7,7},{8,8},{9,12},{12,9... | collective-permute-start | bytes 786440 | tf_op jit(solution)/shard_map/ppermute | solution.py:312
  294.3 1.4 collective-permute-start.10
Sparse Core Ops, SparseCore 0:
  11.0 91.7 all-gather.1

commit v2 on v1

--- a/solution.py
+++ b/solution.py
@@ -50,20 +50,47 @@
     return inverse * (grad_unit - unit * shrink), grad_normed * unit
 
 
-def key_value_kernel(tok_ref, w_ref, gain_ref, cos_ref, sin_ref, kv_ref):
-    raw = mm(tok_ref[...], w_ref[...])
+def prepare_kernel(where, src_ref, toks_ref, toks_theirs_ref, turned_ref):
+    planes, columns = src_ref.shape[:2]
+    core = where[1]
+
+    def piece(plane, y, side):
+        return src_ref[plane, y, side].astype(f32)
+
+    group = 4
+    for side, out_ref in ((core, toks_ref), (1 - core, toks_theirs_ref)):
+        for i in range(0, planes, group):
+            rows = jnp.concatenate(
+                [piece(i + j, y, side) for j in range(group) for y in range(columns)], axis=0
+            ).astype(bf16)
+            wide = rows.shape[0]
+            out_ref[:, i // group * wide : (i // group + 1) * wide] = rows.T
+    for y in range(columns):
+        for side in range(2):
+            turned_ref[2 * y + side] = jnp.concatenate(
+                [piece(i, y, side) for i in range(planes)], axis=0
+            ).astype(bf16)
+
+
+def key_value_kernel(mine_ref, other_ref, w_ref, w_other_ref, gain_ref, cos_ref, sin_ref, kv_ref, raw_ref):
+    raw = mm(mine_ref[...], w_ref[...]) + mm(other_ref[...], w_other_ref[...])
+    raw_ref[...] = raw[:, :span]
     kv_ref[:, :span] = shape_head(raw[:, :span], gain_ref[...], cos_ref[...], sin_ref[...]).astype(bf16)
     kv_ref[:, span:] = raw[:, span:].astype(bf16)
 
 
-def query_kernel(tok_ref, wq_ref, wkv_ref, gain_ref, cos_ref, sin_ref, q_ref, raw_ref):
-    cols = wq_ref.shape[1]
-    raw_ref[:, :cols] = mm(tok_ref[...], wq_ref[...])
-    raw_ref[:, cols:] = mm(tok_ref[...], wkv_ref[...])[:, :span]
+def query_part_kernel(mine_ref, other_ref, w_ref, part_ref, part_other_ref):
+    part_ref[...] = mm(mine_ref[...], w_ref[...])
+    part_other_ref[...] = mm(other_ref[...], w_ref[...])
+
+
+def query_kernel(part_ref, part_theirs_ref, gain_ref, cos_ref, sin_ref, q_ref, raw_ref):
     gain = gain_ref[...] * (span**-0.5 / math.log(2.0))
-    for h in range(cols // span):
+    for h in range(raw_ref.shape[1] // span):
         part = slice(h * span, (h + 1) * span)
-        q_ref[:, part] = shape_head(raw_ref[:, part], gain, cos_ref[...], sin_ref[...]).astype(bf16)
+        raw = part_ref[:, part] + part_theirs_ref[:, part]
+        raw_ref[:, part] = raw.astype(bf16)
+        q_ref[:, part] = shape_head(raw, gain, cos_ref[...], sin_ref[...]).astype(bf16)
 
 
 def attention_kernel(
@@ -231,79 +258,126 @@
         ],
         compiler_params=pltpu.CompilerParams(vmem_limit_bytes=48 * mib),
         cost_estimate=pl.CostEstimate(
-            flops=8 * 10**9, bytes_accessed=10 * 10**6, transcendentals=9 * 10**6
+            flops=3 * 10**10, bytes_accessed=10 * 10**6, transcendentals=9 * 10**6
         ),
         name="attention",
     )(order, own, q16, g16, kv, kv_other)
 
 
-def grad_rows_kernel(raw_ref, dq_ref, dkv_ref, gq_ref, gk_ref, cos_ref, sin_ref, g_ref, gain_ref):
-    cols = dq_ref.shape[1]
+def grad_query_kernel(raw_ref, dq_ref, gain_ref, cos_ref, sin_ref, g_ref, gain_out):
     cosine, sine = cos_ref[...], sin_ref[...]
-    gain_q = jnp.zeros((1, span), f32)
-    for h in range(cols // span):
+    sums = jnp.zeros((1, span), f32)
+    for h in range(dq_ref.shape[1] // span):
         part = slice(h * span, (h + 1) * span)
-        grad, terms = shape_head_grad(raw_ref[:, part], gq_ref[...], cosine, sine, dq_ref[:, part])
+        grad, terms = shape_head_grad(
+            raw_ref[:, part].astype(f32), gain_ref[...], cosine, sine, dq_ref[:, part]
+        )
         g_ref[:, part] = grad.astype(bf16)
-        gain_q = gain_q + jnp.sum(terms, axis=0, keepdims=True)
+        sums = sums + jnp.sum(terms, axis=0, keepdims=True)
+    gain_out[...] = jnp.broadcast_to(sums, gain_out.shape)
+
+
+def grad_key_value_kernel(raw_ref, dkv_ref, gain_ref, cos_ref, sin_ref, gain_q_ref, g_ref):
+    rows = raw_ref.shape[0]
     dkv = jnp.sum(dkv_ref[...].astype(f32), axis=0)
-    grad, terms = shape_head_grad(raw_ref[:, cols:], gk_ref[...], cosine, sine, dkv[:, :span])
-    g_ref[:, cols : cols + span] = grad.astype(bf16)
-    g_ref[:, cols + span :] = dkv[:, span:].astype(bf16)
+    grad, terms = shape_head_grad(
+        raw_ref[...].astype(f32), gain_ref[...], cos_ref[...], sin_ref[...], dkv[:, :span]
+    )
+    g_ref[:rows, :span] = grad.astype(bf16)
+    g_ref[:rows, span:] = dkv[:, span:].astype(bf16)
     gain_k = jnp.sum(terms, axis=0, keepdims=True)
-    pieces = []
-    for gain in (gain_q, gain_k):
+    split = []
+    for gain in (gain_q_ref[0:1], gain_k):
         high = gain.astype(bf16).astype(f32)
-        pieces += [high, gain - high]
-    row = jnp.concatenate(pieces + [jnp.zeros((1, 2 * span), f32)], axis=1)
-    gain_ref[...] = jnp.where(lax.broadcasted_iota(jnp.int32, gain_ref.shape, 0) == 0, row, 0.0)
-
-
-def weight_grad_kernel(mine_ref, other_ref, g_ref, g_other_ref, gain_ref, out_ref):
-    total = mm(mine_ref[...], g_ref[...]) + mm(other_ref[...], g_other_ref[...])
-    owners, padded = out_ref.shape[0], out_ref.shape[1]
-    own_rows = padded - gain_ref.shape[0]
-    for i in range(owners):
+        split.append(jnp.concatenate([high, gain - high], axis=1))
+    row = lax.broadcasted_iota(jnp.int32, (g_ref.shape[0] - rows, 2 * span), 0)
+    g_ref[rows:] = jnp.where(row == 0, split[0], jnp.where(row == 1, split[1], 0.0)).astype(bf16)
+
+
+def weight_grad_kernel(where, turned_ref, *rest):
+    blocks, out_ref = rest[:-1], rest[-1]
+    columns = len(blocks) // 2
+    toks = turned_ref.shape[2]
+    y, core = where[0], where[1]
+    total, gains = None, None
+    for side in range(2):
+        for k in range(columns):
+            from_y = lax.rem(y + k, columns)
+            from_core = core if side == 0 else 1 - core
+            at = (from_core * 2 + lax.rem(from_y, 2)) * 2 + from_y // 2
+            block = blocks[side * columns + k]
+            part = mm(turned_ref[at], block[:toks])
+            total = part if total is None else total + part
+            if block.shape[0] > toks:
+                row = block[toks:].astype(f32)
+                gains = row if gains is None else gains + row
+    own_rows = total.shape[0] // out_ref.shape[0]
+    extra = []
+    if gains is not None:
+        gain = gains[:, :span] + gains[:, span:]
+        high = gain.astype(bf16).astype(f32)
+        extra = [jnp.concatenate([high, gain - high], axis=1)[:8]]
+    for i in range(out_ref.shape[0]):
         part = total[i * own_rows : (i + 1) * own_rows]
-        out_ref[i] = jnp.concatenate([part, gain_ref[...]], axis=0).astype(bf16)
-
-
-def weight_grad(mine, other, g, g_other, gains, owners):
-    rows, cols = mine.shape[0] // owners, g.shape[1]
-    padded = rows + gains.shape[0]
-    step = math.gcd(owners, 16)
-    toks = mine.shape[1]
-    whole = lambda shape: pl.BlockSpec(shape, lambda i: (0,) * len(shape))
+        out_ref[i] = jnp.concatenate([part] + extra, axis=0).astype(bf16)
+
+
+def weight_grad(where, turned, blocks, planes, padded):
     return pl.pallas_call(
         weight_grad_kernel,
-        grid=(owners // step,),
-        out_shape=jax.ShapeDtypeStruct((owners, padded, cols), bf16),
-        in_specs=[
-            pl.BlockSpec((step * rows, toks), lambda i: (i, 0)),
-            pl.BlockSpec((step * rows, toks), lambda i: (i, 0)),
-            whole(g.shape),
-            whole(g.shape),
-            whole(gains.shape),
-        ],
-        out_specs=pl.BlockSpec((step, padded, cols), lambda i: (i, 0, 0)),
-        compiler_params=pltpu.CompilerParams(vmem_limit_bytes=40 * mib),
+        out_shape=jax.ShapeDtypeStruct((planes, padded, blocks[0].shape[1]), bf16),
+        in_specs=[smem] + [vmem] * (1 + len(blocks)),
+        out_specs=vmem,
+        compiler_params=pltpu.CompilerParams(vmem_limit_bytes=48 * mib),
         name="weight_grad",
-    )(mine, other, g, g_other, gains)
-
-
-def call(kernel, shapes, *args, name):
+    )(where, turned, *blocks)
+
+
+def grad_states_kernel(where, gq_ref, gkv_ref, q_ref, q_theirs_ref, kv_ref, kv_theirs_ref, out_ref):
+    core = where[1]
+    own_rows, group = 40, 640
+    transposed = (((1,), (1,)), ((), ()))
+
+    def product(q, kv, i):
+        part = slice(i * group, (i + 1) * group)
+        return lax.dot_general(
+            q[part], gq_ref[...], transposed, preferred_element_type=f32
+        ) + lax.dot_general(kv[part], gkv_ref[...], transposed, preferred_element_type=f32)
+
+    for i in range(q_ref.shape[0] // group):
+        mine, theirs = product(q_ref, kv_ref, i), product(q_theirs_ref, kv_theirs_ref, i)
+        sides = (jnp.where(core == 0, mine, theirs), jnp.where(core == 0, theirs, mine))
+        rows = jnp.concatenate(
+            [side[j : j + own_rows] for j in range(0, group, own_rows) for side in sides], axis=0
+        )
+        out_ref[:, 2 * i * group : 2 * (i + 1) * group] = rows.astype(bf16).T
+
+
+def finish_kernel(parts_ref, key_ref, value_ref, gain_q_ref, gain_k_ref):
+    sums = jnp.sum(parts_ref[...].astype(f32), axis=0)
+    rows = key_ref.shape[0]
+    key_ref[...] = sums[:rows, :span]
+    value_ref[...] = sums[:rows, span:]
+    gains = sums[rows:, :span] + sums[rows:, span:]
+    gain_q_ref[...] = gains[0:1]
+    gain_k_ref[...] = gains[1:2]
+
+
+def call(kernel, shapes, *args, name, cost=None):
     return pl.pallas_call(
         kernel,
         out_shape=shapes,
-        in_specs=[vmem] * len(args),
+        in_specs=[smem if a.dtype == jnp.int32 else vmem for a in args],
         out_specs=jax.tree.map(lambda _: vmem, shapes),
         compiler_params=pltpu.CompilerParams(vmem_limit_bytes=48 * mib),
+        cost_estimate=cost,
         name=name,
     )(*args)
 
 
 plane = ("x", "z")
-chips = ("x", "z", "y_hi", "y_lo")
+column = ("y_hi", "y_lo")
+chips = plane + column
 swapped = [(0, 0), (1, 2), (2, 1), (3, 3)]
 flipped = [(0, 1), (1, 0)]
 
@@ -320,101 +394,144 @@
     return lax.all_to_all(jnp.broadcast_to(array[None], (count,) + array.shape), axes, 0, 0)
 
 
-def pick(array, index, axis):
-    return lax.dynamic_index_in_dim(array, index, axis, keepdims=False)
+def ring(array, step):
+    return lax.ppermute(array, column, [(i, (i - step) % 4) for i in range(4)])
+
+
+def around(array):
+    mine = [array] + [ring(array, k) for k in range(1, 4)]
+    return mine + [flip(a) for a in mine]
 
 
 def local(hidden_states, block_order, w_query, w_key, w_value, gain_query, gain_key, cotangent):
     tokens = hidden_states[0]
     tok_rows, width = tokens.shape
     q_cols = w_query.shape[1]
+    kv_cols = 2 * span
     own_rows = w_query.shape[0]
-    chip_count = width // own_rows // 2
-    pairs = 16
-    at_x, at_z = lax.axis_index("x"), lax.axis_index("z")
+    planes, columns = 16, 4
+    half = width // 2
+    place = lax.axis_index("x") * 4 + lax.axis_index("z")
     y_hi, core = lax.axis_index("y_hi"), lax.axis_index("core")
+    y = y_hi * 2 + lax.axis_index("y_lo")
+    where = jnp.stack([y, core]).astype(jnp.int32)
     offsets = jnp.arange(span, dtype=jnp.int32)
 
-    def slots_of(half):
-        place = (at_x * 4 + at_z) * 2 + half
-        blocks = lax.dynamic_slice_in_dim(block_order, 2 * place, 2)
+    def angles_of(part):
+        blocks = lax.dynamic_slice_in_dim(block_order, 2 * (place * 2 + part), 2)
         positions = (blocks[:, None] * span + offsets[None, :]).reshape(tok_rows)
         return blocks, rotation(positions, span)
 
-    _, (cos_kv, sin_kv) = slots_of(y_hi)
-    own_blocks, (cosine, sine) = slots_of(core)
+    _, (cosine, sine) = angles_of(y_hi)
+    own_blocks, (cos_there, sin_there) = angles_of(core)
     own = jnp.concatenate([own_blocks, core[None].astype(jnp.int32)])
     gain_q, gain_k = gain_query[None, :], gain_key[None, :]
-
-    w_kv = jnp.concatenate([w_key, w_value], axis=1)
-    kv_mine = to_all(w_kv, chips, chip_count)
+    shape = jax.ShapeDtypeStruct
+
+    q_mine = lax.all_gather(w_query, chips, axis=0, tiled=True)
+    kv_mine = to_all(jnp.concatenate([w_key, w_value], axis=1), chips, planes * columns)
+    kv_mine = kv_mine.reshape(half, kv_cols)
+
+    toks_mine, toks_theirs, turned = pl.pallas_call(
+        prepare_kernel,
+        out_shape=(shape((tok_rows, half), bf16),) * 2 + (shape((2 * columns, width // 8, tok_rows), bf16),),
+        in_specs=[smem, vmem],
+        out_specs=(vmem,) * 3,
+        compiler_params=pltpu.CompilerParams(vmem_limit_bytes=48 * mib),
+        name="prepare",
+    )(where, tokens.T.reshape(planes, columns, 2, own_rows, tok_rows))
+
+    toks_other = flip(toks_theirs)
+    kv_mine, toks_mine, toks_theirs, turned, cosine, sine, cos_there, sin_there, own = (
+        lax.optimization_barrier(
+            (kv_mine, toks_mine, toks_theirs, turned, cosine, sine, cos_there, sin_there, own)
+        )
+    )
     kv_theirs = flip(kv_mine)
-    full_query = lax.all_gather(
-        w_query, ("x", "z", "y_hi", "y_lo", "core"), axis=0, tiled=True
-    )
-    lower = jnp.where(core == 0, kv_mine, kv_theirs)
-    upper = jnp.where(core == 0, kv_theirs, kv_mine)
-    full_kv = jnp.stack([lower, upper], axis=1).reshape(width, 2 * span)
-
-    toks = swap(tokens)
-    grad_out = swap(cotangent[0])
-
-    kv16 = call(
+
+    kv16, raw_k = call(
         key_value_kernel,
-        jax.ShapeDtypeStruct((tok_rows, 2 * span), bf16),
-        tokens, full_kv, gain_k, cos_kv, sin_kv,
+        (shape((tok_rows, kv_cols), bf16), shape((tok_rows, span), f32)),
+        toks_mine, toks_theirs, kv_mine, kv_theirs, gain_k, cosine, sine,
         name="key_value",
     )
-    kv_own = to_all(swap(kv16), plane, pairs)
+    kv_send = jnp.broadcast_to(swap(kv16)[None], (planes, tok_rows, kv_cols))
+    q_mine, _ = lax.optimization_barrier((q_mine, kv_send))
+    kv_own = lax.all_to_all(kv_send, plane, 0, 0)
+    cheap = pl.CostEstimate(flops=1000, bytes_accessed=1000, transcendentals=0)
+    q_part, q_part_other = call(
+        query_part_kernel,
+        (shape((tok_rows, q_cols), f32),) * 2,
+        toks_mine, toks_other, q_mine,
+        name="query_part",
+        cost=cheap,
+    )
+    kv_own, q_part, q_part_other, grad_out = lax.optimization_barrier(
+        (kv_own, q_part, q_part_other, swap(cotangent[0]))
+    )
+    q16, raw_q = call(
+        query_kernel,
+        (shape((tok_rows, q_cols), bf16),) * 2,
+        q_part, flip(q_part_other), gain_q, cosine, sine,
+        name="query",
+        cost=cheap,
+    )
     kv_other = flip(kv_own)
-
-    q16, raw = call(
-        query_kernel,
-        (
-            jax.ShapeDtypeStruct((tok_rows, q_cols), bf16),
-            jax.ShapeDtypeStruct((tok_rows, q_cols + span), f32),
-        ),
-        toks, full_query, full_kv, gain_q, cosine, sine,
-        name="query",
-    )
-    turned = toks.T.reshape(chip_count, 2, own_rows, tok_rows)
-    turned_mine = pick(turned, core, 1).reshape(-1, tok_rows)
-    turned_other = flip(pick(turned, 1 - core, 1).reshape(-1, tok_rows))
-
-    ctx, dq, dkv_mine, dkv_theirs = attention(block_order, own, q16, grad_out, kv_own, kv_other)
-    context = swap(ctx)
+    q16 = swap(q16)
+    turned, raw_q, _ = lax.optimization_barrier((turned, raw_q, q16))
+    turned = lax.all_to_all(turned, column + ("core",), 0, 0)
+    raw_there = swap(jnp.concatenate([raw_q, raw_k.astype(bf16)], axis=1))
+
+    ctx, dq, dkv_mine, dkv_theirs = attention(
+        block_order, own, q16, grad_out, kv_own, kv_other
+    )
+    q_theirs = flip(q_mine)
+    dkv_theirs, dq, turned, raw_there, q_theirs = lax.optimization_barrier(
+        (dkv_theirs, dq, turned, raw_there, q_theirs)
+    )
     dkv = (dkv_mine.astype(f32) + flip(dkv_theirs).astype(f32)).astype(bf16)
     dkv = lax.all_to_all(dkv, plane, 0, 0)
 
-    grad_rows, gains = call(
-        grad_rows_kernel,
-        (
-            jax.ShapeDtypeStruct((tok_rows, q_cols + 2 * span), bf16),
-            jax.ShapeDtypeStruct((8, q_cols + 2 * span), f32),
-        ),
-        raw, dq, dkv, gain_q, gain_k, cosine, sine,
-        name="grad_rows",
-    )
-    partial = weight_grad(turned_mine, turned_other, grad_rows, flip(grad_rows), gains, chip_count)
-    parts = lax.all_to_all(partial, chips, 0, 0)
-    sums = jnp.sum(parts.astype(f32), axis=0)
-    own_grads = sums[:own_rows]
-    gain_row = sums[own_rows, : 4 * span].reshape(2, 2, span).sum(axis=1)
-    gain_sums = gain_row + flip(gain_row)
-
-    own_grad_rows = swap(grad_rows)
-    contract = (((1,), (1,)), ((), ()))
-    grad_tokens = lax.dot_general(
-        own_grad_rows[:, :q_cols], full_query, contract, preferred_element_type=f32
-    ) + lax.dot_general(own_grad_rows[:, q_cols:], full_kv, contract, preferred_element_type=f32)
+    g_q, gains_q = call(
+        grad_query_kernel,
+        (shape((tok_rows, q_cols), bf16), shape((8, span), f32)),
+        raw_there[:, :q_cols], dq, gain_q, cos_there, sin_there,
+        name="grad_query",
+    )
+    parts = weight_grad(where, turned, around(g_q), planes, own_rows)
+    parts = lax.all_to_all(parts, plane, 0, 0)
+    own_query = jnp.sum(parts.astype(f32), axis=0)
+
+    g_kv = call(
+        grad_key_value_kernel,
+        shape((tok_rows + 16, kv_cols), bf16),
+        raw_there[:, q_cols:], dkv, gain_k, cos_there, sin_there, gains_q,
+        name="grad_key_value",
+    )
+    blocks, g_q_back = lax.optimization_barrier((around(g_kv), swap(g_q)))
+    parts = weight_grad(where, turned, blocks, planes, own_rows + 8)
+    parts = lax.all_to_all(parts, plane, 0, 0)
+    own_key, own_value, gain_sum_q, gain_sum_k = call(
+        finish_kernel,
+        (shape((own_rows, span), f32),) * 2 + (shape((1, span), f32),) * 2,
+        parts,
+        name="finish",
+    )
+
+    grad_states = call(
+        grad_states_kernel,
+        shape((tok_rows, width), bf16),
+        where, g_q_back, swap(g_kv[:tok_rows]), q_mine, q_theirs, kv_mine, kv_theirs,
+        name="grad_states",
+    )
     return (
-        context[None],
-        grad_tokens.astype(bf16)[None],
-        own_grads[:, :q_cols],
-        own_grads[:, q_cols : q_cols + span],
-        own_grads[:, q_cols + span :],
-        gain_sums[0],
-        gain_sums[1],
+        swap(ctx)[None],
+        grad_states[None],
+        own_query,
+        own_key,
+        own_value,
+        gain_sum_q[0],
+        gain_sum_k[0],
     )
 
 

time: 305 us -> 274 us (0.90)
  waiting for transfers between devices: 135 us -> 78.6 us
  starting transfers between devices: 49 us -> 88.5 us
  blocking collectives: 28.2 us -> 0 us
  Pallas kernels: 45.1 us -> 55 us
  local copies, waits for them, and re-layouts: 17.7 us -> 25.6 us
  matrix products: 6.47 us -> 0 us
    ppermute x5 -> x7, waiting for transfers between devices: 89.2 us -> 13.1 us  [swap(): return lax.ppermute(array, ('y_hi', 'core'), swapped)]
    all_gather x1, waiting for transfers between devices: 0.01 us -> 30.5 us  [local(): q_mine = lax.all_gather(w_query, chips, axis=0, tiled=True)]
    all_to_all x1 -> x0, blocking collectives: 28.2 us -> none  [to_all(): lax.all_to_all(jnp.broadcast_to(array[None], (count,) + array.shape), axe...]
    all_to_all x1, waiting for transfers between devices: 21.3 us -> 4.23 us  [local(): dkv = lax.all_to_all(dkv, plane, 0, 0)]
    all_to_all x1 -> x4, starting transfers between devices: 10.8 us -> 26.3 us  [the longest x2 14.9 us: local(): parts = lax.all_to_all(parts, plane, 0, 0)]
    all_to_all x1, waiting for transfers between devices: 17.5 us -> 6.88 us  [to_all(): lax.all_to_all(jnp.broadcast_to(array[None], (count,) + array.shape), axe...]
    ppermute x0 -> x6, waiting for transfers between devices: none -> 10.2 us  [ring(): return lax.ppermute(array, column, [(i, (i - step) % 4) for i in range(4)])]
    pallas_call x4 -> x10, Pallas kernels: 12.2 us -> 22.3 us  [the longest x7 14.6 us: call(): pl.pallas_call(kernel, out_shape=shapes, in_specs=[smem if a.dtype == jnp...]
  transfers between devices with their start and end apart: 15 -> 34, of which waited for: 8 -> 14; matrix products, arithmetic and copies ran while one was open for 6% -> 5% of each run, Pallas kernels for 3% -> 20%
where the time goes in v2:
time: 274 us; the launch traced here: 271 us
  starting transfers between devices  88.5 us (32%)
  waiting for transfers between devices  78.6 us (29%)
  Pallas kernels  55 us (20%)
  local copies, waits for them, and re-layouts  25.6 us (9%)
  between operations  14.4 us (5%)
  other arithmetic  9.12 us (3%)
    pallas_call x1, Pallas kernels, attention(): pl.pallas_call(attention_kernel, out_shape=(jax.ShapeDtypeStruct((rows_he...  32.7 us
    all_gather x1, waiting for transfers between devices, local(): q_mine = lax.all_gather(w_query, chips, axis=0, tiled=True)  30.5 us
    ppermute x7, starting transfers between devices, swap(): return lax.ppermute(array, ('y_hi', 'core'), swapped)  24.8 us
    unnamed x53, local copies, waits for them, and re-layouts  18.5 us
    all_to_all x2, starting transfers between devices, local(): parts = lax.all_to_all(parts, plane, 0, 0)  14.9 us
    pallas_call x7, Pallas kernels, call(): pl.pallas_call(kernel, out_shape=shapes, in_specs=[smem if a.dtype == jnp...  14.6 us
    ppermute x14, starting transfers between devices, flip(): return lax.ppermute(array, 'core', flipped)  13.9 us
    ppermute x7, waiting for transfers between devices, swap(): return lax.ppermute(array, ('y_hi', 'core'), swapped)  13.1 us
  transfers between devices with their start and end apart: 34, of which 14 were waited for; matrix products, arithmetic and copies ran while one was open for 5% of the time, Pallas kernels for 20%

profile of v2, /device:TPU:39, one launch (start us, length us, event | category | flops | bytes accessed | tf_op | source)
XLA Modules:
  0.0 271.3 jit_solution(13428362611076657857)
XLA Ops:
  9.8 10.7 %all-to-all-start = ((bf16[64,40,256]{2,1,0:T(8,128)(2,1)}), bf16[64,40,256]{2,1,0:T(8,128)(2,1)S(1)}, u32[]{:S(2)}, u32[]{:S(2)}) async-start(bf16[64,40,256]{2,1,0:T(8,128)(2,1)} %broadcast_in_dim.12), calls=%async_computation | async-start | bytes 2621440 | tf_op jit(solution)/shard_map/all_to_all | solution.py:394
  20.5 4.4 %copy.15 = bf16[5120,256]{1,0:T(8,128)(2,1)} copy(bf16[5120,256]{0,1:T(8,128)(2,1)} %bitcast.26) | data formatting | bytes 5242880 | tf_op jit(solution)/shard_map/transpose | solution.py:442
  24.9 2.6 prepare.1
  31.4 6.9 %all-to-all-done = bf16[64,40,256]{2,1,0:T(8,128)(2,1)S(1)} async-done(((bf16[64,40,256]{2,1,0:T(8,128)(2,1)}), bf16[64,40,256]{2,1,0:T(8,128)(2,1)S(1)}, u32[]{:S(2)}, u32[]{:S(2)}) %all-to-all-start) | async-done | bytes 1310752 | tf_op jit(solution)/shard_map/all_to_all | solution.py:394
  40.5 2.7 collective-permute-done.w_other_ref.kv_theirs_ref
  46.0 2.4 collective-permute-start.1
  48.4 5.3 %collective-permute-done.1 = bf16[256,256]{1,0:T(8,128)(2,1)S(1)} collective-permute-done((bf16[256,256]{1,0:T(8,128)(2,1)S(1)}, bf16[256,256]{1,0:T(8,128)(2,1)S(1)}, u32[]{:S(2)}, u32[]{:S(2)}) %collective-permute-start.1) | collective-permute-done | bytes 131104 | tf_op jit(solution)/shard_map/ppermute | solution.py:386
  55.3 7.7 %all-to-all-start.1 = ((bf16[16,256,256]{2,1,0:T(8,128)(2,1)}), bf16[16,256,256]{2,1,0:T(8,128)(2,1)}, u32[]{:S(2)}, u32[]{:S(2)}) async-start(bf16[16,256,256]{2,1,0:T(8,128)(2,1)} %broadcast_in_dim.14), calls=%async_computation.1 | async-start | bytes 4194304 | tf_op jit(solution)/shard_map/all_to_all | solution.py:460
  63.1 3.3 %collective-permute-start.3 = (bf16[256,512]{1,0:T(8,128)(2,1)}, bf16[256,512]{1,0:T(8,128)(2,1)S(1)}, u32[]{:S(2)}, u32[]{:S(2)}) collective-permute-start(bf16[256,512]{1,0:T(8,128)(2,1)} %bitcast.28), channel_id=1, source_target_pairs={{0,0},{1,4},{4,1},{5,5},{2,2},{3,6},{6,3},{7,7},{8,8},{9,12},{12,9... | collective-permute-start | bytes 786440 | tf_op jit(solution)/shard_map/ppermute | solution.py:386
  66.3 30.5 %all-gather.2.cloned.1.call-done.w_ref.q_ref = bf16[2560,512]{1,0:T(8,128)(2,1)} async-done(((bf16[40,512]{1,0:T(8,128)(2,1)}), bf16[2560,512]{1,0:T(8,128)(2,1)}) %all-gather.2.cloned.1.call-update) | async-done | bytes 2621456 | tf_op jit(solution)/shard_map/all_gather | solution.py:431
  96.8 3.2 %query_part.1 = (f32[256,512]{1,0:T(8,128)S(1)}, f32[256,512]{1,0:T(8,128)S(1)}) custom-call(bf16[256,2560]{1,0:T(8,128)(2,1)S(1)} %get-tuple-element.60.mine_ref, bf16[256,2560]{1,0:T(8,128)(2,1)S(1)} %collective-permute-done.2.other_ref, bf16[2560,512]{1,0:T(8,128)(2,1)} %all-gather.2.cloned.1.call-done.w_ref.q_ref), custom_call_target="tpu_custom_call" | custom-call | flops 1000 | bytes 1000 | tf_op jit(solution)/shard_map/query_part/pallas_call | solution.py:367
  104.2 4.6 %collective-permute-done.4.part_theirs_ref = f32[256,512]{1,0:T(8,128)S(1)} collective-permute-done((f32[256,512]{1,0:T(8,128)}, f32[256,512]{1,0:T(8,128)S(1)}, u32[]{:S(2)}, u32[]{:S(2)}) %collective-permute-start.4) | collective-permute-done | bytes 524320 | tf_op jit(solution)/shard_map/ppermute | solution.py:390
  110.4 3.1 %collective-permute-start.5 = (bf16[256,512]{1,0:T(8,128)(2,1)S(1)}, bf16[256,512]{1,0:T(8,128)(2,1)S(1)}, u32[]{:S(2)}, u32[]{:S(2)}) collective-permute-start(bf16[256,512]{1,0:T(8,128)(2,1)S(1)} %get-tuple-element.71), channel_id=1, source_target_pairs={{0,0},{1,4},{4,1},{5,5},{2,2},{3,6},{6,3},{7,7},{8,8},{9,12},{12,9... | collective-permute-start | bytes 786440 | tf_op jit(solution)/shard_map/ppermute | solution.py:386
  114.2 5.4 %collective-permute-done.5.q_ref = bf16[256,512]{1,0:T(8,128)(2,1)S(1)} collective-permute-done((bf16[256,512]{1,0:T(8,128)(2,1)S(1)}, bf16[256,512]{1,0:T(8,128)(2,1)S(1)}, u32[]{:S(2)}, u32[]{:S(2)}) %collective-permute-start.5) | collective-permute-done | bytes 262176 | tf_op jit(solution)/shard_map/ppermute | solution.py:386
  120.4 3.7 %all-to-all-start.2 = ((bf16[8,640,256]{2,1,0:T(8,128)(2,1)}), bf16[8,640,256]{2,1,0:T(8,128)(2,1)S(1)}, u32[]{:S(2)}, u32[]{:S(2)}) async-start(bf16[8,640,256]{2,1,0:T(8,128)(2,1)} %copy-done.4), calls=%async_computation.2 | async-start | bytes 5242880 | tf_op jit(solution)/shard_map/all_to_all | solution.py:482
  124.1 4.3 %collective-permute-start.8 = (bf16[256,640]{1,0:T(8,128)(2,1)S(1)}, bf16[256,640]{1,0:T(8,128)(2,1)S(1)}, u32[]{:S(2)}, u32[]{:S(2)}) collective-permute-start(bf16[256,640]{1,0:T(8,128)(2,1)S(1)} %pad_maximum_fusion), channel_id=1, source_target_pairs={{0,0},{1,4},{4,1},{5,5},{2,2},{3,6},{6,3},{7,7},{8,8},{9,12},{12,9... | collective-permute-start | bytes 983048 | tf_op jit(solution)/shard_map/ppermute | solution.py:386
  129.4 32.7 %attention.1 = (bf16[256,512]{1,0:T(8,128)(2,1)S(1)}, f32[256,512]{1,0:T(8,128)S(1)}, bf16[16,256,256]{2,1,0:T(8,128)(2,1)S(1)}, bf16[16,256,256]{2,1,0:T(8,128)(2,1)S(1)}) custom-call(s32[64]{0:T(128)S(1)} %copy-done.15, s32[3]{0:T(128)S(1)} %copy-done.24, bf16[256,512]{1,0:T(8,128)(2,1)S(1)} %copy-done.23, bf16[256,512]{1,0:T(8,128)(2,1)S(1)} %copy-done.21, ...), custom_call_target="tpu_custom_call" | custom-call | flops 30000001024 | bytes 10000000 | tf_op jit(solution)/shard_map/attention/pallas_call | solution.py:232
  166.5 4.4 %collective-permute-done.10 = bf16[16,256,256]{2,1,0:T(8,128)(2,1)S(1)} collective-permute-done((bf16[16,256,256]{2,1,0:T(8,128)(2,1)}, bf16[16,256,256]{2,1,0:T(8,128)(2,1)S(1)}, u32[]{:S(2)}, u32[]{:S(2)}) %collective-permute-start.10) | collective-permute-done | bytes 2097184 | tf_op jit(solution)/shard_map/ppermute | solution.py:390
  170.8 3.5 %add_convert_fusion = bf16[16,256,256]{2,1,0:T(8,128)(2,1)} fusion(bf16[16,256,256]{2,1,0:T(8,128)(2,1)S(1)} %collective-permute-done.10, bf16[16,256,256]{2,1,0:T(8,128)(2,1)} %copy-done.5), kind=kLoop, calls=%fused_computation | loop fusion | flops 4194304 | bytes 6291456 | tf_op jit(solution)/shard_map/convert_element_type | solution.py:492
  174.4 6.6 %all-to-all-start.3 = ((bf16[16,256,256]{2,1,0:T(8,128)(2,1)}), bf16[16,256,256]{2,1,0:T(8,128)(2,1)}, u32[]{:S(2)}, u32[]{:S(2)}) async-start(bf16[16,256,256]{2,1,0:T(8,128)(2,1)} %add_convert_fusion), calls=%async_computation.3 | async-start | bytes 4194304 | tf_op jit(solution)/shard_map/all_to_all | solution.py:493
  187.0 5.4 %collective-permute-done.22.rest_3_ = bf16[256,512]{1,0:T(8,128)(2,1)S(1)} collective-permute-done((bf16[256,512]{1,0:T(8,128)(2,1)S(1)}, bf16[256,512]{1,0:T(8,128)(2,1)S(1)}, u32[]{:S(2)}, u32[]{:S(2)}) %collective-permute-start.22) | collective-permute-done | bytes 262176 | tf_op jit(solution)/shard_map/ppermute | solution.py:398
  192.3 6.0 %collective-permute-start.26 = (bf16[256,512]{1,0:T(8,128)(2,1)S(1)}, bf16[256,512]{1,0:T(8,128)(2,1)S(1)}, u32[]{:S(2)}, u32[]{:S(2)}) collective-permute-start(bf16[256,512]{1,0:T(8,128)(2,1)S(1)} %collective-permute-done.22.rest_3_), channel_id=1, source_target_pairs={{0,1},{1,0},{2,3},{3,2},{4,5},{5,4},{6,7},{7,6},{8,9},{9,8},{10,11... | collective-permute-start | bytes 786440 | tf_op jit(solution)/shard_map/ppermute | solution.py:390
  200.3 2.9 %weight_grad.2 = bf16[16,40,512]{2,1,0:T(8,128)(2,1)} custom-call(s32[2]{0:T(128)S(1)} %pad_add_fusion.where, bf16[8,640,256]{2,1,0:T(8,128)(2,1)S(1)} %all-to-all-done.2.turned_ref, bf16[256,512]{1,0:T(8,128)(2,1)S(1)} %get-tuple-element.89.rest_0_, bf16[256,512]{1,0:T(8,128)(2,1)S(1)} %collective-permute-done.20.rest_1_, ...), custom_call_target="tpu_custom_call" | custom-call | tf_op jit(solution)/shard_map/weight_grad/pallas_call | solution.py:326
  203.2 4.2 %all-to-all-done.3.dkv_ref = bf16[16,256,256]{2,1,0:T(8,128)(2,1)} async-done(((bf16[16,256,256]{2,1,0:T(8,128)(2,1)}), bf16[16,256,256]{2,1,0:T(8,128)(2,1)}, u32[]{:S(2)}, u32[]{:S(2)}) %all-to-all-start.3) | async-done | bytes 2097184 | tf_op jit(solution)/shard_map/all_to_all | solution.py:493
  207.4 8.2 %all-to-all-start.4 = ((bf16[16,40,512]{2,1,0:T(8,128)(2,1)}), bf16[16,40,512]{2,1,0:T(8,128)(2,1)}, u32[]{:S(2)}, u32[]{:S(2)}) async-start(bf16[16,40,512]{2,1,0:T(8,128)(2,1)} %weight_grad.2), calls=%async_computation.4 | async-start | bytes 1310720 | tf_op jit(solution)/shard_map/all_to_all | solution.py:502
  215.6 3.9 %collective-permute-start.18 = (bf16[256,512]{1,0:T(8,128)(2,1)S(1)}, bf16[256,512]{1,0:T(8,128)(2,1)S(1)}, u32[]{:S(2)}, u32[]{:S(2)}) collective-permute-start(bf16[256,512]{1,0:T(8,128)(2,1)S(1)} %get-tuple-element.89.rest_0_), channel_id=1, source_target_pairs={{0,0},{1,4},{4,1},{5,5},{2,2},{3,6},{6,3},{7,7},{8,8},{9,12},{12,9... | collective-permute-start | bytes 786440 | tf_op jit(solution)/shard_map/ppermute | solution.py:386
  222.5 2.5 collective-permute-start.11
  225.9 4.9 %collective-permute-done.13.rest_3_ = bf16[272,256]{1,0:T(8,128)(2,1)S(1)} collective-permute-done((bf16[272,256]{1,0:T(8,128)(2,1)S(1)}, bf16[272,256]{1,0:T(8,128)(2,1)S(1)}, u32[]{:S(2)}, u32[]{:S(2)}) %collective-permute-start.13) | collective-permute-done | bytes 139296 | tf_op jit(solution)/shard_map/ppermute | solution.py:398
  232.2 4.2 %collective-permute-start.7 = (bf16[256,512]{1,0:T(8,128)(2,1)}, bf16[256,512]{1,0:T(8,128)(2,1)}, u32[]{:S(2)}, u32[]{:S(2)}) collective-permute-start(bf16[256,512]{1,0:T(8,128)(2,1)} %copy-done.19), channel_id=1, source_target_pairs={{0,0},{1,4},{4,1},{5,5},{2,2},{3,6},{6,3},{7,7},{8,8},{9,12},{12,9... | collective-permute-start | bytes 786440 | tf_op jit(solution)/shard_map/ppermute | solution.py:386
  238.6 6.7 %all-to-all-start.5 = ((bf16[16,48,256]{2,1,0:T(8,128)(2,1)}), bf16[16,48,256]{2,1,0:T(8,128)(2,1)S(1)}, u32[]{:S(2)}, u32[]{:S(2)}) async-start(bf16[16,48,256]{2,1,0:T(8,128)(2,1)} %weight_grad.3), calls=%async_computation.5 | async-start | bytes 786432 | tf_op jit(solution)/shard_map/all_to_all | solution.py:513
  245.3 3.6 %collective-permute-start.19 = (bf16[256,256]{1,0:T(8,128)(2,1)S(1)}, bf16[256,256]{1,0:T(8,128)(2,1)S(1)}, u32[]{:S(2)}, u32[]{:S(2)}) collective-permute-start(bf16[256,256]{1,0:T(8,128)(2,1)S(1)} %slice.12), channel_id=1, source_target_pairs={{0,0},{1,4},{4,1},{5,5},{2,2},{3,6},{6,3},{7,7},{8,8},{9,12},{12,9... | collective-permute-start | bytes 393224 | tf_op jit(solution)/shard_map/ppermute | solution.py:386
  255.7 6.4 %grad_states.1 = bf16[256,5120]{1,0:T(8,128)(2,1)} custom-call(s32[2]{0:T(128)S(1)} %pad_add_fusion.where, bf16[256,512]{1,0:T(8,128)(2,1)S(1)} %copy-done.13, bf16[256,256]{1,0:T(8,128)(2,1)S(1)} %collective-permute-done.19.gkv_ref, bf16[2560,512]{1,0:T(8,128)(2,1)} %all-gather.2.cloned.1.call-done.w_ref.q_ref, ...), custom_call_target="tpu_custom_call" | custom-call | tf_op jit(solution)/shard_map/grad_states/pallas_call | solution.py:367
  (122 shorter events, 50.0 us)
Async XLA Ops:
  7.2 89.6 %all-gather.2.cloned.1.call-start = ((), (), s32[]{:S(2)}) async-start(), calls=%async_computation.6 | async-start | bytes 2662400 | tf_op jit(solution)/shard_map/all_gather | solution.py:431
  9.8 28.5 %all-to-all-start = ((bf16[64,40,256]{2,1,0:T(8,128)(2,1)}), bf16[64,40,256]{2,1,0:T(8,128)(2,1)S(1)}, u32[]{:S(2)}, u32[]{:S(2)}) async-start(bf16[64,40,256]{2,1,0:T(8,128)(2,1)} %broadcast_in_dim.12), calls=%async_computation | async-start | bytes 2621440 | tf_op jit(solution)/shard_map/all_to_all | solution.py:394
  38.3 4.9 %collective-permute-start = (bf16[2560,256]{1,0:T(8,128)(2,1)S(1)}, bf16[2560,256]{1,0:T(8,128)(2,1)S(1)}, u32[]{:S(2)}, u32[]{:S(2)}) collective-permute-start(bf16[2560,256]{1,0:T(8,128)(2,1)S(1)} %bitcast.18), channel_id=1, source_target_pairs={{0,1},{1,0},{2,3},{3,2},{4,5},{5,4},{6,7},{7,6},{8,9},{9,8},{10,11... | collective-permute-start | bytes 3932168 | tf_op jit(solution)/shard_map/ppermute | solution.py:390
  46.0 7.8 %collective-permute-start.1 = (bf16[256,256]{1,0:T(8,128)(2,1)S(1)}, bf16[256,256]{1,0:T(8,128)(2,1)S(1)}, u32[]{:S(2)}, u32[]{:S(2)}) collective-permute-start(bf16[256,256]{1,0:T(8,128)(2,1)S(1)} %get-tuple-element.65), channel_id=1, source_target_pairs={{0,0},{1,4},{4,1},{5,5},{2,2},{3,6},{6,3},{7,7},{8,8},{9,12},{12,9... | collective-permute-start | bytes 393224 | tf_op jit(solution)/shard_map/ppermute | solution.py:386
  55.3 47.1 %all-to-all-start.1 = ((bf16[16,256,256]{2,1,0:T(8,128)(2,1)}), bf16[16,256,256]{2,1,0:T(8,128)(2,1)}, u32[]{:S(2)}, u32[]{:S(2)}) async-start(bf16[16,256,256]{2,1,0:T(8,128)(2,1)} %broadcast_in_dim.14), calls=%async_computation.1 | async-start | bytes 4194304 | tf_op jit(solution)/shard_map/all_to_all | solution.py:460
  63.0 33.8 %collective-permute-start.2 = (bf16[256,2560]{1,0:T(8,128)(2,1)}, bf16[256,2560]{1,0:T(8,128)(2,1)S(1)}, u32[]{:S(2)}, u32[]{:S(2)}) collective-permute-start(bf16[256,2560]{1,0:T(8,128)(2,1)} %copy-done.6), channel_id=1, source_target_pairs={{0,1},{1,0},{2,3},{3,2},{4,5},{5,4},{6,7},{7,6},{8,9},{9,8},{10,11... | collective-permute-start | bytes 3932168 | tf_op jit(solution)/shard_map/ppermute | solution.py:390
  63.1 38.6 %collective-permute-start.3 = (bf16[256,512]{1,0:T(8,128)(2,1)}, bf16[256,512]{1,0:T(8,128)(2,1)S(1)}, u32[]{:S(2)}, u32[]{:S(2)}) collective-permute-start(bf16[256,512]{1,0:T(8,128)(2,1)} %bitcast.28), channel_id=1, source_target_pairs={{0,0},{1,4},{4,1},{5,5},{2,2},{3,6},{6,3},{7,7},{8,8},{9,12},{12,9... | collective-permute-start | bytes 786440 | tf_op jit(solution)/shard_map/ppermute | solution.py:386
  102.4 26.1 %collective-permute-start.6 = (bf16[16,256,256]{2,1,0:T(8,128)(2,1)}, bf16[16,256,256]{2,1,0:T(8,128)(2,1)}, u32[]{:S(2)}, u32[]{:S(2)}) collective-permute-start(bf16[16,256,256]{2,1,0:T(8,128)(2,1)} %all-to-all-done.1.kv_ref), channel_id=1, source_target_pairs={{0,1},{1,0},{2,3},{3,2},{4,5},{5,4},{6,7},{7,6},{8,9},{9,8},{10,11... | collective-permute-start | bytes 6291464 | tf_op jit(solution)/shard_map/ppermute | solution.py:390
  104.2 4.6 %collective-permute-start.4 = (f32[256,512]{1,0:T(8,128)}, f32[256,512]{1,0:T(8,128)S(1)}, u32[]{:S(2)}, u32[]{:S(2)}) collective-permute-start(f32[256,512]{1,0:T(8,128)} %copy-done.18), channel_id=1, source_target_pairs={{0,1},{1,0},{2,3},{3,2},{4,5},{5,4},{6,7},{7,6},{8,9},{9,8},{10,11... | collective-permute-start | bytes 1572872 | tf_op jit(solution)/shard_map/ppermute | solution.py:390
  110.4 9.2 %collective-permute-start.5 = (bf16[256,512]{1,0:T(8,128)(2,1)S(1)}, bf16[256,512]{1,0:T(8,128)(2,1)S(1)}, u32[]{:S(2)}, u32[]{:S(2)}) collective-permute-start(bf16[256,512]{1,0:T(8,128)(2,1)S(1)} %get-tuple-element.71), channel_id=1, source_target_pairs={{0,0},{1,4},{4,1},{5,5},{2,2},{3,6},{6,3},{7,7},{8,8},{9,12},{12,9... | collective-permute-start | bytes 786440 | tf_op jit(solution)/shard_map/ppermute | solution.py:386
  114.2 52.1 %collective-permute-start.9 = (bf16[2560,512]{1,0:T(8,128)(2,1)}, bf16[2560,512]{1,0:T(8,128)(2,1)}, u32[]{:S(2)}, u32[]{:S(2)}) collective-permute-start(bf16[2560,512]{1,0:T(8,128)(2,1)} %all-gather.2.cloned.1.call-done.w_ref.q_ref), channel_id=1, source_target_pairs={{0,1},{1,0},{2,3},{3,2},{4,5},{5,4},{6,7},{7,6},{8,9},{9,8},{10,11... | collective-permute-start | bytes 7864328 | tf_op jit(solution)/shard_map/ppermute | solution.py:390
  120.4 46.0 %all-to-all-start.2 = ((bf16[8,640,256]{2,1,0:T(8,128)(2,1)}), bf16[8,640,256]{2,1,0:T(8,128)(2,1)S(1)}, u32[]{:S(2)}, u32[]{:S(2)}) async-start(bf16[8,640,256]{2,1,0:T(8,128)(2,1)} %copy-done.4), calls=%async_computation.2 | async-start | bytes 5242880 | tf_op jit(solution)/shard_map/all_to_all | solution.py:482
  124.1 42.2 %collective-permute-start.8 = (bf16[256,640]{1,0:T(8,128)(2,1)S(1)}, bf16[256,640]{1,0:T(8,128)(2,1)S(1)}, u32[]{:S(2)}, u32[]{:S(2)}) collective-permute-start(bf16[256,640]{1,0:T(8,128)(2,1)S(1)} %pad_maximum_fusion), channel_id=1, source_target_pairs={{0,0},{1,4},{4,1},{5,5},{2,2},{3,6},{6,3},{7,7},{8,8},{9,12},{12,9... | collective-permute-start | bytes 983048 | tf_op jit(solution)/shard_map/ppermute | solution.py:386
  166.4 4.5 %collective-permute-start.10 = (bf16[16,256,256]{2,1,0:T(8,128)(2,1)}, bf16[16,256,256]{2,1,0:T(8,128)(2,1)S(1)}, u32[]{:S(2)}, u32[]{:S(2)}) collective-permute-start(bf16[16,256,256]{2,1,0:T(8,128)(2,1)} %copy-done.17), channel_id=1, source_target_pairs={{0,1},{1,0},{2,3},{3,2},{4,5},{5,4},{6,7},{7,6},{8,9},{9,8},{10,11... | collective-permute-start | bytes 6291464 | tf_op jit(solution)/shard_map/ppermute | solution.py:390
  174.4 33.0 %all-to-all-start.3 = ((bf16[16,256,256]{2,1,0:T(8,128)(2,1)}), bf16[16,256,256]{2,1,0:T(8,128)(2,1)}, u32[]{:S(2)}, u32[]{:S(2)}) async-start(bf16[16,256,256]{2,1,0:T(8,128)(2,1)} %add_convert_fusion), calls=%async_computation.3 | async-start | bytes 4194304 | tf_op jit(solution)/shard_map/all_to_all | solution.py:493
  182.7 9.6 %collective-permute-start.22 = (bf16[256,512]{1,0:T(8,128)(2,1)S(1)}, bf16[256,512]{1,0:T(8,128)(2,1)S(1)}, u32[]{:S(2)}, u32[]{:S(2)}) collective-permute-start(bf16[256,512]{1,0:T(8,128)(2,1)S(1)} %get-tuple-element.89.rest_0_), channel_id=1, source_target_pairs={{0,2},{2,4},{4,6},{6,0},{1,3},{3,5},{5,7},{7,1},{8,10},{10,12},{12... | collective-permute-start | bytes 786440 | tf_op jit(solution)/shard_map/ppermute | solution.py:398
  183.0 15.3 %collective-permute-start.21 = (bf16[256,512]{1,0:T(8,128)(2,1)S(1)}, bf16[256,512]{1,0:T(8,128)(2,1)S(1)}, u32[]{:S(2)}, u32[]{:S(2)}) collective-permute-start(bf16[256,512]{1,0:T(8,128)(2,1)S(1)} %get-tuple-element.89.rest_0_), channel_id=1, source_target_pairs={{0,4},{2,6},{4,0},{6,2},{1,5},{3,7},{5,1},{7,3},{8,12},{10,14},{12... | collective-permute-start | bytes 786440 | tf_op jit(solution)/shard_map/ppermute | solution.py:398
  184.7 13.7 %collective-permute-start.20 = (bf16[256,512]{1,0:T(8,128)(2,1)S(1)}, bf16[256,512]{1,0:T(8,128)(2,1)S(1)}, u32[]{:S(2)}, u32[]{:S(2)}) collective-permute-start(bf16[256,512]{1,0:T(8,128)(2,1)S(1)} %get-tuple-element.89.rest_0_), channel_id=1, source_target_pairs={{0,6},{2,0},{4,2},{6,4},{1,7},{3,1},{5,3},{7,5},{8,14},{10,8},{12,... | collective-permute-start | bytes 786440 | tf_op jit(solution)/shard_map/ppermute | solution.py:398
  185.5 13.5 %collective-permute-start.23 = (bf16[256,512]{1,0:T(8,128)(2,1)S(1)}, bf16[256,512]{1,0:T(8,128)(2,1)S(1)}, u32[]{:S(2)}, u32[]{:S(2)}) collective-permute-start(bf16[256,512]{1,0:T(8,128)(2,1)S(1)} %get-tuple-element.89.rest_0_), channel_id=1, source_target_pairs={{0,1},{1,0},{2,3},{3,2},{4,5},{5,4},{6,7},{7,6},{8,9},{9,8},{10,11... | collective-permute-start | bytes 786440 | tf_op jit(solution)/shard_map/ppermute | solution.py:390
  192.3 7.2 %collective-permute-start.26 = (bf16[256,512]{1,0:T(8,128)(2,1)S(1)}, bf16[256,512]{1,0:T(8,128)(2,1)S(1)}, u32[]{:S(2)}, u32[]{:S(2)}) collective-permute-start(bf16[256,512]{1,0:T(8,128)(2,1)S(1)} %collective-permute-done.22.rest_3_), channel_id=1, source_target_pairs={{0,1},{1,0},{2,3},{3,2},{4,5},{5,4},{6,7},{7,6},{8,9},{9,8},{10,11... | collective-permute-start | bytes 786440 | tf_op jit(solution)/shard_map/ppermute | solution.py:390
  207.4 31.2 %all-to-all-start.4 = ((bf16[16,40,512]{2,1,0:T(8,128)(2,1)}), bf16[16,40,512]{2,1,0:T(8,128)(2,1)}, u32[]{:S(2)}, u32[]{:S(2)}) async-start(bf16[16,40,512]{2,1,0:T(8,128)(2,1)} %weight_grad.2), calls=%async_computation.4 | async-start | bytes 1310720 | tf_op jit(solution)/shard_map/all_to_all | solution.py:502
  215.6 15.9 %collective-permute-start.18 = (bf16[256,512]{1,0:T(8,128)(2,1)S(1)}, bf16[256,512]{1,0:T(8,128)(2,1)S(1)}, u32[]{:S(2)}, u32[]{:S(2)}) collective-permute-start(bf16[256,512]{1,0:T(8,128)(2,1)S(1)} %get-tuple-element.89.rest_0_), channel_id=1, source_target_pairs={{0,0},{1,4},{4,1},{5,5},{2,2},{3,6},{6,3},{7,7},{8,8},{9,12},{12,9... | collective-permute-start | bytes 786440 | tf_op jit(solution)/shard_map/ppermute | solution.py:386
  221.6 9.2 %collective-permute-start.13 = (bf16[272,256]{1,0:T(8,128)(2,1)S(1)}, bf16[272,256]{1,0:T(8,128)(2,1)S(1)}, u32[]{:S(2)}, u32[]{:S(2)}) collective-permute-start(bf16[272,256]{1,0:T(8,128)(2,1)S(1)} %grad_key_value.1.rest_0_), channel_id=1, source_target_pairs={{0,2},{2,4},{4,6},{6,0},{1,3},{3,5},{5,7},{7,1},{8,10},{10,12},{12... | collective-permute-start | bytes 417800 | tf_op jit(solution)/shard_map/ppermute | solution.py:398
  222.5 8.5 %collective-permute-start.12 = (bf16[272,256]{1,0:T(8,128)(2,1)S(1)}, bf16[272,256]{1,0:T(8,128)(2,1)S(1)}, u32[]{:S(2)}, u32[]{:S(2)}) collective-permute-start(bf16[272,256]{1,0:T(8,128)(2,1)S(1)} %grad_key_value.1.rest_0_), channel_id=1, source_target_pairs={{0,4},{2,6},{4,0},{6,2},{1,5},{3,7},{5,1},{7,3},{8,12},{10,14},{12... | collective-permute-start | bytes 417800 | tf_op jit(solution)/shard_map/ppermute | solution.py:398
  222.5 8.8 %collective-permute-start.11 = (bf16[272,256]{1,0:T(8,128)(2,1)S(1)}, bf16[272,256]{1,0:T(8,128)(2,1)S(1)}, u32[]{:S(2)}, u32[]{:S(2)}) collective-permute-start(bf16[272,256]{1,0:T(8,128)(2,1)S(1)} %grad_key_value.1.rest_0_), channel_id=1, source_target_pairs={{0,6},{2,0},{4,2},{6,4},{1,7},{3,1},{5,3},{7,5},{8,14},{10,8},{12,... | collective-permute-start | bytes 417800 | tf_op jit(solution)/shard_map/ppermute | solution.py:398
  225.0 11.4 %collective-permute-start.14 = (bf16[272,256]{1,0:T(8,128)(2,1)S(1)}, bf16[272,256]{1,0:T(8,128)(2,1)S(1)}, u32[]{:S(2)}, u32[]{:S(2)}) collective-permute-start(bf16[272,256]{1,0:T(8,128)(2,1)S(1)} %grad_key_value.1.rest_0_), channel_id=1, source_target_pairs={{0,1},{1,0},{2,3},{3,2},{4,5},{5,4},{6,7},{7,6},{8,9},{9,8},{10,11... | collective-permute-start | bytes 417800 | tf_op jit(solution)/shard_map/ppermute | solution.py:390
  230.8 5.7 %collective-permute-start.17 = (bf16[272,256]{1,0:T(8,128)(2,1)S(1)}, bf16[272,256]{1,0:T(8,128)(2,1)S(1)}, u32[]{:S(2)}, u32[]{:S(2)}) collective-permute-start(bf16[272,256]{1,0:T(8,128)(2,1)S(1)} %collective-permute-done.13.rest_3_), channel_id=1, source_target_pairs={{0,1},{1,0},{2,3},{3,2},{4,5},{5,4},{6,7},{7,6},{8,9},{9,8},{10,11... | collective-permute-start | bytes 417800 | tf_op jit(solution)/shard_map/ppermute | solution.py:390
  231.0 5.4 %collective-permute-start.16 = (bf16[272,256]{1,0:T(8,128)(2,1)S(1)}, bf16[272,256]{1,0:T(8,128)(2,1)S(1)}, u32[]{:S(2)}, u32[]{:S(2)}) collective-permute-start(bf16[272,256]{1,0:T(8,128)(2,1)S(1)} %collective-permute-done.12.rest_2_), channel_id=1, source_target_pairs={{0,1},{1,0},{2,3},{3,2},{4,5},{5,4},{6,7},{7,6},{8,9},{9,8},{10,11... | collective-permute-start | bytes 417800 | tf_op jit(solution)/shard_map/ppermute | solution.py:390
  231.3 5.2 %collective-permute-start.15 = (bf16[272,256]{1,0:T(8,128)(2,1)S(1)}, bf16[272,256]{1,0:T(8,128)(2,1)S(1)}, u32[]{:S(2)}, u32[]{:S(2)}) collective-permute-start(bf16[272,256]{1,0:T(8,128)(2,1)S(1)} %collective-permute-done.11.rest_1_), channel_id=1, source_target_pairs={{0,1},{1,0},{2,3},{3,2},{4,5},{5,4},{6,7},{7,6},{8,9},{9,8},{10,11... | collective-permute-start | bytes 417800 | tf_op jit(solution)/shard_map/ppermute | solution.py:390
  232.2 13.0 %collective-permute-start.7 = (bf16[256,512]{1,0:T(8,128)(2,1)}, bf16[256,512]{1,0:T(8,128)(2,1)}, u32[]{:S(2)}, u32[]{:S(2)}) collective-permute-start(bf16[256,512]{1,0:T(8,128)(2,1)} %copy-done.19), channel_id=1, source_target_pairs={{0,0},{1,4},{4,1},{5,5},{2,2},{3,6},{6,3},{7,7},{8,8},{9,12},{12,9... | collective-permute-start | bytes 786440 | tf_op jit(solution)/shard_map/ppermute | solution.py:386
  238.6 23.5 %all-to-all-start.5 = ((bf16[16,48,256]{2,1,0:T(8,128)(2,1)}), bf16[16,48,256]{2,1,0:T(8,128)(2,1)S(1)}, u32[]{:S(2)}, u32[]{:S(2)}) async-start(bf16[16,48,256]{2,1,0:T(8,128)(2,1)} %weight_grad.3), calls=%async_computation.5 | async-start | bytes 786432 | tf_op jit(solution)/shard_map/all_to_all | solution.py:513
  245.3 7.8 %collective-permute-start.19 = (bf16[256,256]{1,0:T(8,128)(2,1)S(1)}, bf16[256,256]{1,0:T(8,128)(2,1)S(1)}, u32[]{:S(2)}, u32[]{:S(2)}) collective-permute-start(bf16[256,256]{1,0:T(8,128)(2,1)S(1)} %slice.12), channel_id=1, source_target_pairs={{0,0},{1,4},{4,1},{5,5},{2,2},{3,6},{6,3},{7,7},{8,8},{9,12},{12,9... | collective-permute-start | bytes 393224 | tf_op jit(solution)/shard_map/ppermute | solution.py:386
  (28 other events, 142.0 us)
Sparse Core Ops, SparseCore 0:
  10.9 85.9 all-gather.1

commit v3 on v2

--- a/solution.py
+++ b/solution.py
@@ -1,3 +1,4 @@
+import functools
 import math
 
 import jax
@@ -51,37 +52,34 @@
 
 
 def prepare_kernel(where, src_ref, toks_ref, toks_theirs_ref, turned_ref):
-    planes, columns = src_ref.shape[:2]
+    sizes = src_ref.shape[:3]
     core = where[1]
 
-    def piece(plane, y, side):
-        return src_ref[plane, y, side].astype(f32)
-
-    group = 4
-    for side, out_ref in ((core, toks_ref), (1 - core, toks_theirs_ref)):
-        for i in range(0, planes, group):
-            rows = jnp.concatenate(
-                [piece(i + j, y, side) for j in range(group) for y in range(columns)], axis=0
-            ).astype(bf16)
-            wide = rows.shape[0]
-            out_ref[:, i // group * wide : (i // group + 1) * wide] = rows.T
-    for y in range(columns):
+    def rows(y, side):
+        pieces = [src_ref[x, z, y, side].astype(f32) for z in range(sizes[1]) for x in range(sizes[0])]
+        return jnp.concatenate(pieces, axis=0).astype(bf16)
+
+    for y in range(sizes[2]):
+        toks_ref[y] = rows(y, core).T
+        toks_theirs_ref[y] = rows(y, 1 - core).T
         for side in range(2):
-            turned_ref[2 * y + side] = jnp.concatenate(
-                [piece(i, y, side) for i in range(planes)], axis=0
-            ).astype(bf16)
+            turned_ref[2 * y + side] = rows(y, side)
 
 
 def key_value_kernel(mine_ref, other_ref, w_ref, w_other_ref, gain_ref, cos_ref, sin_ref, kv_ref, raw_ref):
-    raw = mm(mine_ref[...], w_ref[...]) + mm(other_ref[...], w_other_ref[...])
+    raw = sum(mm(mine_ref[y], w_ref[y]) + mm(other_ref[y], w_other_ref[y]) for y in range(w_ref.shape[0]))
     raw_ref[...] = raw[:, :span]
     kv_ref[:, :span] = shape_head(raw[:, :span], gain_ref[...], cos_ref[...], sin_ref[...]).astype(bf16)
     kv_ref[:, span:] = raw[:, span:].astype(bf16)
 
 
-def query_part_kernel(mine_ref, other_ref, w_ref, part_ref, part_other_ref):
-    part_ref[...] = mm(mine_ref[...], w_ref[...])
-    part_other_ref[...] = mm(other_ref[...], w_ref[...])
+def query_part_kernel(mine_ref, other_ref, w_ref, w_upper_ref, part_ref, part_other_ref):
+    cols = w_ref.shape[2]
+    for toks_ref, out_ref in ((mine_ref, part_ref), (other_ref, part_other_ref)):
+        for i, w in enumerate((w_ref, w_upper_ref)):
+            out_ref[:, i * cols : (i + 1) * cols] = sum(
+                mm(toks_ref[y], w[y]) for y in range(w.shape[0])
+            )
 
 
 def query_kernel(part_ref, part_theirs_ref, gain_ref, cos_ref, sin_ref, q_ref, raw_ref):
@@ -257,9 +255,7 @@
             pltpu.VMEM((span, rows), f32),
         ],
         compiler_params=pltpu.CompilerParams(vmem_limit_bytes=48 * mib),
-        cost_estimate=pl.CostEstimate(
-            flops=3 * 10**10, bytes_accessed=10 * 10**6, transcendentals=9 * 10**6
-        ),
+        cost_estimate=cheap,
         name="attention",
     )(order, own, q16, g16, kv, kv_other)
 
@@ -329,28 +325,32 @@
         in_specs=[smem] + [vmem] * (1 + len(blocks)),
         out_specs=vmem,
         compiler_params=pltpu.CompilerParams(vmem_limit_bytes=48 * mib),
+        cost_estimate=cheap,
         name="weight_grad",
     )(where, turned, *blocks)
 
 
-def grad_states_kernel(where, gq_ref, gkv_ref, q_ref, q_theirs_ref, kv_ref, kv_theirs_ref, out_ref):
+def grad_states_kernel(
+    where, gq_ref, gkv_ref, kv_ref, kv_theirs_ref, q_ref, q_theirs_ref, upper_ref, upper_theirs_ref, out_ref, blocks,
+):
     core = where[1]
-    own_rows, group = 40, 640
-    transposed = (((1,), (1,)), ((), ()))
-
-    def product(q, kv, i):
-        part = slice(i * group, (i + 1) * group)
-        return lax.dot_general(
-            q[part], gq_ref[...], transposed, preferred_element_type=f32
-        ) + lax.dot_general(kv[part], gkv_ref[...], transposed, preferred_element_type=f32)
-
-    for i in range(q_ref.shape[0] // group):
-        mine, theirs = product(q_ref, kv_ref, i), product(q_theirs_ref, kv_theirs_ref, i)
-        sides = (jnp.where(core == 0, mine, theirs), jnp.where(core == 0, theirs, mine))
-        rows = jnp.concatenate(
-            [side[j : j + own_rows] for j in range(0, group, own_rows) for side in sides], axis=0
-        )
-        out_ref[:, 2 * i * group : 2 * (i + 1) * group] = rows.astype(bf16).T
+    columns, cols = kv_ref.shape[0], kv_ref.shape[2]
+    own_rows = 40
+    grads = (gkv_ref[...], gq_ref[:, :cols], gq_ref[:, cols:])
+    sides = ((core, (kv_ref, q_ref, upper_ref)), (1 - core, (kv_theirs_ref, q_theirs_ref, upper_theirs_ref)))
+    for at_core, weights in sides:
+        for y in range(columns):
+            blocks[y, at_core] = sum(
+                lax.dot_general(w[y], grad, (((1,), (1,)), ((), ())), preferred_element_type=f32)
+                for w, grad in zip(weights, grads)
+            )
+    for x in range(4):
+        pieces = []
+        for z in range(4):
+            part = slice((z * 4 + x) * own_rows, (z * 4 + x + 1) * own_rows)
+            pieces += [blocks[y, c, part] for y in range(columns) for c in range(2)]
+        rows = jnp.concatenate(pieces, axis=0)
+        out_ref[:, x * rows.shape[0] : (x + 1) * rows.shape[0]] = rows.astype(bf16).T
 
 
 def finish_kernel(parts_ref, key_ref, value_ref, gain_q_ref, gain_k_ref):
@@ -363,21 +363,25 @@
     gain_k_ref[...] = gains[1:2]
 
 
-def call(kernel, shapes, *args, name, cost=None):
+cheap = pl.CostEstimate(flops=1000, bytes_accessed=1000, transcendentals=0)
+
+
+def call(kernel, shapes, *args, name):
     return pl.pallas_call(
         kernel,
         out_shape=shapes,
         in_specs=[smem if a.dtype == jnp.int32 else vmem for a in args],
         out_specs=jax.tree.map(lambda _: vmem, shapes),
         compiler_params=pltpu.CompilerParams(vmem_limit_bytes=48 * mib),
-        cost_estimate=cost,
+        cost_estimate=cheap,
         name=name,
     )(*args)
 
 
 plane = ("x", "z")
+owners = ("z", "x")
 column = ("y_hi", "y_lo")
-chips = plane + column
+chips = column + owners
 swapped = [(0, 0), (1, 2), (2, 1), (3, 3)]
 flipped = [(0, 1), (1, 0)]
 
@@ -396,6 +400,33 @@
 
 def ring(array, step):
     return lax.ppermute(array, column, [(i, (i - step) % 4) for i in range(4)])
+
+
+def place_kernel(axis, where, *refs):
+    out_ref = refs[-1]
+    inner = out_ref.shape[:axis]
+    for k, block in enumerate(refs[:-1]):
+        at = lax.rem(where[0] + k, 4)
+        if axis == 0:
+            out_ref[at] = block[...]
+        elif axis == 1:
+            for i in range(inner[0]):
+                out_ref[i, at] = block[i]
+        else:
+            for i in range(inner[0]):
+                for j in range(inner[1]):
+                    out_ref[i, j, at] = block[i, j]
+
+
+def collect(array, name, axis):
+    parts = [array] + [
+        lax.ppermute(array, name, [(i, (i - k) % 4) for i in range(4)]) for k in range(1, 4)
+    ]
+    where = lax.axis_index(name).astype(jnp.int32)[None]
+    shape = array.shape[:axis] + (4,) + array.shape[axis:]
+    return call(
+        functools.partial(place_kernel, axis), jax.ShapeDtypeStruct(shape, bf16), where, *parts, name="place"
+    )
 
 
 def around(array):
@@ -428,18 +459,29 @@
     gain_q, gain_k = gain_query[None, :], gain_key[None, :]
     shape = jax.ShapeDtypeStruct
 
-    q_mine = lax.all_gather(w_query, chips, axis=0, tiled=True)
-    kv_mine = to_all(jnp.concatenate([w_key, w_value], axis=1), chips, planes * columns)
-    kv_mine = kv_mine.reshape(half, kv_cols)
+    w_kv = jnp.concatenate([w_key, w_value], axis=1)
+    kv_mine, q_low = collect(w_kv, "x", 0), collect(w_query[:, :kv_cols], column, 0)
+    kv_mine, q_low = lax.optimization_barrier((kv_mine, q_low))
+    kv_mine, q_low = collect(kv_mine, column, 0), collect(q_low, "z", 1)
+    q_high = collect(w_query[:, kv_cols:], "z", 0)
+    kv_mine, q_low, q_high = lax.optimization_barrier((kv_mine, q_low, q_high))
+    kv_mine, q_low = collect(kv_mine, "z", 1), collect(q_low, "x", 2)
+    q_high = collect(q_high, "x", 1)
+    kv_mine, q_low, q_high = lax.optimization_barrier((kv_mine, q_low, q_high))
+    q_high = collect(q_high, column, 0)
+    by_y = (columns, half // columns, kv_cols)
+    kv_mine, q_low, q_high = kv_mine.reshape(by_y), q_low.reshape(by_y), q_high.reshape(by_y)
 
     toks_mine, toks_theirs, turned = pl.pallas_call(
         prepare_kernel,
-        out_shape=(shape((tok_rows, half), bf16),) * 2 + (shape((2 * columns, width // 8, tok_rows), bf16),),
+        out_shape=(shape((columns, tok_rows, half // columns), bf16),) * 2
+        + (shape((2 * columns, half // columns, tok_rows), bf16),),
         in_specs=[smem, vmem],
         out_specs=(vmem,) * 3,
         compiler_params=pltpu.CompilerParams(vmem_limit_bytes=48 * mib),
+        cost_estimate=cheap,
         name="prepare",
-    )(where, tokens.T.reshape(planes, columns, 2, own_rows, tok_rows))
+    )(where, tokens.T.reshape(4, 4, columns, 2, own_rows, tok_rows))
 
     toks_other = flip(toks_theirs)
     kv_mine, toks_mine, toks_theirs, turned, cosine, sine, cos_there, sin_there, own = (
@@ -456,15 +498,12 @@
         name="key_value",
     )
     kv_send = jnp.broadcast_to(swap(kv16)[None], (planes, tok_rows, kv_cols))
-    q_mine, _ = lax.optimization_barrier((q_mine, kv_send))
     kv_own = lax.all_to_all(kv_send, plane, 0, 0)
-    cheap = pl.CostEstimate(flops=1000, bytes_accessed=1000, transcendentals=0)
     q_part, q_part_other = call(
         query_part_kernel,
         (shape((tok_rows, q_cols), f32),) * 2,
-        toks_mine, toks_other, q_mine,
+        toks_mine, toks_other, q_low, q_high,
         name="query_part",
-        cost=cheap,
     )
     kv_own, q_part, q_part_other, grad_out = lax.optimization_barrier(
         (kv_own, q_part, q_part_other, swap(cotangent[0]))
@@ -474,7 +513,6 @@
         (shape((tok_rows, q_cols), bf16),) * 2,
         q_part, flip(q_part_other), gain_q, cosine, sine,
         name="query",
-        cost=cheap,
     )
     kv_other = flip(kv_own)
     q16 = swap(q16)
@@ -485,9 +523,8 @@
     ctx, dq, dkv_mine, dkv_theirs = attention(
         block_order, own, q16, grad_out, kv_own, kv_other
     )
-    q_theirs = flip(q_mine)
-    dkv_theirs, dq, turned, raw_there, q_theirs = lax.optimization_barrier(
-        (dkv_theirs, dq, turned, raw_there, q_theirs)
+    dkv_theirs, dq, turned, raw_there, low_theirs, high_theirs = lax.optimization_barrier(
+        (dkv_theirs, dq, turned, raw_there, flip(q_low), flip(q_high))
     )
     dkv = (dkv_mine.astype(f32) + flip(dkv_theirs).astype(f32)).astype(bf16)
     dkv = lax.all_to_all(dkv, plane, 0, 0)
@@ -499,7 +536,7 @@
         name="grad_query",
     )
     parts = weight_grad(where, turned, around(g_q), planes, own_rows)
-    parts = lax.all_to_all(parts, plane, 0, 0)
+    parts = lax.all_to_all(parts, owners, 0, 0)
     own_query = jnp.sum(parts.astype(f32), axis=0)
 
     g_kv = call(
@@ -508,9 +545,9 @@
         raw_there[:, q_cols:], dkv, gain_k, cos_there, sin_there, gains_q,
         name="grad_key_value",
     )
-    blocks, g_q_back = lax.optimization_barrier((around(g_kv), swap(g_q)))
+    blocks, g_q_back, g_kv_back = lax.optimization_barrier((around(g_kv), swap(g_q), swap(g_kv)))
     parts = weight_grad(where, turned, blocks, planes, own_rows + 8)
-    parts = lax.all_to_all(parts, plane, 0, 0)
+    parts = lax.all_to_all(parts, owners, 0, 0)
     own_key, own_value, gain_sum_q, gain_sum_k = call(
         finish_kernel,
         (shape((own_rows, span), f32),) * 2 + (shape((1, span), f32),) * 2,
@@ -518,12 +555,16 @@
         name="finish",
     )
 
-    grad_states = call(
+    grad_states = pl.pallas_call(
         grad_states_kernel,
-        shape((tok_rows, width), bf16),
-        where, g_q_back, swap(g_kv[:tok_rows]), q_mine, q_theirs, kv_mine, kv_theirs,
+        out_shape=shape((tok_rows, width), bf16),
+        in_specs=[smem] + [vmem] * 8,
+        out_specs=vmem,
+        scratch_shapes=[pltpu.VMEM((columns, 2, half // columns, tok_rows), f32)],
+        compiler_params=pltpu.CompilerParams(vmem_limit_bytes=48 * mib),
+        cost_estimate=cheap,
         name="grad_states",
-    )
+    )(where, g_q_back, g_kv_back[:tok_rows], kv_mine, kv_theirs, q_low, low_theirs, q_high, high_theirs)
     return (
         swap(ctx)[None],
         grad_states[None],

time: 274 us -> 276 us (level)
  starting transfers between devices: 88.5 us -> 125 us
  waiting for transfers between devices: 78.6 us -> 50.3 us
  between operations: 14.4 us -> 1.18 us
  local copies, waits for them, and re-layouts: 25.6 us -> 34 us
    ppermute x0 -> x27, starting transfers between devices: none -> 31.4 us  [collect(): lax.ppermute(array, name, [(i, (i - k) % 4) for i in range(4)])]
    all_gather x1 -> x0, waiting for transfers between devices: 30.5 us -> none  [local(): q_mine = lax.all_gather(w_query, chips, axis=0, tiled=True)]
    ppermute x0 -> x27, waiting for transfers between devices: none -> 19.3 us  [collect(): lax.ppermute(array, name, [(i, (i - k) % 4) for i in range(4)])]
    all_to_all x3 -> x2, starting transfers between devices: 25.5 us -> 14.9 us  [local(): parts = lax.all_to_all(parts, owners, 0, 0)]
    ppermute x14 -> x15, starting transfers between devices: 13.9 us -> 23.9 us  [flip(): return lax.ppermute(array, 'core', flipped)]
    all_to_all x3 -> x2, waiting for transfers between devices: 6.89 us -> 0.01 us  [local(): parts = lax.all_to_all(parts, owners, 0, 0)]
    pallas_call x1 -> x2, Pallas kernels: 2.61 us -> 8.82 us  [the longest x1 6.23 us: local(): pl.pallas_call(grad_states_kernel, out_shape=shape((tok_rows, width), bf1...]
    pallas_call x7 -> x15, Pallas kernels: 14.6 us -> 8.63 us  [call(): pl.pallas_call(kernel, out_shape=shapes, in_specs=[smem if a.dtype == jnp...]
  transfers between devices with their start and end apart: 34 -> 60, of which waited for: 14 -> 16; matrix products, arithmetic and copies ran while one was open for 5% -> 5% of each run, Pallas kernels for 20% -> 19%
where the time goes in v3:
time: 276 us; the launch traced here: 273 us
  starting transfers between devices  125 us (45%)
  Pallas kernels  55 us (20%)
  waiting for transfers between devices  50.3 us (18%)
  local copies, waits for them, and re-layouts  34 us (12%)
  other arithmetic  7.82 us (3%)
    pallas_call x1, Pallas kernels, attention(): pl.pallas_call(attention_kernel, out_shape=(jax.ShapeDtypeStruct((rows_he...  32.5 us
    ppermute x27, starting transfers between devices, collect(): lax.ppermute(array, name, [(i, (i - k) % 4) for i in range(4)])  31.4 us
    ppermute x7, starting transfers between devices, swap(): return lax.ppermute(array, ('y_hi', 'core'), swapped)  30.3 us
    unnamed x64, local copies, waits for them, and re-layouts  23.9 us
    ppermute x15, starting transfers between devices, flip(): return lax.ppermute(array, 'core', flipped)  23.9 us
    ppermute x27, waiting for transfers between devices, collect(): lax.ppermute(array, name, [(i, (i - k) % 4) for i in range(4)])  19.3 us
    all_to_all x2, starting transfers between devices, local(): parts = lax.all_to_all(parts, owners, 0, 0)  14.9 us
    ppermute x7, waiting for transfers between devices, swap(): return lax.ppermute(array, ('y_hi', 'core'), swapped)  10 us
  transfers between devices with their start and end apart: 60, of which 16 were waited for; matrix products, arithmetic and copies ran while one was open for 5% of the time, Pallas kernels for 19%

profile of v3, /device:TPU:39, one launch (start us, length us, event | category | flops | bytes accessed | tf_op | source)
XLA Modules:
  0.0 273.3 jit_solution(3521976886706527504)
XLA Ops:
  1.4 2.7 %collective-permute-start.3 = (bf16[40,256]{1,0:T(8,128)(2,1)S(1)}, bf16[40,256]{1,0:T(8,128)(2,1)S(1)}, u32[]{:S(2)}, u32[]{:S(2)}) collective-permute-start(bf16[40,256]{1,0:T(8,128)(2,1)S(1)} %get-tuple-element.126.refs_0_), channel_id=1, source_target_pairs={{0,6},{2,0},{4,2},{6,4},{1,7},{3,1},{5,3},{7,5},{8,14},{10,8},{12,... | collective-permute-start | bytes 61448 | tf_op jit(solution)/shard_map/ppermute | solution.py:423
  10.7 2.8 %collective-permute-start.13 = (bf16[40,256]{1,0:T(8,128)(2,1)S(1)}, bf16[40,256]{1,0:T(8,128)(2,1)S(1)}, u32[]{:S(2)}, u32[]{:S(2)}) collective-permute-start(bf16[40,256]{1,0:T(8,128)(2,1)S(1)} %get-tuple-element.125.refs_0_), channel_id=1, source_target_pairs={{0,16},{8,24},{16,0},{24,8},{1,17},{9,25},{17,1},{25,9},{2,18},{10... | collective-permute-start | bytes 61448 | tf_op jit(solution)/shard_map/ppermute | solution.py:423
  22.2 4.4 %copy.15 = bf16[5120,256]{1,0:T(8,128)(2,1)} copy(bf16[5120,256]{0,1:T(8,128)(2,1)} %bitcast.36) | data formatting | bytes 5242880 | tf_op jit(solution)/shard_map/transpose | solution.py:484
  32.3 4.8 %collective-permute-done.21.refs_1_ = bf16[4,40,256]{2,1,0:T(8,128)(2,1)S(1)} collective-permute-done((bf16[4,40,256]{2,1,0:T(8,128)(2,1)S(1)}, bf16[4,40,256]{2,1,0:T(8,128)(2,1)S(1)}, u32[]{:S(2)}, u32[]{:S(2)}) %collective-permute-start.21) | collective-permute-done | bytes 81952 | tf_op jit(solution)/shard_map/ppermute | solution.py:423
  37.1 2.8 %collective-permute-start.15 = (bf16[4,4,40,256]{3,2,1,0:T(8,128)(2,1)S(1)}, bf16[4,4,40,256]{3,2,1,0:T(8,128)(2,1)S(1)}, u32[]{:S(2)}, u32[]{:S(2)}) collective-permute-start(bf16[4,4,40,256]{3,2,1,0:T(8,128)(2,1)S(1)} %place.11.refs_0_), channel_id=1, source_target_pairs={{0,24},{8,0},{16,8},{24,16},{1,25},{9,1},{17,9},{25,17},{2,26},{10... | collective-permute-start | bytes 983048 | tf_op jit(solution)/shard_map/ppermute | solution.py:423
  48.6 13.1 %collective-permute-start.24 = (bf16[4,640,256]{2,1,0:T(8,128)(2,1)S(1)}, bf16[4,640,256]{2,1,0:T(8,128)(2,1)S(1)}, u32[]{:S(2)}, u32[]{:S(2)}) collective-permute-start(bf16[4,640,256]{2,1,0:T(8,128)(2,1)S(1)} %bitcast.28), channel_id=1, source_target_pairs={{0,1},{1,0},{2,3},{3,2},{4,5},{5,4},{6,7},{7,6},{8,9},{9,8},{10,11... | collective-permute-start | bytes 3932168 | tf_op jit(solution)/shard_map/ppermute | solution.py:394
  61.7 2.7 collective-permute-done.24.w_other_ref.kv_theirs_ref
  66.2 4.0 %collective-permute-start.25 = (bf16[256,256]{1,0:T(8,128)(2,1)S(1)}, bf16[256,256]{1,0:T(8,128)(2,1)S(1)}, u32[]{:S(2)}, u32[]{:S(2)}) collective-permute-start(bf16[256,256]{1,0:T(8,128)(2,1)S(1)} %get-tuple-element.80), channel_id=1, source_target_pairs={{0,0},{1,4},{4,1},{5,5},{2,2},{3,6},{6,3},{7,7},{8,8},{9,12},{12,9... | collective-permute-start | bytes 393224 | tf_op jit(solution)/shard_map/ppermute | solution.py:390
  70.2 3.8 %collective-permute-done.25 = bf16[256,256]{1,0:T(8,128)(2,1)S(1)} collective-permute-done((bf16[256,256]{1,0:T(8,128)(2,1)S(1)}, bf16[256,256]{1,0:T(8,128)(2,1)S(1)}, u32[]{:S(2)}, u32[]{:S(2)}) %collective-permute-start.25) | collective-permute-done | bytes 131104 | tf_op jit(solution)/shard_map/ppermute | solution.py:390
  75.5 8.1 %all-to-all-start = ((bf16[16,256,256]{2,1,0:T(8,128)(2,1)}), bf16[16,256,256]{2,1,0:T(8,128)(2,1)}, u32[]{:S(2)}, u32[]{:S(2)}) async-start(bf16[16,256,256]{2,1,0:T(8,128)(2,1)} %broadcast_in_dim.20), calls=%async_computation | async-start | bytes 4194304 | tf_op jit(solution)/shard_map/all_to_all | solution.py:501
  83.7 3.5 %collective-permute-start.27 = (bf16[4,4,40,256]{3,2,1,0:T(8,128)(2,1)S(1)}, bf16[4,4,40,256]{3,2,1,0:T(8,128)(2,1)S(1)}, u32[]{:S(2)}, u32[]{:S(2)}) collective-permute-start(bf16[4,4,40,256]{3,2,1,0:T(8,128)(2,1)S(1)} %place.16.refs_0_), channel_id=1, source_target_pairs={{0,6},{2,0},{4,2},{6,4},{1,7},{3,1},{5,3},{7,5},{8,14},{10,8},{12,... | collective-permute-start | bytes 983048 | tf_op jit(solution)/shard_map/ppermute | solution.py:423
  87.8 4.8 %collective-permute-start.30 = (bf16[256,512]{1,0:T(8,128)(2,1)}, bf16[256,512]{1,0:T(8,128)(2,1)S(1)}, u32[]{:S(2)}, u32[]{:S(2)}) collective-permute-start(bf16[256,512]{1,0:T(8,128)(2,1)} %bitcast.39), channel_id=1, source_target_pairs={{0,0},{1,4},{4,1},{5,5},{2,2},{3,6},{6,3},{7,7},{8,8},{9,12},{12,9... | collective-permute-start | bytes 786440 | tf_op jit(solution)/shard_map/ppermute | solution.py:390
  92.6 11.5 %collective-permute-done.27.refs_1_ = bf16[4,4,40,256]{3,2,1,0:T(8,128)(2,1)S(1)} collective-permute-done((bf16[4,4,40,256]{3,2,1,0:T(8,128)(2,1)S(1)}, bf16[4,4,40,256]{3,2,1,0:T(8,128)(2,1)S(1)}, u32[]{:S(2)}, u32[]{:S(2)}) %collective-permute-start.27) | collective-permute-done | bytes 327712 | tf_op jit(solution)/shard_map/ppermute | solution.py:423
  106.0 3.1 %query_part.1 = (f32[256,512]{1,0:T(8,128)S(1)}, f32[256,512]{1,0:T(8,128)S(1)}) custom-call(bf16[4,256,640]{2,1,0:T(8,128)(2,1)S(1)} %get-tuple-element.75.mine_ref, bf16[4,256,640]{2,1,0:T(8,128)(2,1)S(1)} %collective-permute-done.26.other_ref, bf16[4,640,256]{2,1,0:T(8,128)(2,1)S(1)} %bitcast.22, bf16[4,640,256]{2,1,0:T(8,128)(2,1)} %bitcast.25), custom_call_target="tpu_custom_call" | custom-call | flops 1000 | bytes 1000 | tf_op jit(solution)/shard_map/query_part/pallas_call | solution.py:370
  115.5 3.0 %collective-permute-start.32 = (bf16[256,512]{1,0:T(8,128)(2,1)S(1)}, bf16[256,512]{1,0:T(8,128)(2,1)S(1)}, u32[]{:S(2)}, u32[]{:S(2)}) collective-permute-start(bf16[256,512]{1,0:T(8,128)(2,1)S(1)} %get-tuple-element.87), channel_id=1, source_target_pairs={{0,0},{1,4},{4,1},{5,5},{2,2},{3,6},{6,3},{7,7},{8,8},{9,12},{12,9... | collective-permute-start | bytes 786440 | tf_op jit(solution)/shard_map/ppermute | solution.py:390
  118.6 6.2 %collective-permute-done.32.q_ref = bf16[256,512]{1,0:T(8,128)(2,1)S(1)} collective-permute-done((bf16[256,512]{1,0:T(8,128)(2,1)S(1)}, bf16[256,512]{1,0:T(8,128)(2,1)S(1)}, u32[]{:S(2)}, u32[]{:S(2)}) %collective-permute-start.32) | collective-permute-done | bytes 262176 | tf_op jit(solution)/shard_map/ppermute | solution.py:390
  125.4 4.9 %all-to-all-start.1 = ((bf16[8,640,256]{2,1,0:T(8,128)(2,1)}), bf16[8,640,256]{2,1,0:T(8,128)(2,1)S(1)}, u32[]{:S(2)}, u32[]{:S(2)}) async-start(bf16[8,640,256]{2,1,0:T(8,128)(2,1)} %copy-done.7), calls=%async_computation.1 | async-start | bytes 5242880 | tf_op jit(solution)/shard_map/all_to_all | solution.py:520
  130.9 5.2 %collective-permute-start.35 = (bf16[256,640]{1,0:T(8,128)(2,1)S(1)}, bf16[256,640]{1,0:T(8,128)(2,1)}, u32[]{:S(2)}, u32[]{:S(2)}) collective-permute-start(bf16[256,640]{1,0:T(8,128)(2,1)S(1)} %pad_maximum_fusion), channel_id=1, source_target_pairs={{0,0},{1,4},{4,1},{5,5},{2,2},{3,6},{6,3},{7,7},{8,8},{9,12},{12,9... | collective-permute-start | bytes 983048 | tf_op jit(solution)/shard_map/ppermute | solution.py:390
  139.3 32.5 %attention.1 = (bf16[256,512]{1,0:T(8,128)(2,1)S(1)}, f32[256,512]{1,0:T(8,128)S(1)}, bf16[16,256,256]{2,1,0:T(8,128)(2,1)S(1)}, bf16[16,256,256]{2,1,0:T(8,128)(2,1)S(1)}) custom-call(s32[64]{0:T(128)S(1)} %copy-done.21, s32[3]{0:T(128)S(1)} %pad_add_fusion.1.own, bf16[256,512]{1,0:T(8,128)(2,1)S(1)} %copy-done.18, bf16[256,512]{1,0:T(8,128)(2,1)S(1)} %copy-done.16, ...), custom_call_target="tpu_custom_call" | custom-call | flops 1000 | bytes 1000 | tf_op jit(solution)/shard_map/attention/pallas_call | solution.py:230
  177.4 4.4 %collective-permute-done.38 = bf16[16,256,256]{2,1,0:T(8,128)(2,1)S(1)} collective-permute-done((bf16[16,256,256]{2,1,0:T(8,128)(2,1)}, bf16[16,256,256]{2,1,0:T(8,128)(2,1)S(1)}, u32[]{:S(2)}, u32[]{:S(2)}) %collective-permute-start.38) | collective-permute-done | bytes 2097184 | tf_op jit(solution)/shard_map/ppermute | solution.py:394
  181.7 3.5 %add_convert_fusion = bf16[16,256,256]{2,1,0:T(8,128)(2,1)} fusion(bf16[16,256,256]{2,1,0:T(8,128)(2,1)S(1)} %collective-permute-done.38, bf16[16,256,256]{2,1,0:T(8,128)(2,1)} %copy-done.8), kind=kLoop, calls=%fused_computation | loop fusion | flops 4194304 | bytes 6291456 | tf_op jit(solution)/shard_map/convert_element_type | solution.py:529
  185.3 6.7 %all-to-all-start.2 = ((bf16[16,256,256]{2,1,0:T(8,128)(2,1)}), bf16[16,256,256]{2,1,0:T(8,128)(2,1)}, u32[]{:S(2)}, u32[]{:S(2)}) async-start(bf16[16,256,256]{2,1,0:T(8,128)(2,1)} %add_convert_fusion), calls=%async_computation.2 | async-start | bytes 4194304 | tf_op jit(solution)/shard_map/all_to_all | solution.py:530
  197.9 3.0 %collective-permute-done.48.rest_1_ = bf16[256,512]{1,0:T(8,128)(2,1)S(1)} collective-permute-done((bf16[256,512]{1,0:T(8,128)(2,1)S(1)}, bf16[256,512]{1,0:T(8,128)(2,1)S(1)}, u32[]{:S(2)}, u32[]{:S(2)}) %collective-permute-start.48) | collective-permute-done | bytes 262176 | tf_op jit(solution)/shard_map/ppermute | solution.py:402
  200.9 6.4 %collective-permute-start.52 = (bf16[256,512]{1,0:T(8,128)(2,1)S(1)}, bf16[256,512]{1,0:T(8,128)(2,1)S(1)}, u32[]{:S(2)}, u32[]{:S(2)}) collective-permute-start(bf16[256,512]{1,0:T(8,128)(2,1)S(1)} %collective-permute-done.48.rest_1_), channel_id=1, source_target_pairs={{0,1},{1,0},{2,3},{3,2},{4,5},{5,4},{6,7},{7,6},{8,9},{9,8},{10,11... | collective-permute-start | bytes 786440 | tf_op jit(solution)/shard_map/ppermute | solution.py:394
  207.3 3.3 %collective-permute-done.50.rest_3_ = bf16[256,512]{1,0:T(8,128)(2,1)S(1)} collective-permute-done((bf16[256,512]{1,0:T(8,128)(2,1)S(1)}, bf16[256,512]{1,0:T(8,128)(2,1)S(1)}, u32[]{:S(2)}, u32[]{:S(2)}) %collective-permute-start.50) | collective-permute-done | bytes 262176 | tf_op jit(solution)/shard_map/ppermute | solution.py:402
  212.2 2.9 %weight_grad.2 = bf16[16,40,512]{2,1,0:T(8,128)(2,1)} custom-call(s32[2]{0:T(128)S(1)} %pad_add_fusion.where, bf16[8,640,256]{2,1,0:T(8,128)(2,1)S(1)} %all-to-all-done.1.turned_ref, bf16[256,512]{1,0:T(8,128)(2,1)S(1)} %get-tuple-element.105.rest_0_, bf16[256,512]{1,0:T(8,128)(2,1)S(1)} %collective-permute-done.48.rest_1_, ...), custom_call_target="tpu_custom_call" | custom-call | flops 1000 | bytes 1000 | tf_op jit(solution)/shard_map/weight_grad/pallas_call | solution.py:322
  215.8 2.6 all-to-all-done.2.dkv_ref
  218.4 8.2 %all-to-all-start.3 = ((bf16[16,40,512]{2,1,0:T(8,128)(2,1)}), bf16[16,40,512]{2,1,0:T(8,128)(2,1)}, u32[]{:S(2)}, u32[]{:S(2)}) async-start(bf16[16,40,512]{2,1,0:T(8,128)(2,1)} %weight_grad.2), calls=%async_computation.3 | async-start | bytes 1310720 | tf_op jit(solution)/shard_map/all_to_all | solution.py:539
  226.6 5.5 %collective-permute-start.46 = (bf16[256,512]{1,0:T(8,128)(2,1)}, bf16[256,512]{1,0:T(8,128)(2,1)S(1)}, u32[]{:S(2)}, u32[]{:S(2)}) collective-permute-start(bf16[256,512]{1,0:T(8,128)(2,1)} %copy-done.14), channel_id=1, source_target_pairs={{0,0},{1,4},{4,1},{5,5},{2,2},{3,6},{6,3},{7,7},{8,8},{9,12},{12,9... | collective-permute-start | bytes 786440 | tf_op jit(solution)/shard_map/ppermute | solution.py:390
  237.1 5.3 %collective-permute-start.47 = (bf16[272,256]{1,0:T(8,128)(2,1)S(1)}, bf16[272,256]{1,0:T(8,128)(2,1)S(1)}, u32[]{:S(2)}, u32[]{:S(2)}) collective-permute-start(bf16[272,256]{1,0:T(8,128)(2,1)S(1)} %grad_key_value.1.rest_0_), channel_id=1, source_target_pairs={{0,0},{1,4},{4,1},{5,5},{2,2},{3,6},{6,3},{7,7},{8,8},{9,12},{12,9... | collective-permute-start | bytes 417800 | tf_op jit(solution)/shard_map/ppermute | solution.py:390
  251.0 6.7 %all-to-all-start.4 = ((bf16[16,48,256]{2,1,0:T(8,128)(2,1)}), bf16[16,48,256]{2,1,0:T(8,128)(2,1)S(1)}, u32[]{:S(2)}, u32[]{:S(2)}) async-start(bf16[16,48,256]{2,1,0:T(8,128)(2,1)} %weight_grad.3), calls=%async_computation.4 | async-start | bytes 786432 | tf_op jit(solution)/shard_map/all_to_all | solution.py:550
  265.7 6.2 %grad_states.1 = bf16[256,5120]{1,0:T(8,128)(2,1)} custom-call(s32[2]{0:T(128)S(1)} %pad_add_fusion.where, bf16[256,512]{1,0:T(8,128)(2,1)S(1)} %collective-permute-done.46.gq_ref, bf16[256,256]{1,0:T(8,128)(2,1)S(1)} %slice.19.gkv_ref, bf16[4,640,256]{2,1,0:T(8,128)(2,1)S(1)} %bitcast.30, bf16[4,640,256]{2,1,0:T(8,128)(2,1)S(1)} %copy-done.6, ...), custom_call_target="tpu_custom_call" | custom-call | flops 1000 | bytes 1000 | tf_op jit(solution)/shard_map/grad_states/pallas_call | solution.py:558
  (193 shorter events, 83.6 us)
Async XLA Ops:
  17.6 9.0 %collective-permute-start.7 = (bf16[4,40,256]{2,1,0:T(8,128)(2,1)S(1)}, bf16[4,40,256]{2,1,0:T(8,128)(2,1)S(1)}, u32[]{:S(2)}, u32[]{:S(2)}) collective-permute-start(bf16[4,40,256]{2,1,0:T(8,128)(2,1)S(1)} %place.9.refs_0_), channel_id=1, source_target_pairs={{0,4},{2,6},{4,0},{6,2},{1,5},{3,7},{5,1},{7,3},{8,12},{10,14},{12... | collective-permute-start | bytes 245768 | tf_op jit(solution)/shard_map/ppermute | solution.py:423
  26.7 13.1 %collective-permute-start.18 = (bf16[4,4,40,256]{3,2,1,0:T(8,128)(2,1)S(1)}, bf16[4,4,40,256]{3,2,1,0:T(8,128)(2,1)S(1)}, u32[]{:S(2)}, u32[]{:S(2)}) collective-permute-start(bf16[4,4,40,256]{3,2,1,0:T(8,128)(2,1)S(1)} %place.12.refs_0_), channel_id=1, source_target_pairs={{0,96},{32,0},{64,32},{96,64},{1,97},{33,1},{65,33},{97,65},{2,98}... | collective-permute-start | bytes 983048 | tf_op jit(solution)/shard_map/ppermute | solution.py:423
  27.1 10.0 %collective-permute-start.21 = (bf16[4,40,256]{2,1,0:T(8,128)(2,1)S(1)}, bf16[4,40,256]{2,1,0:T(8,128)(2,1)S(1)}, u32[]{:S(2)}, u32[]{:S(2)}) collective-permute-start(bf16[4,40,256]{2,1,0:T(8,128)(2,1)S(1)} %place.13.refs_0_), channel_id=1, source_target_pairs={{0,96},{32,0},{64,32},{96,64},{1,97},{33,1},{65,33},{97,65},{2,98}... | collective-permute-start | bytes 245768 | tf_op jit(solution)/shard_map/ppermute | solution.py:423
  28.6 8.5 %collective-permute-start.22 = (bf16[4,40,256]{2,1,0:T(8,128)(2,1)S(1)}, bf16[4,40,256]{2,1,0:T(8,128)(2,1)S(1)}, u32[]{:S(2)}, u32[]{:S(2)}) collective-permute-start(bf16[4,40,256]{2,1,0:T(8,128)(2,1)S(1)} %place.13.refs_0_), channel_id=1, source_target_pairs={{0,64},{32,96},{64,0},{96,32},{1,65},{33,97},{65,1},{97,33},{2,66}... | collective-permute-start | bytes 245768 | tf_op jit(solution)/shard_map/ppermute | solution.py:423
  30.9 8.9 %collective-permute-start.23 = (bf16[4,40,256]{2,1,0:T(8,128)(2,1)S(1)}, bf16[4,40,256]{2,1,0:T(8,128)(2,1)S(1)}, u32[]{:S(2)}, u32[]{:S(2)}) collective-permute-start(bf16[4,40,256]{2,1,0:T(8,128)(2,1)S(1)} %place.13.refs_0_), channel_id=1, source_target_pairs={{0,32},{32,64},{64,96},{96,0},{1,33},{33,65},{65,97},{97,1},{2,34}... | collective-permute-start | bytes 245768 | tf_op jit(solution)/shard_map/ppermute | solution.py:423
  31.4 14.7 %collective-permute-start.19 = (bf16[4,4,40,256]{3,2,1,0:T(8,128)(2,1)S(1)}, bf16[4,4,40,256]{3,2,1,0:T(8,128)(2,1)S(1)}, u32[]{:S(2)}, u32[]{:S(2)}) collective-permute-start(bf16[4,4,40,256]{3,2,1,0:T(8,128)(2,1)S(1)} %place.12.refs_0_), channel_id=1, source_target_pairs={{0,64},{32,96},{64,0},{96,32},{1,65},{33,97},{65,1},{97,33},{2,66}... | collective-permute-start | bytes 983048 | tf_op jit(solution)/shard_map/ppermute | solution.py:423
  37.1 9.7 %collective-permute-start.20 = (bf16[4,4,40,256]{3,2,1,0:T(8,128)(2,1)S(1)}, bf16[4,4,40,256]{3,2,1,0:T(8,128)(2,1)S(1)}, u32[]{:S(2)}, u32[]{:S(2)}) collective-permute-start(bf16[4,4,40,256]{3,2,1,0:T(8,128)(2,1)S(1)} %place.12.refs_0_), channel_id=1, source_target_pairs={{0,32},{32,64},{64,96},{96,0},{1,33},{33,65},{65,97},{97,1},{2,34}... | collective-permute-start | bytes 983048 | tf_op jit(solution)/shard_map/ppermute | solution.py:423
  37.1 9.8 %collective-permute-start.15 = (bf16[4,4,40,256]{3,2,1,0:T(8,128)(2,1)S(1)}, bf16[4,4,40,256]{3,2,1,0:T(8,128)(2,1)S(1)}, u32[]{:S(2)}, u32[]{:S(2)}) collective-permute-start(bf16[4,4,40,256]{3,2,1,0:T(8,128)(2,1)S(1)} %place.11.refs_0_), channel_id=1, source_target_pairs={{0,24},{8,0},{16,8},{24,16},{1,25},{9,1},{17,9},{25,17},{2,26},{10... | collective-permute-start | bytes 983048 | tf_op jit(solution)/shard_map/ppermute | solution.py:423
  39.9 8.7 %collective-permute-start.17 = (bf16[4,4,40,256]{3,2,1,0:T(8,128)(2,1)S(1)}, bf16[4,4,40,256]{3,2,1,0:T(8,128)(2,1)S(1)}, u32[]{:S(2)}, u32[]{:S(2)}) collective-permute-start(bf16[4,4,40,256]{3,2,1,0:T(8,128)(2,1)S(1)} %place.11.refs_0_), channel_id=1, source_target_pairs={{0,8},{8,16},{16,24},{24,0},{1,9},{9,17},{17,25},{25,1},{2,10},{10... | collective-permute-start | bytes 983048 | tf_op jit(solution)/shard_map/ppermute | solution.py:423
  48.6 15.8 %collective-permute-start.24 = (bf16[4,640,256]{2,1,0:T(8,128)(2,1)S(1)}, bf16[4,640,256]{2,1,0:T(8,128)(2,1)S(1)}, u32[]{:S(2)}, u32[]{:S(2)}) collective-permute-start(bf16[4,640,256]{2,1,0:T(8,128)(2,1)S(1)} %bitcast.28), channel_id=1, source_target_pairs={{0,1},{1,0},{2,3},{3,2},{4,5},{5,4},{6,7},{7,6},{8,9},{9,8},{10,11... | collective-permute-start | bytes 3932168 | tf_op jit(solution)/shard_map/ppermute | solution.py:394
  75.5 35.8 %all-to-all-start = ((bf16[16,256,256]{2,1,0:T(8,128)(2,1)}), bf16[16,256,256]{2,1,0:T(8,128)(2,1)}, u32[]{:S(2)}, u32[]{:S(2)}) async-start(bf16[16,256,256]{2,1,0:T(8,128)(2,1)} %broadcast_in_dim.20), calls=%async_computation | async-start | bytes 4194304 | tf_op jit(solution)/shard_map/all_to_all | solution.py:501
  83.7 22.3 %collective-permute-start.26 = (bf16[4,256,640]{2,1,0:T(8,128)(2,1)}, bf16[4,256,640]{2,1,0:T(8,128)(2,1)S(1)}, u32[]{:S(2)}, u32[]{:S(2)}) collective-permute-start(bf16[4,256,640]{2,1,0:T(8,128)(2,1)} %copy-done.9), channel_id=1, source_target_pairs={{0,1},{1,0},{2,3},{3,2},{4,5},{5,4},{6,7},{7,6},{8,9},{9,8},{10,11... | collective-permute-start | bytes 3932168 | tf_op jit(solution)/shard_map/ppermute | solution.py:394
  83.7 20.4 %collective-permute-start.27 = (bf16[4,4,40,256]{3,2,1,0:T(8,128)(2,1)S(1)}, bf16[4,4,40,256]{3,2,1,0:T(8,128)(2,1)S(1)}, u32[]{:S(2)}, u32[]{:S(2)}) collective-permute-start(bf16[4,4,40,256]{3,2,1,0:T(8,128)(2,1)S(1)} %place.16.refs_0_), channel_id=1, source_target_pairs={{0,6},{2,0},{4,2},{6,4},{1,7},{3,1},{5,3},{7,5},{8,14},{10,8},{12,... | collective-permute-start | bytes 983048 | tf_op jit(solution)/shard_map/ppermute | solution.py:423
  87.2 16.9 %collective-permute-start.28 = (bf16[4,4,40,256]{3,2,1,0:T(8,128)(2,1)S(1)}, bf16[4,4,40,256]{3,2,1,0:T(8,128)(2,1)S(1)}, u32[]{:S(2)}, u32[]{:S(2)}) collective-permute-start(bf16[4,4,40,256]{3,2,1,0:T(8,128)(2,1)S(1)} %place.16.refs_0_), channel_id=1, source_target_pairs={{0,4},{2,6},{4,0},{6,2},{1,5},{3,7},{5,1},{7,3},{8,12},{10,14},{12... | collective-permute-start | bytes 983048 | tf_op jit(solution)/shard_map/ppermute | solution.py:423
  87.2 17.6 %collective-permute-start.29 = (bf16[4,4,40,256]{3,2,1,0:T(8,128)(2,1)S(1)}, bf16[4,4,40,256]{3,2,1,0:T(8,128)(2,1)S(1)}, u32[]{:S(2)}, u32[]{:S(2)}) collective-permute-start(bf16[4,4,40,256]{3,2,1,0:T(8,128)(2,1)S(1)} %place.16.refs_0_), channel_id=1, source_target_pairs={{0,2},{2,4},{4,6},{6,0},{1,3},{3,5},{5,7},{7,1},{8,10},{10,12},{12... | collective-permute-start | bytes 983048 | tf_op jit(solution)/shard_map/ppermute | solution.py:423
  87.8 22.9 %collective-permute-start.30 = (bf16[256,512]{1,0:T(8,128)(2,1)}, bf16[256,512]{1,0:T(8,128)(2,1)S(1)}, u32[]{:S(2)}, u32[]{:S(2)}) collective-permute-start(bf16[256,512]{1,0:T(8,128)(2,1)} %bitcast.39), channel_id=1, source_target_pairs={{0,0},{1,4},{4,1},{5,5},{2,2},{3,6},{6,3},{7,7},{8,8},{9,12},{12,9... | collective-permute-start | bytes 786440 | tf_op jit(solution)/shard_map/ppermute | solution.py:390
  115.5 9.2 %collective-permute-start.32 = (bf16[256,512]{1,0:T(8,128)(2,1)S(1)}, bf16[256,512]{1,0:T(8,128)(2,1)S(1)}, u32[]{:S(2)}, u32[]{:S(2)}) collective-permute-start(bf16[256,512]{1,0:T(8,128)(2,1)S(1)} %get-tuple-element.87), channel_id=1, source_target_pairs={{0,0},{1,4},{4,1},{5,5},{2,2},{3,6},{6,3},{7,7},{8,8},{9,12},{12,9... | collective-permute-start | bytes 786440 | tf_op jit(solution)/shard_map/ppermute | solution.py:390
  125.4 51.9 %all-to-all-start.1 = ((bf16[8,640,256]{2,1,0:T(8,128)(2,1)}), bf16[8,640,256]{2,1,0:T(8,128)(2,1)S(1)}, u32[]{:S(2)}, u32[]{:S(2)}) async-start(bf16[8,640,256]{2,1,0:T(8,128)(2,1)} %copy-done.7), calls=%async_computation.1 | async-start | bytes 5242880 | tf_op jit(solution)/shard_map/all_to_all | solution.py:520
  130.3 44.9 %collective-permute-start.36 = (bf16[4,640,256]{2,1,0:T(8,128)(2,1)}, bf16[4,640,256]{2,1,0:T(8,128)(2,1)S(1)}, u32[]{:S(2)}, u32[]{:S(2)}) collective-permute-start(bf16[4,640,256]{2,1,0:T(8,128)(2,1)} %bitcast.23), channel_id=1, source_target_pairs={{0,1},{1,0},{2,3},{3,2},{4,5},{5,4},{6,7},{7,6},{8,9},{9,8},{10,11... | collective-permute-start | bytes 3932168 | tf_op jit(solution)/shard_map/ppermute | solution.py:394
  130.8 45.5 %collective-permute-start.37 = (bf16[4,640,256]{2,1,0:T(8,128)(2,1)}, bf16[4,640,256]{2,1,0:T(8,128)(2,1)S(1)}, u32[]{:S(2)}, u32[]{:S(2)}) collective-permute-start(bf16[4,640,256]{2,1,0:T(8,128)(2,1)} %bitcast.26), channel_id=1, source_target_pairs={{0,1},{1,0},{2,3},{3,2},{4,5},{5,4},{6,7},{7,6},{8,9},{9,8},{10,11... | collective-permute-start | bytes 3932168 | tf_op jit(solution)/shard_map/ppermute | solution.py:394
  130.9 46.5 %collective-permute-start.35 = (bf16[256,640]{1,0:T(8,128)(2,1)S(1)}, bf16[256,640]{1,0:T(8,128)(2,1)}, u32[]{:S(2)}, u32[]{:S(2)}) collective-permute-start(bf16[256,640]{1,0:T(8,128)(2,1)S(1)} %pad_maximum_fusion), channel_id=1, source_target_pairs={{0,0},{1,4},{4,1},{5,5},{2,2},{3,6},{6,3},{7,7},{8,8},{9,12},{12,9... | collective-permute-start | bytes 983048 | tf_op jit(solution)/shard_map/ppermute | solution.py:390
  185.3 33.1 %all-to-all-start.2 = ((bf16[16,256,256]{2,1,0:T(8,128)(2,1)}), bf16[16,256,256]{2,1,0:T(8,128)(2,1)}, u32[]{:S(2)}, u32[]{:S(2)}) async-start(bf16[16,256,256]{2,1,0:T(8,128)(2,1)} %add_convert_fusion), calls=%async_computation.2 | async-start | bytes 4194304 | tf_op jit(solution)/shard_map/all_to_all | solution.py:530
  195.2 12.2 %collective-permute-start.49 = (bf16[256,512]{1,0:T(8,128)(2,1)S(1)}, bf16[256,512]{1,0:T(8,128)(2,1)S(1)}, u32[]{:S(2)}, u32[]{:S(2)}) collective-permute-start(bf16[256,512]{1,0:T(8,128)(2,1)S(1)} %get-tuple-element.105.rest_0_), channel_id=1, source_target_pairs={{0,4},{2,6},{4,0},{6,2},{1,5},{3,7},{5,1},{7,3},{8,12},{10,14},{12... | collective-permute-start | bytes 786440 | tf_op jit(solution)/shard_map/ppermute | solution.py:402
  195.7 14.9 %collective-permute-start.50 = (bf16[256,512]{1,0:T(8,128)(2,1)S(1)}, bf16[256,512]{1,0:T(8,128)(2,1)S(1)}, u32[]{:S(2)}, u32[]{:S(2)}) collective-permute-start(bf16[256,512]{1,0:T(8,128)(2,1)S(1)} %get-tuple-element.105.rest_0_), channel_id=1, source_target_pairs={{0,2},{2,4},{4,6},{6,0},{1,3},{3,5},{5,7},{7,1},{8,10},{10,12},{12... | collective-permute-start | bytes 786440 | tf_op jit(solution)/shard_map/ppermute | solution.py:402
  196.3 14.7 %collective-permute-start.51 = (bf16[256,512]{1,0:T(8,128)(2,1)S(1)}, bf16[256,512]{1,0:T(8,128)(2,1)S(1)}, u32[]{:S(2)}, u32[]{:S(2)}) collective-permute-start(bf16[256,512]{1,0:T(8,128)(2,1)S(1)} %get-tuple-element.105.rest_0_), channel_id=1, source_target_pairs={{0,1},{1,0},{2,3},{3,2},{4,5},{5,4},{6,7},{7,6},{8,9},{9,8},{10,11... | collective-permute-start | bytes 786440 | tf_op jit(solution)/shard_map/ppermute | solution.py:394
  200.9 10.1 %collective-permute-start.52 = (bf16[256,512]{1,0:T(8,128)(2,1)S(1)}, bf16[256,512]{1,0:T(8,128)(2,1)S(1)}, u32[]{:S(2)}, u32[]{:S(2)}) collective-permute-start(bf16[256,512]{1,0:T(8,128)(2,1)S(1)} %collective-permute-done.48.rest_1_), channel_id=1, source_target_pairs={{0,1},{1,0},{2,3},{3,2},{4,5},{5,4},{6,7},{7,6},{8,9},{9,8},{10,11... | collective-permute-start | bytes 786440 | tf_op jit(solution)/shard_map/ppermute | solution.py:394
  218.4 32.6 %all-to-all-start.3 = ((bf16[16,40,512]{2,1,0:T(8,128)(2,1)}), bf16[16,40,512]{2,1,0:T(8,128)(2,1)}, u32[]{:S(2)}, u32[]{:S(2)}) async-start(bf16[16,40,512]{2,1,0:T(8,128)(2,1)} %weight_grad.2), calls=%async_computation.3 | async-start | bytes 1310720 | tf_op jit(solution)/shard_map/all_to_all | solution.py:539
  226.6 10.5 %collective-permute-start.46 = (bf16[256,512]{1,0:T(8,128)(2,1)}, bf16[256,512]{1,0:T(8,128)(2,1)S(1)}, u32[]{:S(2)}, u32[]{:S(2)}) collective-permute-start(bf16[256,512]{1,0:T(8,128)(2,1)} %copy-done.14), channel_id=1, source_target_pairs={{0,0},{1,4},{4,1},{5,5},{2,2},{3,6},{6,3},{7,7},{8,8},{9,12},{12,9... | collective-permute-start | bytes 786440 | tf_op jit(solution)/shard_map/ppermute | solution.py:390
  237.1 8.5 %collective-permute-start.42 = (bf16[272,256]{1,0:T(8,128)(2,1)S(1)}, bf16[272,256]{1,0:T(8,128)(2,1)S(1)}, u32[]{:S(2)}, u32[]{:S(2)}) collective-permute-start(bf16[272,256]{1,0:T(8,128)(2,1)S(1)} %grad_key_value.1.rest_0_), channel_id=1, source_target_pairs={{0,1},{1,0},{2,3},{3,2},{4,5},{5,4},{6,7},{7,6},{8,9},{9,8},{10,11... | collective-permute-start | bytes 417800 | tf_op jit(solution)/shard_map/ppermute | solution.py:394
  237.1 11.1 %collective-permute-start.47 = (bf16[272,256]{1,0:T(8,128)(2,1)S(1)}, bf16[272,256]{1,0:T(8,128)(2,1)S(1)}, u32[]{:S(2)}, u32[]{:S(2)}) collective-permute-start(bf16[272,256]{1,0:T(8,128)(2,1)S(1)} %grad_key_value.1.rest_0_), channel_id=1, source_target_pairs={{0,0},{1,4},{4,1},{5,5},{2,2},{3,6},{6,3},{7,7},{8,8},{9,12},{12,9... | collective-permute-start | bytes 417800 | tf_op jit(solution)/shard_map/ppermute | solution.py:390
  245.6 12.1 %collective-permute-start.34 = (bf16[256,512]{1,0:T(8,128)(2,1)S(1)}, bf16[256,512]{1,0:T(8,128)(2,1)S(1)}, u32[]{:S(2)}, u32[]{:S(2)}) collective-permute-start(bf16[256,512]{1,0:T(8,128)(2,1)S(1)} %copy-done.27), channel_id=1, source_target_pairs={{0,0},{1,4},{4,1},{5,5},{2,2},{3,6},{6,3},{7,7},{8,8},{9,12},{12,9... | collective-permute-start | bytes 786440 | tf_op jit(solution)/shard_map/ppermute | solution.py:390
  251.0 20.9 %all-to-all-start.4 = ((bf16[16,48,256]{2,1,0:T(8,128)(2,1)}), bf16[16,48,256]{2,1,0:T(8,128)(2,1)S(1)}, u32[]{:S(2)}, u32[]{:S(2)}) async-start(bf16[16,48,256]{2,1,0:T(8,128)(2,1)} %weight_grad.3), calls=%async_computation.4 | async-start | bytes 786432 | tf_op jit(solution)/shard_map/all_to_all | solution.py:550
  (59 other events, 368.7 us)

commit v4 on v3

--- a/solution.py
+++ b/solution.py
@@ -1,4 +1,3 @@
-import functools
 import math
 
 import jax
@@ -73,13 +72,12 @@
     kv_ref[:, span:] = raw[:, span:].astype(bf16)
 
 
-def query_part_kernel(mine_ref, other_ref, w_ref, w_upper_ref, part_ref, part_other_ref):
-    cols = w_ref.shape[2]
+def query_part_kernel(where, mine_ref, other_ref, w0, w1, w2, w3, part_ref, part_other_ref):
     for toks_ref, out_ref in ((mine_ref, part_ref), (other_ref, part_other_ref)):
-        for i, w in enumerate((w_ref, w_upper_ref)):
-            out_ref[:, i * cols : (i + 1) * cols] = sum(
-                mm(toks_ref[y], w[y]) for y in range(w.shape[0])
-            )
+        total = 0.0
+        for k, w in enumerate((w0, w1, w2, w3)):
+            total = total + mm(toks_ref[lax.rem(where[0] + k, 4)], w[...])
+        out_ref[...] = total
 
 
 def query_kernel(part_ref, part_theirs_ref, gain_ref, cos_ref, sin_ref, q_ref, raw_ref):
@@ -277,7 +275,7 @@
     rows = raw_ref.shape[0]
     dkv = jnp.sum(dkv_ref[...].astype(f32), axis=0)
     grad, terms = shape_head_grad(
-        raw_ref[...].astype(f32), gain_ref[...], cos_ref[...], sin_ref[...], dkv[:, :span]
+        raw_ref[:, -span:].astype(f32), gain_ref[...], cos_ref[...], sin_ref[...], dkv[:, :span]
     )
     g_ref[:rows, :span] = grad.astype(bf16)
     g_ref[:rows, span:] = dkv[:, span:].astype(bf16)
@@ -330,25 +328,25 @@
     )(where, turned, *blocks)
 
 
-def grad_states_kernel(
-    where, gq_ref, gkv_ref, kv_ref, kv_theirs_ref, q_ref, q_theirs_ref, upper_ref, upper_theirs_ref, out_ref, blocks,
-):
-    core = where[1]
-    columns, cols = kv_ref.shape[0], kv_ref.shape[2]
+def grad_states_kernel(where, gq_ref, gkv_ref, kv_ref, kv_theirs_ref, *rest):
+    weights, (out_ref, blocks) = rest[:-2], rest[-2:]
+    columns = len(weights) // 2
+    y, core = where[0], where[1]
     own_rows = 40
-    grads = (gkv_ref[...], gq_ref[:, :cols], gq_ref[:, cols:])
-    sides = ((core, (kv_ref, q_ref, upper_ref)), (1 - core, (kv_theirs_ref, q_theirs_ref, upper_theirs_ref)))
-    for at_core, weights in sides:
-        for y in range(columns):
-            blocks[y, at_core] = sum(
-                lax.dot_general(w[y], grad, (((1,), (1,)), ((), ())), preferred_element_type=f32)
-                for w, grad in zip(weights, grads)
-            )
+    toks = gq_ref.shape[0]
+    transposed = (((1,), (1,)), ((), ()))
+    for side, kv in ((0, kv_ref), (1, kv_theirs_ref)):
+        at_core = core if side == 0 else 1 - core
+        for k in range(columns):
+            at = lax.rem(y + k, columns)
+            blocks[at, at_core] = lax.dot_general(
+                weights[side * columns + k][...], gq_ref[...], transposed, preferred_element_type=f32
+            ) + lax.dot_general(kv[at], gkv_ref[:toks], transposed, preferred_element_type=f32)
     for x in range(4):
         pieces = []
         for z in range(4):
             part = slice((z * 4 + x) * own_rows, (z * 4 + x + 1) * own_rows)
-            pieces += [blocks[y, c, part] for y in range(columns) for c in range(2)]
+            pieces += [blocks[at, c, part] for at in range(columns) for c in range(2)]
         rows = jnp.concatenate(pieces, axis=0)
         out_ref[:, x * rows.shape[0] : (x + 1) * rows.shape[0]] = rows.astype(bf16).T
 
@@ -400,33 +398,6 @@
 
 def ring(array, step):
     return lax.ppermute(array, column, [(i, (i - step) % 4) for i in range(4)])
-
-
-def place_kernel(axis, where, *refs):
-    out_ref = refs[-1]
-    inner = out_ref.shape[:axis]
-    for k, block in enumerate(refs[:-1]):
-        at = lax.rem(where[0] + k, 4)
-        if axis == 0:
-            out_ref[at] = block[...]
-        elif axis == 1:
-            for i in range(inner[0]):
-                out_ref[i, at] = block[i]
-        else:
-            for i in range(inner[0]):
-                for j in range(inner[1]):
-                    out_ref[i, j, at] = block[i, j]
-
-
-def collect(array, name, axis):
-    parts = [array] + [
-        lax.ppermute(array, name, [(i, (i - k) % 4) for i in range(4)]) for k in range(1, 4)
-    ]
-    where = lax.axis_index(name).astype(jnp.int32)[None]
-    shape = array.shape[:axis] + (4,) + array.shape[axis:]
-    return call(
-        functools.partial(place_kernel, axis), jax.ShapeDtypeStruct(shape, bf16), where, *parts, name="place"
-    )
 
 
 def around(array):
@@ -459,18 +430,8 @@
     gain_q, gain_k = gain_query[None, :], gain_key[None, :]
     shape = jax.ShapeDtypeStruct
 
-    w_kv = jnp.concatenate([w_key, w_value], axis=1)
-    kv_mine, q_low = collect(w_kv, "x", 0), collect(w_query[:, :kv_cols], column, 0)
-    kv_mine, q_low = lax.optimization_barrier((kv_mine, q_low))
-    kv_mine, q_low = collect(kv_mine, column, 0), collect(q_low, "z", 1)
-    q_high = collect(w_query[:, kv_cols:], "z", 0)
-    kv_mine, q_low, q_high = lax.optimization_barrier((kv_mine, q_low, q_high))
-    kv_mine, q_low = collect(kv_mine, "z", 1), collect(q_low, "x", 2)
-    q_high = collect(q_high, "x", 1)
-    kv_mine, q_low, q_high = lax.optimization_barrier((kv_mine, q_low, q_high))
-    q_high = collect(q_high, column, 0)
-    by_y = (columns, half // columns, kv_cols)
-    kv_mine, q_low, q_high = kv_mine.reshape(by_y), q_low.reshape(by_y), q_high.reshape(by_y)
+    kv_mine = to_all(jnp.concatenate([w_key, w_value], axis=1), chips, planes * columns)
+    kv_mine = kv_mine.reshape(columns, half // columns, kv_cols)
 
     toks_mine, toks_theirs, turned = pl.pallas_call(
         prepare_kernel,
@@ -490,6 +451,8 @@
         )
     )
     kv_theirs = flip(kv_mine)
+    q_rows, _ = lax.optimization_barrier((w_query, kv_mine))
+    q_rows = to_all(q_rows, owners, planes).reshape(planes * own_rows, q_cols)
 
     kv16, raw_k = call(
         key_value_kernel,
@@ -498,11 +461,13 @@
         name="key_value",
     )
     kv_send = jnp.broadcast_to(swap(kv16)[None], (planes, tok_rows, kv_cols))
+    kv_send, q_rows = lax.optimization_barrier((kv_send, q_rows))
     kv_own = lax.all_to_all(kv_send, plane, 0, 0)
+    q_mine = [q_rows] + [ring(q_rows, k) for k in range(1, columns)]
     q_part, q_part_other = call(
         query_part_kernel,
         (shape((tok_rows, q_cols), f32),) * 2,
-        toks_mine, toks_other, q_low, q_high,
+        where, toks_mine, toks_other, *q_mine,
         name="query_part",
     )
     kv_own, q_part, q_part_other, grad_out = lax.optimization_barrier(
@@ -514,7 +479,7 @@
         q_part, flip(q_part_other), gain_q, cosine, sine,
         name="query",
     )
-    kv_other = flip(kv_own)
+    kv_other, q16, raw_q = lax.optimization_barrier((flip(kv_own), q16, raw_q))
     q16 = swap(q16)
     turned, raw_q, _ = lax.optimization_barrier((turned, raw_q, q16))
     turned = lax.all_to_all(turned, column + ("core",), 0, 0)
@@ -523,8 +488,9 @@
     ctx, dq, dkv_mine, dkv_theirs = attention(
         block_order, own, q16, grad_out, kv_own, kv_other
     )
-    dkv_theirs, dq, turned, raw_there, low_theirs, high_theirs = lax.optimization_barrier(
-        (dkv_theirs, dq, turned, raw_there, flip(q_low), flip(q_high))
+    q_theirs = [flip(block) for block in q_mine]
+    dkv_theirs, dq, turned, raw_there, q_theirs = lax.optimization_barrier(
+        (dkv_theirs, dq, turned, raw_there, q_theirs)
     )
     dkv = (dkv_mine.astype(f32) + flip(dkv_theirs).astype(f32)).astype(bf16)
     dkv = lax.all_to_all(dkv, plane, 0, 0)
@@ -532,7 +498,7 @@
     g_q, gains_q = call(
         grad_query_kernel,
         (shape((tok_rows, q_cols), bf16), shape((8, span), f32)),
-        raw_there[:, :q_cols], dq, gain_q, cos_there, sin_there,
+        raw_there, dq, gain_q, cos_there, sin_there,
         name="grad_query",
     )
     parts = weight_grad(where, turned, around(g_q), planes, own_rows)
@@ -542,7 +508,7 @@
     g_kv = call(
         grad_key_value_kernel,
         shape((tok_rows + 16, kv_cols), bf16),
-        raw_there[:, q_cols:], dkv, gain_k, cos_there, sin_there, gains_q,
+        raw_there, dkv, gain_k, cos_there, sin_there, gains_q,
         name="grad_key_value",
     )
     blocks, g_q_back, g_kv_back = lax.optimization_barrier((around(g_kv), swap(g_q), swap(g_kv)))
@@ -558,13 +524,13 @@
     grad_states = pl.pallas_call(
         grad_states_kernel,
         out_shape=shape((tok_rows, width), bf16),
-        in_specs=[smem] + [vmem] * 8,
+        in_specs=[smem] + [vmem] * (4 + 2 * columns),
         out_specs=vmem,
         scratch_shapes=[pltpu.VMEM((columns, 2, half // columns, tok_rows), f32)],
         compiler_params=pltpu.CompilerParams(vmem_limit_bytes=48 * mib),
         cost_estimate=cheap,
         name="grad_states",
-    )(where, g_q_back, g_kv_back[:tok_rows], kv_mine, kv_theirs, q_low, low_theirs, q_high, high_theirs)
+    )(where, g_q_back, g_kv_back, kv_mine, kv_theirs, *q_mine, *q_theirs)
     return (
         swap(ctx)[None],
         grad_states[None],

time: 276 us -> 277 us (level)
  starting transfers between devices: 125 us -> 99.2 us
  waiting for transfers between devices: 50.3 us -> 61.5 us
  local copies, waits for them, and re-layouts: 34 us -> 44.4 us
  other arithmetic: 7.82 us -> 11.5 us
    ppermute x27 -> x0, starting transfers between devices: 31.4 us -> none  [collect(): lax.ppermute(array, name, [(i, (i - k) % 4) for i in range(4)])]
    ppermute x6 -> x9, waiting for transfers between devices: 8.37 us -> 35.7 us  [ring(): return lax.ppermute(array, column, [(i, (i - step) % 4) for i in range(4)])]
    ppermute x27 -> x0, waiting for transfers between devices: 19.3 us -> none  [collect(): lax.ppermute(array, name, [(i, (i - k) % 4) for i in range(4)])]
    all_to_all x0 -> x2, starting transfers between devices: none -> 17.9 us  [to_all(): lax.all_to_all(jnp.broadcast_to(array[None], (count,) + array.shape), axe...]
    unnamed x64 -> x103, local copies, waits for them, and re-layouts: 23.9 us -> 35.7 us
    ppermute x15 -> x17, starting transfers between devices: 23.9 us -> 13.5 us  [flip(): return lax.ppermute(array, 'core', flipped)]
    all_to_all x0 -> x2, waiting for transfers between devices: none -> 3.72 us  [to_all(): lax.all_to_all(jnp.broadcast_to(array[None], (count,) + array.shape), axe...]
    slice x4 -> x0, local copies, waits for them, and re-layouts: 3.48 us -> none  [the longest x1 0.97 us: local(): raw_there[:, :q_cols]]
  transfers between devices with their start and end apart: 60 -> 40, of which waited for: 16 -> 14; matrix products, arithmetic and copies ran while one was open for 5% -> 5% of each run, Pallas kernels for 19% -> 20%
where the time goes in v4:
time: 277 us; the launch traced here: 273 us
  starting transfers between devices  99.2 us (36%)
  waiting for transfers between devices  61.5 us (22%)
  Pallas kernels  54.9 us (20%)
  local copies, waits for them, and re-layouts  44.4 us (16%)
  other arithmetic  11.5 us (4%)
    ppermute x9, waiting for transfers between devices, ring(): return lax.ppermute(array, column, [(i, (i - step) % 4) for i in range(4)])  35.7 us
    unnamed x103, local copies, waits for them, and re-layouts  35.7 us
    pallas_call x1, Pallas kernels, attention(): pl.pallas_call(attention_kernel, out_shape=(jax.ShapeDtypeStruct((rows_he...  33.4 us
    ppermute x7, starting transfers between devices, swap(): return lax.ppermute(array, ('y_hi', 'core'), swapped)  27 us
    all_to_all x2, starting transfers between devices, to_all(): lax.all_to_all(jnp.broadcast_to(array[None], (count,) + array.shape), axe...  17.9 us
    all_to_all x2, starting transfers between devices, local(): parts = lax.all_to_all(parts, owners, 0, 0)  14.9 us
    ppermute x17, starting transfers between devices, flip(): return lax.ppermute(array, 'core', flipped)  13.5 us
    ppermute x17, waiting for transfers between devices, flip(): return lax.ppermute(array, 'core', flipped)  9.95 us
  transfers between devices with their start and end apart: 40, of which 14 were waited for; matrix products, arithmetic and copies ran while one was open for 5% of the time, Pallas kernels for 20%

profile of v4, /device:TPU:39, one launch (start us, length us, event | category | flops | bytes accessed | tf_op | source)
XLA Modules:
  0.0 272.5 jit_solution(8094379381210481318)
XLA Ops:
  2.5 10.4 %all-to-all-start = ((bf16[64,40,256]{2,1,0:T(8,128)(2,1)}), bf16[64,40,256]{2,1,0:T(8,128)(2,1)S(1)}, u32[]{:S(2)}, u32[]{:S(2)}) async-start(bf16[64,40,256]{2,1,0:T(8,128)(2,1)} %broadcast_in_dim.14), calls=%async_computation | async-start | bytes 2621440 | tf_op jit(solution)/shard_map/all_to_all | solution.py:396
  13.0 4.4 %copy.15 = bf16[5120,256]{1,0:T(8,128)(2,1)} copy(bf16[5120,256]{0,1:T(8,128)(2,1)} %bitcast.33) | data formatting | bytes 5242880 | tf_op jit(solution)/shard_map/transpose | solution.py:445
  17.4 2.6 prepare.1
  29.3 2.7 collective-permute-start
  33.7 7.5 %all-to-all-start.1 = ((bf16[16,40,512]{2,1,0:T(8,128)(2,1)}), bf16[16,40,512]{2,1,0:T(8,128)(2,1)S(1)}, u32[]{:S(2)}, u32[]{:S(2)}) async-start(bf16[16,40,512]{2,1,0:T(8,128)(2,1)} %broadcast_in_dim.17), calls=%async_computation.1 | async-start | bytes 1310720 | tf_op jit(solution)/shard_map/all_to_all | solution.py:396
  50.8 3.9 %collective-permute-done.1 = bf16[256,256]{1,0:T(8,128)(2,1)S(1)} collective-permute-done((bf16[256,256]{1,0:T(8,128)(2,1)}, bf16[256,256]{1,0:T(8,128)(2,1)S(1)}, u32[]{:S(2)}, u32[]{:S(2)}) %collective-permute-start.1) | collective-permute-done | bytes 131104 | tf_op jit(solution)/shard_map/ppermute | solution.py:388
  56.3 7.0 %all-to-all-start.2 = ((bf16[16,256,256]{2,1,0:T(8,128)(2,1)}), bf16[16,256,256]{2,1,0:T(8,128)(2,1)}, u32[]{:S(2)}, u32[]{:S(2)}) async-start(bf16[16,256,256]{2,1,0:T(8,128)(2,1)} %broadcast_in_dim.16), calls=%async_computation.2 | async-start | bytes 4194304 | tf_op jit(solution)/shard_map/all_to_all | solution.py:465
  65.4 6.2 %collective-permute-start.6 = (bf16[256,512]{1,0:T(8,128)(2,1)}, bf16[256,512]{1,0:T(8,128)(2,1)S(1)}, u32[]{:S(2)}, u32[]{:S(2)}) collective-permute-start(bf16[256,512]{1,0:T(8,128)(2,1)} %bitcast.35), channel_id=1, source_target_pairs={{0,0},{1,4},{4,1},{5,5},{2,2},{3,6},{6,3},{7,7},{8,8},{9,12},{12,9... | collective-permute-start | bytes 786440 | tf_op jit(solution)/shard_map/ppermute | solution.py:388
  71.7 7.7 %collective-permute-done.3.w1.rest_1_ = bf16[640,512]{1,0:T(8,128)(2,1)S(1)} collective-permute-done((bf16[640,512]{1,0:T(8,128)(2,1)S(1)}, bf16[640,512]{1,0:T(8,128)(2,1)S(1)}, u32[]{:S(2)}, u32[]{:S(2)}) %collective-permute-start.3) | collective-permute-done | bytes 655392 | tf_op jit(solution)/shard_map/ppermute | solution.py:400
  79.4 2.9 %collective-permute-done.4.w2.rest_2_ = bf16[640,512]{1,0:T(8,128)(2,1)S(1)} collective-permute-done((bf16[640,512]{1,0:T(8,128)(2,1)S(1)}, bf16[640,512]{1,0:T(8,128)(2,1)S(1)}, u32[]{:S(2)}, u32[]{:S(2)}) %collective-permute-start.4) | collective-permute-done | bytes 655392 | tf_op jit(solution)/shard_map/ppermute | solution.py:400
  82.3 14.7 %collective-permute-done.5.w3.rest_3_ = bf16[640,512]{1,0:T(8,128)(2,1)S(1)} collective-permute-done((bf16[640,512]{1,0:T(8,128)(2,1)S(1)}, bf16[640,512]{1,0:T(8,128)(2,1)S(1)}, u32[]{:S(2)}, u32[]{:S(2)}) %collective-permute-start.5) | collective-permute-done | bytes 655392 | tf_op jit(solution)/shard_map/ppermute | solution.py:400
  97.0 3.3 %query_part.1 = (f32[256,512]{1,0:T(8,128)S(1)}, f32[256,512]{1,0:T(8,128)S(1)}) custom-call(s32[2]{0:T(128)S(1)} %pad_add_fusion.where, bf16[4,256,640]{2,1,0:T(8,128)(2,1)S(1)} %copy-done.4, bf16[4,256,640]{2,1,0:T(8,128)(2,1)} %copy-done.50, bf16[640,512]{1,0:T(8,128)(2,1)S(1)} %bitcast.25, bf16[640,512]{1,0:T(8,128)(2,1)S(1)} %collective-permute-done.3.w1.rest_1_, ...), custom_call_target="tpu_custom_call" | custom-call | flops 1000 | bytes 1000 | tf_op jit(solution)/shard_map/query_part/pallas_call | solution.py:368
  101.6 4.4 %collective-permute-done.8.part_theirs_ref = f32[256,512]{1,0:T(8,128)S(1)} collective-permute-done((f32[256,512]{1,0:T(8,128)S(1)}, f32[256,512]{1,0:T(8,128)S(1)}, u32[]{:S(2)}, u32[]{:S(2)}) %collective-permute-start.8) | collective-permute-done | bytes 524320 | tf_op jit(solution)/shard_map/ppermute | solution.py:392
  107.4 3.6 %collective-permute-start.9 = (bf16[256,512]{1,0:T(8,128)(2,1)S(1)}, bf16[256,512]{1,0:T(8,128)(2,1)S(1)}, u32[]{:S(2)}, u32[]{:S(2)}) collective-permute-start(bf16[256,512]{1,0:T(8,128)(2,1)S(1)} %get-tuple-element.85), channel_id=1, source_target_pairs={{0,0},{1,4},{4,1},{5,5},{2,2},{3,6},{6,3},{7,7},{8,8},{9,12},{12,9... | collective-permute-start | bytes 786440 | tf_op jit(solution)/shard_map/ppermute | solution.py:388
  111.0 5.7 %collective-permute-done.9.q_ref = bf16[256,512]{1,0:T(8,128)(2,1)S(1)} collective-permute-done((bf16[256,512]{1,0:T(8,128)(2,1)S(1)}, bf16[256,512]{1,0:T(8,128)(2,1)S(1)}, u32[]{:S(2)}, u32[]{:S(2)}) %collective-permute-start.9) | collective-permute-done | bytes 262176 | tf_op jit(solution)/shard_map/ppermute | solution.py:388
  117.4 4.7 %all-to-all-start.3 = ((bf16[8,640,256]{2,1,0:T(8,128)(2,1)}), bf16[8,640,256]{2,1,0:T(8,128)(2,1)S(1)}, u32[]{:S(2)}, u32[]{:S(2)}) async-start(bf16[8,640,256]{2,1,0:T(8,128)(2,1)} %copy-done.11), calls=%async_computation.3 | async-start | bytes 5242880 | tf_op jit(solution)/shard_map/all_to_all | solution.py:485
  125.0 5.0 %collective-permute-start.11 = (bf16[256,640]{1,0:T(8,128)(2,1)S(1)}, bf16[256,640]{1,0:T(8,128)(2,1)S(1)}, u32[]{:S(2)}, u32[]{:S(2)}) collective-permute-start(bf16[256,640]{1,0:T(8,128)(2,1)S(1)} %pad_maximum_fusion), channel_id=1, source_target_pairs={{0,0},{1,4},{4,1},{5,5},{2,2},{3,6},{6,3},{7,7},{8,8},{9,12},{12,9... | collective-permute-start | bytes 983048 | tf_op jit(solution)/shard_map/ppermute | solution.py:388
  131.7 33.4 %attention.1 = (bf16[256,512]{1,0:T(8,128)(2,1)}, f32[256,512]{1,0:T(8,128)S(1)}, bf16[16,256,256]{2,1,0:T(8,128)(2,1)S(1)}, bf16[16,256,256]{2,1,0:T(8,128)(2,1)S(1)}) custom-call(s32[64]{0:T(128)S(1)} %copy-done.44, s32[3]{0:T(128)S(1)} %copy-done.47, bf16[256,512]{1,0:T(8,128)(2,1)S(1)} %copy-done.39, bf16[256,512]{1,0:T(8,128)(2,1)S(1)} %copy-done.36, ...), custom_call_target="tpu_custom_call" | custom-call | flops 1000 | bytes 1000 | tf_op jit(solution)/shard_map/attention/pallas_call | solution.py:228
  172.7 4.4 %collective-permute-done.16 = bf16[16,256,256]{2,1,0:T(8,128)(2,1)S(1)} collective-permute-done((bf16[16,256,256]{2,1,0:T(8,128)(2,1)}, bf16[16,256,256]{2,1,0:T(8,128)(2,1)S(1)}, u32[]{:S(2)}, u32[]{:S(2)}) %collective-permute-start.16) | collective-permute-done | bytes 2097184 | tf_op jit(solution)/shard_map/ppermute | solution.py:392
  177.0 3.5 %add_convert_fusion = bf16[16,256,256]{2,1,0:T(8,128)(2,1)} fusion(bf16[16,256,256]{2,1,0:T(8,128)(2,1)S(1)} %collective-permute-done.16, bf16[16,256,256]{2,1,0:T(8,128)(2,1)} %copy-done.13), kind=kLoop, calls=%fused_computation | loop fusion | flops 4194304 | bytes 6291456 | tf_op jit(solution)/shard_map/convert_element_type | solution.py:495
  180.6 6.8 %all-to-all-start.4 = ((bf16[16,256,256]{2,1,0:T(8,128)(2,1)}), bf16[16,256,256]{2,1,0:T(8,128)(2,1)}, u32[]{:S(2)}, u32[]{:S(2)}) async-start(bf16[16,256,256]{2,1,0:T(8,128)(2,1)} %add_convert_fusion), calls=%async_computation.4 | async-start | bytes 4194304 | tf_op jit(solution)/shard_map/all_to_all | solution.py:496
  193.5 3.9 %collective-permute-done.26.rest_1_ = bf16[256,512]{1,0:T(8,128)(2,1)S(1)} collective-permute-done((bf16[256,512]{1,0:T(8,128)(2,1)S(1)}, bf16[256,512]{1,0:T(8,128)(2,1)S(1)}, u32[]{:S(2)}, u32[]{:S(2)}) %collective-permute-start.26) | collective-permute-done | bytes 262176 | tf_op jit(solution)/shard_map/ppermute | solution.py:400
  197.4 2.7 collective-permute-start.30
  200.1 2.7 %collective-permute-start.31 = (bf16[256,512]{1,0:T(8,128)(2,1)S(1)}, bf16[256,512]{1,0:T(8,128)(2,1)S(1)}, u32[]{:S(2)}, u32[]{:S(2)}) collective-permute-start(bf16[256,512]{1,0:T(8,128)(2,1)S(1)} %collective-permute-done.27.rest_2_), channel_id=1, source_target_pairs={{0,1},{1,0},{2,3},{3,2},{4,5},{5,4},{6,7},{7,6},{8,9},{9,8},{10,11... | collective-permute-start | bytes 786440 | tf_op jit(solution)/shard_map/ppermute | solution.py:392
  202.9 3.4 %collective-permute-done.28.rest_3_ = bf16[256,512]{1,0:T(8,128)(2,1)S(1)} collective-permute-done((bf16[256,512]{1,0:T(8,128)(2,1)S(1)}, bf16[256,512]{1,0:T(8,128)(2,1)S(1)}, u32[]{:S(2)}, u32[]{:S(2)}) %collective-permute-start.28) | collective-permute-done | bytes 262176 | tf_op jit(solution)/shard_map/ppermute | solution.py:400
  213.9 8.2 %all-to-all-start.5 = ((bf16[16,40,512]{2,1,0:T(8,128)(2,1)}), bf16[16,40,512]{2,1,0:T(8,128)(2,1)}, u32[]{:S(2)}, u32[]{:S(2)}) async-start(bf16[16,40,512]{2,1,0:T(8,128)(2,1)} %copy-done.12), calls=%async_computation.5 | async-start | bytes 1310720 | tf_op jit(solution)/shard_map/all_to_all | solution.py:505
  222.1 3.3 %collective-permute-start.24 = (bf16[256,512]{1,0:T(8,128)(2,1)}, bf16[256,512]{1,0:T(8,128)(2,1)S(1)}, u32[]{:S(2)}, u32[]{:S(2)}) collective-permute-start(bf16[256,512]{1,0:T(8,128)(2,1)} %copy-done.37), channel_id=1, source_target_pairs={{0,0},{1,4},{4,1},{5,5},{2,2},{3,6},{6,3},{7,7},{8,8},{9,12},{12,9... | collective-permute-start | bytes 786440 | tf_op jit(solution)/shard_map/ppermute | solution.py:388
  228.4 3.2 %collective-permute-start.18 = (bf16[272,256]{1,0:T(8,128)(2,1)S(1)}, bf16[272,256]{1,0:T(8,128)(2,1)S(1)}, u32[]{:S(2)}, u32[]{:S(2)}) collective-permute-start(bf16[272,256]{1,0:T(8,128)(2,1)S(1)} %grad_key_value.1.rest_0_), channel_id=1, source_target_pairs={{0,4},{2,6},{4,0},{6,2},{1,5},{3,7},{5,1},{7,3},{8,12},{10,14},{12... | collective-permute-start | bytes 417800 | tf_op jit(solution)/shard_map/ppermute | solution.py:400
  232.8 4.2 %collective-permute-start.25 = (bf16[272,256]{1,0:T(8,128)(2,1)S(1)}, bf16[272,256]{1,0:T(8,128)(2,1)S(1)}, u32[]{:S(2)}, u32[]{:S(2)}) collective-permute-start(bf16[272,256]{1,0:T(8,128)(2,1)S(1)} %grad_key_value.1.rest_0_), channel_id=1, source_target_pairs={{0,0},{1,4},{4,1},{5,5},{2,2},{3,6},{6,3},{7,7},{8,8},{9,12},{12,9... | collective-permute-start | bytes 417800 | tf_op jit(solution)/shard_map/ppermute | solution.py:388
  238.2 3.0 %collective-permute-done.19.rest_3_ = bf16[272,256]{1,0:T(8,128)(2,1)S(1)} collective-permute-done((bf16[272,256]{1,0:T(8,128)(2,1)S(1)}, bf16[272,256]{1,0:T(8,128)(2,1)S(1)}, u32[]{:S(2)}, u32[]{:S(2)}) %collective-permute-start.19) | collective-permute-done | bytes 139296 | tf_op jit(solution)/shard_map/ppermute | solution.py:400
  246.8 6.7 %all-to-all-start.6 = ((bf16[16,48,256]{2,1,0:T(8,128)(2,1)}), bf16[16,48,256]{2,1,0:T(8,128)(2,1)S(1)}, u32[]{:S(2)}, u32[]{:S(2)}) async-start(bf16[16,48,256]{2,1,0:T(8,128)(2,1)} %copy-done.14), calls=%async_computation.6 | async-start | bytes 786432 | tf_op jit(solution)/shard_map/all_to_all | solution.py:516
  263.8 6.4 %grad_states.1 = bf16[256,5120]{1,0:T(8,128)(2,1)} custom-call(s32[2]{0:T(128)S(1)} %pad_add_fusion.where, bf16[256,512]{1,0:T(8,128)(2,1)S(1)} %copy-done.34, bf16[272,256]{1,0:T(8,128)(2,1)S(1)} %copy-done.42, bf16[4,640,256]{2,1,0:T(8,128)(2,1)} %bitcast.21, bf16[4,640,256]{2,1,0:T(8,128)(2,1)} %copy-done.1, bf16[640,512]{1,0:T(8,128)(2,1)S(1)} %bitcast.27, ...), custom_call_target="tpu_custom_call" | custom-call | flops 1000 | bytes 1000 | tf_op jit(solution)/shard_map/grad_states/pallas_call | solution.py:524
  (181 shorter events, 78.8 us)
Async XLA Ops:
  2.5 26.8 %all-to-all-start = ((bf16[64,40,256]{2,1,0:T(8,128)(2,1)}), bf16[64,40,256]{2,1,0:T(8,128)(2,1)S(1)}, u32[]{:S(2)}, u32[]{:S(2)}) async-start(bf16[64,40,256]{2,1,0:T(8,128)(2,1)} %broadcast_in_dim.14), calls=%async_computation | async-start | bytes 2621440 | tf_op jit(solution)/shard_map/all_to_all | solution.py:396
  29.3 11.9 %collective-permute-start = (bf16[4,640,256]{2,1,0:T(8,128)(2,1)S(1)}, bf16[4,640,256]{2,1,0:T(8,128)(2,1)S(1)}, u32[]{:S(2)}, u32[]{:S(2)}) collective-permute-start(bf16[4,640,256]{2,1,0:T(8,128)(2,1)S(1)} %bitcast.19), channel_id=1, source_target_pairs={{0,1},{1,0},{2,3},{3,2},{4,5},{5,4},{6,7},{7,6},{8,9},{9,8},{10,11... | collective-permute-start | bytes 3932168 | tf_op jit(solution)/shard_map/ppermute | solution.py:392
  33.7 17.2 %all-to-all-start.1 = ((bf16[16,40,512]{2,1,0:T(8,128)(2,1)}), bf16[16,40,512]{2,1,0:T(8,128)(2,1)S(1)}, u32[]{:S(2)}, u32[]{:S(2)}) async-start(bf16[16,40,512]{2,1,0:T(8,128)(2,1)} %broadcast_in_dim.17), calls=%async_computation.1 | async-start | bytes 1310720 | tf_op jit(solution)/shard_map/all_to_all | solution.py:396
  46.8 8.0 %collective-permute-start.1 = (bf16[256,256]{1,0:T(8,128)(2,1)}, bf16[256,256]{1,0:T(8,128)(2,1)S(1)}, u32[]{:S(2)}, u32[]{:S(2)}) collective-permute-start(bf16[256,256]{1,0:T(8,128)(2,1)} %get-tuple-element.74), channel_id=1, source_target_pairs={{0,0},{1,4},{4,1},{5,5},{2,2},{3,6},{6,3},{7,7},{8,8},{9,12},{12,9... | collective-permute-start | bytes 393224 | tf_op jit(solution)/shard_map/ppermute | solution.py:388
  56.3 44.8 %all-to-all-start.2 = ((bf16[16,256,256]{2,1,0:T(8,128)(2,1)}), bf16[16,256,256]{2,1,0:T(8,128)(2,1)}, u32[]{:S(2)}, u32[]{:S(2)}) async-start(bf16[16,256,256]{2,1,0:T(8,128)(2,1)} %broadcast_in_dim.16), calls=%async_computation.2 | async-start | bytes 4194304 | tf_op jit(solution)/shard_map/all_to_all | solution.py:465
  63.2 8.4 %collective-permute-start.2 = (bf16[4,256,640]{2,1,0:T(8,128)(2,1)S(1)}, bf16[4,256,640]{2,1,0:T(8,128)(2,1)S(1)}, u32[]{:S(2)}, u32[]{:S(2)}) collective-permute-start(bf16[4,256,640]{2,1,0:T(8,128)(2,1)S(1)} %copy-done.20), channel_id=1, source_target_pairs={{0,1},{1,0},{2,3},{3,2},{4,5},{5,4},{6,7},{7,6},{8,9},{9,8},{10,11... | collective-permute-start | bytes 3932168 | tf_op jit(solution)/shard_map/ppermute | solution.py:392
  63.3 16.1 %collective-permute-start.3 = (bf16[640,512]{1,0:T(8,128)(2,1)S(1)}, bf16[640,512]{1,0:T(8,128)(2,1)S(1)}, u32[]{:S(2)}, u32[]{:S(2)}) collective-permute-start(bf16[640,512]{1,0:T(8,128)(2,1)S(1)} %bitcast.22), channel_id=1, source_target_pairs={{0,6},{2,0},{4,2},{6,4},{1,7},{3,1},{5,3},{7,5},{8,14},{10,8},{12,... | collective-permute-start | bytes 1966088 | tf_op jit(solution)/shard_map/ppermute | solution.py:400
  64.8 17.5 %collective-permute-start.4 = (bf16[640,512]{1,0:T(8,128)(2,1)S(1)}, bf16[640,512]{1,0:T(8,128)(2,1)S(1)}, u32[]{:S(2)}, u32[]{:S(2)}) collective-permute-start(bf16[640,512]{1,0:T(8,128)(2,1)S(1)} %bitcast.23), channel_id=1, source_target_pairs={{0,4},{2,6},{4,0},{6,2},{1,5},{3,7},{5,1},{7,3},{8,12},{10,14},{12... | collective-permute-start | bytes 1966088 | tf_op jit(solution)/shard_map/ppermute | solution.py:400
  65.2 31.8 %collective-permute-start.5 = (bf16[640,512]{1,0:T(8,128)(2,1)S(1)}, bf16[640,512]{1,0:T(8,128)(2,1)S(1)}, u32[]{:S(2)}, u32[]{:S(2)}) collective-permute-start(bf16[640,512]{1,0:T(8,128)(2,1)S(1)} %bitcast.24), channel_id=1, source_target_pairs={{0,2},{2,4},{4,6},{6,0},{1,3},{3,5},{5,7},{7,1},{8,10},{10,12},{12... | collective-permute-start | bytes 1966088 | tf_op jit(solution)/shard_map/ppermute | solution.py:400
  65.4 35.0 %collective-permute-start.6 = (bf16[256,512]{1,0:T(8,128)(2,1)}, bf16[256,512]{1,0:T(8,128)(2,1)S(1)}, u32[]{:S(2)}, u32[]{:S(2)}) collective-permute-start(bf16[256,512]{1,0:T(8,128)(2,1)} %bitcast.35), channel_id=1, source_target_pairs={{0,0},{1,4},{4,1},{5,5},{2,2},{3,6},{6,3},{7,7},{8,8},{9,12},{12,9... | collective-permute-start | bytes 786440 | tf_op jit(solution)/shard_map/ppermute | solution.py:388
  107.4 9.3 %collective-permute-start.9 = (bf16[256,512]{1,0:T(8,128)(2,1)S(1)}, bf16[256,512]{1,0:T(8,128)(2,1)S(1)}, u32[]{:S(2)}, u32[]{:S(2)}) collective-permute-start(bf16[256,512]{1,0:T(8,128)(2,1)S(1)} %get-tuple-element.85), channel_id=1, source_target_pairs={{0,0},{1,4},{4,1},{5,5},{2,2},{3,6},{6,3},{7,7},{8,8},{9,12},{12,9... | collective-permute-start | bytes 786440 | tf_op jit(solution)/shard_map/ppermute | solution.py:388
  117.4 55.3 %all-to-all-start.3 = ((bf16[8,640,256]{2,1,0:T(8,128)(2,1)}), bf16[8,640,256]{2,1,0:T(8,128)(2,1)S(1)}, u32[]{:S(2)}, u32[]{:S(2)}) async-start(bf16[8,640,256]{2,1,0:T(8,128)(2,1)} %copy-done.11), calls=%async_computation.3 | async-start | bytes 5242880 | tf_op jit(solution)/shard_map/all_to_all | solution.py:485
  122.1 46.4 %collective-permute-start.12 = (bf16[640,512]{1,0:T(8,128)(2,1)S(1)}, bf16[640,512]{1,0:T(8,128)(2,1)S(1)}, u32[]{:S(2)}, u32[]{:S(2)}) collective-permute-start(bf16[640,512]{1,0:T(8,128)(2,1)S(1)} %bitcast.26), channel_id=1, source_target_pairs={{0,1},{1,0},{2,3},{3,2},{4,5},{5,4},{6,7},{7,6},{8,9},{9,8},{10,11... | collective-permute-start | bytes 1966088 | tf_op jit(solution)/shard_map/ppermute | solution.py:392
  122.1 47.3 %collective-permute-start.13 = (bf16[640,512]{1,0:T(8,128)(2,1)}, bf16[640,512]{1,0:T(8,128)(2,1)S(1)}, u32[]{:S(2)}, u32[]{:S(2)}) collective-permute-start(bf16[640,512]{1,0:T(8,128)(2,1)} %copy-done.5), channel_id=1, source_target_pairs={{0,1},{1,0},{2,3},{3,2},{4,5},{5,4},{6,7},{7,6},{8,9},{9,8},{10,11... | collective-permute-start | bytes 1966088 | tf_op jit(solution)/shard_map/ppermute | solution.py:392
  122.6 47.6 %collective-permute-start.14 = (bf16[640,512]{1,0:T(8,128)(2,1)}, bf16[640,512]{1,0:T(8,128)(2,1)S(1)}, u32[]{:S(2)}, u32[]{:S(2)}) collective-permute-start(bf16[640,512]{1,0:T(8,128)(2,1)} %copy-done.7), channel_id=1, source_target_pairs={{0,1},{1,0},{2,3},{3,2},{4,5},{5,4},{6,7},{7,6},{8,9},{9,8},{10,11... | collective-permute-start | bytes 1966088 | tf_op jit(solution)/shard_map/ppermute | solution.py:392
  122.6 48.5 %collective-permute-start.15 = (bf16[640,512]{1,0:T(8,128)(2,1)}, bf16[640,512]{1,0:T(8,128)(2,1)S(1)}, u32[]{:S(2)}, u32[]{:S(2)}) collective-permute-start(bf16[640,512]{1,0:T(8,128)(2,1)} %copy-done.9), channel_id=1, source_target_pairs={{0,1},{1,0},{2,3},{3,2},{4,5},{5,4},{6,7},{7,6},{8,9},{9,8},{10,11... | collective-permute-start | bytes 1966088 | tf_op jit(solution)/shard_map/ppermute | solution.py:392
  125.0 47.0 %collective-permute-start.11 = (bf16[256,640]{1,0:T(8,128)(2,1)S(1)}, bf16[256,640]{1,0:T(8,128)(2,1)S(1)}, u32[]{:S(2)}, u32[]{:S(2)}) collective-permute-start(bf16[256,640]{1,0:T(8,128)(2,1)S(1)} %pad_maximum_fusion), channel_id=1, source_target_pairs={{0,0},{1,4},{4,1},{5,5},{2,2},{3,6},{6,3},{7,7},{8,8},{9,12},{12,9... | collective-permute-start | bytes 983048 | tf_op jit(solution)/shard_map/ppermute | solution.py:388
  180.6 33.3 %all-to-all-start.4 = ((bf16[16,256,256]{2,1,0:T(8,128)(2,1)}), bf16[16,256,256]{2,1,0:T(8,128)(2,1)}, u32[]{:S(2)}, u32[]{:S(2)}) async-start(bf16[16,256,256]{2,1,0:T(8,128)(2,1)} %add_convert_fusion), calls=%async_computation.4 | async-start | bytes 4194304 | tf_op jit(solution)/shard_map/all_to_all | solution.py:496
  190.8 9.3 %collective-permute-start.27 = (bf16[256,512]{1,0:T(8,128)(2,1)S(1)}, bf16[256,512]{1,0:T(8,128)(2,1)S(1)}, u32[]{:S(2)}, u32[]{:S(2)}) collective-permute-start(bf16[256,512]{1,0:T(8,128)(2,1)S(1)} %get-tuple-element.103.rest_0_), channel_id=1, source_target_pairs={{0,4},{2,6},{4,0},{6,2},{1,5},{3,7},{5,1},{7,3},{8,12},{10,14},{12... | collective-permute-start | bytes 786440 | tf_op jit(solution)/shard_map/ppermute | solution.py:400
  192.2 14.1 %collective-permute-start.28 = (bf16[256,512]{1,0:T(8,128)(2,1)S(1)}, bf16[256,512]{1,0:T(8,128)(2,1)S(1)}, u32[]{:S(2)}, u32[]{:S(2)}) collective-permute-start(bf16[256,512]{1,0:T(8,128)(2,1)S(1)} %get-tuple-element.103.rest_0_), channel_id=1, source_target_pairs={{0,2},{2,4},{4,6},{6,0},{1,3},{3,5},{5,7},{7,1},{8,10},{10,12},{12... | collective-permute-start | bytes 786440 | tf_op jit(solution)/shard_map/ppermute | solution.py:400
  192.2 14.5 %collective-permute-start.29 = (bf16[256,512]{1,0:T(8,128)(2,1)S(1)}, bf16[256,512]{1,0:T(8,128)(2,1)S(1)}, u32[]{:S(2)}, u32[]{:S(2)}) collective-permute-start(bf16[256,512]{1,0:T(8,128)(2,1)S(1)} %get-tuple-element.103.rest_0_), channel_id=1, source_target_pairs={{0,1},{1,0},{2,3},{3,2},{4,5},{5,4},{6,7},{7,6},{8,9},{9,8},{10,11... | collective-permute-start | bytes 786440 | tf_op jit(solution)/shard_map/ppermute | solution.py:392
  197.4 9.3 %collective-permute-start.30 = (bf16[256,512]{1,0:T(8,128)(2,1)S(1)}, bf16[256,512]{1,0:T(8,128)(2,1)S(1)}, u32[]{:S(2)}, u32[]{:S(2)}) collective-permute-start(bf16[256,512]{1,0:T(8,128)(2,1)S(1)} %collective-permute-done.26.rest_1_), channel_id=1, source_target_pairs={{0,1},{1,0},{2,3},{3,2},{4,5},{5,4},{6,7},{7,6},{8,9},{9,8},{10,11... | collective-permute-start | bytes 786440 | tf_op jit(solution)/shard_map/ppermute | solution.py:392
  213.9 32.9 %all-to-all-start.5 = ((bf16[16,40,512]{2,1,0:T(8,128)(2,1)}), bf16[16,40,512]{2,1,0:T(8,128)(2,1)}, u32[]{:S(2)}, u32[]{:S(2)}) async-start(bf16[16,40,512]{2,1,0:T(8,128)(2,1)} %copy-done.12), calls=%async_computation.5 | async-start | bytes 1310720 | tf_op jit(solution)/shard_map/all_to_all | solution.py:505
  222.1 10.0 %collective-permute-start.24 = (bf16[256,512]{1,0:T(8,128)(2,1)}, bf16[256,512]{1,0:T(8,128)(2,1)S(1)}, u32[]{:S(2)}, u32[]{:S(2)}) collective-permute-start(bf16[256,512]{1,0:T(8,128)(2,1)} %copy-done.37), channel_id=1, source_target_pairs={{0,0},{1,4},{4,1},{5,5},{2,2},{3,6},{6,3},{7,7},{8,8},{9,12},{12,9... | collective-permute-start | bytes 786440 | tf_op jit(solution)/shard_map/ppermute | solution.py:388
  228.4 8.6 %collective-permute-start.17 = (bf16[272,256]{1,0:T(8,128)(2,1)S(1)}, bf16[272,256]{1,0:T(8,128)(2,1)S(1)}, u32[]{:S(2)}, u32[]{:S(2)}) collective-permute-start(bf16[272,256]{1,0:T(8,128)(2,1)S(1)} %grad_key_value.1.rest_0_), channel_id=1, source_target_pairs={{0,6},{2,0},{4,2},{6,4},{1,7},{3,1},{5,3},{7,5},{8,14},{10,8},{12,... | collective-permute-start | bytes 417800 | tf_op jit(solution)/shard_map/ppermute | solution.py:400
  228.4 8.7 %collective-permute-start.18 = (bf16[272,256]{1,0:T(8,128)(2,1)S(1)}, bf16[272,256]{1,0:T(8,128)(2,1)S(1)}, u32[]{:S(2)}, u32[]{:S(2)}) collective-permute-start(bf16[272,256]{1,0:T(8,128)(2,1)S(1)} %grad_key_value.1.rest_0_), channel_id=1, source_target_pairs={{0,4},{2,6},{4,0},{6,2},{1,5},{3,7},{5,1},{7,3},{8,12},{10,14},{12... | collective-permute-start | bytes 417800 | tf_op jit(solution)/shard_map/ppermute | solution.py:400
  231.6 9.6 %collective-permute-start.19 = (bf16[272,256]{1,0:T(8,128)(2,1)S(1)}, bf16[272,256]{1,0:T(8,128)(2,1)S(1)}, u32[]{:S(2)}, u32[]{:S(2)}) collective-permute-start(bf16[272,256]{1,0:T(8,128)(2,1)S(1)} %grad_key_value.1.rest_0_), channel_id=1, source_target_pairs={{0,2},{2,4},{4,6},{6,0},{1,3},{3,5},{5,7},{7,1},{8,10},{10,12},{12... | collective-permute-start | bytes 417800 | tf_op jit(solution)/shard_map/ppermute | solution.py:400
  231.6 10.0 %collective-permute-start.20 = (bf16[272,256]{1,0:T(8,128)(2,1)S(1)}, bf16[272,256]{1,0:T(8,128)(2,1)S(1)}, u32[]{:S(2)}, u32[]{:S(2)}) collective-permute-start(bf16[272,256]{1,0:T(8,128)(2,1)S(1)} %grad_key_value.1.rest_0_), channel_id=1, source_target_pairs={{0,1},{1,0},{2,3},{3,2},{4,5},{5,4},{6,7},{7,6},{8,9},{9,8},{10,11... | collective-permute-start | bytes 417800 | tf_op jit(solution)/shard_map/ppermute | solution.py:392
  232.8 11.1 %collective-permute-start.25 = (bf16[272,256]{1,0:T(8,128)(2,1)S(1)}, bf16[272,256]{1,0:T(8,128)(2,1)S(1)}, u32[]{:S(2)}, u32[]{:S(2)}) collective-permute-start(bf16[272,256]{1,0:T(8,128)(2,1)S(1)} %grad_key_value.1.rest_0_), channel_id=1, source_target_pairs={{0,0},{1,4},{4,1},{5,5},{2,2},{3,6},{6,3},{7,7},{8,8},{9,12},{12,9... | collective-permute-start | bytes 417800 | tf_op jit(solution)/shard_map/ppermute | solution.py:388
  237.0 7.6 %collective-permute-start.21 = (bf16[272,256]{1,0:T(8,128)(2,1)S(1)}, bf16[272,256]{1,0:T(8,128)(2,1)S(1)}, u32[]{:S(2)}, u32[]{:S(2)}) collective-permute-start(bf16[272,256]{1,0:T(8,128)(2,1)S(1)} %collective-permute-done.17.rest_1_), channel_id=1, source_target_pairs={{0,1},{1,0},{2,3},{3,2},{4,5},{5,4},{6,7},{7,6},{8,9},{9,8},{10,11... | collective-permute-start | bytes 417800 | tf_op jit(solution)/shard_map/ppermute | solution.py:392
  241.6 11.8 %collective-permute-start.10 = (bf16[256,512]{1,0:T(8,128)(2,1)}, bf16[256,512]{1,0:T(8,128)(2,1)}, u32[]{:S(2)}, u32[]{:S(2)}) collective-permute-start(bf16[256,512]{1,0:T(8,128)(2,1)} %get-tuple-element.88), channel_id=1, source_target_pairs={{0,0},{1,4},{4,1},{5,5},{2,2},{3,6},{6,3},{7,7},{8,8},{9,12},{12,9... | collective-permute-start | bytes 786440 | tf_op jit(solution)/shard_map/ppermute | solution.py:388
  246.8 23.4 %all-to-all-start.6 = ((bf16[16,48,256]{2,1,0:T(8,128)(2,1)}), bf16[16,48,256]{2,1,0:T(8,128)(2,1)S(1)}, u32[]{:S(2)}, u32[]{:S(2)}) async-start(bf16[16,48,256]{2,1,0:T(8,128)(2,1)} %copy-done.14), calls=%async_computation.6 | async-start | bytes 786432 | tf_op jit(solution)/shard_map/all_to_all | solution.py:516
  (59 other events, 330.5 us)

commit v5 on v4

--- a/solution.py
+++ b/solution.py
@@ -17,6 +17,7 @@
 mib = 2**20
 smem = pl.BlockSpec(memory_space=pltpu.SMEM)
 vmem = pl.BlockSpec(memory_space=pltpu.VMEM)
+anywhere = pl.BlockSpec(memory_space=pl.ANY)
 
 
 def mm(a, b):
@@ -50,9 +51,11 @@
     return inverse * (grad_unit - unit * shrink), grad_normed * unit
 
 
-def prepare_kernel(where, src_ref, toks_ref, toks_theirs_ref, turned_ref):
+def prepare_kernel(where, src_ref, *rest):
+    toks_ref, toks_theirs_ref, turned_ref, done_ref = rest[-4:]
     sizes = src_ref.shape[:3]
     core = where[1]
+    done_ref[...] = jnp.zeros_like(done_ref)
 
     def rows(y, side):
         pieces = [src_ref[x, z, y, side].astype(f32) for z in range(sizes[1]) for x in range(sizes[0])]
@@ -72,7 +75,8 @@
     kv_ref[:, span:] = raw[:, span:].astype(bf16)
 
 
-def query_part_kernel(where, mine_ref, other_ref, w0, w1, w2, w3, part_ref, part_other_ref):
+def query_part_kernel(where, mine_ref, other_ref, w0, w1, w2, w3, part_ref, part_other_ref, done_ref):
+    done_ref[...] = jnp.zeros_like(done_ref)
     for toks_ref, out_ref in ((mine_ref, part_ref), (other_ref, part_other_ref)):
         total = 0.0
         for k, w in enumerate((w0, w1, w2, w3)):
@@ -80,9 +84,10 @@
         out_ref[...] = total
 
 
-def query_kernel(part_ref, part_theirs_ref, gain_ref, cos_ref, sin_ref, q_ref, raw_ref):
+def query_kernel(part_ref, part_theirs_ref, raw_k_ref, gain_ref, cos_ref, sin_ref, q_ref, raw_ref):
     gain = gain_ref[...] * (span**-0.5 / math.log(2.0))
-    for h in range(raw_ref.shape[1] // span):
+    raw_ref[:, -span:] = raw_k_ref[...].astype(bf16)
+    for h in range(q_ref.shape[1] // span):
         part = slice(h * span, (h + 1) * span)
         raw = part_ref[:, part] + part_theirs_ref[:, part]
         raw_ref[:, part] = raw.astype(bf16)
@@ -328,20 +333,27 @@
     )(where, turned, *blocks)
 
 
-def grad_states_kernel(where, gq_ref, gkv_ref, kv_ref, kv_theirs_ref, *rest):
-    weights, (out_ref, blocks) = rest[:-2], rest[-2:]
-    columns = len(weights) // 2
+def grad_states_kernel(where, gq_ref, gkv_ref, *rest):
+    sources, (out_ref, blocks, loaded_kv, loaded_q, sems) = rest[:-5], rest[-5:]
+    columns = loaded_q.shape[0] // 2
     y, core = where[0], where[1]
     own_rows = 40
     toks = gq_ref.shape[0]
+    kv, weights = sources[:2], sources[2:]
+    copies = [pltpu.make_async_copy(kv[i], loaded_kv.at[i], sems.at[i]) for i in range(2)]
+    copies += [pltpu.make_async_copy(w, loaded_q.at[i], sems.at[2 + i]) for i, w in enumerate(weights)]
+    for copy in copies:
+        copy.start()
     transposed = (((1,), (1,)), ((), ()))
-    for side, kv in ((0, kv_ref), (1, kv_theirs_ref)):
+    for side in range(2):
         at_core = core if side == 0 else 1 - core
+        copies[side].wait()
         for k in range(columns):
             at = lax.rem(y + k, columns)
+            copies[2 + side * columns + k].wait()
             blocks[at, at_core] = lax.dot_general(
-                weights[side * columns + k][...], gq_ref[...], transposed, preferred_element_type=f32
-            ) + lax.dot_general(kv[at], gkv_ref[:toks], transposed, preferred_element_type=f32)
+                loaded_q[side * columns + k], gq_ref[...], transposed, preferred_element_type=f32
+            ) + lax.dot_general(loaded_kv[side, at], gkv_ref[:toks], transposed, preferred_element_type=f32)
     for x in range(4):
         pieces = []
         for z in range(4):
@@ -364,16 +376,21 @@
 cheap = pl.CostEstimate(flops=1000, bytes_accessed=1000, transcendentals=0)
 
 
-def call(kernel, shapes, *args, name):
+def call(kernel, shapes, *args, name, after=()):
+    count = len(args)
+
+    def run(*refs):
+        kernel(*refs[:count], *refs[count + len(after) :])
+
     return pl.pallas_call(
-        kernel,
+        run,
         out_shape=shapes,
-        in_specs=[smem if a.dtype == jnp.int32 else vmem for a in args],
+        in_specs=[smem if a.dtype == jnp.int32 else vmem for a in args] + [anywhere] * len(after),
         out_specs=jax.tree.map(lambda _: vmem, shapes),
         compiler_params=pltpu.CompilerParams(vmem_limit_bytes=48 * mib),
         cost_estimate=cheap,
         name=name,
-    )(*args)
+    )(*args, *after)
 
 
 plane = ("x", "z")
@@ -398,6 +415,19 @@
 
 def ring(array, step):
     return lax.ppermute(array, column, [(i, (i - step) % 4) for i in range(4)])
+
+
+def place_kernel(where, *refs):
+    for k, block in enumerate(refs[:-1]):
+        refs[-1][lax.rem(where[0] + k, 4)] = block[...]
+
+
+def collect(array, name):
+    parts = [array] + [
+        lax.ppermute(array, name, [(i, (i - k) % 4) for i in range(4)]) for k in range(1, 4)
+    ]
+    at = lax.axis_index(name).astype(jnp.int32)[None]
+    return call(place_kernel, jax.ShapeDtypeStruct((4,) + array.shape, bf16), at, *parts, name="place")
 
 
 def around(array):
@@ -433,65 +463,59 @@
     kv_mine = to_all(jnp.concatenate([w_key, w_value], axis=1), chips, planes * columns)
     kv_mine = kv_mine.reshape(columns, half // columns, kv_cols)
 
-    toks_mine, toks_theirs, turned = pl.pallas_call(
+    early = (cosine, sine, cos_there, sin_there)
+    toks_mine, toks_theirs, turned, done = pl.pallas_call(
         prepare_kernel,
         out_shape=(shape((columns, tok_rows, half // columns), bf16),) * 2
-        + (shape((2 * columns, half // columns, tok_rows), bf16),),
-        in_specs=[smem, vmem],
-        out_specs=(vmem,) * 3,
+        + (shape((2 * columns, half // columns, tok_rows), bf16), shape((8, span), f32)),
+        in_specs=[smem, vmem] + [anywhere] * len(early),
+        out_specs=(vmem,) * 4,
         compiler_params=pltpu.CompilerParams(vmem_limit_bytes=48 * mib),
         cost_estimate=cheap,
         name="prepare",
-    )(where, tokens.T.reshape(4, 4, columns, 2, own_rows, tok_rows))
-
+    )(where, tokens.T.reshape(4, 4, columns, 2, own_rows, tok_rows), *early)
     toks_other = flip(toks_theirs)
-    kv_mine, toks_mine, toks_theirs, turned, cosine, sine, cos_there, sin_there, own = (
-        lax.optimization_barrier(
-            (kv_mine, toks_mine, toks_theirs, turned, cosine, sine, cos_there, sin_there, own)
-        )
-    )
+    q_rows = collect(collect(w_query, "x"), "z").reshape(planes * own_rows, q_cols)
+    kv_mine, q_rows, done, own = lax.optimization_barrier((kv_mine, q_rows, done, own))
     kv_theirs = flip(kv_mine)
-    q_rows, _ = lax.optimization_barrier((w_query, kv_mine))
-    q_rows = to_all(q_rows, owners, planes).reshape(planes * own_rows, q_cols)
 
     kv16, raw_k = call(
         key_value_kernel,
         (shape((tok_rows, kv_cols), bf16), shape((tok_rows, span), f32)),
         toks_mine, toks_theirs, kv_mine, kv_theirs, gain_k, cosine, sine,
         name="key_value",
+        after=(done,),
     )
     kv_send = jnp.broadcast_to(swap(kv16)[None], (planes, tok_rows, kv_cols))
-    kv_send, q_rows = lax.optimization_barrier((kv_send, q_rows))
     kv_own = lax.all_to_all(kv_send, plane, 0, 0)
     q_mine = [q_rows] + [ring(q_rows, k) for k in range(1, columns)]
-    q_part, q_part_other = call(
+    grad_out = swap(cotangent[0])
+    q_part, q_part_other, done = call(
         query_part_kernel,
-        (shape((tok_rows, q_cols), f32),) * 2,
+        (shape((tok_rows, q_cols), f32),) * 2 + (shape((8, span), f32),),
         where, toks_mine, toks_other, *q_mine,
         name="query_part",
-    )
-    kv_own, q_part, q_part_other, grad_out = lax.optimization_barrier(
-        (kv_own, q_part, q_part_other, swap(cotangent[0]))
-    )
-    q16, raw_q = call(
+        after=(grad_out,),
+    )
+    kv_own, q_part_other = lax.optimization_barrier((kv_own, q_part_other))
+    q16, raw = call(
         query_kernel,
-        (shape((tok_rows, q_cols), bf16),) * 2,
-        q_part, flip(q_part_other), gain_q, cosine, sine,
+        (shape((tok_rows, q_cols), bf16), shape((tok_rows, q_cols + span), bf16)),
+        q_part, flip(q_part_other), raw_k, gain_q, cosine, sine,
         name="query",
     )
-    kv_other, q16, raw_q = lax.optimization_barrier((flip(kv_own), q16, raw_q))
+    kv_other = flip(kv_own)
     q16 = swap(q16)
-    turned, raw_q, _ = lax.optimization_barrier((turned, raw_q, q16))
+    turned, done = lax.optimization_barrier((turned, done))
     turned = lax.all_to_all(turned, column + ("core",), 0, 0)
-    raw_there = swap(jnp.concatenate([raw_q, raw_k.astype(bf16)], axis=1))
+    raw, q_piece = lax.optimization_barrier((raw, q16[:8, :span]))
+    raw_there = swap(raw)
 
     ctx, dq, dkv_mine, dkv_theirs = attention(
         block_order, own, q16, grad_out, kv_own, kv_other
     )
+    dkv_theirs, turned, raw_there = lax.optimization_barrier((dkv_theirs, turned, raw_there))
     q_theirs = [flip(block) for block in q_mine]
-    dkv_theirs, dq, turned, raw_there, q_theirs = lax.optimization_barrier(
-        (dkv_theirs, dq, turned, raw_there, q_theirs)
-    )
     dkv = (dkv_mine.astype(f32) + flip(dkv_theirs).astype(f32)).astype(bf16)
     dkv = lax.all_to_all(dkv, plane, 0, 0)
 
@@ -500,6 +524,7 @@
         (shape((tok_rows, q_cols), bf16), shape((8, span), f32)),
         raw_there, dq, gain_q, cos_there, sin_there,
         name="grad_query",
+        after=(done, q_piece),
     )
     parts = weight_grad(where, turned, around(g_q), planes, own_rows)
     parts = lax.all_to_all(parts, owners, 0, 0)
@@ -524,9 +549,14 @@
     grad_states = pl.pallas_call(
         grad_states_kernel,
         out_shape=shape((tok_rows, width), bf16),
-        in_specs=[smem] + [vmem] * (4 + 2 * columns),
+        in_specs=[smem] + [vmem] * 2 + [anywhere] * (2 + 2 * columns),
         out_specs=vmem,
-        scratch_shapes=[pltpu.VMEM((columns, 2, half // columns, tok_rows), f32)],
+        scratch_shapes=[
+            pltpu.VMEM((columns, 2, half // columns, tok_rows), f32),
+            pltpu.VMEM((2, columns, half // columns, kv_cols), bf16),
+            pltpu.VMEM((2 * columns, half // columns, q_cols), bf16),
+            pltpu.SemaphoreType.DMA((2 + 2 * columns,)),
+        ],
         compiler_params=pltpu.CompilerParams(vmem_limit_bytes=48 * mib),
         cost_estimate=cheap,
         name="grad_states",

time: 277 us -> 288 us (1.040)
  waiting for transfers between devices: 61.5 us -> 80 us
  local copies, waits for them, and re-layouts: 44.4 us -> 31.5 us
  Pallas kernels: 54.9 us -> 62.4 us
    ppermute x7, waiting for transfers between devices: 9.64 us -> 54 us  [swap(): return lax.ppermute(array, ('y_hi', 'core'), swapped)]
    ppermute x9, waiting for transfers between devices: 35.7 us -> 5.89 us  [ring(): return lax.ppermute(array, column, [(i, (i - step) % 4) for i in range(4)])]
    unnamed x103 -> x77, local copies, waits for them, and re-layouts: 35.7 us -> 24.4 us
    all_to_all x2 -> x1, starting transfers between devices: 17.9 us -> 10.3 us  [to_all(): lax.all_to_all(jnp.broadcast_to(array[None], (count,) + array.shape), axe...]
    ppermute x0 -> x6, starting transfers between devices: none -> 7.2 us  [collect(): lax.ppermute(array, name, [(i, (i - k) % 4) for i in range(4)])]
    ppermute x0 -> x6, waiting for transfers between devices: none -> 6.46 us  [collect(): lax.ppermute(array, name, [(i, (i - k) % 4) for i in range(4)])]
    pallas_call x1, Pallas kernels: 6.41 us -> 10.2 us  [local(): pl.pallas_call(grad_states_kernel, out_shape=shape((tok_rows, width), bf1...]
    all_to_all x2 -> x1, waiting for transfers between devices: 3.72 us -> 0.01 us  [to_all(): lax.all_to_all(jnp.broadcast_to(array[None], (count,) + array.shape), axe...]
  transfers between devices with their start and end apart: 40 -> 45, of which waited for: 14 -> 12; matrix products, arithmetic and copies ran while one was open for 5% -> 4% of each run, Pallas kernels for 20% -> 21%
where the time goes in v5:
time: 288 us; the launch traced here: 285 us
  starting transfers between devices  100 us (35%)
  waiting for transfers between devices  80 us (28%)
  Pallas kernels  62.4 us (22%)
  local copies, waits for them, and re-layouts  31.5 us (11%)
  other arithmetic  9.47 us (3%)
    ppermute x7, waiting for transfers between devices, swap(): return lax.ppermute(array, ('y_hi', 'core'), swapped)  54 us
    pallas_call x1, Pallas kernels, attention(): pl.pallas_call(attention_kernel, out_shape=(jax.ShapeDtypeStruct((rows_he...  33.4 us
    ppermute x7, starting transfers between devices, swap(): return lax.ppermute(array, ('y_hi', 'core'), swapped)  27.3 us
    unnamed x77, local copies, waits for them, and re-layouts  24.4 us
    ppermute x17, starting transfers between devices, flip(): return lax.ppermute(array, 'core', flipped)  16.1 us
    ppermute x17, waiting for transfers between devices, flip(): return lax.ppermute(array, 'core', flipped)  13.6 us
    all_to_all x2, starting transfers between devices, local(): parts = lax.all_to_all(parts, owners, 0, 0)  13.3 us
    pallas_call x8, Pallas kernels, call(): pl.pallas_call(run, out_shape=shapes, in_specs=[smem if a.dtype == jnp.in...  12.3 us
  transfers between devices with their start and end apart: 45, of which 12 were waited for; matrix products, arithmetic and copies ran while one was open for 4% of the time, Pallas kernels for 21%

profile of v5, /device:TPU:39, one launch (start us, length us, event | category | flops | bytes accessed | tf_op | source)
XLA Modules:
  0.0 284.7 jit_solution(15149098824119267884)
XLA Ops:
  5.8 10.3 %all-to-all-start = ((bf16[64,40,256]{2,1,0:T(8,128)(2,1)}), bf16[64,40,256]{2,1,0:T(8,128)(2,1)S(1)}, u32[]{:S(2)}, u32[]{:S(2)}) async-start(bf16[64,40,256]{2,1,0:T(8,128)(2,1)} %broadcast_in_dim.16), calls=%async_computation | async-start | bytes 2621440 | tf_op jit(solution)/shard_map/all_to_all | solution.py:413
  23.0 4.4 %copy.15 = bf16[5120,256]{1,0:T(8,128)(2,1)} copy(bf16[5120,256]{0,1:T(8,128)(2,1)} %bitcast.35) | data formatting | bytes 5242880 | tf_op jit(solution)/shard_map/transpose | solution.py:476
  27.5 2.6 prepare.1
  33.3 3.1 %collective-permute-done.3.refs_2_ = bf16[4,40,512]{2,1,0:T(8,128)(2,1)S(1)} collective-permute-done((bf16[4,40,512]{2,1,0:T(8,128)(2,1)S(1)}, bf16[4,40,512]{2,1,0:T(8,128)(2,1)S(1)}, u32[]{:S(2)}, u32[]{:S(2)}) %collective-permute-start.3) | collective-permute-done | bytes 163872 | tf_op jit(solution)/shard_map/ppermute | solution.py:427
  37.1 3.3 %collective-permute-done.4.refs_3_ = bf16[4,40,512]{2,1,0:T(8,128)(2,1)} collective-permute-done((bf16[4,40,512]{2,1,0:T(8,128)(2,1)S(1)}, bf16[4,40,512]{2,1,0:T(8,128)(2,1)}, u32[]{:S(2)}, u32[]{:S(2)}) %collective-permute-start.4) | collective-permute-done | bytes 163872 | tf_op jit(solution)/shard_map/ppermute | solution.py:427
  43.3 2.7 collective-permute-done.11.refs_3_.rest_1_
  50.2 4.6 %collective-permute-start.12 = (bf16[256,256]{1,0:T(8,128)(2,1)S(1)}, bf16[256,256]{1,0:T(8,128)(2,1)S(1)}, u32[]{:S(2)}, u32[]{:S(2)}) collective-permute-start(bf16[256,256]{1,0:T(8,128)(2,1)S(1)} %get-tuple-element.59), channel_id=1, source_target_pairs={{0,0},{1,4},{4,1},{5,5},{2,2},{3,6},{6,3},{7,7},{8,8},{9,12},{12,9... | collective-permute-start | bytes 393224 | tf_op jit(solution)/shard_map/ppermute | solution.py:405
  54.7 3.2 %collective-permute-done.12 = bf16[256,256]{1,0:T(8,128)(2,1)S(1)} collective-permute-done((bf16[256,256]{1,0:T(8,128)(2,1)S(1)}, bf16[256,256]{1,0:T(8,128)(2,1)S(1)}, u32[]{:S(2)}, u32[]{:S(2)}) %collective-permute-start.12) | collective-permute-done | bytes 131104 | tf_op jit(solution)/shard_map/ppermute | solution.py:405
  59.5 6.5 %all-to-all-start.1 = ((bf16[16,256,256]{2,1,0:T(8,128)(2,1)}), bf16[16,256,256]{2,1,0:T(8,128)(2,1)}, u32[]{:S(2)}, u32[]{:S(2)}) async-start(bf16[16,256,256]{2,1,0:T(8,128)(2,1)} %broadcast_in_dim.20), calls=%async_computation.1 | async-start | bytes 4194304 | tf_op jit(solution)/shard_map/all_to_all | solution.py:490
  69.5 4.8 %collective-permute-start.10 = (bf16[256,512]{1,0:T(8,128)(2,1)}, bf16[256,512]{1,0:T(8,128)(2,1)S(1)}, u32[]{:S(2)}, u32[]{:S(2)}) collective-permute-start(bf16[256,512]{1,0:T(8,128)(2,1)} %bitcast.37), channel_id=1, source_target_pairs={{0,0},{1,4},{4,1},{5,5},{2,2},{3,6},{6,3},{7,7},{8,8},{9,12},{12,9... | collective-permute-start | bytes 786440 | tf_op jit(solution)/shard_map/ppermute | solution.py:405
  74.3 28.8 %collective-permute-done.10.refs_7_.g_ref = bf16[256,512]{1,0:T(8,128)(2,1)S(1)} collective-permute-done((bf16[256,512]{1,0:T(8,128)(2,1)}, bf16[256,512]{1,0:T(8,128)(2,1)S(1)}, u32[]{:S(2)}, u32[]{:S(2)}) %collective-permute-start.10) | collective-permute-done | bytes 262176 | tf_op jit(solution)/shard_map/ppermute | solution.py:405
  104.3 3.7 %query_part.1 = (f32[256,512]{1,0:T(8,128)S(1)}, f32[256,512]{1,0:T(8,128)S(1)}, f32[8,128]{1,0:T(8,128)S(1)}) custom-call(s32[2]{0:T(128)S(1)} %pad_add_fusion.where.refs_0_, bf16[4,256,640]{2,1,0:T(8,128)(2,1)S(1)} %get-tuple-element.53.refs_1_.refs_0_, bf16[4,256,640]{2,1,0:T(8,128)(2,1)} %copy-done.36, bf16[640,512]{1,0:T(8,128)(2,1)S(1)} %bitcast.27, ...), custom_call_target="tpu_custom_call" | custom-call | flops 1000 | bytes 1000 | tf_op jit(solution)/shard_map/query_part/pallas_call | solution.py:385
  109.7 3.7 %all-to-all-start.2 = ((bf16[8,640,256]{2,1,0:T(8,128)(2,1)}), bf16[8,640,256]{2,1,0:T(8,128)(2,1)S(1)}, u32[]{:S(2)}, u32[]{:S(2)}) async-start(bf16[8,640,256]{2,1,0:T(8,128)(2,1)} %copy-done.2), calls=%async_computation.2 | async-start | bytes 5242880 | tf_op jit(solution)/shard_map/all_to_all | solution.py:510
  114.0 4.6 %collective-permute-done.13.refs_1_ = f32[256,512]{1,0:T(8,128)S(1)} collective-permute-done((f32[256,512]{1,0:T(8,128)}, f32[256,512]{1,0:T(8,128)S(1)}, u32[]{:S(2)}, u32[]{:S(2)}) %collective-permute-start.13) | collective-permute-done | bytes 524320 | tf_op jit(solution)/shard_map/ppermute | solution.py:409
  122.8 4.1 %collective-permute-start.14 = (bf16[256,512]{1,0:T(8,128)(2,1)S(1)}, bf16[256,512]{1,0:T(8,128)(2,1)S(1)}, u32[]{:S(2)}, u32[]{:S(2)}) collective-permute-start(bf16[256,512]{1,0:T(8,128)(2,1)S(1)} %get-tuple-element.63), channel_id=1, source_target_pairs={{0,0},{1,4},{4,1},{5,5},{2,2},{3,6},{6,3},{7,7},{8,8},{9,12},{12,9... | collective-permute-start | bytes 786440 | tf_op jit(solution)/shard_map/ppermute | solution.py:405
  126.9 20.5 %collective-permute-done.14.q_ref = bf16[256,512]{1,0:T(8,128)(2,1)S(1)} collective-permute-done((bf16[256,512]{1,0:T(8,128)(2,1)S(1)}, bf16[256,512]{1,0:T(8,128)(2,1)S(1)}, u32[]{:S(2)}, u32[]{:S(2)}) %collective-permute-start.14) | collective-permute-done | bytes 262176 | tf_op jit(solution)/shard_map/ppermute | solution.py:405
  147.4 2.8 collective-permute-start.17
  153.1 33.4 %attention.1 = (bf16[256,512]{1,0:T(8,128)(2,1)}, f32[256,512]{1,0:T(8,128)S(1)}, bf16[16,256,256]{2,1,0:T(8,128)(2,1)S(1)}, bf16[16,256,256]{2,1,0:T(8,128)(2,1)S(1)}) custom-call(s32[64]{0:T(128)S(1)} %copy-done.27, s32[3]{0:T(128)S(1)} %copy-done.32, bf16[256,512]{1,0:T(8,128)(2,1)S(1)} %collective-permute-done.14.q_ref, bf16[256,512]{1,0:T(8,128)(2,1)S(1)} %copy-done.15, ...), custom_call_target="tpu_custom_call" | custom-call | flops 1000 | bytes 1000 | tf_op jit(solution)/shard_map/attention/pallas_call | solution.py:233
  190.0 4.4 %collective-permute-done.18 = bf16[16,256,256]{2,1,0:T(8,128)(2,1)S(1)} collective-permute-done((bf16[16,256,256]{2,1,0:T(8,128)(2,1)}, bf16[16,256,256]{2,1,0:T(8,128)(2,1)S(1)}, u32[]{:S(2)}, u32[]{:S(2)}) %collective-permute-start.18) | collective-permute-done | bytes 2097184 | tf_op jit(solution)/shard_map/ppermute | solution.py:409
  194.4 3.5 %add_convert_fusion = bf16[16,256,256]{2,1,0:T(8,128)(2,1)} fusion(bf16[16,256,256]{2,1,0:T(8,128)(2,1)S(1)} %collective-permute-done.18, bf16[16,256,256]{2,1,0:T(8,128)(2,1)} %copy-done.4), kind=kLoop, calls=%fused_computation | loop fusion | flops 4194304 | bytes 6291456 | tf_op jit(solution)/shard_map/convert_element_type | solution.py:519
  197.9 6.8 %all-to-all-start.3 = ((bf16[16,256,256]{2,1,0:T(8,128)(2,1)}), bf16[16,256,256]{2,1,0:T(8,128)(2,1)}, u32[]{:S(2)}, u32[]{:S(2)}) async-start(bf16[16,256,256]{2,1,0:T(8,128)(2,1)} %add_convert_fusion), calls=%async_computation.3 | async-start | bytes 4194304 | tf_op jit(solution)/shard_map/all_to_all | solution.py:520
  213.6 2.7 collective-permute-done.32.rest_1_
  216.3 6.9 %collective-permute-start.36 = (bf16[256,512]{1,0:T(8,128)(2,1)S(1)}, bf16[256,512]{1,0:T(8,128)(2,1)S(1)}, u32[]{:S(2)}, u32[]{:S(2)}) collective-permute-start(bf16[256,512]{1,0:T(8,128)(2,1)S(1)} %collective-permute-done.32.rest_1_), channel_id=1, source_target_pairs={{0,1},{1,0},{2,3},{3,2},{4,5},{5,4},{6,7},{7,6},{8,9},{9,8},{10,11... | collective-permute-start | bytes 786440 | tf_op jit(solution)/shard_map/ppermute | solution.py:409
  223.2 3.2 %collective-permute-done.34.rest_3_ = bf16[256,512]{1,0:T(8,128)(2,1)S(1)} collective-permute-done((bf16[256,512]{1,0:T(8,128)(2,1)}, bf16[256,512]{1,0:T(8,128)(2,1)S(1)}, u32[]{:S(2)}, u32[]{:S(2)}) %collective-permute-start.34) | collective-permute-done | bytes 262176 | tf_op jit(solution)/shard_map/ppermute | solution.py:417
  226.7 3.0 %collective-permute-start.26 = (bf16[256,512]{1,0:T(8,128)(2,1)}, bf16[256,512]{1,0:T(8,128)(2,1)}, u32[]{:S(2)}, u32[]{:S(2)}) collective-permute-start(bf16[256,512]{1,0:T(8,128)(2,1)} %get-tuple-element.79.rest_0_), channel_id=1, source_target_pairs={{0,0},{1,4},{4,1},{5,5},{2,2},{3,6},{6,3},{7,7},{8,8},{9,12},{12,9... | collective-permute-start | bytes 786440 | tf_op jit(solution)/shard_map/ppermute | solution.py:405
  229.7 2.5 weight_grad.2
  233.1 6.7 %all-to-all-start.4 = ((bf16[16,40,512]{2,1,0:T(8,128)(2,1)}), bf16[16,40,512]{2,1,0:T(8,128)(2,1)}, u32[]{:S(2)}, u32[]{:S(2)}) async-start(bf16[16,40,512]{2,1,0:T(8,128)(2,1)} %copy-done.3), calls=%async_computation.4 | async-start | bytes 1310720 | tf_op jit(solution)/shard_map/all_to_all | solution.py:530
  244.5 2.6 collective-permute-start.22
  247.1 4.1 %collective-permute-start.27 = (bf16[272,256]{1,0:T(8,128)(2,1)S(1)}, bf16[272,256]{1,0:T(8,128)(2,1)S(1)}, u32[]{:S(2)}, u32[]{:S(2)}) collective-permute-start(bf16[272,256]{1,0:T(8,128)(2,1)S(1)} %grad_key_value.1.rest_0_), channel_id=1, source_target_pairs={{0,0},{1,4},{4,1},{5,5},{2,2},{3,6},{6,3},{7,7},{8,8},{9,12},{12,9... | collective-permute-start | bytes 417800 | tf_op jit(solution)/shard_map/ppermute | solution.py:405
  257.5 4.1 %collective-permute-start.16 = (bf16[256,512]{1,0:T(8,128)(2,1)}, bf16[256,512]{1,0:T(8,128)(2,1)}, u32[]{:S(2)}, u32[]{:S(2)}) collective-permute-start(bf16[256,512]{1,0:T(8,128)(2,1)} %get-tuple-element.65), channel_id=1, source_target_pairs={{0,0},{1,4},{4,1},{5,5},{2,2},{3,6},{6,3},{7,7},{8,8},{9,12},{12,9... | collective-permute-start | bytes 786440 | tf_op jit(solution)/shard_map/ppermute | solution.py:405
  263.7 6.7 %all-to-all-start.5 = ((bf16[16,48,256]{2,1,0:T(8,128)(2,1)}), bf16[16,48,256]{2,1,0:T(8,128)(2,1)S(1)}, u32[]{:S(2)}, u32[]{:S(2)}) async-start(bf16[16,48,256]{2,1,0:T(8,128)(2,1)} %copy-done.10), calls=%async_computation.5 | async-start | bytes 786432 | tf_op jit(solution)/shard_map/all_to_all | solution.py:541
  272.2 10.2 %grad_states.1 = bf16[256,5120]{1,0:T(8,128)(2,1)} custom-call(s32[2]{0:T(128)S(1)} %pad_add_fusion.where.refs_0_, bf16[256,512]{1,0:T(8,128)(2,1)} %collective-permute-done.26.gq_ref, bf16[272,256]{1,0:T(8,128)(2,1)S(1)} %collective-permute-done.27.gkv_ref, bf16[4,640,256]{2,1,0:T(8,128)(2,1)} %bitcast.23, bf16[4,640,256]{2,1,0:T(8,128)(2,1)} %copy-done.1, ...), custom_call_target="tpu_custom_call" | custom-call | flops 1000 | bytes 1000 | tf_op jit(solution)/shard_map/grad_states/pallas_call | solution.py:549
  (165 shorter events, 69.3 us)
Async XLA Ops:
  0.6 18.3 %collective-permute-start = (bf16[40,512]{1,0:T(8,128)(2,1)}, bf16[40,512]{1,0:T(8,128)(2,1)S(1)}, u32[]{:S(2)}, u32[]{:S(2)}) collective-permute-start(bf16[40,512]{1,0:T(8,128)(2,1)} %refs_1_.1), channel_id=1, source_target_pairs={{0,96},{32,0},{64,32},{96,64},{1,97},{33,1},{65,33},{97,65},{2,98}... | collective-permute-start | bytes 122888 | tf_op jit(solution)/shard_map/ppermute | solution.py:427
  1.3 17.7 %collective-permute-start.1 = (bf16[40,512]{1,0:T(8,128)(2,1)}, bf16[40,512]{1,0:T(8,128)(2,1)S(1)}, u32[]{:S(2)}, u32[]{:S(2)}) collective-permute-start(bf16[40,512]{1,0:T(8,128)(2,1)} %refs_1_.1), channel_id=1, source_target_pairs={{0,64},{32,96},{64,0},{96,32},{1,65},{33,97},{65,1},{97,33},{2,66}... | collective-permute-start | bytes 122888 | tf_op jit(solution)/shard_map/ppermute | solution.py:427
  2.1 16.8 %collective-permute-start.2 = (bf16[40,512]{1,0:T(8,128)(2,1)}, bf16[40,512]{1,0:T(8,128)(2,1)S(1)}, u32[]{:S(2)}, u32[]{:S(2)}) collective-permute-start(bf16[40,512]{1,0:T(8,128)(2,1)} %refs_1_.1), channel_id=1, source_target_pairs={{0,32},{32,64},{64,96},{96,0},{1,33},{33,65},{65,97},{97,1},{2,34}... | collective-permute-start | bytes 122888 | tf_op jit(solution)/shard_map/ppermute | solution.py:427
  5.8 36.6 %all-to-all-start = ((bf16[64,40,256]{2,1,0:T(8,128)(2,1)}), bf16[64,40,256]{2,1,0:T(8,128)(2,1)S(1)}, u32[]{:S(2)}, u32[]{:S(2)}) async-start(bf16[64,40,256]{2,1,0:T(8,128)(2,1)} %broadcast_in_dim.16), calls=%async_computation | async-start | bytes 2621440 | tf_op jit(solution)/shard_map/all_to_all | solution.py:413
  19.0 17.5 %collective-permute-start.3 = (bf16[4,40,512]{2,1,0:T(8,128)(2,1)S(1)}, bf16[4,40,512]{2,1,0:T(8,128)(2,1)S(1)}, u32[]{:S(2)}, u32[]{:S(2)}) collective-permute-start(bf16[4,40,512]{2,1,0:T(8,128)(2,1)S(1)} %place.2.refs_1_), channel_id=1, source_target_pairs={{0,24},{8,0},{16,8},{24,16},{1,25},{9,1},{17,9},{25,17},{2,26},{10... | collective-permute-start | bytes 491528 | tf_op jit(solution)/shard_map/ppermute | solution.py:427
  19.3 21.1 %collective-permute-start.4 = (bf16[4,40,512]{2,1,0:T(8,128)(2,1)S(1)}, bf16[4,40,512]{2,1,0:T(8,128)(2,1)}, u32[]{:S(2)}, u32[]{:S(2)}) collective-permute-start(bf16[4,40,512]{2,1,0:T(8,128)(2,1)S(1)} %place.2.refs_1_), channel_id=1, source_target_pairs={{0,16},{8,24},{16,0},{24,8},{1,17},{9,25},{17,1},{25,9},{2,18},{10... | collective-permute-start | bytes 491528 | tf_op jit(solution)/shard_map/ppermute | solution.py:427
  21.4 19.0 %collective-permute-start.5 = (bf16[4,40,512]{2,1,0:T(8,128)(2,1)S(1)}, bf16[4,40,512]{2,1,0:T(8,128)(2,1)}, u32[]{:S(2)}, u32[]{:S(2)}) collective-permute-start(bf16[4,40,512]{2,1,0:T(8,128)(2,1)S(1)} %place.2.refs_1_), channel_id=1, source_target_pairs={{0,8},{8,16},{16,24},{24,0},{1,9},{9,17},{17,25},{25,1},{2,10},{10... | collective-permute-start | bytes 491528 | tf_op jit(solution)/shard_map/ppermute | solution.py:427
  59.5 50.2 %all-to-all-start.1 = ((bf16[16,256,256]{2,1,0:T(8,128)(2,1)}), bf16[16,256,256]{2,1,0:T(8,128)(2,1)}, u32[]{:S(2)}, u32[]{:S(2)}) async-start(bf16[16,256,256]{2,1,0:T(8,128)(2,1)} %broadcast_in_dim.20), calls=%async_computation.1 | async-start | bytes 4194304 | tf_op jit(solution)/shard_map/all_to_all | solution.py:490
  66.0 37.1 %collective-permute-start.6 = (bf16[4,256,640]{2,1,0:T(8,128)(2,1)S(1)}, bf16[4,256,640]{2,1,0:T(8,128)(2,1)S(1)}, u32[]{:S(2)}, u32[]{:S(2)}) collective-permute-start(bf16[4,256,640]{2,1,0:T(8,128)(2,1)S(1)} %copy-done.13), channel_id=1, source_target_pairs={{0,1},{1,0},{2,3},{3,2},{4,5},{5,4},{6,7},{7,6},{8,9},{9,8},{10,11... | collective-permute-start | bytes 3932168 | tf_op jit(solution)/shard_map/ppermute | solution.py:409
  66.1 37.0 %collective-permute-start.7 = (bf16[640,512]{1,0:T(8,128)(2,1)S(1)}, bf16[640,512]{1,0:T(8,128)(2,1)}, u32[]{:S(2)}, u32[]{:S(2)}) collective-permute-start(bf16[640,512]{1,0:T(8,128)(2,1)S(1)} %bitcast.24), channel_id=1, source_target_pairs={{0,6},{2,0},{4,2},{6,4},{1,7},{3,1},{5,3},{7,5},{8,14},{10,8},{12,... | collective-permute-start | bytes 1966088 | tf_op jit(solution)/shard_map/ppermute | solution.py:417
  68.2 34.9 %collective-permute-start.8 = (bf16[640,512]{1,0:T(8,128)(2,1)S(1)}, bf16[640,512]{1,0:T(8,128)(2,1)}, u32[]{:S(2)}, u32[]{:S(2)}) collective-permute-start(bf16[640,512]{1,0:T(8,128)(2,1)S(1)} %bitcast.25), channel_id=1, source_target_pairs={{0,4},{2,6},{4,0},{6,2},{1,5},{3,7},{5,1},{7,3},{8,12},{10,14},{12... | collective-permute-start | bytes 1966088 | tf_op jit(solution)/shard_map/ppermute | solution.py:417
  68.6 34.5 %collective-permute-start.9 = (bf16[640,512]{1,0:T(8,128)(2,1)S(1)}, bf16[640,512]{1,0:T(8,128)(2,1)}, u32[]{:S(2)}, u32[]{:S(2)}) collective-permute-start(bf16[640,512]{1,0:T(8,128)(2,1)S(1)} %bitcast.26), channel_id=1, source_target_pairs={{0,2},{2,4},{4,6},{6,0},{1,3},{3,5},{5,7},{7,1},{8,10},{10,12},{12... | collective-permute-start | bytes 1966088 | tf_op jit(solution)/shard_map/ppermute | solution.py:417
  69.5 33.6 %collective-permute-start.10 = (bf16[256,512]{1,0:T(8,128)(2,1)}, bf16[256,512]{1,0:T(8,128)(2,1)S(1)}, u32[]{:S(2)}, u32[]{:S(2)}) collective-permute-start(bf16[256,512]{1,0:T(8,128)(2,1)} %bitcast.37), channel_id=1, source_target_pairs={{0,0},{1,4},{4,1},{5,5},{2,2},{3,6},{6,3},{7,7},{8,8},{9,12},{12,9... | collective-permute-start | bytes 786440 | tf_op jit(solution)/shard_map/ppermute | solution.py:405
  109.7 80.3 %all-to-all-start.2 = ((bf16[8,640,256]{2,1,0:T(8,128)(2,1)}), bf16[8,640,256]{2,1,0:T(8,128)(2,1)S(1)}, u32[]{:S(2)}, u32[]{:S(2)}) async-start(bf16[8,640,256]{2,1,0:T(8,128)(2,1)} %copy-done.2), calls=%async_computation.2 | async-start | bytes 5242880 | tf_op jit(solution)/shard_map/all_to_all | solution.py:510
  113.4 36.8 %collective-permute-start.15 = (bf16[16,256,256]{2,1,0:T(8,128)(2,1)}, bf16[16,256,256]{2,1,0:T(8,128)(2,1)S(1)}, u32[]{:S(2)}, u32[]{:S(2)}) collective-permute-start(bf16[16,256,256]{2,1,0:T(8,128)(2,1)} %all-to-all-done.1.kv_ref), channel_id=1, source_target_pairs={{0,1},{1,0},{2,3},{3,2},{4,5},{5,4},{6,7},{7,6},{8,9},{9,8},{10,11... | collective-permute-start | bytes 6291464 | tf_op jit(solution)/shard_map/ppermute | solution.py:409
  122.8 24.6 %collective-permute-start.14 = (bf16[256,512]{1,0:T(8,128)(2,1)S(1)}, bf16[256,512]{1,0:T(8,128)(2,1)S(1)}, u32[]{:S(2)}, u32[]{:S(2)}) collective-permute-start(bf16[256,512]{1,0:T(8,128)(2,1)S(1)} %get-tuple-element.63), channel_id=1, source_target_pairs={{0,0},{1,4},{4,1},{5,5},{2,2},{3,6},{6,3},{7,7},{8,8},{9,12},{12,9... | collective-permute-start | bytes 786440 | tf_op jit(solution)/shard_map/ppermute | solution.py:405
  147.4 42.6 %collective-permute-start.17 = (bf16[256,640]{1,0:T(8,128)(2,1)}, bf16[256,640]{1,0:T(8,128)(2,1)}, u32[]{:S(2)}, u32[]{:S(2)}) collective-permute-start(bf16[256,640]{1,0:T(8,128)(2,1)} %get-tuple-element.71), channel_id=1, source_target_pairs={{0,0},{1,4},{4,1},{5,5},{2,2},{3,6},{6,3},{7,7},{8,8},{9,12},{12,9... | collective-permute-start | bytes 983048 | tf_op jit(solution)/shard_map/ppermute | solution.py:405
  197.9 35.1 %all-to-all-start.3 = ((bf16[16,256,256]{2,1,0:T(8,128)(2,1)}), bf16[16,256,256]{2,1,0:T(8,128)(2,1)}, u32[]{:S(2)}, u32[]{:S(2)}) async-start(bf16[16,256,256]{2,1,0:T(8,128)(2,1)} %add_convert_fusion), calls=%async_computation.3 | async-start | bytes 4194304 | tf_op jit(solution)/shard_map/all_to_all | solution.py:520
  210.7 12.5 %collective-permute-start.33 = (bf16[256,512]{1,0:T(8,128)(2,1)}, bf16[256,512]{1,0:T(8,128)(2,1)S(1)}, u32[]{:S(2)}, u32[]{:S(2)}) collective-permute-start(bf16[256,512]{1,0:T(8,128)(2,1)} %get-tuple-element.79.rest_0_), channel_id=1, source_target_pairs={{0,4},{2,6},{4,0},{6,2},{1,5},{3,7},{5,1},{7,3},{8,12},{10,14},{12... | collective-permute-start | bytes 786440 | tf_op jit(solution)/shard_map/ppermute | solution.py:417
  211.7 14.6 %collective-permute-start.34 = (bf16[256,512]{1,0:T(8,128)(2,1)}, bf16[256,512]{1,0:T(8,128)(2,1)S(1)}, u32[]{:S(2)}, u32[]{:S(2)}) collective-permute-start(bf16[256,512]{1,0:T(8,128)(2,1)} %get-tuple-element.79.rest_0_), channel_id=1, source_target_pairs={{0,2},{2,4},{4,6},{6,0},{1,3},{3,5},{5,7},{7,1},{8,10},{10,12},{12... | collective-permute-start | bytes 786440 | tf_op jit(solution)/shard_map/ppermute | solution.py:417
  211.8 17.9 %collective-permute-start.35 = (bf16[256,512]{1,0:T(8,128)(2,1)}, bf16[256,512]{1,0:T(8,128)(2,1)S(1)}, u32[]{:S(2)}, u32[]{:S(2)}) collective-permute-start(bf16[256,512]{1,0:T(8,128)(2,1)} %get-tuple-element.79.rest_0_), channel_id=1, source_target_pairs={{0,1},{1,0},{2,3},{3,2},{4,5},{5,4},{6,7},{7,6},{8,9},{9,8},{10,11... | collective-permute-start | bytes 786440 | tf_op jit(solution)/shard_map/ppermute | solution.py:409
  216.3 13.4 %collective-permute-start.36 = (bf16[256,512]{1,0:T(8,128)(2,1)S(1)}, bf16[256,512]{1,0:T(8,128)(2,1)S(1)}, u32[]{:S(2)}, u32[]{:S(2)}) collective-permute-start(bf16[256,512]{1,0:T(8,128)(2,1)S(1)} %collective-permute-done.32.rest_1_), channel_id=1, source_target_pairs={{0,1},{1,0},{2,3},{3,2},{4,5},{5,4},{6,7},{7,6},{8,9},{9,8},{10,11... | collective-permute-start | bytes 786440 | tf_op jit(solution)/shard_map/ppermute | solution.py:409
  226.7 20.4 %collective-permute-start.26 = (bf16[256,512]{1,0:T(8,128)(2,1)}, bf16[256,512]{1,0:T(8,128)(2,1)}, u32[]{:S(2)}, u32[]{:S(2)}) collective-permute-start(bf16[256,512]{1,0:T(8,128)(2,1)} %get-tuple-element.79.rest_0_), channel_id=1, source_target_pairs={{0,0},{1,4},{4,1},{5,5},{2,2},{3,6},{6,3},{7,7},{8,8},{9,12},{12,9... | collective-permute-start | bytes 786440 | tf_op jit(solution)/shard_map/ppermute | solution.py:405
  233.1 30.6 %all-to-all-start.4 = ((bf16[16,40,512]{2,1,0:T(8,128)(2,1)}), bf16[16,40,512]{2,1,0:T(8,128)(2,1)}, u32[]{:S(2)}, u32[]{:S(2)}) async-start(bf16[16,40,512]{2,1,0:T(8,128)(2,1)} %copy-done.3), calls=%async_computation.4 | async-start | bytes 1310720 | tf_op jit(solution)/shard_map/all_to_all | solution.py:530
  241.9 9.3 %collective-permute-start.19 = (bf16[272,256]{1,0:T(8,128)(2,1)S(1)}, bf16[272,256]{1,0:T(8,128)(2,1)S(1)}, u32[]{:S(2)}, u32[]{:S(2)}) collective-permute-start(bf16[272,256]{1,0:T(8,128)(2,1)S(1)} %grad_key_value.1.rest_0_), channel_id=1, source_target_pairs={{0,6},{2,0},{4,2},{6,4},{1,7},{3,1},{5,3},{7,5},{8,14},{10,8},{12,... | collective-permute-start | bytes 417800 | tf_op jit(solution)/shard_map/ppermute | solution.py:417
  244.5 9.0 %collective-permute-start.22 = (bf16[272,256]{1,0:T(8,128)(2,1)S(1)}, bf16[272,256]{1,0:T(8,128)(2,1)S(1)}, u32[]{:S(2)}, u32[]{:S(2)}) collective-permute-start(bf16[272,256]{1,0:T(8,128)(2,1)S(1)} %grad_key_value.1.rest_0_), channel_id=1, source_target_pairs={{0,1},{1,0},{2,3},{3,2},{4,5},{5,4},{6,7},{7,6},{8,9},{9,8},{10,11... | collective-permute-start | bytes 417800 | tf_op jit(solution)/shard_map/ppermute | solution.py:409
  252.0 20.2 %collective-permute-start.28 = (bf16[640,512]{1,0:T(8,128)(2,1)S(1)}, bf16[640,512]{1,0:T(8,128)(2,1)}, u32[]{:S(2)}, u32[]{:S(2)}) collective-permute-start(bf16[640,512]{1,0:T(8,128)(2,1)S(1)} %bitcast.28), channel_id=1, source_target_pairs={{0,1},{1,0},{2,3},{3,2},{4,5},{5,4},{6,7},{7,6},{8,9},{9,8},{10,11... | collective-permute-start | bytes 1966088 | tf_op jit(solution)/shard_map/ppermute | solution.py:409
  253.5 18.7 %collective-permute-start.29 = (bf16[640,512]{1,0:T(8,128)(2,1)}, bf16[640,512]{1,0:T(8,128)(2,1)}, u32[]{:S(2)}, u32[]{:S(2)}) collective-permute-start(bf16[640,512]{1,0:T(8,128)(2,1)} %collective-permute-done.7.refs_4_.rest_3_), channel_id=1, source_target_pairs={{0,1},{1,0},{2,3},{3,2},{4,5},{5,4},{6,7},{7,6},{8,9},{9,8},{10,11... | collective-permute-start | bytes 1966088 | tf_op jit(solution)/shard_map/ppermute | solution.py:409
  255.0 17.2 %collective-permute-start.30 = (bf16[640,512]{1,0:T(8,128)(2,1)}, bf16[640,512]{1,0:T(8,128)(2,1)}, u32[]{:S(2)}, u32[]{:S(2)}) collective-permute-start(bf16[640,512]{1,0:T(8,128)(2,1)} %collective-permute-done.8.refs_5_.rest_4_), channel_id=1, source_target_pairs={{0,1},{1,0},{2,3},{3,2},{4,5},{5,4},{6,7},{7,6},{8,9},{9,8},{10,11... | collective-permute-start | bytes 1966088 | tf_op jit(solution)/shard_map/ppermute | solution.py:409
  255.0 17.2 %collective-permute-start.31 = (bf16[640,512]{1,0:T(8,128)(2,1)}, bf16[640,512]{1,0:T(8,128)(2,1)}, u32[]{:S(2)}, u32[]{:S(2)}) collective-permute-start(bf16[640,512]{1,0:T(8,128)(2,1)} %collective-permute-done.9.refs_6_.rest_5_), channel_id=1, source_target_pairs={{0,1},{1,0},{2,3},{3,2},{4,5},{5,4},{6,7},{7,6},{8,9},{9,8},{10,11... | collective-permute-start | bytes 1966088 | tf_op jit(solution)/shard_map/ppermute | solution.py:409
  257.5 12.9 %collective-permute-start.16 = (bf16[256,512]{1,0:T(8,128)(2,1)}, bf16[256,512]{1,0:T(8,128)(2,1)}, u32[]{:S(2)}, u32[]{:S(2)}) collective-permute-start(bf16[256,512]{1,0:T(8,128)(2,1)} %get-tuple-element.65), channel_id=1, source_target_pairs={{0,0},{1,4},{4,1},{5,5},{2,2},{3,6},{6,3},{7,7},{8,8},{9,12},{12,9... | collective-permute-start | bytes 786440 | tf_op jit(solution)/shard_map/ppermute | solution.py:405
  263.7 18.7 %all-to-all-start.5 = ((bf16[16,48,256]{2,1,0:T(8,128)(2,1)}), bf16[16,48,256]{2,1,0:T(8,128)(2,1)S(1)}, u32[]{:S(2)}, u32[]{:S(2)}) async-start(bf16[16,48,256]{2,1,0:T(8,128)(2,1)} %copy-done.10), calls=%async_computation.5 | async-start | bytes 786432 | tf_op jit(solution)/shard_map/all_to_all | solution.py:541
  (51 other events, 250.5 us)

commit v6 on v5

--- a/solution.py
+++ b/solution.py
@@ -75,21 +75,34 @@
     kv_ref[:, span:] = raw[:, span:].astype(bf16)
 
 
-def query_part_kernel(where, mine_ref, other_ref, w0, w1, w2, w3, part_ref, part_other_ref, done_ref):
-    done_ref[...] = jnp.zeros_like(done_ref)
-    for toks_ref, out_ref in ((mine_ref, part_ref), (other_ref, part_other_ref)):
-        total = 0.0
-        for k, w in enumerate((w0, w1, w2, w3)):
-            total = total + mm(toks_ref[lax.rem(where[0] + k, 4)], w[...])
-        out_ref[...] = total
-
-
-def query_kernel(part_ref, part_theirs_ref, raw_k_ref, gain_ref, cos_ref, sin_ref, q_ref, raw_ref):
+def split_kernel(where, src_ref, low_ref, high_ref):
+    planes = src_ref.shape[0]
+    columns = low_ref.shape[0]
+    rows = src_ref.shape[1] // (columns + 1)
+    blocks = [src_ref[i].astype(f32) for i in range(planes)]
+    for k in range(columns + 1):
+        part = jnp.concatenate([block[k * rows : (k + 1) * rows] for block in blocks], axis=0).astype(bf16)
+        if k < columns:
+            low_ref[lax.rem(where[0] + k, columns)] = part
+        else:
+            high_ref[...] = part
+
+
+def query_kernel(where, mine_ref, theirs_ref, low_ref, low_theirs_ref, *rest):
+    highs, (raw_k_ref, gain_ref, cos_ref, sin_ref, q_ref, raw_ref) = rest[:-6], rest[-6:]
+    columns, cols = low_ref.shape[0], low_ref.shape[2]
+    low, high = 0.0, 0.0
+    for y in range(columns):
+        low = low + mm(mine_ref[y], low_ref[y]) + mm(theirs_ref[y], low_theirs_ref[y])
+    for k in range(columns):
+        at = lax.rem(where[0] + k, columns)
+        high = high + mm(mine_ref[at], highs[k][...]) + mm(theirs_ref[at], highs[columns + k][...])
+    raw_ref[:, -span:] = raw_k_ref[...].astype(bf16)
     gain = gain_ref[...] * (span**-0.5 / math.log(2.0))
-    raw_ref[:, -span:] = raw_k_ref[...].astype(bf16)
     for h in range(q_ref.shape[1] // span):
         part = slice(h * span, (h + 1) * span)
-        raw = part_ref[:, part] + part_theirs_ref[:, part]
+        half, at = (low, h * span) if h * span < cols else (high, h * span - cols)
+        raw = half[:, at : at + span]
         raw_ref[:, part] = raw.astype(bf16)
         q_ref[:, part] = shape_head(raw, gain, cos_ref[...], sin_ref[...]).astype(bf16)
 
@@ -321,39 +334,50 @@
         out_ref[i] = jnp.concatenate([part] + extra, axis=0).astype(bf16)
 
 
-def weight_grad(where, turned, blocks, planes, padded):
-    return pl.pallas_call(
+def weight_grad(where, turned, blocks, planes, padded, after=()):
+    return call(
         weight_grad_kernel,
-        out_shape=jax.ShapeDtypeStruct((planes, padded, blocks[0].shape[1]), bf16),
-        in_specs=[smem] + [vmem] * (1 + len(blocks)),
-        out_specs=vmem,
-        compiler_params=pltpu.CompilerParams(vmem_limit_bytes=48 * mib),
-        cost_estimate=cheap,
+        jax.ShapeDtypeStruct((planes, padded, blocks[0].shape[1]), bf16),
+        where, turned, *blocks,
         name="weight_grad",
-    )(where, turned, *blocks)
-
-
-def grad_states_kernel(where, gq_ref, gkv_ref, *rest):
-    sources, (out_ref, blocks, loaded_kv, loaded_q, sems) = rest[:-5], rest[-5:]
-    columns = loaded_q.shape[0] // 2
+        after=after,
+    )
+
+
+transposed = (((1,), (1,)), ((), ()))
+
+
+def grad_states_query_kernel(where, gq_ref, low_ref, low_theirs_ref, *rest):
+    highs, (out_ref, loaded, loaded_high, sems) = rest[:-4], rest[-4:]
+    columns, cols = loaded.shape[1], loaded.shape[3]
     y, core = where[0], where[1]
-    own_rows = 40
-    toks = gq_ref.shape[0]
-    kv, weights = sources[:2], sources[2:]
-    copies = [pltpu.make_async_copy(kv[i], loaded_kv.at[i], sems.at[i]) for i in range(2)]
-    copies += [pltpu.make_async_copy(w, loaded_q.at[i], sems.at[2 + i]) for i, w in enumerate(weights)]
+    copies = [pltpu.make_async_copy(low, loaded.at[i], sems.at[i]) for i, low in enumerate((low_ref, low_theirs_ref))]
+    copies += [pltpu.make_async_copy(high, loaded_high.at[i], sems.at[2 + i]) for i, high in enumerate(highs)]
     for copy in copies:
         copy.start()
-    transposed = (((1,), (1,)), ((), ()))
     for side in range(2):
         at_core = core if side == 0 else 1 - core
         copies[side].wait()
         for k in range(columns):
             at = lax.rem(y + k, columns)
             copies[2 + side * columns + k].wait()
-            blocks[at, at_core] = lax.dot_general(
-                loaded_q[side * columns + k], gq_ref[...], transposed, preferred_element_type=f32
-            ) + lax.dot_general(loaded_kv[side, at], gkv_ref[:toks], transposed, preferred_element_type=f32)
+            out_ref[at, at_core] = (
+                lax.dot_general(loaded[side, at], gq_ref[:, :cols], transposed, preferred_element_type=f32)
+                + lax.dot_general(
+                    loaded_high[side * columns + k], gq_ref[:, cols:], transposed, preferred_element_type=f32
+                )
+            ).astype(bf16)
+
+
+def grad_states_kernel(where, gkv_ref, query_ref, kv_ref, kv_theirs_ref, out_ref, blocks):
+    core = where[1]
+    columns, own_rows = kv_ref.shape[0], 40
+    toks = out_ref.shape[0]
+    for at_core, kv in ((core, kv_ref), (1 - core, kv_theirs_ref)):
+        for y in range(columns):
+            blocks[y, at_core] = query_ref[y, at_core].astype(f32) + lax.dot_general(
+                kv[y], gkv_ref[:toks], transposed, preferred_element_type=f32
+            )
     for x in range(4):
         pieces = []
         for z in range(4):
@@ -415,19 +439,6 @@
 
 def ring(array, step):
     return lax.ppermute(array, column, [(i, (i - step) % 4) for i in range(4)])
-
-
-def place_kernel(where, *refs):
-    for k, block in enumerate(refs[:-1]):
-        refs[-1][lax.rem(where[0] + k, 4)] = block[...]
-
-
-def collect(array, name):
-    parts = [array] + [
-        lax.ppermute(array, name, [(i, (i - k) % 4) for i in range(4)]) for k in range(1, 4)
-    ]
-    at = lax.axis_index(name).astype(jnp.int32)[None]
-    return call(place_kernel, jax.ShapeDtypeStruct((4,) + array.shape, bf16), at, *parts, name="place")
 
 
 def around(array):
@@ -474,10 +485,16 @@
         cost_estimate=cheap,
         name="prepare",
     )(where, tokens.T.reshape(4, 4, columns, 2, own_rows, tok_rows), *early)
-    toks_other = flip(toks_theirs)
-    q_rows = collect(collect(w_query, "x"), "z").reshape(planes * own_rows, q_cols)
-    kv_mine, q_rows, done, own = lax.optimization_barrier((kv_mine, q_rows, done, own))
+    w_low = w_query[:, :kv_cols]
+    w_both = jnp.concatenate([w_low] + [ring(w_low, k) for k in range(1, columns)] + [w_query[:, kv_cols:]])
+    kv_mine, w_both, done, own = lax.optimization_barrier((kv_mine, w_both, done, own))
     kv_theirs = flip(kv_mine)
+    q_low, q_high = call(
+        split_kernel,
+        (shape((columns, half // columns, kv_cols), bf16), shape((half // columns, kv_cols), bf16)),
+        where, to_all(w_both, owners, planes),
+        name="split",
+    )
 
     kv16, raw_k = call(
         key_value_kernel,
@@ -487,35 +504,30 @@
         after=(done,),
     )
     kv_send = jnp.broadcast_to(swap(kv16)[None], (planes, tok_rows, kv_cols))
+    kv_send, q_high = lax.optimization_barrier((kv_send, q_high))
     kv_own = lax.all_to_all(kv_send, plane, 0, 0)
-    q_mine = [q_rows] + [ring(q_rows, k) for k in range(1, columns)]
+    low_theirs = flip(q_low)
+    highs = [q_high] + [ring(q_high, k) for k in range(1, columns)]
+    highs += [flip(block) for block in highs]
     grad_out = swap(cotangent[0])
-    q_part, q_part_other, done = call(
-        query_part_kernel,
-        (shape((tok_rows, q_cols), f32),) * 2 + (shape((8, span), f32),),
-        where, toks_mine, toks_other, *q_mine,
-        name="query_part",
-        after=(grad_out,),
-    )
-    kv_own, q_part_other = lax.optimization_barrier((kv_own, q_part_other))
     q16, raw = call(
         query_kernel,
         (shape((tok_rows, q_cols), bf16), shape((tok_rows, q_cols + span), bf16)),
-        q_part, flip(q_part_other), raw_k, gain_q, cosine, sine,
+        where, toks_mine, toks_theirs, q_low, low_theirs, *highs, raw_k, gain_q, cosine, sine,
         name="query",
-    )
+        after=(grad_out,),
+    )
+    kv_own, raw = lax.optimization_barrier((kv_own, raw))
     kv_other = flip(kv_own)
     q16 = swap(q16)
-    turned, done = lax.optimization_barrier((turned, done))
+    turned, raw, q_piece = lax.optimization_barrier((turned, raw, q16[:8, :span]))
     turned = lax.all_to_all(turned, column + ("core",), 0, 0)
-    raw, q_piece = lax.optimization_barrier((raw, q16[:8, :span]))
     raw_there = swap(raw)
 
     ctx, dq, dkv_mine, dkv_theirs = attention(
         block_order, own, q16, grad_out, kv_own, kv_other
     )
     dkv_theirs, turned, raw_there = lax.optimization_barrier((dkv_theirs, turned, raw_there))
-    q_theirs = [flip(block) for block in q_mine]
     dkv = (dkv_mine.astype(f32) + flip(dkv_theirs).astype(f32)).astype(bf16)
     dkv = lax.all_to_all(dkv, plane, 0, 0)
 
@@ -524,11 +536,24 @@
         (shape((tok_rows, q_cols), bf16), shape((8, span), f32)),
         raw_there, dq, gain_q, cos_there, sin_there,
         name="grad_query",
-        after=(done, q_piece),
-    )
-    parts = weight_grad(where, turned, around(g_q), planes, own_rows)
-    parts = lax.all_to_all(parts, owners, 0, 0)
-    own_query = jnp.sum(parts.astype(f32), axis=0)
+        after=(q_piece,),
+    )
+    grad_states_query = pl.pallas_call(
+        grad_states_query_kernel,
+        out_shape=shape((columns, 2, half // columns, tok_rows), bf16),
+        in_specs=[smem, vmem] + [anywhere] * (2 + 2 * columns),
+        out_specs=vmem,
+        scratch_shapes=[
+            pltpu.VMEM((2, columns, half // columns, kv_cols), bf16),
+            pltpu.VMEM((2 * columns, half // columns, kv_cols), bf16),
+            pltpu.SemaphoreType.DMA((2 + 2 * columns,)),
+        ],
+        compiler_params=pltpu.CompilerParams(vmem_limit_bytes=48 * mib),
+        cost_estimate=cheap,
+        name="grad_states_query",
+    )(where, swap(g_q), q_low, low_theirs, *highs)
+    blocks_q = around(g_q)
+    dkv, grad_states_query = lax.optimization_barrier((dkv, grad_states_query))
 
     g_kv = call(
         grad_key_value_kernel,
@@ -536,8 +561,11 @@
         raw_there, dkv, gain_k, cos_there, sin_there, gains_q,
         name="grad_key_value",
     )
-    blocks, g_q_back, g_kv_back = lax.optimization_barrier((around(g_kv), swap(g_q), swap(g_kv)))
-    parts = weight_grad(where, turned, blocks, planes, own_rows + 8)
+    blocks_kv = around(g_kv)
+    parts = weight_grad(where, turned, blocks_q, planes, own_rows, after=(blocks_kv[1],))
+    parts = lax.all_to_all(parts, owners, 0, 0)
+    own_query = jnp.sum(parts.astype(f32), axis=0)
+    parts = weight_grad(where, turned, blocks_kv, planes, own_rows + 8)
     parts = lax.all_to_all(parts, owners, 0, 0)
     own_key, own_value, gain_sum_q, gain_sum_k = call(
         finish_kernel,
@@ -549,18 +577,13 @@
     grad_states = pl.pallas_call(
         grad_states_kernel,
         out_shape=shape((tok_rows, width), bf16),
-        in_specs=[smem] + [vmem] * 2 + [anywhere] * (2 + 2 * columns),
+        in_specs=[smem] + [vmem] * 4,
         out_specs=vmem,
-        scratch_shapes=[
-            pltpu.VMEM((columns, 2, half // columns, tok_rows), f32),
-            pltpu.VMEM((2, columns, half // columns, kv_cols), bf16),
-            pltpu.VMEM((2 * columns, half // columns, q_cols), bf16),
-            pltpu.SemaphoreType.DMA((2 + 2 * columns,)),
-        ],
+        scratch_shapes=[pltpu.VMEM((columns, 2, half // columns, tok_rows), f32)],
         compiler_params=pltpu.CompilerParams(vmem_limit_bytes=48 * mib),
         cost_estimate=cheap,
         name="grad_states",
-    )(where, g_q_back, g_kv_back, kv_mine, kv_theirs, *q_mine, *q_theirs)
+    )(where, swap(g_kv), grad_states_query, kv_mine, kv_theirs)
     return (
         swap(ctx)[None],
         grad_states[None],

time: 288 us -> 282 us (0.979)
  waiting for transfers between devices: 80 us -> 50.5 us
  local copies, waits for them, and re-layouts: 31.5 us -> 50.6 us
  starting transfers between devices: 100 us -> 107 us
    ppermute x7, waiting for transfers between devices: 54 us -> 28.8 us  [swap(): return lax.ppermute(array, ('y_hi', 'core'), swapped)]
    unnamed x77 -> x114, local copies, waits for them, and re-layouts: 24.4 us -> 40.6 us
    all_to_all x1 -> x2, starting transfers between devices: 10.3 us -> 18 us  [to_all(): lax.all_to_all(jnp.broadcast_to(array[None], (count,) + array.shape), axe...]
    ppermute x6 -> x0, starting transfers between devices: 7.2 us -> none  [collect(): lax.ppermute(array, name, [(i, (i - k) % 4) for i in range(4)])]
    all_to_all x1 -> x2, waiting for transfers between devices: 0.01 us -> 7 us  [to_all(): lax.all_to_all(jnp.broadcast_to(array[None], (count,) + array.shape), axe...]
    ppermute x6 -> x0, waiting for transfers between devices: 6.46 us -> none  [collect(): lax.ppermute(array, name, [(i, (i - k) % 4) for i in range(4)])]
    pallas_call x1, Pallas kernels: 10.2 us -> 3.7 us  [local(): pl.pallas_call(grad_states_kernel, out_shape=shape((tok_rows, width), bf1...]
    pallas_call x8, Pallas kernels: 12.3 us -> 16.3 us  [call(): pl.pallas_call(run, out_shape=shapes, in_specs=[smem if a.dtype == jnp.in...]
  transfers between devices with their start and end apart: 45 -> 42, of which waited for: 12 -> 19; matrix products, arithmetic and copies ran while one was open for 4% -> 3% of each run, Pallas kernels for 21% -> 22%
where the time goes in v6:
time: 282 us; the launch traced here: 278 us
  starting transfers between devices  107 us (38%)
  Pallas kernels  62.5 us (22%)
  local copies, waits for them, and re-layouts  50.6 us (18%)
  waiting for transfers between devices  50.5 us (18%)
  other arithmetic  6.73 us (2%)
    unnamed x114, local copies, waits for them, and re-layouts  40.6 us
    pallas_call x1, Pallas kernels, attention(): pl.pallas_call(attention_kernel, out_shape=(jax.ShapeDtypeStruct((rows_he...  32.6 us
    ppermute x7, waiting for transfers between devices, swap(): return lax.ppermute(array, ('y_hi', 'core'), swapped)  28.8 us
    ppermute x7, starting transfers between devices, swap(): return lax.ppermute(array, ('y_hi', 'core'), swapped)  28.4 us
    all_to_all x2, starting transfers between devices, to_all(): lax.all_to_all(jnp.broadcast_to(array[None], (count,) + array.shape), axe...  18 us
    pallas_call x8, Pallas kernels, call(): pl.pallas_call(run, out_shape=shapes, in_specs=[smem if a.dtype == jnp.in...  16.3 us
    ppermute x16, starting transfers between devices, flip(): return lax.ppermute(array, 'core', flipped)  16.1 us
    all_to_all x2, starting transfers between devices, local(): parts = lax.all_to_all(parts, owners, 0, 0)  13.5 us
  transfers between devices with their start and end apart: 42, of which 19 were waited for; matrix products, arithmetic and copies ran while one was open for 3% of the time, Pallas kernels for 22%

profile of v6, /device:TPU:39, one launch (start us, length us, event | category | flops | bytes accessed | tf_op | source)
XLA Modules:
  0.0 278.3 jit_solution(11781858840582345447)
XLA Ops:
  7.0 9.5 %all-to-all-start = ((bf16[64,40,256]{2,1,0:T(8,128)(2,1)}), bf16[64,40,256]{2,1,0:T(8,128)(2,1)S(1)}, u32[]{:S(2)}, u32[]{:S(2)}) async-start(bf16[64,40,256]{2,1,0:T(8,128)(2,1)} %broadcast_in_dim.14), calls=%async_computation | async-start | bytes 2621440 | tf_op jit(solution)/shard_map/all_to_all | solution.py:437
  18.3 4.4 %copy.15 = bf16[5120,256]{1,0:T(8,128)(2,1)} copy(bf16[5120,256]{0,1:T(8,128)(2,1)} %bitcast.27) | data formatting | bytes 5242880 | tf_op jit(solution)/shard_map/transpose | solution.py:487
  29.1 2.8 %all-to-all-done = bf16[64,40,256]{2,1,0:T(8,128)(2,1)S(1)} async-done(((bf16[64,40,256]{2,1,0:T(8,128)(2,1)}), bf16[64,40,256]{2,1,0:T(8,128)(2,1)S(1)}, u32[]{:S(2)}, u32[]{:S(2)}) %all-to-all-start) | async-done | bytes 1310752 | tf_op jit(solution)/shard_map/all_to_all | solution.py:437
  33.2 8.5 %all-to-all-start.1 = ((bf16[16,200,256]{2,1,0:T(8,128)(2,1)}), bf16[16,200,256]{2,1,0:T(8,128)(2,1)S(1)}, u32[]{:S(2)}, u32[]{:S(2)}) async-start(bf16[16,200,256]{2,1,0:T(8,128)(2,1)} %broadcast_in_dim.15), calls=%async_computation.1 | async-start | bytes 3276800 | tf_op jit(solution)/shard_map/all_to_all | solution.py:437
  41.7 3.1 %collective-permute-start.4 = (bf16[4,640,256]{2,1,0:T(8,128)(2,1)S(1)}, bf16[4,640,256]{2,1,0:T(8,128)(2,1)S(1)}, u32[]{:S(2)}, u32[]{:S(2)}) collective-permute-start(bf16[4,640,256]{2,1,0:T(8,128)(2,1)S(1)} %bitcast.18), channel_id=1, source_target_pairs={{0,1},{1,0},{2,3},{3,2},{4,5},{5,4},{6,7},{7,6},{8,9},{9,8},{10,11... | collective-permute-start | bytes 3932168 | tf_op jit(solution)/shard_map/ppermute | solution.py:433
  55.5 4.2 %all-to-all-done.1.refs_1_ = bf16[16,200,256]{2,1,0:T(8,128)(2,1)S(1)} async-done(((bf16[16,200,256]{2,1,0:T(8,128)(2,1)}), bf16[16,200,256]{2,1,0:T(8,128)(2,1)S(1)}, u32[]{:S(2)}, u32[]{:S(2)}) %all-to-all-start.1) | async-done | bytes 1638432 | tf_op jit(solution)/shard_map/all_to_all | solution.py:437
  63.6 8.0 %all-to-all-start.2 = ((bf16[16,256,256]{2,1,0:T(8,128)(2,1)}), bf16[16,256,256]{2,1,0:T(8,128)(2,1)}, u32[]{:S(2)}, u32[]{:S(2)}) async-start(bf16[16,256,256]{2,1,0:T(8,128)(2,1)} %broadcast_in_dim.17), calls=%async_computation.2 | async-start | bytes 4194304 | tf_op jit(solution)/shard_map/all_to_all | solution.py:508
  71.6 3.7 %collective-permute-start.3 = (bf16[4,640,256]{2,1,0:T(8,128)(2,1)S(1)}, bf16[4,640,256]{2,1,0:T(8,128)(2,1)S(1)}, u32[]{:S(2)}, u32[]{:S(2)}) collective-permute-start(bf16[4,640,256]{2,1,0:T(8,128)(2,1)S(1)} %get-tuple-element.48.refs_3_.low_ref), channel_id=1, source_target_pairs={{0,1},{1,0},{2,3},{3,2},{4,5},{5,4},{6,7},{7,6},{8,9},{9,8},{10,11... | collective-permute-start | bytes 3932168 | tf_op jit(solution)/shard_map/ppermute | solution.py:433
  77.0 6.1 %collective-permute-start.13 = (bf16[256,512]{1,0:T(8,128)(2,1)}, bf16[256,512]{1,0:T(8,128)(2,1)S(1)}, u32[]{:S(2)}, u32[]{:S(2)}) collective-permute-start(bf16[256,512]{1,0:T(8,128)(2,1)} %bitcast.29), channel_id=1, source_target_pairs={{0,0},{1,4},{4,1},{5,5},{2,2},{3,6},{6,3},{7,7},{8,8},{9,12},{12,9... | collective-permute-start | bytes 786440 | tf_op jit(solution)/shard_map/ppermute | solution.py:429
  83.1 13.9 %collective-permute-done.13.refs_17_.g_ref = bf16[256,512]{1,0:T(8,128)(2,1)S(1)} collective-permute-done((bf16[256,512]{1,0:T(8,128)(2,1)}, bf16[256,512]{1,0:T(8,128)(2,1)S(1)}, u32[]{:S(2)}, u32[]{:S(2)}) %collective-permute-start.13) | collective-permute-done | bytes 262176 | tf_op jit(solution)/shard_map/ppermute | solution.py:429
  102.0 4.2 %query.1 = (bf16[256,512]{1,0:T(8,128)(2,1)S(1)}, bf16[256,640]{1,0:T(8,128)(2,1)S(1)}) custom-call(s32[2]{0:T(128)S(1)} %pad_add_fusion.where.refs_0_, bf16[4,256,640]{2,1,0:T(8,128)(2,1)S(1)} %copy-done.11, bf16[4,256,640]{2,1,0:T(8,128)(2,1)} %copy-done.12, bf16[4,640,256]{2,1,0:T(8,128)(2,1)} %copy-done.3, bf16[4,640,256]{2,1,0:T(8,128)(2,1)} %copy-done.5, ...), custom_call_target="tpu_custom_call" | custom-call | flops 1000 | bytes 1000 | tf_op jit(solution)/shard_map/query/pallas_call | solution.py:409
  112.0 3.3 %collective-permute-start.14 = (bf16[256,512]{1,0:T(8,128)(2,1)S(1)}, bf16[256,512]{1,0:T(8,128)(2,1)S(1)}, u32[]{:S(2)}, u32[]{:S(2)}) collective-permute-start(bf16[256,512]{1,0:T(8,128)(2,1)S(1)} %get-tuple-element.55), channel_id=1, source_target_pairs={{0,0},{1,4},{4,1},{5,5},{2,2},{3,6},{6,3},{7,7},{8,8},{9,12},{12,9... | collective-permute-start | bytes 786440 | tf_op jit(solution)/shard_map/ppermute | solution.py:429
  115.3 5.9 %collective-permute-done.14.q_ref = bf16[256,512]{1,0:T(8,128)(2,1)S(1)} collective-permute-done((bf16[256,512]{1,0:T(8,128)(2,1)S(1)}, bf16[256,512]{1,0:T(8,128)(2,1)S(1)}, u32[]{:S(2)}, u32[]{:S(2)}) %collective-permute-start.14) | collective-permute-done | bytes 262176 | tf_op jit(solution)/shard_map/ppermute | solution.py:429
  121.9 3.7 %all-to-all-start.3 = ((bf16[8,640,256]{2,1,0:T(8,128)(2,1)}), bf16[8,640,256]{2,1,0:T(8,128)(2,1)S(1)}, u32[]{:S(2)}, u32[]{:S(2)}) async-start(bf16[8,640,256]{2,1,0:T(8,128)(2,1)} %copy-done.14), calls=%async_computation.3 | async-start | bytes 5242880 | tf_op jit(solution)/shard_map/all_to_all | solution.py:524
  125.7 4.6 %collective-permute-start.17 = (bf16[256,640]{1,0:T(8,128)(2,1)}, bf16[256,640]{1,0:T(8,128)(2,1)S(1)}, u32[]{:S(2)}, u32[]{:S(2)}) collective-permute-start(bf16[256,640]{1,0:T(8,128)(2,1)} %copy-done.51), channel_id=1, source_target_pairs={{0,0},{1,4},{4,1},{5,5},{2,2},{3,6},{6,3},{7,7},{8,8},{9,12},{12,9... | collective-permute-start | bytes 983048 | tf_op jit(solution)/shard_map/ppermute | solution.py:429
  132.6 32.6 %attention.1 = (bf16[256,512]{1,0:T(8,128)(2,1)S(1)}, f32[256,512]{1,0:T(8,128)S(1)}, bf16[16,256,256]{2,1,0:T(8,128)(2,1)S(1)}, bf16[16,256,256]{2,1,0:T(8,128)(2,1)S(1)}) custom-call(s32[64]{0:T(128)S(1)} %copy-done.47, s32[3]{0:T(128)S(1)} %pad_add_fusion.1.own, bf16[256,512]{1,0:T(8,128)(2,1)S(1)} %copy-done.40, bf16[256,512]{1,0:T(8,128)(2,1)S(1)} %copy-done.36, ...), custom_call_target="tpu_custom_call" | custom-call | flops 1000 | bytes 1000 | tf_op jit(solution)/shard_map/attention/pallas_call | solution.py:246
  170.2 4.2 %collective-permute-done.18 = bf16[16,256,256]{2,1,0:T(8,128)(2,1)S(1)} collective-permute-done((bf16[16,256,256]{2,1,0:T(8,128)(2,1)}, bf16[16,256,256]{2,1,0:T(8,128)(2,1)S(1)}, u32[]{:S(2)}, u32[]{:S(2)}) %collective-permute-start.18) | collective-permute-done | bytes 2097184 | tf_op jit(solution)/shard_map/ppermute | solution.py:433
  174.5 3.6 %add_convert_fusion = bf16[16,256,256]{2,1,0:T(8,128)(2,1)} fusion(bf16[16,256,256]{2,1,0:T(8,128)(2,1)S(1)} %collective-permute-done.18, bf16[16,256,256]{2,1,0:T(8,128)(2,1)} %copy-done.15), kind=kLoop, calls=%fused_computation | loop fusion | flops 4194304 | bytes 6291456 | tf_op jit(solution)/shard_map/convert_element_type | solution.py:531
  178.0 6.6 %all-to-all-start.4 = ((bf16[16,256,256]{2,1,0:T(8,128)(2,1)}), bf16[16,256,256]{2,1,0:T(8,128)(2,1)}, u32[]{:S(2)}, u32[]{:S(2)}) async-start(bf16[16,256,256]{2,1,0:T(8,128)(2,1)} %add_convert_fusion), calls=%async_computation.4 | async-start | bytes 4194304 | tf_op jit(solution)/shard_map/all_to_all | solution.py:532
  188.1 5.0 %collective-permute-start.19 = (bf16[256,512]{1,0:T(8,128)(2,1)}, bf16[256,512]{1,0:T(8,128)(2,1)S(1)}, u32[]{:S(2)}, u32[]{:S(2)}) collective-permute-start(bf16[256,512]{1,0:T(8,128)(2,1)} %get-tuple-element.70.refs_2_), channel_id=1, source_target_pairs={{0,0},{1,4},{4,1},{5,5},{2,2},{3,6},{6,3},{7,7},{8,8},{9,12},{12,9... | collective-permute-start | bytes 786440 | tf_op jit(solution)/shard_map/ppermute | solution.py:429
  193.0 4.4 %collective-permute-done.19.gq_ref = bf16[256,512]{1,0:T(8,128)(2,1)S(1)} collective-permute-done((bf16[256,512]{1,0:T(8,128)(2,1)}, bf16[256,512]{1,0:T(8,128)(2,1)S(1)}, u32[]{:S(2)}, u32[]{:S(2)}) %collective-permute-start.19) | collective-permute-done | bytes 262176 | tf_op jit(solution)/shard_map/ppermute | solution.py:429
  206.9 7.3 %grad_states_query.1.query_ref = bf16[4,2,640,256]{3,2,1,0:T(8,128)(2,1)} custom-call(s32[2]{0:T(128)S(1)} %pad_add_fusion.where.refs_0_, bf16[256,512]{1,0:T(8,128)(2,1)S(1)} %collective-permute-done.19.gq_ref, bf16[4,640,256]{2,1,0:T(8,128)(2,1)S(1)} %copy-done.4, bf16[4,640,256]{2,1,0:T(8,128)(2,1)S(1)} %copy-done.6, bf16[640,256]{1,0:T(8,128)(2,1)S(1)} %copy-done.17, ...), custom_call_target="tpu_custom_call" | custom-call | flops 1000 | bytes 1000 | tf_op jit(solution)/shard_map/grad_states_query/pallas_call | solution.py:541
  217.3 3.1 %collective-permute-start.29 = (bf16[272,256]{1,0:T(8,128)(2,1)S(1)}, bf16[272,256]{1,0:T(8,128)(2,1)S(1)}, u32[]{:S(2)}, u32[]{:S(2)}) collective-permute-start(bf16[272,256]{1,0:T(8,128)(2,1)S(1)} %grad_key_value.1.refs_2_), channel_id=1, source_target_pairs={{0,4},{2,6},{4,0},{6,2},{1,5},{3,7},{5,1},{7,3},{8,12},{10,14},{12... | collective-permute-start | bytes 417800 | tf_op jit(solution)/shard_map/ppermute | solution.py:441
  222.2 3.8 %collective-permute-start.32 = (bf16[272,256]{1,0:T(8,128)(2,1)S(1)}, bf16[272,256]{1,0:T(8,128)(2,1)S(1)}, u32[]{:S(2)}, u32[]{:S(2)}) collective-permute-start(bf16[272,256]{1,0:T(8,128)(2,1)S(1)} %collective-permute-done.28.refs_10_.refs_3_), channel_id=1, source_target_pairs={{0,1},{1,0},{2,3},{3,2},{4,5},{5,4},{6,7},{7,6},{8,9},{9,8},{10,11... | collective-permute-start | bytes 417800 | tf_op jit(solution)/shard_map/ppermute | solution.py:433
  226.0 3.4 %collective-permute-start.21 = (bf16[256,512]{1,0:T(8,128)(2,1)}, bf16[256,512]{1,0:T(8,128)(2,1)S(1)}, u32[]{:S(2)}, u32[]{:S(2)}) collective-permute-start(bf16[256,512]{1,0:T(8,128)(2,1)} %get-tuple-element.70.refs_2_), channel_id=1, source_target_pairs={{0,6},{2,0},{4,2},{6,4},{1,7},{3,1},{5,3},{7,5},{8,14},{10,8},{12,... | collective-permute-start | bytes 786440 | tf_op jit(solution)/shard_map/ppermute | solution.py:441
  234.2 6.7 %all-to-all-start.6 = ((bf16[16,48,256]{2,1,0:T(8,128)(2,1)}), bf16[16,48,256]{2,1,0:T(8,128)(2,1)S(1)}, u32[]{:S(2)}, u32[]{:S(2)}) async-start(bf16[16,48,256]{2,1,0:T(8,128)(2,1)} %weight_grad.3), calls=%async_computation.6 | async-start | bytes 786432 | tf_op jit(solution)/shard_map/all_to_all | solution.py:569
  242.1 3.0 %collective-permute-done.23.refs_5_ = bf16[256,512]{1,0:T(8,128)(2,1)} collective-permute-done((bf16[256,512]{1,0:T(8,128)(2,1)}, bf16[256,512]{1,0:T(8,128)(2,1)}, u32[]{:S(2)}, u32[]{:S(2)}) %collective-permute-start.23) | collective-permute-done | bytes 262176 | tf_op jit(solution)/shard_map/ppermute | solution.py:441
  247.6 3.5 %weight_grad.2 = bf16[16,40,512]{2,1,0:T(8,128)(2,1)} custom-call(s32[2]{0:T(128)S(1)} %copy-done.45, bf16[8,640,256]{2,1,0:T(8,128)(2,1)S(1)} %all-to-all-done.3.refs_1_, bf16[256,512]{1,0:T(8,128)(2,1)} %get-tuple-element.70.refs_2_, bf16[256,512]{1,0:T(8,128)(2,1)S(1)} %collective-permute-done.21.refs_3_, ...), custom_call_target="tpu_custom_call" | custom-call | flops 1000 | bytes 1000 | tf_op jit(solution)/shard_map/weight_grad/pallas_call | solution.py:409
  251.1 6.8 %all-to-all-start.5 = ((bf16[16,40,512]{2,1,0:T(8,128)(2,1)}), bf16[16,40,512]{2,1,0:T(8,128)(2,1)S(1)}, u32[]{:S(2)}, u32[]{:S(2)}) async-start(bf16[16,40,512]{2,1,0:T(8,128)(2,1)} %weight_grad.2), calls=%async_computation.5 | async-start | bytes 1310720 | tf_op jit(solution)/shard_map/all_to_all | solution.py:566
  257.9 2.7 collective-permute-start.16
  260.6 4.3 %collective-permute-start.20 = (bf16[272,256]{1,0:T(8,128)(2,1)S(1)}, bf16[272,256]{1,0:T(8,128)(2,1)S(1)}, u32[]{:S(2)}, u32[]{:S(2)}) collective-permute-start(bf16[272,256]{1,0:T(8,128)(2,1)S(1)} %grad_key_value.1.refs_2_), channel_id=1, source_target_pairs={{0,0},{1,4},{4,1},{5,5},{2,2},{3,6},{6,3},{7,7},{8,8},{9,12},{12,9... | collective-permute-start | bytes 417800 | tf_op jit(solution)/shard_map/ppermute | solution.py:429
  272.5 3.7 %grad_states.1 = bf16[256,5120]{1,0:T(8,128)(2,1)} custom-call(s32[2]{0:T(128)S(1)} %copy-done.46, bf16[272,256]{1,0:T(8,128)(2,1)S(1)} %collective-permute-done.20.gkv_ref, bf16[4,2,640,256]{3,2,1,0:T(8,128)(2,1)S(1)} %copy-done.2, bf16[4,640,256]{2,1,0:T(8,128)(2,1)S(1)} %bitcast.20, bf16[4,640,256]{2,1,0:T(8,128)(2,1)S(1)} %copy-done.8), custom_call_target="tpu_custom_call" | custom-call | flops 1000 | bytes 1000 | tf_op jit(solution)/shard_map/grad_states/pallas_call | solution.py:577
  (198 shorter events, 86.7 us)
Async XLA Ops:
  1.4 27.6 %collective-permute-start = (bf16[40,256]{1,0:T(8,128)(2,1)S(1)}, bf16[40,256]{1,0:T(8,128)(2,1)S(1)}, u32[]{:S(2)}, u32[]{:S(2)}) collective-permute-start(bf16[40,256]{1,0:T(8,128)(2,1)S(1)} %get-tuple-element.81), channel_id=1, source_target_pairs={{0,6},{2,0},{4,2},{6,4},{1,7},{3,1},{5,3},{7,5},{8,14},{10,8},{12,... | collective-permute-start | bytes 61448 | tf_op jit(solution)/shard_map/ppermute | solution.py:441
  4.1 24.9 %collective-permute-start.1 = (bf16[40,256]{1,0:T(8,128)(2,1)S(1)}, bf16[40,256]{1,0:T(8,128)(2,1)S(1)}, u32[]{:S(2)}, u32[]{:S(2)}) collective-permute-start(bf16[40,256]{1,0:T(8,128)(2,1)S(1)} %get-tuple-element.81), channel_id=1, source_target_pairs={{0,4},{2,6},{4,0},{6,2},{1,5},{3,7},{5,1},{7,3},{8,12},{10,14},{12... | collective-permute-start | bytes 61448 | tf_op jit(solution)/shard_map/ppermute | solution.py:441
  4.5 24.6 %collective-permute-start.2 = (bf16[40,256]{1,0:T(8,128)(2,1)S(1)}, bf16[40,256]{1,0:T(8,128)(2,1)S(1)}, u32[]{:S(2)}, u32[]{:S(2)}) collective-permute-start(bf16[40,256]{1,0:T(8,128)(2,1)S(1)} %get-tuple-element.81), channel_id=1, source_target_pairs={{0,2},{2,4},{4,6},{6,0},{1,3},{3,5},{5,7},{7,1},{8,10},{10,12},{12... | collective-permute-start | bytes 61448 | tf_op jit(solution)/shard_map/ppermute | solution.py:441
  7.0 24.8 %all-to-all-start = ((bf16[64,40,256]{2,1,0:T(8,128)(2,1)}), bf16[64,40,256]{2,1,0:T(8,128)(2,1)S(1)}, u32[]{:S(2)}, u32[]{:S(2)}) async-start(bf16[64,40,256]{2,1,0:T(8,128)(2,1)} %broadcast_in_dim.14), calls=%async_computation | async-start | bytes 2621440 | tf_op jit(solution)/shard_map/all_to_all | solution.py:437
  33.2 26.5 %all-to-all-start.1 = ((bf16[16,200,256]{2,1,0:T(8,128)(2,1)}), bf16[16,200,256]{2,1,0:T(8,128)(2,1)S(1)}, u32[]{:S(2)}, u32[]{:S(2)}) async-start(bf16[16,200,256]{2,1,0:T(8,128)(2,1)} %broadcast_in_dim.15), calls=%async_computation.1 | async-start | bytes 3276800 | tf_op jit(solution)/shard_map/all_to_all | solution.py:437
  41.7 5.8 %collective-permute-start.4 = (bf16[4,640,256]{2,1,0:T(8,128)(2,1)S(1)}, bf16[4,640,256]{2,1,0:T(8,128)(2,1)S(1)}, u32[]{:S(2)}, u32[]{:S(2)}) collective-permute-start(bf16[4,640,256]{2,1,0:T(8,128)(2,1)S(1)} %bitcast.18), channel_id=1, source_target_pairs={{0,1},{1,0},{2,3},{3,2},{4,5},{5,4},{6,7},{7,6},{8,9},{9,8},{10,11... | collective-permute-start | bytes 3932168 | tf_op jit(solution)/shard_map/ppermute | solution.py:433
  53.0 8.1 %collective-permute-start.5 = (bf16[256,256]{1,0:T(8,128)(2,1)}, bf16[256,256]{1,0:T(8,128)(2,1)}, u32[]{:S(2)}, u32[]{:S(2)}) collective-permute-start(bf16[256,256]{1,0:T(8,128)(2,1)} %get-tuple-element.51), channel_id=1, source_target_pairs={{0,0},{1,4},{4,1},{5,5},{2,2},{3,6},{6,3},{7,7},{8,8},{9,12},{12,9... | collective-permute-start | bytes 393224 | tf_op jit(solution)/shard_map/ppermute | solution.py:429
  63.6 58.3 %all-to-all-start.2 = ((bf16[16,256,256]{2,1,0:T(8,128)(2,1)}), bf16[16,256,256]{2,1,0:T(8,128)(2,1)}, u32[]{:S(2)}, u32[]{:S(2)}) async-start(bf16[16,256,256]{2,1,0:T(8,128)(2,1)} %broadcast_in_dim.17), calls=%async_computation.2 | async-start | bytes 4194304 | tf_op jit(solution)/shard_map/all_to_all | solution.py:508
  71.6 28.4 %collective-permute-start.3 = (bf16[4,640,256]{2,1,0:T(8,128)(2,1)S(1)}, bf16[4,640,256]{2,1,0:T(8,128)(2,1)S(1)}, u32[]{:S(2)}, u32[]{:S(2)}) collective-permute-start(bf16[4,640,256]{2,1,0:T(8,128)(2,1)S(1)} %get-tuple-element.48.refs_3_.low_ref), channel_id=1, source_target_pairs={{0,1},{1,0},{2,3},{3,2},{4,5},{5,4},{6,7},{7,6},{8,9},{9,8},{10,11... | collective-permute-start | bytes 3932168 | tf_op jit(solution)/shard_map/ppermute | solution.py:433
  75.3 21.7 %collective-permute-start.6 = (bf16[640,256]{1,0:T(8,128)(2,1)S(1)}, bf16[640,256]{1,0:T(8,128)(2,1)S(1)}, u32[]{:S(2)}, u32[]{:S(2)}) collective-permute-start(bf16[640,256]{1,0:T(8,128)(2,1)S(1)} %copy-done.17), channel_id=1, source_target_pairs={{0,6},{2,0},{4,2},{6,4},{1,7},{3,1},{5,3},{7,5},{8,14},{10,8},{12,... | collective-permute-start | bytes 983048 | tf_op jit(solution)/shard_map/ppermute | solution.py:441
  75.9 21.6 %collective-permute-start.7 = (bf16[640,256]{1,0:T(8,128)(2,1)S(1)}, bf16[640,256]{1,0:T(8,128)(2,1)S(1)}, u32[]{:S(2)}, u32[]{:S(2)}) collective-permute-start(bf16[640,256]{1,0:T(8,128)(2,1)S(1)} %copy-done.17), channel_id=1, source_target_pairs={{0,4},{2,6},{4,0},{6,2},{1,5},{3,7},{5,1},{7,3},{8,12},{10,14},{12... | collective-permute-start | bytes 983048 | tf_op jit(solution)/shard_map/ppermute | solution.py:441
  77.0 20.6 %collective-permute-start.8 = (bf16[640,256]{1,0:T(8,128)(2,1)S(1)}, bf16[640,256]{1,0:T(8,128)(2,1)S(1)}, u32[]{:S(2)}, u32[]{:S(2)}) collective-permute-start(bf16[640,256]{1,0:T(8,128)(2,1)S(1)} %copy-done.17), channel_id=1, source_target_pairs={{0,2},{2,4},{4,6},{6,0},{1,3},{3,5},{5,7},{7,1},{8,10},{10,12},{12... | collective-permute-start | bytes 983048 | tf_op jit(solution)/shard_map/ppermute | solution.py:441
  77.0 20.0 %collective-permute-start.13 = (bf16[256,512]{1,0:T(8,128)(2,1)}, bf16[256,512]{1,0:T(8,128)(2,1)S(1)}, u32[]{:S(2)}, u32[]{:S(2)}) collective-permute-start(bf16[256,512]{1,0:T(8,128)(2,1)} %bitcast.29), channel_id=1, source_target_pairs={{0,0},{1,4},{4,1},{5,5},{2,2},{3,6},{6,3},{7,7},{8,8},{9,12},{12,9... | collective-permute-start | bytes 786440 | tf_op jit(solution)/shard_map/ppermute | solution.py:429
  112.0 9.2 %collective-permute-start.14 = (bf16[256,512]{1,0:T(8,128)(2,1)S(1)}, bf16[256,512]{1,0:T(8,128)(2,1)S(1)}, u32[]{:S(2)}, u32[]{:S(2)}) collective-permute-start(bf16[256,512]{1,0:T(8,128)(2,1)S(1)} %get-tuple-element.55), channel_id=1, source_target_pairs={{0,0},{1,4},{4,1},{5,5},{2,2},{3,6},{6,3},{7,7},{8,8},{9,12},{12,9... | collective-permute-start | bytes 786440 | tf_op jit(solution)/shard_map/ppermute | solution.py:429
  121.9 48.2 %all-to-all-start.3 = ((bf16[8,640,256]{2,1,0:T(8,128)(2,1)}), bf16[8,640,256]{2,1,0:T(8,128)(2,1)S(1)}, u32[]{:S(2)}, u32[]{:S(2)}) async-start(bf16[8,640,256]{2,1,0:T(8,128)(2,1)} %copy-done.14), calls=%async_computation.3 | async-start | bytes 5242880 | tf_op jit(solution)/shard_map/all_to_all | solution.py:524
  125.6 4.7 %collective-permute-start.15 = (bf16[16,256,256]{2,1,0:T(8,128)(2,1)}, bf16[16,256,256]{2,1,0:T(8,128)(2,1)S(1)}, u32[]{:S(2)}, u32[]{:S(2)}) collective-permute-start(bf16[16,256,256]{2,1,0:T(8,128)(2,1)} %all-to-all-done.2.kv_ref), channel_id=1, source_target_pairs={{0,1},{1,0},{2,3},{3,2},{4,5},{5,4},{6,7},{7,6},{8,9},{9,8},{10,11... | collective-permute-start | bytes 6291464 | tf_op jit(solution)/shard_map/ppermute | solution.py:433
  125.7 43.6 %collective-permute-start.17 = (bf16[256,640]{1,0:T(8,128)(2,1)}, bf16[256,640]{1,0:T(8,128)(2,1)S(1)}, u32[]{:S(2)}, u32[]{:S(2)}) collective-permute-start(bf16[256,640]{1,0:T(8,128)(2,1)} %copy-done.51), channel_id=1, source_target_pairs={{0,0},{1,4},{4,1},{5,5},{2,2},{3,6},{6,3},{7,7},{8,8},{9,12},{12,9... | collective-permute-start | bytes 983048 | tf_op jit(solution)/shard_map/ppermute | solution.py:429
  178.0 36.2 %all-to-all-start.4 = ((bf16[16,256,256]{2,1,0:T(8,128)(2,1)}), bf16[16,256,256]{2,1,0:T(8,128)(2,1)}, u32[]{:S(2)}, u32[]{:S(2)}) async-start(bf16[16,256,256]{2,1,0:T(8,128)(2,1)} %add_convert_fusion), calls=%async_computation.4 | async-start | bytes 4194304 | tf_op jit(solution)/shard_map/all_to_all | solution.py:532
  188.1 9.4 %collective-permute-start.19 = (bf16[256,512]{1,0:T(8,128)(2,1)}, bf16[256,512]{1,0:T(8,128)(2,1)S(1)}, u32[]{:S(2)}, u32[]{:S(2)}) collective-permute-start(bf16[256,512]{1,0:T(8,128)(2,1)} %get-tuple-element.70.refs_2_), channel_id=1, source_target_pairs={{0,0},{1,4},{4,1},{5,5},{2,2},{3,6},{6,3},{7,7},{8,8},{9,12},{12,9... | collective-permute-start | bytes 786440 | tf_op jit(solution)/shard_map/ppermute | solution.py:429
  217.2 5.0 %collective-permute-start.28 = (bf16[272,256]{1,0:T(8,128)(2,1)S(1)}, bf16[272,256]{1,0:T(8,128)(2,1)S(1)}, u32[]{:S(2)}, u32[]{:S(2)}) collective-permute-start(bf16[272,256]{1,0:T(8,128)(2,1)S(1)} %grad_key_value.1.refs_2_), channel_id=1, source_target_pairs={{0,6},{2,0},{4,2},{6,4},{1,7},{3,1},{5,3},{7,5},{8,14},{10,8},{12,... | collective-permute-start | bytes 417800 | tf_op jit(solution)/shard_map/ppermute | solution.py:441
  217.3 12.1 %collective-permute-start.29 = (bf16[272,256]{1,0:T(8,128)(2,1)S(1)}, bf16[272,256]{1,0:T(8,128)(2,1)S(1)}, u32[]{:S(2)}, u32[]{:S(2)}) collective-permute-start(bf16[272,256]{1,0:T(8,128)(2,1)S(1)} %grad_key_value.1.refs_2_), channel_id=1, source_target_pairs={{0,4},{2,6},{4,0},{6,2},{1,5},{3,7},{5,1},{7,3},{8,12},{10,14},{12... | collective-permute-start | bytes 417800 | tf_op jit(solution)/shard_map/ppermute | solution.py:441
  220.4 9.0 %collective-permute-start.30 = (bf16[272,256]{1,0:T(8,128)(2,1)S(1)}, bf16[272,256]{1,0:T(8,128)(2,1)S(1)}, u32[]{:S(2)}, u32[]{:S(2)}) collective-permute-start(bf16[272,256]{1,0:T(8,128)(2,1)S(1)} %grad_key_value.1.refs_2_), channel_id=1, source_target_pairs={{0,2},{2,4},{4,6},{6,0},{1,3},{3,5},{5,7},{7,1},{8,10},{10,12},{12... | collective-permute-start | bytes 417800 | tf_op jit(solution)/shard_map/ppermute | solution.py:441
  220.4 9.6 %collective-permute-start.31 = (bf16[272,256]{1,0:T(8,128)(2,1)S(1)}, bf16[272,256]{1,0:T(8,128)(2,1)S(1)}, u32[]{:S(2)}, u32[]{:S(2)}) collective-permute-start(bf16[272,256]{1,0:T(8,128)(2,1)S(1)} %grad_key_value.1.refs_2_), channel_id=1, source_target_pairs={{0,1},{1,0},{2,3},{3,2},{4,5},{5,4},{6,7},{7,6},{8,9},{9,8},{10,11... | collective-permute-start | bytes 417800 | tf_op jit(solution)/shard_map/ppermute | solution.py:433
  222.2 8.4 %collective-permute-start.32 = (bf16[272,256]{1,0:T(8,128)(2,1)S(1)}, bf16[272,256]{1,0:T(8,128)(2,1)S(1)}, u32[]{:S(2)}, u32[]{:S(2)}) collective-permute-start(bf16[272,256]{1,0:T(8,128)(2,1)S(1)} %collective-permute-done.28.refs_10_.refs_3_), channel_id=1, source_target_pairs={{0,1},{1,0},{2,3},{3,2},{4,5},{5,4},{6,7},{7,6},{8,9},{9,8},{10,11... | collective-permute-start | bytes 417800 | tf_op jit(solution)/shard_map/ppermute | solution.py:433
  226.0 15.5 %collective-permute-start.21 = (bf16[256,512]{1,0:T(8,128)(2,1)}, bf16[256,512]{1,0:T(8,128)(2,1)S(1)}, u32[]{:S(2)}, u32[]{:S(2)}) collective-permute-start(bf16[256,512]{1,0:T(8,128)(2,1)} %get-tuple-element.70.refs_2_), channel_id=1, source_target_pairs={{0,6},{2,0},{4,2},{6,4},{1,7},{3,1},{5,3},{7,5},{8,14},{10,8},{12,... | collective-permute-start | bytes 786440 | tf_op jit(solution)/shard_map/ppermute | solution.py:441
  229.4 12.5 %collective-permute-start.22 = (bf16[256,512]{1,0:T(8,128)(2,1)}, bf16[256,512]{1,0:T(8,128)(2,1)}, u32[]{:S(2)}, u32[]{:S(2)}) collective-permute-start(bf16[256,512]{1,0:T(8,128)(2,1)} %get-tuple-element.70.refs_2_), channel_id=1, source_target_pairs={{0,4},{2,6},{4,0},{6,2},{1,5},{3,7},{5,1},{7,3},{8,12},{10,14},{12... | collective-permute-start | bytes 786440 | tf_op jit(solution)/shard_map/ppermute | solution.py:441
  229.4 15.7 %collective-permute-start.23 = (bf16[256,512]{1,0:T(8,128)(2,1)}, bf16[256,512]{1,0:T(8,128)(2,1)}, u32[]{:S(2)}, u32[]{:S(2)}) collective-permute-start(bf16[256,512]{1,0:T(8,128)(2,1)} %get-tuple-element.70.refs_2_), channel_id=1, source_target_pairs={{0,2},{2,4},{4,6},{6,0},{1,3},{3,5},{5,7},{7,1},{8,10},{10,12},{12... | collective-permute-start | bytes 786440 | tf_op jit(solution)/shard_map/ppermute | solution.py:441
  234.2 16.9 %all-to-all-start.6 = ((bf16[16,48,256]{2,1,0:T(8,128)(2,1)}), bf16[16,48,256]{2,1,0:T(8,128)(2,1)S(1)}, u32[]{:S(2)}, u32[]{:S(2)}) async-start(bf16[16,48,256]{2,1,0:T(8,128)(2,1)} %weight_grad.3), calls=%async_computation.6 | async-start | bytes 786432 | tf_op jit(solution)/shard_map/all_to_all | solution.py:569
  240.8 4.8 %collective-permute-start.24 = (bf16[256,512]{1,0:T(8,128)(2,1)}, bf16[256,512]{1,0:T(8,128)(2,1)S(1)}, u32[]{:S(2)}, u32[]{:S(2)}) collective-permute-start(bf16[256,512]{1,0:T(8,128)(2,1)} %get-tuple-element.70.refs_2_), channel_id=1, source_target_pairs={{0,1},{1,0},{2,3},{3,2},{4,5},{5,4},{6,7},{7,6},{8,9},{9,8},{10,11... | collective-permute-start | bytes 786440 | tf_op jit(solution)/shard_map/ppermute | solution.py:433
  251.1 25.8 %all-to-all-start.5 = ((bf16[16,40,512]{2,1,0:T(8,128)(2,1)}), bf16[16,40,512]{2,1,0:T(8,128)(2,1)S(1)}, u32[]{:S(2)}, u32[]{:S(2)}) async-start(bf16[16,40,512]{2,1,0:T(8,128)(2,1)} %weight_grad.2), calls=%async_computation.5 | async-start | bytes 1310720 | tf_op jit(solution)/shard_map/all_to_all | solution.py:566
  257.9 9.7 %collective-permute-start.16 = (bf16[256,512]{1,0:T(8,128)(2,1)}, bf16[256,512]{1,0:T(8,128)(2,1)S(1)}, u32[]{:S(2)}, u32[]{:S(2)}) collective-permute-start(bf16[256,512]{1,0:T(8,128)(2,1)} %copy-done.52), channel_id=1, source_target_pairs={{0,0},{1,4},{4,1},{5,5},{2,2},{3,6},{6,3},{7,7},{8,8},{9,12},{12,9... | collective-permute-start | bytes 786440 | tf_op jit(solution)/shard_map/ppermute | solution.py:429
  260.6 8.1 %collective-permute-start.20 = (bf16[272,256]{1,0:T(8,128)(2,1)S(1)}, bf16[272,256]{1,0:T(8,128)(2,1)S(1)}, u32[]{:S(2)}, u32[]{:S(2)}) collective-permute-start(bf16[272,256]{1,0:T(8,128)(2,1)S(1)} %grad_key_value.1.refs_2_), channel_id=1, source_target_pairs={{0,0},{1,4},{4,1},{5,5},{2,2},{3,6},{6,3},{7,7},{8,8},{9,12},{12,9... | collective-permute-start | bytes 417800 | tf_op jit(solution)/shard_map/ppermute | solution.py:429
  (65 other events, 458.6 us)

commit v7 on v2

--- a/solution.py
+++ b/solution.py
@@ -17,6 +17,7 @@
 mib = 2**20
 smem = pl.BlockSpec(memory_space=pltpu.SMEM)
 vmem = pl.BlockSpec(memory_space=pltpu.VMEM)
+anywhere = pl.BlockSpec(memory_space=pl.ANY)
 
 
 def mm(a, b):
@@ -50,9 +51,10 @@
     return inverse * (grad_unit - unit * shrink), grad_normed * unit
 
 
-def prepare_kernel(where, src_ref, toks_ref, toks_theirs_ref, turned_ref):
+def prepare_kernel(where, src_ref, toks_ref, toks_theirs_ref, turned_ref, done_ref):
     planes, columns = src_ref.shape[:2]
     core = where[1]
+    done_ref[...] = jnp.zeros_like(done_ref)
 
     def piece(plane, y, side):
         return src_ref[plane, y, side].astype(f32)
@@ -79,18 +81,14 @@
     kv_ref[:, span:] = raw[:, span:].astype(bf16)
 
 
-def query_part_kernel(mine_ref, other_ref, w_ref, part_ref, part_other_ref):
-    part_ref[...] = mm(mine_ref[...], w_ref[...])
-    part_other_ref[...] = mm(other_ref[...], w_ref[...])
-
-
-def query_kernel(part_ref, part_theirs_ref, gain_ref, cos_ref, sin_ref, q_ref, raw_ref):
+def query_kernel(mine_ref, other_ref, w_ref, w_other_ref, raw_k_ref, gain_ref, cos_ref, sin_ref, q_ref, raw_ref):
+    rows = mm(mine_ref[...], w_ref[...]) + mm(other_ref[...], w_other_ref[...])
+    raw_ref[:, -span:] = raw_k_ref[...].astype(bf16)
     gain = gain_ref[...] * (span**-0.5 / math.log(2.0))
-    for h in range(raw_ref.shape[1] // span):
+    for h in range(q_ref.shape[1] // span):
         part = slice(h * span, (h + 1) * span)
-        raw = part_ref[:, part] + part_theirs_ref[:, part]
-        raw_ref[:, part] = raw.astype(bf16)
-        q_ref[:, part] = shape_head(raw, gain, cos_ref[...], sin_ref[...]).astype(bf16)
+        raw_ref[:, part] = rows[:, part].astype(bf16)
+        q_ref[:, part] = shape_head(rows[:, part], gain, cos_ref[...], sin_ref[...]).astype(bf16)
 
 
 def attention_kernel(
@@ -256,9 +254,9 @@
             pltpu.VMEM((1, rows), f32),
             pltpu.VMEM((span, rows), f32),
         ],
-        compiler_params=pltpu.CompilerParams(vmem_limit_bytes=48 * mib),
+        compiler_params=pltpu.CompilerParams(vmem_limit_bytes=28 * mib),
         cost_estimate=pl.CostEstimate(
-            flops=3 * 10**10, bytes_accessed=10 * 10**6, transcendentals=9 * 10**6
+            flops=1000, bytes_accessed=1000, transcendentals=0
         ),
         name="attention",
     )(order, own, q16, g16, kv, kv_other)
@@ -281,7 +279,7 @@
     rows = raw_ref.shape[0]
     dkv = jnp.sum(dkv_ref[...].astype(f32), axis=0)
     grad, terms = shape_head_grad(
-        raw_ref[...].astype(f32), gain_ref[...], cos_ref[...], sin_ref[...], dkv[:, :span]
+        raw_ref[:, -span:].astype(f32), gain_ref[...], cos_ref[...], sin_ref[...], dkv[:, :span]
     )
     g_ref[:rows, :span] = grad.astype(bf16)
     g_ref[:rows, span:] = dkv[:, span:].astype(bf16)
@@ -296,41 +294,26 @@
 
 def weight_grad_kernel(where, turned_ref, *rest):
     blocks, out_ref = rest[:-1], rest[-1]
-    columns = len(blocks) // 2
+    count = len(blocks) // 2
+    columns = count // 2
     toks = turned_ref.shape[2]
     y, core = where[0], where[1]
-    total, gains = None, None
-    for side in range(2):
-        for k in range(columns):
-            from_y = lax.rem(y + k, columns)
-            from_core = core if side == 0 else 1 - core
-            at = (from_core * 2 + lax.rem(from_y, 2)) * 2 + from_y // 2
-            block = blocks[side * columns + k]
-            part = mm(turned_ref[at], block[:toks])
-            total = part if total is None else total + part
-            if block.shape[0] > toks:
-                row = block[toks:].astype(f32)
-                gains = row if gains is None else gains + row
+    query, rows, gains = 0.0, 0.0, 0.0
+    for i in range(count):
+        from_y = lax.rem(y + i % columns, columns)
+        from_core = core if i < columns else 1 - core
+        at = (from_core * 2 + lax.rem(from_y, 2)) * 2 + from_y // 2
+        query = query + mm(turned_ref[at], blocks[i][...])
+        rows = rows + mm(turned_ref[at], blocks[count + i][:toks])
+        gains = gains + blocks[count + i][toks:].astype(f32)
+    gain = gains[:8, :span] + gains[:8, span:]
+    high = gain.astype(bf16).astype(f32)
+    extra = jnp.concatenate([jnp.zeros((8, query.shape[1]), f32), high, gain - high], axis=1)
+    total = jnp.concatenate([query, rows], axis=1)
     own_rows = total.shape[0] // out_ref.shape[0]
-    extra = []
-    if gains is not None:
-        gain = gains[:, :span] + gains[:, span:]
-        high = gain.astype(bf16).astype(f32)
-        extra = [jnp.concatenate([high, gain - high], axis=1)[:8]]
     for i in range(out_ref.shape[0]):
         part = total[i * own_rows : (i + 1) * own_rows]
-        out_ref[i] = jnp.concatenate([part] + extra, axis=0).astype(bf16)
-
-
-def weight_grad(where, turned, blocks, planes, padded):
-    return pl.pallas_call(
-        weight_grad_kernel,
-        out_shape=jax.ShapeDtypeStruct((planes, padded, blocks[0].shape[1]), bf16),
-        in_specs=[smem] + [vmem] * (1 + len(blocks)),
-        out_specs=vmem,
-        compiler_params=pltpu.CompilerParams(vmem_limit_bytes=48 * mib),
-        name="weight_grad",
-    )(where, turned, *blocks)
+        out_ref[i] = jnp.concatenate([part, extra], axis=0).astype(bf16)
 
 
 def grad_states_kernel(where, gq_ref, gkv_ref, q_ref, q_theirs_ref, kv_ref, kv_theirs_ref, out_ref):
@@ -342,7 +325,7 @@
         part = slice(i * group, (i + 1) * group)
         return lax.dot_general(
             q[part], gq_ref[...], transposed, preferred_element_type=f32
-        ) + lax.dot_general(kv[part], gkv_ref[...], transposed, preferred_element_type=f32)
+        ) + lax.dot_general(kv[part], gkv_ref[: gq_ref.shape[0]], transposed, preferred_element_type=f32)
 
     for i in range(q_ref.shape[0] // group):
         mine, theirs = product(q_ref, kv_ref, i), product(q_theirs_ref, kv_theirs_ref, i)
@@ -353,26 +336,36 @@
         out_ref[:, 2 * i * group : 2 * (i + 1) * group] = rows.astype(bf16).T
 
 
-def finish_kernel(parts_ref, key_ref, value_ref, gain_q_ref, gain_k_ref):
+def finish_kernel(parts_ref, query_ref, key_ref, value_ref, gain_q_ref, gain_k_ref):
     sums = jnp.sum(parts_ref[...].astype(f32), axis=0)
-    rows = key_ref.shape[0]
-    key_ref[...] = sums[:rows, :span]
-    value_ref[...] = sums[:rows, span:]
-    gains = sums[rows:, :span] + sums[rows:, span:]
+    rows, cols = query_ref.shape
+    query_ref[...] = sums[:rows, :cols]
+    key_ref[...] = sums[:rows, cols : cols + span]
+    value_ref[...] = sums[:rows, cols + span :]
+    gains = sums[rows:, cols : cols + span] + sums[rows:, cols + span :]
     gain_q_ref[...] = gains[0:1]
     gain_k_ref[...] = gains[1:2]
 
 
-def call(kernel, shapes, *args, name, cost=None):
+cheap = pl.CostEstimate(flops=1000, bytes_accessed=1000, transcendentals=0)
+
+
+def call(kernel, shapes, *args, name, after=(), limit=16, scratch=()):
+    count = len(args)
+
+    def run(*refs):
+        kernel(*refs[:count], *refs[count + len(after) :])
+
     return pl.pallas_call(
-        kernel,
+        run,
         out_shape=shapes,
-        in_specs=[smem if a.dtype == jnp.int32 else vmem for a in args],
+        in_specs=[smem if a.dtype == jnp.int32 else vmem for a in args] + [anywhere] * len(after),
         out_specs=jax.tree.map(lambda _: vmem, shapes),
-        compiler_params=pltpu.CompilerParams(vmem_limit_bytes=48 * mib),
-        cost_estimate=cost,
+        scratch_shapes=scratch,
+        compiler_params=pltpu.CompilerParams(vmem_limit_bytes=limit * mib),
+        cost_estimate=cheap,
         name=name,
-    )(*args)
+    )(*args, *after)
 
 
 plane = ("x", "z")
@@ -428,100 +421,85 @@
     gain_q, gain_k = gain_query[None, :], gain_key[None, :]
     shape = jax.ShapeDtypeStruct
 
-    q_mine = lax.all_gather(w_query, chips, axis=0, tiled=True)
     kv_mine = to_all(jnp.concatenate([w_key, w_value], axis=1), chips, planes * columns)
+    toks_mine, toks_theirs, turned, done = call(
+        prepare_kernel,
+        (shape((tok_rows, half), bf16),) * 2
+        + (shape((2 * columns, width // 8, tok_rows), bf16), shape((8, span), f32)),
+        where, tokens.T.reshape(planes, columns, 2, own_rows, tok_rows),
+        name="prepare",
+        after=(cosine, sine, cos_there, sin_there),
+    )
+    kv_mine, w_query, done, own = lax.optimization_barrier((kv_mine, w_query, done, own))
     kv_mine = kv_mine.reshape(half, kv_cols)
-
-    toks_mine, toks_theirs, turned = pl.pallas_call(
-        prepare_kernel,
-        out_shape=(shape((tok_rows, half), bf16),) * 2 + (shape((2 * columns, width // 8, tok_rows), bf16),),
-        in_specs=[smem, vmem],
-        out_specs=(vmem,) * 3,
-        compiler_params=pltpu.CompilerParams(vmem_limit_bytes=48 * mib),
-        name="prepare",
-    )(where, tokens.T.reshape(planes, columns, 2, own_rows, tok_rows))
-
-    toks_other = flip(toks_theirs)
-    kv_mine, toks_mine, toks_theirs, turned, cosine, sine, cos_there, sin_there, own = (
-        lax.optimization_barrier(
-            (kv_mine, toks_mine, toks_theirs, turned, cosine, sine, cos_there, sin_there, own)
-        )
-    )
     kv_theirs = flip(kv_mine)
+    q_mine = to_all(w_query, chips, planes * columns).reshape(half, q_cols)
 
     kv16, raw_k = call(
         key_value_kernel,
         (shape((tok_rows, kv_cols), bf16), shape((tok_rows, span), f32)),
         toks_mine, toks_theirs, kv_mine, kv_theirs, gain_k, cosine, sine,
         name="key_value",
-    )
-    kv_send = jnp.broadcast_to(swap(kv16)[None], (planes, tok_rows, kv_cols))
-    q_mine, _ = lax.optimization_barrier((q_mine, kv_send))
-    kv_own = lax.all_to_all(kv_send, plane, 0, 0)
-    cheap = pl.CostEstimate(flops=1000, bytes_accessed=1000, transcendentals=0)
-    q_part, q_part_other = call(
-        query_part_kernel,
-        (shape((tok_rows, q_cols), f32),) * 2,
-        toks_mine, toks_other, q_mine,
-        name="query_part",
-        cost=cheap,
-    )
-    kv_own, q_part, q_part_other, grad_out = lax.optimization_barrier(
-        (kv_own, q_part, q_part_other, swap(cotangent[0]))
-    )
-    q16, raw_q = call(
+        after=(done,),
+    )
+    kv16, q_mine = lax.optimization_barrier((swap(kv16), q_mine))
+    kv_own = to_all(kv16, plane, planes)
+    q_theirs = flip(q_mine)
+    grad_out = swap(cotangent[0])
+    q16, raw = call(
         query_kernel,
-        (shape((tok_rows, q_cols), bf16),) * 2,
-        q_part, flip(q_part_other), gain_q, cosine, sine,
+        (shape((tok_rows, q_cols), bf16), shape((tok_rows, q_cols + span), bf16)),
+        toks_mine, toks_theirs, q_mine, q_theirs, raw_k, gain_q, cosine, sine,
         name="query",
-        cost=cheap,
-    )
+        after=(grad_out,),
+    )
+    q16, raw_there = swap(q16), swap(raw)
+    kv_own, q16 = lax.optimization_barrier((kv_own, q16))
     kv_other = flip(kv_own)
-    q16 = swap(q16)
-    turned, raw_q, _ = lax.optimization_barrier((turned, raw_q, q16))
     turned = lax.all_to_all(turned, column + ("core",), 0, 0)
-    raw_there = swap(jnp.concatenate([raw_q, raw_k.astype(bf16)], axis=1))
-
-    ctx, dq, dkv_mine, dkv_theirs = attention(
-        block_order, own, q16, grad_out, kv_own, kv_other
-    )
-    q_theirs = flip(q_mine)
-    dkv_theirs, dq, turned, raw_there, q_theirs = lax.optimization_barrier(
-        (dkv_theirs, dq, turned, raw_there, q_theirs)
-    )
+
+    ctx, dq, dkv_mine, dkv_theirs = attention(block_order, own, q16, grad_out, kv_own, kv_other)
+    dkv_theirs, turned = lax.optimization_barrier((dkv_theirs, turned))
     dkv = (dkv_mine.astype(f32) + flip(dkv_theirs).astype(f32)).astype(bf16)
     dkv = lax.all_to_all(dkv, plane, 0, 0)
 
     g_q, gains_q = call(
         grad_query_kernel,
         (shape((tok_rows, q_cols), bf16), shape((8, span), f32)),
-        raw_there[:, :q_cols], dq, gain_q, cos_there, sin_there,
+        raw_there, dq, gain_q, cos_there, sin_there,
         name="grad_query",
     )
-    parts = weight_grad(where, turned, around(g_q), planes, own_rows)
-    parts = lax.all_to_all(parts, plane, 0, 0)
-    own_query = jnp.sum(parts.astype(f32), axis=0)
-
+    blocks = around(g_q)
+    g_q_back = swap(g_q)
     g_kv = call(
         grad_key_value_kernel,
         shape((tok_rows + 16, kv_cols), bf16),
-        raw_there[:, q_cols:], dkv, gain_k, cos_there, sin_there, gains_q,
+        raw_there, dkv, gain_k, cos_there, sin_there, gains_q,
         name="grad_key_value",
-    )
-    blocks, g_q_back = lax.optimization_barrier((around(g_kv), swap(g_q)))
-    parts = weight_grad(where, turned, blocks, planes, own_rows + 8)
+        after=tuple(blocks),
+    )
+    blocks_kv = around(g_kv)
+    g_kv_back = swap(g_kv)
+    parts = call(
+        weight_grad_kernel,
+        shape((planes, own_rows + 8, q_cols + kv_cols), bf16),
+        where, turned, *blocks, *blocks_kv,
+        name="weight_grad",
+        after=(g_q_back, g_kv_back),
+    )
     parts = lax.all_to_all(parts, plane, 0, 0)
-    own_key, own_value, gain_sum_q, gain_sum_k = call(
+    own_query, own_key, own_value, gain_sum_q, gain_sum_k = call(
         finish_kernel,
-        (shape((own_rows, span), f32),) * 2 + (shape((1, span), f32),) * 2,
+        (shape((own_rows, q_cols), f32),)
+        + (shape((own_rows, span), f32),) * 2
+        + (shape((1, span), f32),) * 2,
         parts,
         name="finish",
     )
-
     grad_states = call(
         grad_states_kernel,
         shape((tok_rows, width), bf16),
-        where, g_q_back, swap(g_kv[:tok_rows]), q_mine, q_theirs, kv_mine, kv_theirs,
+        where, g_q_back, g_kv_back, q_mine, q_theirs, kv_mine, kv_theirs,
         name="grad_states",
     )
     return (

time: 274 us -> 271 us (0.989)
  local copies, waits for them, and re-layouts: 25.6 us -> 44.8 us
  between operations: 14.4 us -> 1.02 us
    ppermute x7, waiting for transfers between devices: 13.1 us -> 45.4 us  [swap(): return lax.ppermute(array, ('y_hi', 'core'), swapped)]
    all_gather x1 -> x0, waiting for transfers between devices: 30.5 us -> none  [local(): q_mine = lax.all_gather(w_query, chips, axis=0, tiled=True)]
    unnamed x53 -> x89, local copies, waits for them, and re-layouts: 18.5 us -> 34.3 us
    all_to_all x1 -> x3, starting transfers between devices: 10.7 us -> 24.8 us  [to_all(): lax.all_to_all(jnp.broadcast_to(array[None], (count,) + array.shape), axe...]
    all_to_all x1 -> x0, starting transfers between devices: 7.74 us -> none  [local(): kv_own = lax.all_to_all(kv_send, plane, 0, 0)]
    all_to_all x2 -> x1, starting transfers between devices: 14.9 us -> 7.14 us  [local(): parts = lax.all_to_all(parts, plane, 0, 0)]
    all_to_all x1 -> x3, waiting for transfers between devices: 6.88 us -> 12.2 us  [to_all(): lax.all_to_all(jnp.broadcast_to(array[None], (count,) + array.shape), axe...]
    broadcast_in_dim x1 -> x3, local copies, waits for them, and re-layouts: 1.16 us -> 6.03 us  [to_all(): jnp.broadcast_to(array[None], (count,) + array.shape)]
  transfers between devices with their start and end apart: 34 -> 31, of which waited for: 14 -> 13; matrix products, arithmetic and copies ran while one was open for 5% -> 3% of each run, Pallas kernels for 20% -> 18%
where the time goes in v7:
time: 271 us; the launch traced here: 267 us
  starting transfers between devices  85.8 us (32%)
  waiting for transfers between devices  76.2 us (28%)
  Pallas kernels  53.2 us (20%)
  local copies, waits for them, and re-layouts  44.8 us (17%)
  other arithmetic  6.48 us (2%)
    ppermute x7, waiting for transfers between devices, swap(): return lax.ppermute(array, ('y_hi', 'core'), swapped)  45.4 us
    unnamed x89, local copies, waits for them, and re-layouts  34.3 us
    pallas_call x1, Pallas kernels, attention(): pl.pallas_call(attention_kernel, out_shape=(jax.ShapeDtypeStruct((rows_he...  32.1 us
    all_to_all x3, starting transfers between devices, to_all(): lax.all_to_all(jnp.broadcast_to(array[None], (count,) + array.shape), axe...  24.8 us
    ppermute x7, starting transfers between devices, swap(): return lax.ppermute(array, ('y_hi', 'core'), swapped)  23.6 us
    pallas_call x8, Pallas kernels, call(): pl.pallas_call(run, out_shape=shapes, in_specs=[smem if a.dtype == jnp.in...  21.1 us
    all_to_all x3, waiting for transfers between devices, to_all(): lax.all_to_all(jnp.broadcast_to(array[None], (count,) + array.shape), axe...  12.2 us
    ppermute x12, waiting for transfers between devices, flip(): return lax.ppermute(array, 'core', flipped)  11.2 us
  transfers between devices with their start and end apart: 31, of which 13 were waited for; matrix products, arithmetic and copies ran while one was open for 3% of the time, Pallas kernels for 18%

profile of v7, /device:TPU:39, one launch (start us, length us, event | category | flops | bytes accessed | tf_op | source)
XLA Modules:
  0.0 267.5 jit_solution(10275569614749571996)
XLA Ops:
  2.5 10.7 %all-to-all-start = ((bf16[64,40,256]{2,1,0:T(8,128)(2,1)}), bf16[64,40,256]{2,1,0:T(8,128)(2,1)S(1)}, u32[]{:S(2)}, u32[]{:S(2)}) async-start(bf16[64,40,256]{2,1,0:T(8,128)(2,1)} %broadcast_in_dim.14), calls=%async_computation | async-start | bytes 2621440 | tf_op jit(solution)/shard_map/all_to_all | solution.py:387
  13.2 4.4 %copy.15 = bf16[5120,256]{1,0:T(8,128)(2,1)} copy(bf16[5120,256]{0,1:T(8,128)(2,1)} %bitcast.30) | data formatting | bytes 5242880 | tf_op jit(solution)/shard_map/transpose | solution.py:429
  26.6 4.2 %all-to-all-done = bf16[64,40,256]{2,1,0:T(8,128)(2,1)S(1)} async-done(((bf16[64,40,256]{2,1,0:T(8,128)(2,1)}), bf16[64,40,256]{2,1,0:T(8,128)(2,1)S(1)}, u32[]{:S(2)}, u32[]{:S(2)}) %all-to-all-start) | async-done | bytes 1310752 | tf_op jit(solution)/shard_map/all_to_all | solution.py:387
  30.8 2.5 broadcast_in_dim.16
  33.3 7.8 %all-to-all-start.1 = ((bf16[64,40,512]{2,1,0:T(8,128)(2,1)}), bf16[64,40,512]{2,1,0:T(8,128)(2,1)S(1)}, u32[]{:S(2)}, u32[]{:S(2)}) async-start(bf16[64,40,512]{2,1,0:T(8,128)(2,1)} %broadcast_in_dim.16), calls=%async_computation.1 | async-start | bytes 5242880 | tf_op jit(solution)/shard_map/all_to_all | solution.py:387
  43.3 2.9 %collective-permute-done.refs_3_.refs_6_ = bf16[2560,256]{1,0:T(8,128)(2,1)S(1)} collective-permute-done((bf16[2560,256]{1,0:T(8,128)(2,1)}, bf16[2560,256]{1,0:T(8,128)(2,1)S(1)}, u32[]{:S(2)}, u32[]{:S(2)}) %collective-permute-start) | collective-permute-done | bytes 1310752 | tf_op jit(solution)/shard_map/ppermute | solution.py:383
  51.6 4.9 %collective-permute-start.1 = (bf16[256,256]{1,0:T(8,128)(2,1)S(1)}, bf16[256,256]{1,0:T(8,128)(2,1)}, u32[]{:S(2)}, u32[]{:S(2)}) collective-permute-start(bf16[256,256]{1,0:T(8,128)(2,1)S(1)} %get-tuple-element.42), channel_id=1, source_target_pairs={{0,0},{1,4},{4,1},{5,5},{2,2},{3,6},{6,3},{7,7},{8,8},{9,12},{12,9... | collective-permute-start | bytes 393224 | tf_op jit(solution)/shard_map/ppermute | solution.py:379
  56.5 21.1 %collective-permute-done.1 = bf16[256,256]{1,0:T(8,128)(2,1)} collective-permute-done((bf16[256,256]{1,0:T(8,128)(2,1)S(1)}, bf16[256,256]{1,0:T(8,128)(2,1)}, u32[]{:S(2)}, u32[]{:S(2)}) %collective-permute-start.1) | collective-permute-done | bytes 131104 | tf_op jit(solution)/shard_map/ppermute | solution.py:379
  77.5 2.4 broadcast_in_dim.17
  80.0 6.3 %all-to-all-start.2 = ((bf16[16,256,256]{2,1,0:T(8,128)(2,1)}), bf16[16,256,256]{2,1,0:T(8,128)(2,1)}, u32[]{:S(2)}, u32[]{:S(2)}) async-start(bf16[16,256,256]{2,1,0:T(8,128)(2,1)} %broadcast_in_dim.17), calls=%async_computation.2 | async-start | bytes 4194304 | tf_op jit(solution)/shard_map/all_to_all | solution.py:387
  88.2 7.9 %collective-permute-done.3.refs_8_.g_ref = bf16[256,512]{1,0:T(8,128)(2,1)S(1)} collective-permute-done((bf16[256,512]{1,0:T(8,128)(2,1)}, bf16[256,512]{1,0:T(8,128)(2,1)S(1)}, u32[]{:S(2)}, u32[]{:S(2)}) %collective-permute-start.3) | collective-permute-done | bytes 262176 | tf_op jit(solution)/shard_map/ppermute | solution.py:379
  98.7 4.3 %query.1 = (bf16[256,512]{1,0:T(8,128)(2,1)}, bf16[256,640]{1,0:T(8,128)(2,1)S(1)}) custom-call(bf16[256,2560]{1,0:T(8,128)(2,1)S(1)} %copy-done.8, bf16[256,2560]{1,0:T(8,128)(2,1)S(1)} %copy-done.11, bf16[2560,512]{1,0:T(8,128)(2,1)S(1)} %bitcast.20, bf16[2560,512]{1,0:T(8,128)(2,1)} %collective-permute-done.2.refs_3_.refs_4_, ...), custom_call_target="tpu_custom_call" | custom-call | flops 1000 | bytes 1000 | tf_op jit(solution)/shard_map/query/pallas_call | solution.py:359
  105.6 8.1 %all-to-all-done.2.kv_ref = bf16[16,256,256]{2,1,0:T(8,128)(2,1)} async-done(((bf16[16,256,256]{2,1,0:T(8,128)(2,1)}), bf16[16,256,256]{2,1,0:T(8,128)(2,1)}, u32[]{:S(2)}, u32[]{:S(2)}) %all-to-all-start.2) | async-done | bytes 2097184 | tf_op jit(solution)/shard_map/all_to_all | solution.py:387
  113.7 5.9 %all-to-all-start.3 = ((bf16[8,640,256]{2,1,0:T(8,128)(2,1)}), bf16[8,640,256]{2,1,0:T(8,128)(2,1)}, u32[]{:S(2)}, u32[]{:S(2)}) async-start(bf16[8,640,256]{2,1,0:T(8,128)(2,1)} %copy-done.13), calls=%async_computation.3 | async-start | bytes 5242880 | tf_op jit(solution)/shard_map/all_to_all | solution.py:459
  119.8 4.2 %collective-permute-done.5.kv_other_ref = bf16[16,256,256]{2,1,0:T(8,128)(2,1)S(1)} collective-permute-done((bf16[16,256,256]{2,1,0:T(8,128)(2,1)}, bf16[16,256,256]{2,1,0:T(8,128)(2,1)S(1)}, u32[]{:S(2)}, u32[]{:S(2)}) %collective-permute-start.5) | collective-permute-done | bytes 2097184 | tf_op jit(solution)/shard_map/ppermute | solution.py:383
  124.0 32.1 %attention.1 = (bf16[256,512]{1,0:T(8,128)(2,1)S(1)}, f32[256,512]{1,0:T(8,128)S(1)}, bf16[16,256,256]{2,1,0:T(8,128)(2,1)S(1)}, bf16[16,256,256]{2,1,0:T(8,128)(2,1)S(1)}) custom-call(s32[64]{0:T(128)S(1)} %copy-done.36, s32[3]{0:T(128)S(1)} %copy-done.39, bf16[256,512]{1,0:T(8,128)(2,1)S(1)} %collective-permute-done.4.q_ref, ...), custom_call_target="tpu_custom_call" | custom-call | flops 1000 | bytes 1000 | tf_op jit(solution)/shard_map/attention/pallas_call | solution.py:230
  160.6 4.0 %collective-permute-done.9 = bf16[16,256,256]{2,1,0:T(8,128)(2,1)S(1)} collective-permute-done((bf16[16,256,256]{2,1,0:T(8,128)(2,1)}, bf16[16,256,256]{2,1,0:T(8,128)(2,1)S(1)}, u32[]{:S(2)}, u32[]{:S(2)}) %collective-permute-start.9) | collective-permute-done | bytes 2097184 | tf_op jit(solution)/shard_map/ppermute | solution.py:383
  164.7 3.5 %add_convert_fusion = bf16[16,256,256]{2,1,0:T(8,128)(2,1)} fusion(bf16[16,256,256]{2,1,0:T(8,128)(2,1)S(1)} %collective-permute-done.9, bf16[16,256,256]{2,1,0:T(8,128)(2,1)} %copy-done.14), kind=kLoop, calls=%fused_computation | loop fusion | flops 4194304 | bytes 6291456 | tf_op jit(solution)/shard_map/convert_element_type | solution.py:463
  168.2 7.2 %all-to-all-start.4 = ((bf16[16,256,256]{2,1,0:T(8,128)(2,1)}), bf16[16,256,256]{2,1,0:T(8,128)(2,1)}, u32[]{:S(2)}, u32[]{:S(2)}) async-start(bf16[16,256,256]{2,1,0:T(8,128)(2,1)} %add_convert_fusion), calls=%async_computation.4 | async-start | bytes 4194304 | tf_op jit(solution)/shard_map/all_to_all | solution.py:464
  175.4 5.6 %collective-permute-start.7 = (bf16[256,640]{1,0:T(8,128)(2,1)}, bf16[256,640]{1,0:T(8,128)(2,1)S(1)}, u32[]{:S(2)}, u32[]{:S(2)}) collective-permute-start(bf16[256,640]{1,0:T(8,128)(2,1)} %copy-done.41), channel_id=1, source_target_pairs={{0,0},{1,4},{4,1},{5,5},{2,2},{3,6},{6,3},{7,7},{8,8},{9,12},{12,9... | collective-permute-start | bytes 983048 | tf_op jit(solution)/shard_map/ppermute | solution.py:379
  181.0 7.1 %collective-permute-done.7.refs_0_ = bf16[256,640]{1,0:T(8,128)(2,1)S(1)} collective-permute-done((bf16[256,640]{1,0:T(8,128)(2,1)}, bf16[256,640]{1,0:T(8,128)(2,1)S(1)}, u32[]{:S(2)}, u32[]{:S(2)}) %collective-permute-start.7) | collective-permute-done | bytes 327712 | tf_op jit(solution)/shard_map/ppermute | solution.py:379
  190.1 2.6 collective-permute-start.10
  192.6 4.2 %collective-permute-start.13 = (bf16[256,512]{1,0:T(8,128)(2,1)S(1)}, bf16[256,512]{1,0:T(8,128)(2,1)S(1)}, u32[]{:S(2)}, u32[]{:S(2)}) collective-permute-start(bf16[256,512]{1,0:T(8,128)(2,1)S(1)} %get-tuple-element.53.refs_6_.refs_2_), channel_id=1, source_target_pairs={{0,1},{1,0},{2,3},{3,2},{4,5},{5,4},{6,7},{7,6},{8,9},{9,8},{10,11... | collective-permute-start | bytes 786440 | tf_op jit(solution)/shard_map/ppermute | solution.py:383
  196.8 6.4 %collective-permute-done.12.refs_9_.refs_5_ = bf16[256,512]{1,0:T(8,128)(2,1)S(1)} collective-permute-done((bf16[256,512]{1,0:T(8,128)(2,1)S(1)}, bf16[256,512]{1,0:T(8,128)(2,1)S(1)}, u32[]{:S(2)}, u32[]{:S(2)}) %collective-permute-start.12) | collective-permute-done | bytes 262176 | tf_op jit(solution)/shard_map/ppermute | solution.py:391
  206.9 3.4 %collective-permute-start.8 = (bf16[256,512]{1,0:T(8,128)(2,1)S(1)}, bf16[256,512]{1,0:T(8,128)(2,1)}, u32[]{:S(2)}, u32[]{:S(2)}) collective-permute-start(bf16[256,512]{1,0:T(8,128)(2,1)S(1)} %get-tuple-element.53.refs_6_.refs_2_), channel_id=1, source_target_pairs={{0,0},{1,4},{4,1},{5,5},{2,2},{3,6},{6,3},{7,7},{8,8},{9,12},{12,9... | collective-permute-start | bytes 786440 | tf_op jit(solution)/shard_map/ppermute | solution.py:379
  226.8 2.5 collective-permute-start.17
  231.6 3.0 %collective-permute-done.17.refs_2_.refs_19_ = bf16[272,256]{1,0:T(8,128)(2,1)S(1)} collective-permute-done((bf16[272,256]{1,0:T(8,128)(2,1)S(1)}, bf16[272,256]{1,0:T(8,128)(2,1)S(1)}, u32[]{:S(2)}, u32[]{:S(2)}) %collective-permute-start.17) | collective-permute-done | bytes 139296 | tf_op jit(solution)/shard_map/ppermute | solution.py:379
  234.7 4.0 %weight_grad.1 = bf16[16,48,768]{2,1,0:T(8,128)(2,1)S(1)} custom-call(s32[2]{0:T(128)S(1)} %pad_add_fusion.refs_0_, bf16[8,640,256]{2,1,0:T(8,128)(2,1)} %all-to-all-done.3.refs_1_, bf16[256,512]{1,0:T(8,128)(2,1)S(1)} %get-tuple-element.53.refs_6_.refs_2_, bf16[256,512]{1,0:T(8,128)(2,1)S(1)} %copy-done.23, bf16[256,512]{1,0:T(8,128)(2,1)S(1)} %copy-done.20, ...), custom_call_target="tpu_custom_call" | custom-call | flops 1000 | bytes 1000 | tf_op jit(solution)/shard_map/weight_grad/pallas_call | solution.py:359
  239.7 7.1 %all-to-all-start.5 = ((bf16[16,48,768]{2,1,0:T(8,128)(2,1)}), bf16[16,48,768]{2,1,0:T(8,128)(2,1)}, u32[]{:S(2)}, u32[]{:S(2)}) async-start(bf16[16,48,768]{2,1,0:T(8,128)(2,1)} %copy-done.12), calls=%async_computation.5 | async-start | bytes 2359296 | tf_op jit(solution)/shard_map/all_to_all | solution.py:490
  246.9 3.4 %collective-permute-start.6 = (bf16[256,512]{1,0:T(8,128)(2,1)S(1)}, bf16[256,512]{1,0:T(8,128)(2,1)S(1)}, u32[]{:S(2)}, u32[]{:S(2)}) collective-permute-start(bf16[256,512]{1,0:T(8,128)(2,1)S(1)} %copy-done.43), channel_id=1, source_target_pairs={{0,0},{1,4},{4,1},{5,5},{2,2},{3,6},{6,3},{7,7},{8,8},{9,12},{12,9... | collective-permute-start | bytes 786440 | tf_op jit(solution)/shard_map/ppermute | solution.py:379
  250.2 6.2 %collective-permute-done.6 = bf16[256,512]{1,0:T(8,128)(2,1)S(1)} collective-permute-done((bf16[256,512]{1,0:T(8,128)(2,1)S(1)}, bf16[256,512]{1,0:T(8,128)(2,1)S(1)}, u32[]{:S(2)}, u32[]{:S(2)}) %collective-permute-start.6) | collective-permute-done | bytes 262176 | tf_op jit(solution)/shard_map/ppermute | solution.py:379
  259.1 5.6 %grad_states.1 = bf16[256,5120]{1,0:T(8,128)(2,1)} custom-call(s32[2]{0:T(128)S(1)} %pad_add_fusion.refs_0_, bf16[256,512]{1,0:T(8,128)(2,1)} %collective-permute-done.8.refs_1_.refs_18_, bf16[272,256]{1,0:T(8,128)(2,1)S(1)} %collective-permute-done.17.refs_2_.refs_19_, bf16[2560,512]{1,0:T(8,128)(2,1)S(1)} %bitcast.21, ...), custom_call_target="tpu_custom_call" | custom-call | flops 1000 | bytes 1000 | tf_op jit(solution)/shard_map/grad_states/pallas_call | solution.py:359
  (144 shorter events, 61.0 us)
Async XLA Ops:
  2.5 28.3 %all-to-all-start = ((bf16[64,40,256]{2,1,0:T(8,128)(2,1)}), bf16[64,40,256]{2,1,0:T(8,128)(2,1)S(1)}, u32[]{:S(2)}, u32[]{:S(2)}) async-start(bf16[64,40,256]{2,1,0:T(8,128)(2,1)} %broadcast_in_dim.14), calls=%async_computation | async-start | bytes 2621440 | tf_op jit(solution)/shard_map/all_to_all | solution.py:387
  33.3 44.3 %all-to-all-start.1 = ((bf16[64,40,512]{2,1,0:T(8,128)(2,1)}), bf16[64,40,512]{2,1,0:T(8,128)(2,1)S(1)}, u32[]{:S(2)}, u32[]{:S(2)}) async-start(bf16[64,40,512]{2,1,0:T(8,128)(2,1)} %broadcast_in_dim.16), calls=%async_computation.1 | async-start | bytes 5242880 | tf_op jit(solution)/shard_map/all_to_all | solution.py:387
  41.1 5.0 %collective-permute-start = (bf16[2560,256]{1,0:T(8,128)(2,1)}, bf16[2560,256]{1,0:T(8,128)(2,1)S(1)}, u32[]{:S(2)}, u32[]{:S(2)}) collective-permute-start(bf16[2560,256]{1,0:T(8,128)(2,1)} %bitcast.22), channel_id=1, source_target_pairs={{0,1},{1,0},{2,3},{3,2},{4,5},{5,4},{6,7},{7,6},{8,9},{9,8},{10,11... | collective-permute-start | bytes 3932168 | tf_op jit(solution)/shard_map/ppermute | solution.py:383
  51.6 25.9 %collective-permute-start.1 = (bf16[256,256]{1,0:T(8,128)(2,1)S(1)}, bf16[256,256]{1,0:T(8,128)(2,1)}, u32[]{:S(2)}, u32[]{:S(2)}) collective-permute-start(bf16[256,256]{1,0:T(8,128)(2,1)S(1)} %get-tuple-element.42), channel_id=1, source_target_pairs={{0,0},{1,4},{4,1},{5,5},{2,2},{3,6},{6,3},{7,7},{8,8},{9,12},{12,9... | collective-permute-start | bytes 393224 | tf_op jit(solution)/shard_map/ppermute | solution.py:379
  77.5 18.5 %collective-permute-start.2 = (bf16[2560,512]{1,0:T(8,128)(2,1)S(1)}, bf16[2560,512]{1,0:T(8,128)(2,1)}, u32[]{:S(2)}, u32[]{:S(2)}) collective-permute-start(bf16[2560,512]{1,0:T(8,128)(2,1)S(1)} %bitcast.19), channel_id=1, source_target_pairs={{0,1},{1,0},{2,3},{3,2},{4,5},{5,4},{6,7},{7,6},{8,9},{9,8},{10,11... | collective-permute-start | bytes 7864328 | tf_op jit(solution)/shard_map/ppermute | solution.py:383
  80.0 16.1 %copy-start.37 = (f32[128]{0:T(128)S(1)}, f32[128]{0:T(128)}, u32[]{:S(2)}) copy-start(f32[128]{0:T(128)} %param.13) | copy-start | bytes 1540
  80.0 33.7 %all-to-all-start.2 = ((bf16[16,256,256]{2,1,0:T(8,128)(2,1)}), bf16[16,256,256]{2,1,0:T(8,128)(2,1)}, u32[]{:S(2)}, u32[]{:S(2)}) async-start(bf16[16,256,256]{2,1,0:T(8,128)(2,1)} %broadcast_in_dim.17), calls=%async_computation.2 | async-start | bytes 4194304 | tf_op jit(solution)/shard_map/all_to_all | solution.py:387
  86.3 9.8 %collective-permute-start.3 = (bf16[256,512]{1,0:T(8,128)(2,1)}, bf16[256,512]{1,0:T(8,128)(2,1)S(1)}, u32[]{:S(2)}, u32[]{:S(2)}) collective-permute-start(bf16[256,512]{1,0:T(8,128)(2,1)} %bitcast.33), channel_id=1, source_target_pairs={{0,0},{1,4},{4,1},{5,5},{2,2},{3,6},{6,3},{7,7},{8,8},{9,12},{12,9... | collective-permute-start | bytes 786440 | tf_op jit(solution)/shard_map/ppermute | solution.py:379
  103.7 15.9 %collective-permute-start.4 = (bf16[256,512]{1,0:T(8,128)(2,1)}, bf16[256,512]{1,0:T(8,128)(2,1)S(1)}, u32[]{:S(2)}, u32[]{:S(2)}) collective-permute-start(bf16[256,512]{1,0:T(8,128)(2,1)} %get-tuple-element.47), channel_id=1, source_target_pairs={{0,0},{1,4},{4,1},{5,5},{2,2},{3,6},{6,3},{7,7},{8,8},{9,12},{12,9... | collective-permute-start | bytes 786440 | tf_op jit(solution)/shard_map/ppermute | solution.py:379
  113.7 46.6 %all-to-all-start.3 = ((bf16[8,640,256]{2,1,0:T(8,128)(2,1)}), bf16[8,640,256]{2,1,0:T(8,128)(2,1)}, u32[]{:S(2)}, u32[]{:S(2)}) async-start(bf16[8,640,256]{2,1,0:T(8,128)(2,1)} %copy-done.13), calls=%async_computation.3 | async-start | bytes 5242880 | tf_op jit(solution)/shard_map/all_to_all | solution.py:459
  119.6 4.5 %collective-permute-start.5 = (bf16[16,256,256]{2,1,0:T(8,128)(2,1)}, bf16[16,256,256]{2,1,0:T(8,128)(2,1)S(1)}, u32[]{:S(2)}, u32[]{:S(2)}) collective-permute-start(bf16[16,256,256]{2,1,0:T(8,128)(2,1)} %all-to-all-done.2.kv_ref), channel_id=1, source_target_pairs={{0,1},{1,0},{2,3},{3,2},{4,5},{5,4},{6,7},{7,6},{8,9},{9,8},{10,11... | collective-permute-start | bytes 6291464 | tf_op jit(solution)/shard_map/ppermute | solution.py:383
  160.3 4.4 %collective-permute-start.9 = (bf16[16,256,256]{2,1,0:T(8,128)(2,1)}, bf16[16,256,256]{2,1,0:T(8,128)(2,1)S(1)}, u32[]{:S(2)}, u32[]{:S(2)}) collective-permute-start(bf16[16,256,256]{2,1,0:T(8,128)(2,1)} %copy-done.40), channel_id=1, source_target_pairs={{0,1},{1,0},{2,3},{3,2},{4,5},{5,4},{6,7},{7,6},{8,9},{9,8},{10,11... | collective-permute-start | bytes 6291464 | tf_op jit(solution)/shard_map/ppermute | solution.py:383
  168.2 44.9 %all-to-all-start.4 = ((bf16[16,256,256]{2,1,0:T(8,128)(2,1)}), bf16[16,256,256]{2,1,0:T(8,128)(2,1)}, u32[]{:S(2)}, u32[]{:S(2)}) async-start(bf16[16,256,256]{2,1,0:T(8,128)(2,1)} %add_convert_fusion), calls=%async_computation.4 | async-start | bytes 4194304 | tf_op jit(solution)/shard_map/all_to_all | solution.py:464
  175.4 12.8 %collective-permute-start.7 = (bf16[256,640]{1,0:T(8,128)(2,1)}, bf16[256,640]{1,0:T(8,128)(2,1)S(1)}, u32[]{:S(2)}, u32[]{:S(2)}) collective-permute-start(bf16[256,640]{1,0:T(8,128)(2,1)} %copy-done.41), channel_id=1, source_target_pairs={{0,0},{1,4},{4,1},{5,5},{2,2},{3,6},{6,3},{7,7},{8,8},{9,12},{12,9... | collective-permute-start | bytes 983048 | tf_op jit(solution)/shard_map/ppermute | solution.py:379
  189.9 13.3 %collective-permute-start.12 = (bf16[256,512]{1,0:T(8,128)(2,1)S(1)}, bf16[256,512]{1,0:T(8,128)(2,1)S(1)}, u32[]{:S(2)}, u32[]{:S(2)}) collective-permute-start(bf16[256,512]{1,0:T(8,128)(2,1)S(1)} %get-tuple-element.53.refs_6_.refs_2_), channel_id=1, source_target_pairs={{0,2},{2,4},{4,6},{6,0},{1,3},{3,5},{5,7},{7,1},{8,10},{10,12},{12... | collective-permute-start | bytes 786440 | tf_op jit(solution)/shard_map/ppermute | solution.py:391
  190.0 14.0 %collective-permute-start.11 = (bf16[256,512]{1,0:T(8,128)(2,1)S(1)}, bf16[256,512]{1,0:T(8,128)(2,1)S(1)}, u32[]{:S(2)}, u32[]{:S(2)}) collective-permute-start(bf16[256,512]{1,0:T(8,128)(2,1)S(1)} %get-tuple-element.53.refs_6_.refs_2_), channel_id=1, source_target_pairs={{0,4},{2,6},{4,0},{6,2},{1,5},{3,7},{5,1},{7,3},{8,12},{10,14},{12... | collective-permute-start | bytes 786440 | tf_op jit(solution)/shard_map/ppermute | solution.py:391
  190.1 15.1 %collective-permute-start.10 = (bf16[256,512]{1,0:T(8,128)(2,1)S(1)}, bf16[256,512]{1,0:T(8,128)(2,1)S(1)}, u32[]{:S(2)}, u32[]{:S(2)}) collective-permute-start(bf16[256,512]{1,0:T(8,128)(2,1)S(1)} %get-tuple-element.53.refs_6_.refs_2_), channel_id=1, source_target_pairs={{0,6},{2,0},{4,2},{6,4},{1,7},{3,1},{5,3},{7,5},{8,14},{10,8},{12,... | collective-permute-start | bytes 786440 | tf_op jit(solution)/shard_map/ppermute | solution.py:391
  192.6 17.6 %collective-permute-start.13 = (bf16[256,512]{1,0:T(8,128)(2,1)S(1)}, bf16[256,512]{1,0:T(8,128)(2,1)S(1)}, u32[]{:S(2)}, u32[]{:S(2)}) collective-permute-start(bf16[256,512]{1,0:T(8,128)(2,1)S(1)} %get-tuple-element.53.refs_6_.refs_2_), channel_id=1, source_target_pairs={{0,1},{1,0},{2,3},{3,2},{4,5},{5,4},{6,7},{7,6},{8,9},{9,8},{10,11... | collective-permute-start | bytes 786440 | tf_op jit(solution)/shard_map/ppermute | solution.py:383
  203.2 7.7 %collective-permute-start.16 = (bf16[256,512]{1,0:T(8,128)(2,1)S(1)}, bf16[256,512]{1,0:T(8,128)(2,1)S(1)}, u32[]{:S(2)}, u32[]{:S(2)}) collective-permute-start(bf16[256,512]{1,0:T(8,128)(2,1)S(1)} %collective-permute-done.12.refs_9_.refs_5_), channel_id=1, source_target_pairs={{0,1},{1,0},{2,3},{3,2},{4,5},{5,4},{6,7},{7,6},{8,9},{9,8},{10,11... | collective-permute-start | bytes 786440 | tf_op jit(solution)/shard_map/ppermute | solution.py:383
  203.9 7.7 %collective-permute-start.15 = (bf16[256,512]{1,0:T(8,128)(2,1)S(1)}, bf16[256,512]{1,0:T(8,128)(2,1)S(1)}, u32[]{:S(2)}, u32[]{:S(2)}) collective-permute-start(bf16[256,512]{1,0:T(8,128)(2,1)S(1)} %collective-permute-done.11.refs_8_.refs_4_), channel_id=1, source_target_pairs={{0,1},{1,0},{2,3},{3,2},{4,5},{5,4},{6,7},{7,6},{8,9},{9,8},{10,11... | collective-permute-start | bytes 786440 | tf_op jit(solution)/shard_map/ppermute | solution.py:383
  205.1 7.2 %collective-permute-start.14 = (bf16[256,512]{1,0:T(8,128)(2,1)S(1)}, bf16[256,512]{1,0:T(8,128)(2,1)S(1)}, u32[]{:S(2)}, u32[]{:S(2)}) collective-permute-start(bf16[256,512]{1,0:T(8,128)(2,1)S(1)} %collective-permute-done.10.refs_7_.refs_3_), channel_id=1, source_target_pairs={{0,1},{1,0},{2,3},{3,2},{4,5},{5,4},{6,7},{7,6},{8,9},{9,8},{10,11... | collective-permute-start | bytes 786440 | tf_op jit(solution)/shard_map/ppermute | solution.py:383
  206.9 19.9 %collective-permute-start.8 = (bf16[256,512]{1,0:T(8,128)(2,1)S(1)}, bf16[256,512]{1,0:T(8,128)(2,1)}, u32[]{:S(2)}, u32[]{:S(2)}) collective-permute-start(bf16[256,512]{1,0:T(8,128)(2,1)S(1)} %get-tuple-element.53.refs_6_.refs_2_), channel_id=1, source_target_pairs={{0,0},{1,4},{4,1},{5,5},{2,2},{3,6},{6,3},{7,7},{8,8},{9,12},{12,9... | collective-permute-start | bytes 786440 | tf_op jit(solution)/shard_map/ppermute | solution.py:379
  221.9 7.4 %collective-permute-start.20 = (bf16[272,256]{1,0:T(8,128)(2,1)S(1)}, bf16[272,256]{1,0:T(8,128)(2,1)S(1)}, u32[]{:S(2)}, u32[]{:S(2)}) collective-permute-start(bf16[272,256]{1,0:T(8,128)(2,1)S(1)} %grad_key_value.1.refs_10_), channel_id=1, source_target_pairs={{0,2},{2,4},{4,6},{6,0},{1,3},{3,5},{5,7},{7,1},{8,10},{10,12},{12... | collective-permute-start | bytes 417800 | tf_op jit(solution)/shard_map/ppermute | solution.py:391
  223.0 7.2 %collective-permute-start.19 = (bf16[272,256]{1,0:T(8,128)(2,1)S(1)}, bf16[272,256]{1,0:T(8,128)(2,1)S(1)}, u32[]{:S(2)}, u32[]{:S(2)}) collective-permute-start(bf16[272,256]{1,0:T(8,128)(2,1)S(1)} %grad_key_value.1.refs_10_), channel_id=1, source_target_pairs={{0,4},{2,6},{4,0},{6,2},{1,5},{3,7},{5,1},{7,3},{8,12},{10,14},{12... | collective-permute-start | bytes 417800 | tf_op jit(solution)/shard_map/ppermute | solution.py:391
  223.2 8.1 %collective-permute-start.18 = (bf16[272,256]{1,0:T(8,128)(2,1)S(1)}, bf16[272,256]{1,0:T(8,128)(2,1)S(1)}, u32[]{:S(2)}, u32[]{:S(2)}) collective-permute-start(bf16[272,256]{1,0:T(8,128)(2,1)S(1)} %grad_key_value.1.refs_10_), channel_id=1, source_target_pairs={{0,6},{2,0},{4,2},{6,4},{1,7},{3,1},{5,3},{7,5},{8,14},{10,8},{12,... | collective-permute-start | bytes 417800 | tf_op jit(solution)/shard_map/ppermute | solution.py:391
  225.5 6.1 %collective-permute-start.21 = (bf16[272,256]{1,0:T(8,128)(2,1)S(1)}, bf16[272,256]{1,0:T(8,128)(2,1)S(1)}, u32[]{:S(2)}, u32[]{:S(2)}) collective-permute-start(bf16[272,256]{1,0:T(8,128)(2,1)S(1)} %grad_key_value.1.refs_10_), channel_id=1, source_target_pairs={{0,1},{1,0},{2,3},{3,2},{4,5},{5,4},{6,7},{7,6},{8,9},{9,8},{10,11... | collective-permute-start | bytes 417800 | tf_op jit(solution)/shard_map/ppermute | solution.py:383
  226.8 7.9 %collective-permute-start.17 = (bf16[272,256]{1,0:T(8,128)(2,1)S(1)}, bf16[272,256]{1,0:T(8,128)(2,1)S(1)}, u32[]{:S(2)}, u32[]{:S(2)}) collective-permute-start(bf16[272,256]{1,0:T(8,128)(2,1)S(1)} %grad_key_value.1.refs_10_), channel_id=1, source_target_pairs={{0,0},{1,4},{4,1},{5,5},{2,2},{3,6},{6,3},{7,7},{8,8},{9,12},{12,9... | collective-permute-start | bytes 417800 | tf_op jit(solution)/shard_map/ppermute | solution.py:379
  229.3 5.3 %collective-permute-start.24 = (bf16[272,256]{1,0:T(8,128)(2,1)S(1)}, bf16[272,256]{1,0:T(8,128)(2,1)S(1)}, u32[]{:S(2)}, u32[]{:S(2)}) collective-permute-start(bf16[272,256]{1,0:T(8,128)(2,1)S(1)} %collective-permute-done.20.refs_13_), channel_id=1, source_target_pairs={{0,1},{1,0},{2,3},{3,2},{4,5},{5,4},{6,7},{7,6},{8,9},{9,8},{10,11... | collective-permute-start | bytes 417800 | tf_op jit(solution)/shard_map/ppermute | solution.py:383
  230.2 4.4 %collective-permute-start.23 = (bf16[272,256]{1,0:T(8,128)(2,1)S(1)}, bf16[272,256]{1,0:T(8,128)(2,1)S(1)}, u32[]{:S(2)}, u32[]{:S(2)}) collective-permute-start(bf16[272,256]{1,0:T(8,128)(2,1)S(1)} %collective-permute-done.19.refs_12_), channel_id=1, source_target_pairs={{0,1},{1,0},{2,3},{3,2},{4,5},{5,4},{6,7},{7,6},{8,9},{9,8},{10,11... | collective-permute-start | bytes 417800 | tf_op jit(solution)/shard_map/ppermute | solution.py:383
  231.3 3.4 %collective-permute-start.22 = (bf16[272,256]{1,0:T(8,128)(2,1)S(1)}, bf16[272,256]{1,0:T(8,128)(2,1)S(1)}, u32[]{:S(2)}, u32[]{:S(2)}) collective-permute-start(bf16[272,256]{1,0:T(8,128)(2,1)S(1)} %collective-permute-done.18.refs_11_), channel_id=1, source_target_pairs={{0,1},{1,0},{2,3},{3,2},{4,5},{5,4},{6,7},{7,6},{8,9},{9,8},{10,11... | collective-permute-start | bytes 417800 | tf_op jit(solution)/shard_map/ppermute | solution.py:383
  239.7 25.0 %all-to-all-start.5 = ((bf16[16,48,768]{2,1,0:T(8,128)(2,1)}), bf16[16,48,768]{2,1,0:T(8,128)(2,1)}, u32[]{:S(2)}, u32[]{:S(2)}) async-start(bf16[16,48,768]{2,1,0:T(8,128)(2,1)} %copy-done.12), calls=%async_computation.5 | async-start | bytes 2359296 | tf_op jit(solution)/shard_map/all_to_all | solution.py:490
  246.9 9.6 %collective-permute-start.6 = (bf16[256,512]{1,0:T(8,128)(2,1)S(1)}, bf16[256,512]{1,0:T(8,128)(2,1)S(1)}, u32[]{:S(2)}, u32[]{:S(2)}) collective-permute-start(bf16[256,512]{1,0:T(8,128)(2,1)S(1)} %copy-done.43), channel_id=1, source_target_pairs={{0,0},{1,4},{4,1},{5,5},{2,2},{3,6},{6,3},{7,7},{8,8},{9,12},{12,9... | collective-permute-start | bytes 786440 | tf_op jit(solution)/shard_map/ppermute | solution.py:379
  (43 other events, 151.0 us)

commit v8 on v7

--- a/solution.py
+++ b/solution.py
@@ -51,7 +51,7 @@
     return inverse * (grad_unit - unit * shrink), grad_normed * unit
 
 
-def prepare_kernel(where, src_ref, toks_ref, toks_theirs_ref, turned_ref, done_ref):
+def prepare_kernel(where, src_ref, toks_ref, toks_theirs_ref, turned_ref, turned_theirs_ref, done_ref):
     planes, columns = src_ref.shape[:2]
     core = where[1]
     done_ref[...] = jnp.zeros_like(done_ref)
@@ -68,10 +68,24 @@
             wide = rows.shape[0]
             out_ref[:, i // group * wide : (i // group + 1) * wide] = rows.T
     for y in range(columns):
-        for side in range(2):
-            turned_ref[2 * y + side] = jnp.concatenate(
-                [piece(i, y, side) for i in range(planes)], axis=0
-            ).astype(bf16)
+        for side, out_ref in ((core, turned_ref), (1 - core, turned_theirs_ref)):
+            out_ref[y] = jnp.concatenate([piece(i, y, side) for i in range(planes)], axis=0).astype(bf16)
+
+
+def pack_kernel(where, mine_ref, other_ref, *outs):
+    core = where[1]
+    outs, done_ref = outs[:-1], outs[-1]
+    done_ref[...] = jnp.zeros_like(done_ref)
+    for k, out_ref in enumerate(outs):
+        at = lax.rem(where[0] + k, len(outs))
+        out_ref[core] = mine_ref[at]
+        out_ref[1 - core] = other_ref[at]
+
+
+def place_kernel(where, *refs):
+    blocks, out_ref = refs[:-1], refs[-1]
+    for k, block in enumerate(blocks):
+        out_ref[lax.rem(where[0] + k, len(blocks))] = block[...]
 
 
 def key_value_kernel(mine_ref, other_ref, w_ref, w_other_ref, gain_ref, cos_ref, sin_ref, kv_ref, raw_ref):
@@ -94,6 +108,7 @@
 def attention_kernel(
     order, own, q_ref, g_ref, kv_ref, kv_other_ref, ctx_ref, dq_ref, dkv_ref, dkv_other_ref,
     slot_of, ks, vs, kt, vt, acc_kv, qs, gs, qt, gt, acc_o, row_max, row_sum, row_delta, acc_q,
+    sums, sums_other, sems,
 ):
     spans, heads = order.shape[0], q_ref.shape[1] // span
     chunks = spans // per_chunk
@@ -208,17 +223,25 @@
 
             @pl.when(mine)
             def _():
-                dkv_ref[pair, pl.ds(rows_at, span), :span] = dk
-                dkv_ref[pair, pl.ds(rows_at, span), span:] = dv
+                sums[pair, pl.ds(rows_at, span), :span] = dk
+                sums[pair, pl.ds(rows_at, span), span:] = dv
 
             @pl.when(jnp.logical_not(mine))
             def _():
-                dkv_other_ref[pair, pl.ds(rows_at, span), :span] = dk
-                dkv_other_ref[pair, pl.ds(rows_at, span), span:] = dv
+                sums_other[pair, pl.ds(rows_at, span), :span] = dk
+                sums_other[pair, pl.ds(rows_at, span), span:] = dv
 
         return carry
 
     lax.fori_loop(0, chunks, give, 0)
+    copies = [
+        pltpu.make_async_copy(sums_other, dkv_other_ref, sems.at[0]),
+        pltpu.make_async_copy(sums, dkv_ref, sems.at[1]),
+    ]
+    for copy in copies:
+        copy.start()
+    for copy in copies:
+        copy.wait()
 
 
 def attention(order, own, q16, g16, kv, kv_other):
@@ -236,7 +259,7 @@
             share,
         ),
         in_specs=[smem, smem] + [vmem] * 4,
-        out_specs=(vmem,) * 4,
+        out_specs=(vmem, vmem, anywhere, anywhere),
         scratch_shapes=[
             pltpu.SMEM((spans,), jnp.int32),
             pltpu.VMEM((chunks, chunk, span), bf16),
@@ -253,8 +276,11 @@
             pltpu.VMEM((1, rows), f32),
             pltpu.VMEM((1, rows), f32),
             pltpu.VMEM((span, rows), f32),
+            pltpu.VMEM(kv.shape, bf16),
+            pltpu.VMEM(kv.shape, bf16),
+            pltpu.SemaphoreType.DMA((2,)),
         ],
-        compiler_params=pltpu.CompilerParams(vmem_limit_bytes=28 * mib),
+        compiler_params=pltpu.CompilerParams(vmem_limit_bytes=32 * mib),
         cost_estimate=pl.CostEstimate(
             flops=1000, bytes_accessed=1000, transcendentals=0
         ),
@@ -359,7 +385,7 @@
     return pl.pallas_call(
         run,
         out_shape=shapes,
-        in_specs=[smem if a.dtype == jnp.int32 else vmem for a in args] + [anywhere] * len(after),
+        in_specs=[smem if a.dtype == jnp.int32 else vmem for a in args] + [vmem] * len(after),
         out_specs=jax.tree.map(lambda _: vmem, shapes),
         scratch_shapes=scratch,
         compiler_params=pltpu.CompilerParams(vmem_limit_bytes=limit * mib),
@@ -422,10 +448,11 @@
     shape = jax.ShapeDtypeStruct
 
     kv_mine = to_all(jnp.concatenate([w_key, w_value], axis=1), chips, planes * columns)
-    toks_mine, toks_theirs, turned, done = call(
+    toks_mine, toks_theirs, turned, turned_theirs, done = call(
         prepare_kernel,
         (shape((tok_rows, half), bf16),) * 2
-        + (shape((2 * columns, width // 8, tok_rows), bf16), shape((8, span), f32)),
+        + (shape((columns, half // columns, tok_rows), bf16),) * 2
+        + (shape((8, span), f32),),
         where, tokens.T.reshape(planes, columns, 2, own_rows, tok_rows),
         name="prepare",
         after=(cosine, sine, cos_there, sin_there),
@@ -442,8 +469,15 @@
         name="key_value",
         after=(done,),
     )
-    kv16, q_mine = lax.optimization_barrier((swap(kv16), q_mine))
-    kv_own = to_all(kv16, plane, planes)
+    kv_send = jnp.broadcast_to(swap(kv16)[None], (planes, tok_rows, kv_cols))
+    *packed, packed_done = call(
+        pack_kernel,
+        (shape((2, half // columns, tok_rows), bf16),) * columns + (shape((8, span), f32),),
+        where, turned, flip(turned_theirs),
+        name="pack",
+    )
+    kv_send, q_mine = lax.optimization_barrier((kv_send, q_mine))
+    kv_own = lax.all_to_all(kv_send, plane, 0, 0)
     q_theirs = flip(q_mine)
     grad_out = swap(cotangent[0])
     q16, raw = call(
@@ -451,15 +485,24 @@
         (shape((tok_rows, q_cols), bf16), shape((tok_rows, q_cols + span), bf16)),
         toks_mine, toks_theirs, q_mine, q_theirs, raw_k, gain_q, cosine, sine,
         name="query",
-        after=(grad_out,),
+        after=(grad_out, packed_done),
     )
     q16, raw_there = swap(q16), swap(raw)
     kv_own, q16 = lax.optimization_barrier((kv_own, q16))
     kv_other = flip(kv_own)
-    turned = lax.all_to_all(turned, column + ("core",), 0, 0)
+    turned = [packed[0]] + [
+        lax.ppermute(packed[k], column, [(i, (i + k) % columns) for i in range(columns)])
+        for k in range(1, columns)
+    ]
 
     ctx, dq, dkv_mine, dkv_theirs = attention(block_order, own, q16, grad_out, kv_own, kv_other)
     dkv_theirs, turned = lax.optimization_barrier((dkv_theirs, turned))
+    turned = call(
+        place_kernel,
+        shape((columns, 2, half // columns, tok_rows), bf16),
+        where, turned[0], turned[3], turned[2], turned[1],
+        name="place",
+    ).reshape(2 * columns, half // columns, tok_rows)
     dkv = (dkv_mine.astype(f32) + flip(dkv_theirs).astype(f32)).astype(bf16)
     dkv = lax.all_to_all(dkv, plane, 0, 0)
 

time: 271 us -> 263 us (0.970)
  waiting for transfers between devices: 76.2 us -> 69.8 us
  starting transfers between devices: 85.8 us -> 82.5 us
    all_to_all x1, waiting for transfers between devices: 0.01 us -> 9.89 us  [local(): kv_own = lax.all_to_all(kv_send, plane, 0, 0)]
    all_to_all x3 -> x2, waiting for transfers between devices: 12.2 us -> 3.54 us  [to_all(): lax.all_to_all(jnp.broadcast_to(array[None], (count,) + array.shape), axe...]
    ppermute x7, waiting for transfers between devices: 45.4 us -> 38.4 us  [swap(): return lax.ppermute(array, ('y_hi', 'core'), swapped)]
    all_to_all x3 -> x2, starting transfers between devices: 24.8 us -> 18.4 us  [to_all(): lax.all_to_all(jnp.broadcast_to(array[None], (count,) + array.shape), axe...]
    broadcast_in_dim x3 -> x2, local copies, waits for them, and re-layouts: 6.03 us -> 2.92 us  [to_all(): jnp.broadcast_to(array[None], (count,) + array.shape)]
    ppermute x12 -> x13, waiting for transfers between devices: 11.2 us -> 8.88 us  [flip(): return lax.ppermute(array, 'core', flipped)]
    unnamed x89 -> x117, local copies, waits for them, and re-layouts: 34.3 us -> 36.1 us
    ppermute x12 -> x13, starting transfers between devices: 10.9 us -> 9.82 us  [flip(): return lax.ppermute(array, 'core', flipped)]
  transfers between devices with their start and end apart: 31 -> 34, of which waited for: 13 -> 15; matrix products, arithmetic and copies ran while one was open for 3% -> 3% of each run, Pallas kernels for 18% -> 19%
where the time goes in v8:
time: 263 us; the launch traced here: 258 us
  starting transfers between devices  82.5 us (31%)
  waiting for transfers between devices  69.8 us (27%)
  Pallas kernels  54.2 us (21%)
  local copies, waits for them, and re-layouts  45.9 us (17%)
  other arithmetic  4.89 us (2%)
    ppermute x7, waiting for transfers between devices, swap(): return lax.ppermute(array, ('y_hi', 'core'), swapped)  38.4 us
    unnamed x117, local copies, waits for them, and re-layouts  36.1 us
    pallas_call x1, Pallas kernels, attention(): pl.pallas_call(attention_kernel, out_shape=(jax.ShapeDtypeStruct((rows_he...  32.4 us
    ppermute x7, starting transfers between devices, swap(): return lax.ppermute(array, ('y_hi', 'core'), swapped)  24.8 us
    pallas_call x10, Pallas kernels, call(): pl.pallas_call(run, out_shape=shapes, in_specs=[smem if a.dtype == jnp.in...  21.8 us
    all_to_all x2, starting transfers between devices, to_all(): lax.all_to_all(jnp.broadcast_to(array[None], (count,) + array.shape), axe...  18.4 us
    all_to_all x1, waiting for transfers between devices, local(): kv_own = lax.all_to_all(kv_send, plane, 0, 0)  9.89 us
    ppermute x13, starting transfers between devices, flip(): return lax.ppermute(array, 'core', flipped)  9.82 us
  transfers between devices with their start and end apart: 34, of which 15 were waited for; matrix products, arithmetic and copies ran while one was open for 3% of the time, Pallas kernels for 19%

profile of v8, /device:TPU:39, one launch (start us, length us, event | category | flops | bytes accessed | tf_op | source)
XLA Modules:
  0.0 258.4 jit_solution(10593609351566389439)
XLA Ops:
  2.5 10.7 %all-to-all-start = ((bf16[64,40,256]{2,1,0:T(8,128)(2,1)}), bf16[64,40,256]{2,1,0:T(8,128)(2,1)S(1)}, u32[]{:S(2)}, u32[]{:S(2)}) async-start(bf16[64,40,256]{2,1,0:T(8,128)(2,1)} %broadcast_in_dim.14), calls=%async_computation | async-start | bytes 2621440 | tf_op jit(solution)/shard_map/all_to_all | solution.py:413
  13.2 4.4 %copy.15 = bf16[5120,256]{1,0:T(8,128)(2,1)} copy(bf16[5120,256]{0,1:T(8,128)(2,1)} %bitcast.32) | data formatting | bytes 5242880 | tf_op jit(solution)/shard_map/transpose | solution.py:456
  27.3 3.5 %all-to-all-done = bf16[64,40,256]{2,1,0:T(8,128)(2,1)S(1)} async-done(((bf16[64,40,256]{2,1,0:T(8,128)(2,1)}), bf16[64,40,256]{2,1,0:T(8,128)(2,1)S(1)}, u32[]{:S(2)}, u32[]{:S(2)}) %all-to-all-start) | async-done | bytes 1310752 | tf_op jit(solution)/shard_map/all_to_all | solution.py:413
  32.8 7.7 %all-to-all-start.1 = ((bf16[64,40,512]{2,1,0:T(8,128)(2,1)}), bf16[64,40,512]{2,1,0:T(8,128)(2,1)S(1)}, u32[]{:S(2)}, u32[]{:S(2)}) async-start(bf16[64,40,512]{2,1,0:T(8,128)(2,1)} %broadcast_in_dim.17), calls=%async_computation.1 | async-start | bytes 5242880 | tf_op jit(solution)/shard_map/all_to_all | solution.py:413
  40.5 2.2 collective-permute-start
  42.6 2.9 %collective-permute-done.refs_3_.refs_6_ = bf16[2560,256]{1,0:T(8,128)(2,1)S(1)} collective-permute-done((bf16[2560,256]{1,0:T(8,128)(2,1)}, bf16[2560,256]{1,0:T(8,128)(2,1)S(1)}, u32[]{:S(2)}, u32[]{:S(2)}) %collective-permute-start) | collective-permute-done | bytes 1310752 | tf_op jit(solution)/shard_map/ppermute | solution.py:409
  50.9 4.9 %collective-permute-start.1 = (bf16[256,256]{1,0:T(8,128)(2,1)S(1)}, bf16[256,256]{1,0:T(8,128)(2,1)}, u32[]{:S(2)}, u32[]{:S(2)}) collective-permute-start(bf16[256,256]{1,0:T(8,128)(2,1)S(1)} %get-tuple-element.51), channel_id=1, source_target_pairs={{0,0},{1,4},{4,1},{5,5},{2,2},{3,6},{6,3},{7,7},{8,8},{9,12},{12,9... | collective-permute-start | bytes 393224 | tf_op jit(solution)/shard_map/ppermute | solution.py:405
  55.8 21.1 %collective-permute-done.1 = bf16[256,256]{1,0:T(8,128)(2,1)} collective-permute-done((bf16[256,256]{1,0:T(8,128)(2,1)S(1)}, bf16[256,256]{1,0:T(8,128)(2,1)}, u32[]{:S(2)}, u32[]{:S(2)}) %collective-permute-start.1) | collective-permute-done | bytes 131104 | tf_op jit(solution)/shard_map/ppermute | solution.py:405
  76.9 2.4 broadcast_in_dim.16
  79.3 6.3 %all-to-all-start.2 = ((bf16[16,256,256]{2,1,0:T(8,128)(2,1)}), bf16[16,256,256]{2,1,0:T(8,128)(2,1)}, u32[]{:S(2)}, u32[]{:S(2)}) async-start(bf16[16,256,256]{2,1,0:T(8,128)(2,1)} %broadcast_in_dim.16), calls=%async_computation.2 | async-start | bytes 4194304 | tf_op jit(solution)/shard_map/all_to_all | solution.py:480
  86.3 2.0 collective-permute-start.3
  92.9 3.3 %collective-permute-done.3.refs_8_.g_ref = bf16[256,512]{1,0:T(8,128)(2,1)S(1)} collective-permute-done((bf16[256,512]{1,0:T(8,128)(2,1)}, bf16[256,512]{1,0:T(8,128)(2,1)S(1)}, u32[]{:S(2)}, u32[]{:S(2)}) %collective-permute-start.3) | collective-permute-done | bytes 262176 | tf_op jit(solution)/shard_map/ppermute | solution.py:405
  96.2 4.3 %query.1 = (bf16[256,512]{1,0:T(8,128)(2,1)}, bf16[256,640]{1,0:T(8,128)(2,1)S(1)}) custom-call(bf16[256,2560]{1,0:T(8,128)(2,1)S(1)} %copy-done.8, bf16[256,2560]{1,0:T(8,128)(2,1)S(1)} %copy-done.11, bf16[2560,512]{1,0:T(8,128)(2,1)S(1)} %bitcast.21, bf16[2560,512]{1,0:T(8,128)(2,1)} %collective-permute-done.2.refs_3_.refs_4_, ...), custom_call_target="tpu_custom_call" | custom-call | flops 1000 | bytes 1000 | tf_op jit(solution)/shard_map/query/pallas_call | solution.py:385
  103.1 9.9 %all-to-all-done.2.kv_ref = bf16[16,256,256]{2,1,0:T(8,128)(2,1)} async-done(((bf16[16,256,256]{2,1,0:T(8,128)(2,1)}), bf16[16,256,256]{2,1,0:T(8,128)(2,1)}, u32[]{:S(2)}, u32[]{:S(2)}) %all-to-all-start.2) | async-done | bytes 2097184 | tf_op jit(solution)/shard_map/all_to_all | solution.py:480
  115.1 2.1 collective-permute-start.12
  119.2 32.4 %attention.1 = (bf16[256,512]{1,0:T(8,128)(2,1)S(1)}, f32[256,512]{1,0:T(8,128)S(1)}, bf16[16,256,256]{2,1,0:T(8,128)(2,1)S(1)}, bf16[16,256,256]{2,1,0:T(8,128)(2,1)S(1)}) custom-call(s32[64]{0:T(128)S(1)} %copy-done.46, s32[3]{0:T(128)S(1)} %copy-done.49, bf16[256,512]{1,0:T(8,128)(2,1)S(1)} %collective-permute-done.5.q_ref, ...), custom_call_target="tpu_custom_call" | custom-call | flops 1000 | bytes 1000 | tf_op jit(solution)/shard_map/attention/pallas_call | solution.py:253
  156.1 3.8 %collective-permute-done.13 = bf16[16,256,256]{2,1,0:T(8,128)(2,1)S(1)} collective-permute-done((bf16[16,256,256]{2,1,0:T(8,128)(2,1)S(1)}, bf16[16,256,256]{2,1,0:T(8,128)(2,1)S(1)}, u32[]{:S(2)}, u32[]{:S(2)}) %collective-permute-start.13) | collective-permute-done | bytes 2097184 | tf_op jit(solution)/shard_map/ppermute | solution.py:409
  161.8 7.2 %all-to-all-start.3 = ((bf16[16,256,256]{2,1,0:T(8,128)(2,1)}), bf16[16,256,256]{2,1,0:T(8,128)(2,1)}, u32[]{:S(2)}, u32[]{:S(2)}) async-start(bf16[16,256,256]{2,1,0:T(8,128)(2,1)} %add_convert_fusion), calls=%async_computation.3 | async-start | bytes 4194304 | tf_op jit(solution)/shard_map/all_to_all | solution.py:507
  169.0 4.2 %collective-permute-start.8 = (bf16[256,640]{1,0:T(8,128)(2,1)}, bf16[256,640]{1,0:T(8,128)(2,1)S(1)}, u32[]{:S(2)}, u32[]{:S(2)}) collective-permute-start(bf16[256,640]{1,0:T(8,128)(2,1)} %copy-done.54), channel_id=1, source_target_pairs={{0,0},{1,4},{4,1},{5,5},{2,2},{3,6},{6,3},{7,7},{8,8},{9,12},{12,9... | collective-permute-start | bytes 983048 | tf_op jit(solution)/shard_map/ppermute | solution.py:405
  173.2 8.5 %collective-permute-done.8.refs_0_ = bf16[256,640]{1,0:T(8,128)(2,1)S(1)} collective-permute-done((bf16[256,640]{1,0:T(8,128)(2,1)}, bf16[256,640]{1,0:T(8,128)(2,1)S(1)}, u32[]{:S(2)}, u32[]{:S(2)}) %collective-permute-start.8) | collective-permute-done | bytes 327712 | tf_op jit(solution)/shard_map/ppermute | solution.py:405
  183.7 2.6 collective-permute-start.14
  186.3 2.3 collective-permute-start.17
  188.5 7.5 %collective-permute-done.16.refs_9_.refs_5_ = bf16[256,512]{1,0:T(8,128)(2,1)S(1)} collective-permute-done((bf16[256,512]{1,0:T(8,128)(2,1)S(1)}, bf16[256,512]{1,0:T(8,128)(2,1)S(1)}, u32[]{:S(2)}, u32[]{:S(2)}) %collective-permute-start.16) | collective-permute-done | bytes 262176 | tf_op jit(solution)/shard_map/ppermute | solution.py:417
  198.7 4.2 %collective-permute-start.9 = (bf16[256,512]{1,0:T(8,128)(2,1)S(1)}, bf16[256,512]{1,0:T(8,128)(2,1)}, u32[]{:S(2)}, u32[]{:S(2)}) collective-permute-start(bf16[256,512]{1,0:T(8,128)(2,1)S(1)} %get-tuple-element.65.refs_6_.refs_2_), channel_id=1, source_target_pairs={{0,0},{1,4},{4,1},{5,5},{2,2},{3,6},{6,3},{7,7},{8,8},{9,12},{12,9... | collective-permute-start | bytes 786440 | tf_op jit(solution)/shard_map/ppermute | solution.py:405
  212.4 2.2 grad_key_value.1.refs_10_
  216.1 2.3 collective-permute-start.22
  218.7 3.3 %collective-permute-start.21 = (bf16[272,256]{1,0:T(8,128)(2,1)S(1)}, bf16[272,256]{1,0:T(8,128)(2,1)S(1)}, u32[]{:S(2)}, u32[]{:S(2)}) collective-permute-start(bf16[272,256]{1,0:T(8,128)(2,1)S(1)} %grad_key_value.1.refs_10_), channel_id=1, source_target_pairs={{0,0},{1,4},{4,1},{5,5},{2,2},{3,6},{6,3},{7,7},{8,8},{9,12},{12,9... | collective-permute-start | bytes 417800 | tf_op jit(solution)/shard_map/ppermute | solution.py:405
  226.7 3.2 %weight_grad.1 = bf16[16,48,768]{2,1,0:T(8,128)(2,1)S(1)} custom-call(s32[2]{0:T(128)S(1)} %pad_add_fusion.refs_0_, bf16[8,640,256]{2,1,0:T(8,128)(2,1)S(1)} %bitcast.27, bf16[256,512]{1,0:T(8,128)(2,1)S(1)} %get-tuple-element.65.refs_6_.refs_2_, bf16[256,512]{1,0:T(8,128)(2,1)S(1)} %copy-done.23, bf16[256,512]{1,0:T(8,128)(2,1)S(1)} %copy-done.20, ...), custom_call_target="tpu_custom_call" | custom-call | flops 1000 | bytes 1000 | tf_op jit(solution)/shard_map/weight_grad/pallas_call | solution.py:385
  230.9 6.8 %all-to-all-start.4 = ((bf16[16,48,768]{2,1,0:T(8,128)(2,1)}), bf16[16,48,768]{2,1,0:T(8,128)(2,1)}, u32[]{:S(2)}, u32[]{:S(2)}) async-start(bf16[16,48,768]{2,1,0:T(8,128)(2,1)} %copy-done.12), calls=%async_computation.4 | async-start | bytes 2359296 | tf_op jit(solution)/shard_map/all_to_all | solution.py:533
  237.7 4.3 %collective-permute-start.7 = (bf16[256,512]{1,0:T(8,128)(2,1)S(1)}, bf16[256,512]{1,0:T(8,128)(2,1)S(1)}, u32[]{:S(2)}, u32[]{:S(2)}) collective-permute-start(bf16[256,512]{1,0:T(8,128)(2,1)S(1)} %copy-done.56), channel_id=1, source_target_pairs={{0,0},{1,4},{4,1},{5,5},{2,2},{3,6},{6,3},{7,7},{8,8},{9,12},{12,9... | collective-permute-start | bytes 786440 | tf_op jit(solution)/shard_map/ppermute | solution.py:405
  242.1 5.3 %collective-permute-done.7 = bf16[256,512]{1,0:T(8,128)(2,1)S(1)} collective-permute-done((bf16[256,512]{1,0:T(8,128)(2,1)S(1)}, bf16[256,512]{1,0:T(8,128)(2,1)S(1)}, u32[]{:S(2)}, u32[]{:S(2)}) %collective-permute-start.7) | collective-permute-done | bytes 262176 | tf_op jit(solution)/shard_map/ppermute | solution.py:405
  250.0 5.6 %grad_states.1 = bf16[256,5120]{1,0:T(8,128)(2,1)} custom-call(s32[2]{0:T(128)S(1)} %pad_add_fusion.refs_0_, bf16[256,512]{1,0:T(8,128)(2,1)} %collective-permute-done.9.refs_1_.refs_18_, bf16[272,256]{1,0:T(8,128)(2,1)S(1)} %collective-permute-done.21.refs_2_.refs_19_, bf16[2560,512]{1,0:T(8,128)(2,1)S(1)} %bitcast.22, ...), custom_call_target="tpu_custom_call" | custom-call | flops 1000 | bytes 1000 | tf_op jit(solution)/shard_map/grad_states/pallas_call | solution.py:385
  (180 shorter events, 63.9 us)
Async XLA Ops:
  2.5 28.3 %all-to-all-start = ((bf16[64,40,256]{2,1,0:T(8,128)(2,1)}), bf16[64,40,256]{2,1,0:T(8,128)(2,1)S(1)}, u32[]{:S(2)}, u32[]{:S(2)}) async-start(bf16[64,40,256]{2,1,0:T(8,128)(2,1)} %broadcast_in_dim.14), calls=%async_computation | async-start | bytes 2621440 | tf_op jit(solution)/shard_map/all_to_all | solution.py:413
  32.8 44.1 %all-to-all-start.1 = ((bf16[64,40,512]{2,1,0:T(8,128)(2,1)}), bf16[64,40,512]{2,1,0:T(8,128)(2,1)S(1)}, u32[]{:S(2)}, u32[]{:S(2)}) async-start(bf16[64,40,512]{2,1,0:T(8,128)(2,1)} %broadcast_in_dim.17), calls=%async_computation.1 | async-start | bytes 5242880 | tf_op jit(solution)/shard_map/all_to_all | solution.py:413
  40.5 5.0 %collective-permute-start = (bf16[2560,256]{1,0:T(8,128)(2,1)}, bf16[2560,256]{1,0:T(8,128)(2,1)S(1)}, u32[]{:S(2)}, u32[]{:S(2)}) collective-permute-start(bf16[2560,256]{1,0:T(8,128)(2,1)} %bitcast.23), channel_id=1, source_target_pairs={{0,1},{1,0},{2,3},{3,2},{4,5},{5,4},{6,7},{7,6},{8,9},{9,8},{10,11... | collective-permute-start | bytes 3932168 | tf_op jit(solution)/shard_map/ppermute | solution.py:409
  50.9 25.9 %collective-permute-start.1 = (bf16[256,256]{1,0:T(8,128)(2,1)S(1)}, bf16[256,256]{1,0:T(8,128)(2,1)}, u32[]{:S(2)}, u32[]{:S(2)}) collective-permute-start(bf16[256,256]{1,0:T(8,128)(2,1)S(1)} %get-tuple-element.51), channel_id=1, source_target_pairs={{0,0},{1,4},{4,1},{5,5},{2,2},{3,6},{6,3},{7,7},{8,8},{9,12},{12,9... | collective-permute-start | bytes 393224 | tf_op jit(solution)/shard_map/ppermute | solution.py:405
  79.3 16.9 %collective-permute-start.2 = (bf16[2560,512]{1,0:T(8,128)(2,1)S(1)}, bf16[2560,512]{1,0:T(8,128)(2,1)}, u32[]{:S(2)}, u32[]{:S(2)}) collective-permute-start(bf16[2560,512]{1,0:T(8,128)(2,1)S(1)} %bitcast.20), channel_id=1, source_target_pairs={{0,1},{1,0},{2,3},{3,2},{4,5},{5,4},{6,7},{7,6},{8,9},{9,8},{10,11... | collective-permute-start | bytes 7864328 | tf_op jit(solution)/shard_map/ppermute | solution.py:409
  79.3 33.7 %all-to-all-start.2 = ((bf16[16,256,256]{2,1,0:T(8,128)(2,1)}), bf16[16,256,256]{2,1,0:T(8,128)(2,1)}, u32[]{:S(2)}, u32[]{:S(2)}) async-start(bf16[16,256,256]{2,1,0:T(8,128)(2,1)} %broadcast_in_dim.16), calls=%async_computation.2 | async-start | bytes 4194304 | tf_op jit(solution)/shard_map/all_to_all | solution.py:480
  86.3 9.9 %collective-permute-start.3 = (bf16[256,512]{1,0:T(8,128)(2,1)}, bf16[256,512]{1,0:T(8,128)(2,1)S(1)}, u32[]{:S(2)}, u32[]{:S(2)}) collective-permute-start(bf16[256,512]{1,0:T(8,128)(2,1)} %bitcast.35), channel_id=1, source_target_pairs={{0,0},{1,4},{4,1},{5,5},{2,2},{3,6},{6,3},{7,7},{8,8},{9,12},{12,9... | collective-permute-start | bytes 786440 | tf_op jit(solution)/shard_map/ppermute | solution.py:405
  101.2 11.8 %collective-permute-start.5 = (bf16[256,512]{1,0:T(8,128)(2,1)}, bf16[256,512]{1,0:T(8,128)(2,1)S(1)}, u32[]{:S(2)}, u32[]{:S(2)}) collective-permute-start(bf16[256,512]{1,0:T(8,128)(2,1)} %get-tuple-element.59), channel_id=1, source_target_pairs={{0,0},{1,4},{4,1},{5,5},{2,2},{3,6},{6,3},{7,7},{8,8},{9,12},{12,9... | collective-permute-start | bytes 786440 | tf_op jit(solution)/shard_map/ppermute | solution.py:405
  113.0 5.5 %collective-permute-start.6 = (bf16[16,256,256]{2,1,0:T(8,128)(2,1)}, bf16[16,256,256]{2,1,0:T(8,128)(2,1)S(1)}, u32[]{:S(2)}, u32[]{:S(2)}) collective-permute-start(bf16[16,256,256]{2,1,0:T(8,128)(2,1)} %all-to-all-done.2.kv_ref), channel_id=1, source_target_pairs={{0,1},{1,0},{2,3},{3,2},{4,5},{5,4},{6,7},{7,6},{8,9},{9,8},{10,11... | collective-permute-start | bytes 6291464 | tf_op jit(solution)/shard_map/ppermute | solution.py:409
  114.5 38.6 %collective-permute-start.10 = (bf16[2,640,256]{2,1,0:T(8,128)(2,1)}, bf16[2,640,256]{2,1,0:T(8,128)(2,1)S(1)}, u32[]{:S(2)}, u32[]{:S(2)}) collective-permute-start(bf16[2,640,256]{2,1,0:T(8,128)(2,1)} %copy-done.53), channel_id=1, source_target_pairs={{0,2},{2,4},{4,6},{6,0},{1,3},{3,5},{5,7},{7,1},{8,10},{10,12},{12... | collective-permute-start | bytes 1966088 | tf_op jit(solution)/shard_map/ppermute | solution.py:494
  114.8 39.2 %collective-permute-start.11 = (bf16[2,640,256]{2,1,0:T(8,128)(2,1)}, bf16[2,640,256]{2,1,0:T(8,128)(2,1)S(1)}, u32[]{:S(2)}, u32[]{:S(2)}) collective-permute-start(bf16[2,640,256]{2,1,0:T(8,128)(2,1)} %copy-done.52), channel_id=1, source_target_pairs={{0,4},{2,6},{4,0},{6,2},{1,5},{3,7},{5,1},{7,3},{8,12},{10,14},{12... | collective-permute-start | bytes 1966088 | tf_op jit(solution)/shard_map/ppermute | solution.py:494
  115.1 39.8 %collective-permute-start.12 = (bf16[2,640,256]{2,1,0:T(8,128)(2,1)}, bf16[2,640,256]{2,1,0:T(8,128)(2,1)S(1)}, u32[]{:S(2)}, u32[]{:S(2)}) collective-permute-start(bf16[2,640,256]{2,1,0:T(8,128)(2,1)} %copy-done.51), channel_id=1, source_target_pairs={{0,6},{2,0},{4,2},{6,4},{1,7},{3,1},{5,3},{7,5},{8,14},{10,8},{12,... | collective-permute-start | bytes 1966088 | tf_op jit(solution)/shard_map/ppermute | solution.py:494
  155.7 4.2 %collective-permute-start.13 = (bf16[16,256,256]{2,1,0:T(8,128)(2,1)S(1)}, bf16[16,256,256]{2,1,0:T(8,128)(2,1)S(1)}, u32[]{:S(2)}, u32[]{:S(2)}) collective-permute-start(bf16[16,256,256]{2,1,0:T(8,128)(2,1)S(1)} %get-tuple-element.72), channel_id=1, source_target_pairs={{0,1},{1,0},{2,3},{3,2},{4,5},{5,4},{6,7},{7,6},{8,9},{9,8},{10,11... | collective-permute-start | bytes 6291464 | tf_op jit(solution)/shard_map/ppermute | solution.py:409
  161.8 43.9 %all-to-all-start.3 = ((bf16[16,256,256]{2,1,0:T(8,128)(2,1)}), bf16[16,256,256]{2,1,0:T(8,128)(2,1)}, u32[]{:S(2)}, u32[]{:S(2)}) async-start(bf16[16,256,256]{2,1,0:T(8,128)(2,1)} %add_convert_fusion), calls=%async_computation.3 | async-start | bytes 4194304 | tf_op jit(solution)/shard_map/all_to_all | solution.py:507
  169.0 12.8 %collective-permute-start.8 = (bf16[256,640]{1,0:T(8,128)(2,1)}, bf16[256,640]{1,0:T(8,128)(2,1)S(1)}, u32[]{:S(2)}, u32[]{:S(2)}) collective-permute-start(bf16[256,640]{1,0:T(8,128)(2,1)} %copy-done.54), channel_id=1, source_target_pairs={{0,0},{1,4},{4,1},{5,5},{2,2},{3,6},{6,3},{7,7},{8,8},{9,12},{12,9... | collective-permute-start | bytes 983048 | tf_op jit(solution)/shard_map/ppermute | solution.py:405
  183.5 12.5 %collective-permute-start.16 = (bf16[256,512]{1,0:T(8,128)(2,1)S(1)}, bf16[256,512]{1,0:T(8,128)(2,1)S(1)}, u32[]{:S(2)}, u32[]{:S(2)}) collective-permute-start(bf16[256,512]{1,0:T(8,128)(2,1)S(1)} %get-tuple-element.65.refs_6_.refs_2_), channel_id=1, source_target_pairs={{0,2},{2,4},{4,6},{6,0},{1,3},{3,5},{5,7},{7,1},{8,10},{10,12},{12... | collective-permute-start | bytes 786440 | tf_op jit(solution)/shard_map/ppermute | solution.py:417
  183.6 13.2 %collective-permute-start.15 = (bf16[256,512]{1,0:T(8,128)(2,1)S(1)}, bf16[256,512]{1,0:T(8,128)(2,1)S(1)}, u32[]{:S(2)}, u32[]{:S(2)}) collective-permute-start(bf16[256,512]{1,0:T(8,128)(2,1)S(1)} %get-tuple-element.65.refs_6_.refs_2_), channel_id=1, source_target_pairs={{0,4},{2,6},{4,0},{6,2},{1,5},{3,7},{5,1},{7,3},{8,12},{10,14},{12... | collective-permute-start | bytes 786440 | tf_op jit(solution)/shard_map/ppermute | solution.py:417
  183.7 14.3 %collective-permute-start.14 = (bf16[256,512]{1,0:T(8,128)(2,1)S(1)}, bf16[256,512]{1,0:T(8,128)(2,1)S(1)}, u32[]{:S(2)}, u32[]{:S(2)}) collective-permute-start(bf16[256,512]{1,0:T(8,128)(2,1)S(1)} %get-tuple-element.65.refs_6_.refs_2_), channel_id=1, source_target_pairs={{0,6},{2,0},{4,2},{6,4},{1,7},{3,1},{5,3},{7,5},{8,14},{10,8},{12,... | collective-permute-start | bytes 786440 | tf_op jit(solution)/shard_map/ppermute | solution.py:417
  186.3 16.6 %collective-permute-start.17 = (bf16[256,512]{1,0:T(8,128)(2,1)S(1)}, bf16[256,512]{1,0:T(8,128)(2,1)S(1)}, u32[]{:S(2)}, u32[]{:S(2)}) collective-permute-start(bf16[256,512]{1,0:T(8,128)(2,1)S(1)} %get-tuple-element.65.refs_6_.refs_2_), channel_id=1, source_target_pairs={{0,1},{1,0},{2,3},{3,2},{4,5},{5,4},{6,7},{7,6},{8,9},{9,8},{10,11... | collective-permute-start | bytes 786440 | tf_op jit(solution)/shard_map/ppermute | solution.py:409
  196.0 7.5 %collective-permute-start.20 = (bf16[256,512]{1,0:T(8,128)(2,1)S(1)}, bf16[256,512]{1,0:T(8,128)(2,1)S(1)}, u32[]{:S(2)}, u32[]{:S(2)}) collective-permute-start(bf16[256,512]{1,0:T(8,128)(2,1)S(1)} %collective-permute-done.16.refs_9_.refs_5_), channel_id=1, source_target_pairs={{0,1},{1,0},{2,3},{3,2},{4,5},{5,4},{6,7},{7,6},{8,9},{9,8},{10,11... | collective-permute-start | bytes 786440 | tf_op jit(solution)/shard_map/ppermute | solution.py:409
  196.7 7.5 %collective-permute-start.19 = (bf16[256,512]{1,0:T(8,128)(2,1)S(1)}, bf16[256,512]{1,0:T(8,128)(2,1)S(1)}, u32[]{:S(2)}, u32[]{:S(2)}) collective-permute-start(bf16[256,512]{1,0:T(8,128)(2,1)S(1)} %collective-permute-done.15.refs_8_.refs_4_), channel_id=1, source_target_pairs={{0,1},{1,0},{2,3},{3,2},{4,5},{5,4},{6,7},{7,6},{8,9},{9,8},{10,11... | collective-permute-start | bytes 786440 | tf_op jit(solution)/shard_map/ppermute | solution.py:409
  198.0 7.0 %collective-permute-start.18 = (bf16[256,512]{1,0:T(8,128)(2,1)S(1)}, bf16[256,512]{1,0:T(8,128)(2,1)S(1)}, u32[]{:S(2)}, u32[]{:S(2)}) collective-permute-start(bf16[256,512]{1,0:T(8,128)(2,1)S(1)} %collective-permute-done.14.refs_7_.refs_3_), channel_id=1, source_target_pairs={{0,1},{1,0},{2,3},{3,2},{4,5},{5,4},{6,7},{7,6},{8,9},{9,8},{10,11... | collective-permute-start | bytes 786440 | tf_op jit(solution)/shard_map/ppermute | solution.py:409
  198.7 20.0 %collective-permute-start.9 = (bf16[256,512]{1,0:T(8,128)(2,1)S(1)}, bf16[256,512]{1,0:T(8,128)(2,1)}, u32[]{:S(2)}, u32[]{:S(2)}) collective-permute-start(bf16[256,512]{1,0:T(8,128)(2,1)S(1)} %get-tuple-element.65.refs_6_.refs_2_), channel_id=1, source_target_pairs={{0,0},{1,4},{4,1},{5,5},{2,2},{3,6},{6,3},{7,7},{8,8},{9,12},{12,9... | collective-permute-start | bytes 786440 | tf_op jit(solution)/shard_map/ppermute | solution.py:405
  214.6 8.1 %collective-permute-start.24 = (bf16[272,256]{1,0:T(8,128)(2,1)S(1)}, bf16[272,256]{1,0:T(8,128)(2,1)S(1)}, u32[]{:S(2)}, u32[]{:S(2)}) collective-permute-start(bf16[272,256]{1,0:T(8,128)(2,1)S(1)} %grad_key_value.1.refs_10_), channel_id=1, source_target_pairs={{0,2},{2,4},{4,6},{6,0},{1,3},{3,5},{5,7},{7,1},{8,10},{10,12},{12... | collective-permute-start | bytes 417800 | tf_op jit(solution)/shard_map/ppermute | solution.py:417
  216.0 7.1 %collective-permute-start.23 = (bf16[272,256]{1,0:T(8,128)(2,1)S(1)}, bf16[272,256]{1,0:T(8,128)(2,1)S(1)}, u32[]{:S(2)}, u32[]{:S(2)}) collective-permute-start(bf16[272,256]{1,0:T(8,128)(2,1)S(1)} %grad_key_value.1.refs_10_), channel_id=1, source_target_pairs={{0,4},{2,6},{4,0},{6,2},{1,5},{3,7},{5,1},{7,3},{8,12},{10,14},{12... | collective-permute-start | bytes 417800 | tf_op jit(solution)/shard_map/ppermute | solution.py:417
  216.1 9.0 %collective-permute-start.22 = (bf16[272,256]{1,0:T(8,128)(2,1)S(1)}, bf16[272,256]{1,0:T(8,128)(2,1)S(1)}, u32[]{:S(2)}, u32[]{:S(2)}) collective-permute-start(bf16[272,256]{1,0:T(8,128)(2,1)S(1)} %grad_key_value.1.refs_10_), channel_id=1, source_target_pairs={{0,6},{2,0},{4,2},{6,4},{1,7},{3,1},{5,3},{7,5},{8,14},{10,8},{12,... | collective-permute-start | bytes 417800 | tf_op jit(solution)/shard_map/ppermute | solution.py:417
  218.4 7.9 %collective-permute-start.25 = (bf16[272,256]{1,0:T(8,128)(2,1)S(1)}, bf16[272,256]{1,0:T(8,128)(2,1)S(1)}, u32[]{:S(2)}, u32[]{:S(2)}) collective-permute-start(bf16[272,256]{1,0:T(8,128)(2,1)S(1)} %grad_key_value.1.refs_10_), channel_id=1, source_target_pairs={{0,1},{1,0},{2,3},{3,2},{4,5},{5,4},{6,7},{7,6},{8,9},{9,8},{10,11... | collective-permute-start | bytes 417800 | tf_op jit(solution)/shard_map/ppermute | solution.py:409
  218.7 7.9 %collective-permute-start.21 = (bf16[272,256]{1,0:T(8,128)(2,1)S(1)}, bf16[272,256]{1,0:T(8,128)(2,1)S(1)}, u32[]{:S(2)}, u32[]{:S(2)}) collective-permute-start(bf16[272,256]{1,0:T(8,128)(2,1)S(1)} %grad_key_value.1.refs_10_), channel_id=1, source_target_pairs={{0,0},{1,4},{4,1},{5,5},{2,2},{3,6},{6,3},{7,7},{8,8},{9,12},{12,9... | collective-permute-start | bytes 417800 | tf_op jit(solution)/shard_map/ppermute | solution.py:405
  222.7 3.9 %collective-permute-start.28 = (bf16[272,256]{1,0:T(8,128)(2,1)S(1)}, bf16[272,256]{1,0:T(8,128)(2,1)S(1)}, u32[]{:S(2)}, u32[]{:S(2)}) collective-permute-start(bf16[272,256]{1,0:T(8,128)(2,1)S(1)} %collective-permute-done.24.refs_13_), channel_id=1, source_target_pairs={{0,1},{1,0},{2,3},{3,2},{4,5},{5,4},{6,7},{7,6},{8,9},{9,8},{10,11... | collective-permute-start | bytes 417800 | tf_op jit(solution)/shard_map/ppermute | solution.py:409
  223.1 3.5 %collective-permute-start.27 = (bf16[272,256]{1,0:T(8,128)(2,1)S(1)}, bf16[272,256]{1,0:T(8,128)(2,1)S(1)}, u32[]{:S(2)}, u32[]{:S(2)}) collective-permute-start(bf16[272,256]{1,0:T(8,128)(2,1)S(1)} %collective-permute-done.23.refs_12_), channel_id=1, source_target_pairs={{0,1},{1,0},{2,3},{3,2},{4,5},{5,4},{6,7},{7,6},{8,9},{9,8},{10,11... | collective-permute-start | bytes 417800 | tf_op jit(solution)/shard_map/ppermute | solution.py:409
  230.9 24.7 %all-to-all-start.4 = ((bf16[16,48,768]{2,1,0:T(8,128)(2,1)}), bf16[16,48,768]{2,1,0:T(8,128)(2,1)}, u32[]{:S(2)}, u32[]{:S(2)}) async-start(bf16[16,48,768]{2,1,0:T(8,128)(2,1)} %copy-done.12), calls=%async_computation.4 | async-start | bytes 2359296 | tf_op jit(solution)/shard_map/all_to_all | solution.py:533
  237.7 9.6 %collective-permute-start.7 = (bf16[256,512]{1,0:T(8,128)(2,1)S(1)}, bf16[256,512]{1,0:T(8,128)(2,1)S(1)}, u32[]{:S(2)}, u32[]{:S(2)}) collective-permute-start(bf16[256,512]{1,0:T(8,128)(2,1)S(1)} %copy-done.56), channel_id=1, source_target_pairs={{0,0},{1,4},{4,1},{5,5},{2,2},{3,6},{6,3},{7,7},{8,8},{9,12},{12,9... | collective-permute-start | bytes 786440 | tf_op jit(solution)/shard_map/ppermute | solution.py:405
  (60 other events, 274.6 us)

commit v9 on v8

--- a/solution.py
+++ b/solution.py
@@ -82,8 +82,8 @@
         out_ref[1 - core] = other_ref[at]
 
 
-def place_kernel(where, *refs):
-    blocks, out_ref = refs[:-1], refs[-1]
+def place_kernel(where, dkv_ref, *refs):
+    blocks, out_ref = refs[:-2], refs[-1]
     for k, block in enumerate(blocks):
         out_ref[lax.rem(where[0] + k, len(blocks))] = block[...]
 
@@ -318,24 +318,35 @@
     g_ref[rows:] = jnp.where(row == 0, split[0], jnp.where(row == 1, split[1], 0.0)).astype(bf16)
 
 
-def weight_grad_kernel(where, turned_ref, *rest):
-    blocks, out_ref = rest[:-1], rest[-1]
-    count = len(blocks) // 2
-    columns = count // 2
+def over_tokens(where, turned_ref, blocks):
+    columns = len(blocks) // 2
     toks = turned_ref.shape[2]
     y, core = where[0], where[1]
-    query, rows, gains = 0.0, 0.0, 0.0
-    for i in range(count):
+    total = 0.0
+    for i, block in enumerate(blocks):
         from_y = lax.rem(y + i % columns, columns)
         from_core = core if i < columns else 1 - core
         at = (from_core * 2 + lax.rem(from_y, 2)) * 2 + from_y // 2
-        query = query + mm(turned_ref[at], blocks[i][...])
-        rows = rows + mm(turned_ref[at], blocks[count + i][:toks])
-        gains = gains + blocks[count + i][toks:].astype(f32)
+        total = total + mm(turned_ref[at], block[:toks])
+    return total
+
+
+def query_weight_grad_kernel(where, turned_ref, *rest):
+    blocks, (out_ref, done_ref) = rest[:-2], rest[-2:]
+    out_ref[...] = over_tokens(where, turned_ref, blocks).astype(bf16)
+    done_ref[...] = jnp.zeros_like(done_ref)
+
+
+def weight_grad_kernel(where, turned_ref, query_ref, *rest):
+    blocks, out_ref = rest[:-1], rest[-1]
+    toks = turned_ref.shape[2]
+    gains = sum(block[toks:].astype(f32) for block in blocks)
     gain = gains[:8, :span] + gains[:8, span:]
     high = gain.astype(bf16).astype(f32)
-    extra = jnp.concatenate([jnp.zeros((8, query.shape[1]), f32), high, gain - high], axis=1)
-    total = jnp.concatenate([query, rows], axis=1)
+    extra = jnp.concatenate([jnp.zeros((8, query_ref.shape[1]), f32), high, gain - high], axis=1)
+    total = jnp.concatenate(
+        [query_ref[...].astype(f32), over_tokens(where, turned_ref, blocks)], axis=1
+    )
     own_rows = total.shape[0] // out_ref.shape[0]
     for i in range(out_ref.shape[0]):
         part = total[i * own_rows : (i + 1) * own_rows]
@@ -496,13 +507,20 @@
     ]
 
     ctx, dq, dkv_mine, dkv_theirs = attention(block_order, own, q16, grad_out, kv_own, kv_other)
-    dkv_theirs, turned = lax.optimization_barrier((dkv_theirs, turned))
-    turned = call(
+    dkv_theirs, turned = pl.pallas_call(
         place_kernel,
-        shape((columns, 2, half // columns, tok_rows), bf16),
-        where, turned[0], turned[3], turned[2], turned[1],
+        out_shape=(
+            shape(dkv_theirs.shape, bf16),
+            shape((columns, 2, half // columns, tok_rows), bf16),
+        ),
+        in_specs=[smem, anywhere] + [vmem] * columns,
+        out_specs=(anywhere, vmem),
+        input_output_aliases={1: 0},
+        compiler_params=pltpu.CompilerParams(vmem_limit_bytes=16 * mib),
+        cost_estimate=cheap,
         name="place",
-    ).reshape(2 * columns, half // columns, tok_rows)
+    )(where, dkv_theirs, turned[0], turned[3], turned[2], turned[1])
+    turned = turned.reshape(2 * columns, half // columns, tok_rows)
     dkv = (dkv_mine.astype(f32) + flip(dkv_theirs).astype(f32)).astype(bf16)
     dkv = lax.all_to_all(dkv, plane, 0, 0)
 
@@ -512,21 +530,26 @@
         raw_there, dq, gain_q, cos_there, sin_there,
         name="grad_query",
     )
-    blocks = around(g_q)
+    query_parts, done = call(
+        query_weight_grad_kernel,
+        (shape((half // columns, q_cols), bf16), shape((8, span), f32)),
+        where, turned, *around(g_q),
+        name="query_weight_grad",
+    )
     g_q_back = swap(g_q)
     g_kv = call(
         grad_key_value_kernel,
         shape((tok_rows + 16, kv_cols), bf16),
         raw_there, dkv, gain_k, cos_there, sin_there, gains_q,
         name="grad_key_value",
-        after=tuple(blocks),
+        after=(done,),
     )
     blocks_kv = around(g_kv)
     g_kv_back = swap(g_kv)
     parts = call(
         weight_grad_kernel,
         shape((planes, own_rows + 8, q_cols + kv_cols), bf16),
-        where, turned, *blocks, *blocks_kv,
+        where, turned, query_parts, *blocks_kv,
         name="weight_grad",
         after=(g_q_back, g_kv_back),
     )

time: 263 us -> 255 us (0.970)
  local copies, waits for them, and re-layouts: 45.9 us -> 29.4 us
  starting transfers between devices: 82.5 us -> 88.2 us
  Pallas kernels: 54.2 us -> 57.4 us
    unnamed x117 -> x69, local copies, waits for them, and re-layouts: 36.1 us -> 22.1 us
    ppermute x13, starting transfers between devices: 9.82 us -> 14.5 us  [flip(): return lax.ppermute(array, 'core', flipped)]
    all_to_all x2, waiting for transfers between devices: 3.54 us -> 6.53 us  [to_all(): lax.all_to_all(jnp.broadcast_to(array[None], (count,) + array.shape), axe...]
  transfers between devices with their start and end apart: 34 -> 34, of which waited for: 15 -> 14; matrix products, arithmetic and copies ran while one was open for 3% -> 2% of each run, Pallas kernels for 19% -> 21%
where the time goes in v9:
time: 255 us; the launch traced here: 251 us
  starting transfers between devices  88.2 us (35%)
  waiting for transfers between devices  70.2 us (28%)
  Pallas kernels  57.4 us (23%)
  local copies, waits for them, and re-layouts  29.4 us (12%)
  other arithmetic  4.9 us (2%)
    ppermute x7, waiting for transfers between devices, swap(): return lax.ppermute(array, ('y_hi', 'core'), swapped)  36.9 us
    pallas_call x1, Pallas kernels, attention(): pl.pallas_call(attention_kernel, out_shape=(jax.ShapeDtypeStruct((rows_he...  32.5 us
    ppermute x7, starting transfers between devices, swap(): return lax.ppermute(array, ('y_hi', 'core'), swapped)  25.7 us
    pallas_call x10, Pallas kernels, call(): pl.pallas_call(run, out_shape=shapes, in_specs=[smem if a.dtype == jnp.in...  24.2 us
    unnamed x69, local copies, waits for them, and re-layouts  22.1 us
    all_to_all x2, starting transfers between devices, to_all(): lax.all_to_all(jnp.broadcast_to(array[None], (count,) + array.shape), axe...  18.7 us
    ppermute x13, starting transfers between devices, flip(): return lax.ppermute(array, 'core', flipped)  14.5 us
    all_to_all x1, waiting for transfers between devices, local(): kv_own = lax.all_to_all(kv_send, plane, 0, 0)  9.87 us
  transfers between devices with their start and end apart: 34, of which 14 were waited for; matrix products, arithmetic and copies ran while one was open for 2% of the time, Pallas kernels for 21%

profile of v9, /device:TPU:39, one launch (start us, length us, event | category | flops | bytes accessed | tf_op | source)
XLA Modules:
  0.0 251.2 jit_solution(6554580193210618927)
XLA Ops:
  2.5 10.8 %all-to-all-start = ((bf16[64,40,256]{2,1,0:T(8,128)(2,1)}), bf16[64,40,256]{2,1,0:T(8,128)(2,1)}, u32[]{:S(2)}, u32[]{:S(2)}) async-start(bf16[64,40,256]{2,1,0:T(8,128)(2,1)} %broadcast_in_dim.14), calls=%async_computation | async-start | bytes 2621440 | tf_op jit(solution)/shard_map/all_to_all | solution.py:424
  13.4 3.0 %copy.16 = bf16[5120,256]{1,0:T(8,128)(2,1)S(1)} copy(bf16[5120,256]{0,1:T(8,128)(2,1)} %bitcast.30) | data formatting | bytes 5242880 | tf_op jit(solution)/shard_map/transpose | solution.py:467
  24.4 6.5 %all-to-all-done = bf16[64,40,256]{2,1,0:T(8,128)(2,1)} async-done(((bf16[64,40,256]{2,1,0:T(8,128)(2,1)}), bf16[64,40,256]{2,1,0:T(8,128)(2,1)}, u32[]{:S(2)}, u32[]{:S(2)}) %all-to-all-start) | async-done | bytes 1310752 | tf_op jit(solution)/shard_map/all_to_all | solution.py:424
  32.6 7.9 %all-to-all-start.1 = ((bf16[64,40,512]{2,1,0:T(8,128)(2,1)}), bf16[64,40,512]{2,1,0:T(8,128)(2,1)S(1)}, u32[]{:S(2)}, u32[]{:S(2)}) async-start(bf16[64,40,512]{2,1,0:T(8,128)(2,1)} %broadcast_in_dim.17), calls=%async_computation.1 | async-start | bytes 5242880 | tf_op jit(solution)/shard_map/all_to_all | solution.py:424
  40.4 2.2 collective-permute-start
  42.6 2.9 %collective-permute-done.refs_3_.refs_6_ = bf16[2560,256]{1,0:T(8,128)(2,1)S(1)} collective-permute-done((bf16[2560,256]{1,0:T(8,128)(2,1)}, bf16[2560,256]{1,0:T(8,128)(2,1)S(1)}, u32[]{:S(2)}, u32[]{:S(2)}) %collective-permute-start) | collective-permute-done | bytes 1310752 | tf_op jit(solution)/shard_map/ppermute | solution.py:420
  48.6 2.3 key_value.1
  50.9 4.9 %collective-permute-start.1 = (bf16[256,256]{1,0:T(8,128)(2,1)S(1)}, bf16[256,256]{1,0:T(8,128)(2,1)S(1)}, u32[]{:S(2)}, u32[]{:S(2)}) collective-permute-start(bf16[256,256]{1,0:T(8,128)(2,1)S(1)} %get-tuple-element.50), channel_id=1, source_target_pairs={{0,0},{1,4},{4,1},{5,5},{2,2},{3,6},{6,3},{7,7},{8,8},{9,12},{12,9... | collective-permute-start | bytes 393224 | tf_op jit(solution)/shard_map/ppermute | solution.py:416
  55.8 21.0 %collective-permute-done.1 = bf16[256,256]{1,0:T(8,128)(2,1)S(1)} collective-permute-done((bf16[256,256]{1,0:T(8,128)(2,1)S(1)}, bf16[256,256]{1,0:T(8,128)(2,1)S(1)}, u32[]{:S(2)}, u32[]{:S(2)}) %collective-permute-start.1) | collective-permute-done | bytes 131104 | tf_op jit(solution)/shard_map/ppermute | solution.py:416
  78.3 6.4 %all-to-all-start.2 = ((bf16[16,256,256]{2,1,0:T(8,128)(2,1)}), bf16[16,256,256]{2,1,0:T(8,128)(2,1)}, u32[]{:S(2)}, u32[]{:S(2)}) async-start(bf16[16,256,256]{2,1,0:T(8,128)(2,1)} %broadcast_in_dim.16), calls=%async_computation.2 | async-start | bytes 4194304 | tf_op jit(solution)/shard_map/all_to_all | solution.py:491
  85.3 2.0 collective-permute-start.3
  91.9 3.3 %collective-permute-done.3.refs_8_.g_ref = bf16[256,512]{1,0:T(8,128)(2,1)S(1)} collective-permute-done((bf16[256,512]{1,0:T(8,128)(2,1)}, bf16[256,512]{1,0:T(8,128)(2,1)S(1)}, u32[]{:S(2)}, u32[]{:S(2)}) %collective-permute-start.3) | collective-permute-done | bytes 262176 | tf_op jit(solution)/shard_map/ppermute | solution.py:416
  95.3 4.3 %query.1 = (bf16[256,512]{1,0:T(8,128)(2,1)}, bf16[256,640]{1,0:T(8,128)(2,1)S(1)}) custom-call(bf16[256,2560]{1,0:T(8,128)(2,1)S(1)} %copy-done.7, bf16[256,2560]{1,0:T(8,128)(2,1)S(1)} %copy-done.10, bf16[2560,512]{1,0:T(8,128)(2,1)S(1)} %bitcast.21, bf16[2560,512]{1,0:T(8,128)(2,1)} %collective-permute-done.2.refs_3_.refs_4_, ...), custom_call_target="tpu_custom_call" | custom-call | flops 1000 | bytes 1000 | tf_op jit(solution)/shard_map/query/pallas_call | solution.py:396
  102.2 9.9 %all-to-all-done.2.kv_ref = bf16[16,256,256]{2,1,0:T(8,128)(2,1)} async-done(((bf16[16,256,256]{2,1,0:T(8,128)(2,1)}), bf16[16,256,256]{2,1,0:T(8,128)(2,1)}, u32[]{:S(2)}, u32[]{:S(2)}) %all-to-all-start.2) | async-done | bytes 2097184 | tf_op jit(solution)/shard_map/all_to_all | solution.py:491
  118.2 32.5 %attention.1 = (bf16[256,512]{1,0:T(8,128)(2,1)S(1)}, f32[256,512]{1,0:T(8,128)S(1)}, bf16[16,256,256]{2,1,0:T(8,128)(2,1)S(1)}, bf16[16,256,256]{2,1,0:T(8,128)(2,1)S(1)}) custom-call(s32[64]{0:T(128)S(1)} %copy-done.20, s32[3]{0:T(128)S(1)} %copy-done.23, bf16[256,512]{1,0:T(8,128)(2,1)S(1)} %collective-permute-done.5.q_ref, ...), custom_call_target="tpu_custom_call" | custom-call | flops 1000 | bytes 1000 | tf_op jit(solution)/shard_map/attention/pallas_call | solution.py:253
  153.5 3.8 %collective-permute-done.13 = bf16[16,256,256]{2,1,0:T(8,128)(2,1)S(1)} collective-permute-done((bf16[16,256,256]{2,1,0:T(8,128)(2,1)S(1)}, bf16[16,256,256]{2,1,0:T(8,128)(2,1)S(1)}, u32[]{:S(2)}, u32[]{:S(2)}) %collective-permute-start.13) | collective-permute-done | bytes 2097184 | tf_op jit(solution)/shard_map/ppermute | solution.py:420
  159.3 7.2 %all-to-all-start.3 = ((bf16[16,256,256]{2,1,0:T(8,128)(2,1)}), bf16[16,256,256]{2,1,0:T(8,128)(2,1)}, u32[]{:S(2)}, u32[]{:S(2)}) async-start(bf16[16,256,256]{2,1,0:T(8,128)(2,1)} %add_convert_fusion), calls=%async_computation.3 | async-start | bytes 4194304 | tf_op jit(solution)/shard_map/all_to_all | solution.py:525
  166.4 4.2 %collective-permute-start.8 = (bf16[256,640]{1,0:T(8,128)(2,1)}, bf16[256,640]{1,0:T(8,128)(2,1)S(1)}, u32[]{:S(2)}, u32[]{:S(2)}) collective-permute-start(bf16[256,640]{1,0:T(8,128)(2,1)} %copy-done.28), channel_id=1, source_target_pairs={{0,0},{1,4},{4,1},{5,5},{2,2},{3,6},{6,3},{7,7},{8,8},{9,12},{12,9... | collective-permute-start | bytes 983048 | tf_op jit(solution)/shard_map/ppermute | solution.py:416
  170.7 6.3 %collective-permute-done.8.refs_0_ = bf16[256,640]{1,0:T(8,128)(2,1)S(1)} collective-permute-done((bf16[256,640]{1,0:T(8,128)(2,1)}, bf16[256,640]{1,0:T(8,128)(2,1)S(1)}, u32[]{:S(2)}, u32[]{:S(2)}) %collective-permute-start.8) | collective-permute-done | bytes 327712 | tf_op jit(solution)/shard_map/ppermute | solution.py:416
  179.4 5.4 %collective-permute-start.15 = (bf16[256,512]{1,0:T(8,128)(2,1)}, bf16[256,512]{1,0:T(8,128)(2,1)S(1)}, u32[]{:S(2)}, u32[]{:S(2)}) collective-permute-start(bf16[256,512]{1,0:T(8,128)(2,1)} %get-tuple-element.64.refs_2_), channel_id=1, source_target_pairs={{0,4},{2,6},{4,0},{6,2},{1,5},{3,7},{5,1},{7,3},{8,12},{10,14},{12... | collective-permute-start | bytes 786440 | tf_op jit(solution)/shard_map/ppermute | solution.py:428
  184.8 4.1 %collective-permute-done.14.refs_3_ = bf16[256,512]{1,0:T(8,128)(2,1)S(1)} collective-permute-done((bf16[256,512]{1,0:T(8,128)(2,1)}, bf16[256,512]{1,0:T(8,128)(2,1)S(1)}, u32[]{:S(2)}, u32[]{:S(2)}) %collective-permute-start.14) | collective-permute-done | bytes 262176 | tf_op jit(solution)/shard_map/ppermute | solution.py:428
  188.9 4.5 %collective-permute-start.18 = (bf16[256,512]{1,0:T(8,128)(2,1)S(1)}, bf16[256,512]{1,0:T(8,128)(2,1)S(1)}, u32[]{:S(2)}, u32[]{:S(2)}) collective-permute-start(bf16[256,512]{1,0:T(8,128)(2,1)S(1)} %collective-permute-done.14.refs_3_), channel_id=1, source_target_pairs={{0,1},{1,0},{2,3},{3,2},{4,5},{5,4},{6,7},{7,6},{8,9},{9,8},{10,11... | collective-permute-start | bytes 786440 | tf_op jit(solution)/shard_map/ppermute | solution.py:420
  194.5 3.0 %collective-permute-done.16.refs_5_ = bf16[256,512]{1,0:T(8,128)(2,1)S(1)} collective-permute-done((bf16[256,512]{1,0:T(8,128)(2,1)}, bf16[256,512]{1,0:T(8,128)(2,1)S(1)}, u32[]{:S(2)}, u32[]{:S(2)}) %collective-permute-start.16) | collective-permute-done | bytes 262176 | tf_op jit(solution)/shard_map/ppermute | solution.py:428
  197.9 3.3 %collective-permute-start.9 = (bf16[256,512]{1,0:T(8,128)(2,1)}, bf16[256,512]{1,0:T(8,128)(2,1)S(1)}, u32[]{:S(2)}, u32[]{:S(2)}) collective-permute-start(bf16[256,512]{1,0:T(8,128)(2,1)} %get-tuple-element.64.refs_2_), channel_id=1, source_target_pairs={{0,0},{1,4},{4,1},{5,5},{2,2},{3,6},{6,3},{7,7},{8,8},{9,12},{12,9... | collective-permute-start | bytes 786440 | tf_op jit(solution)/shard_map/ppermute | solution.py:416
  202.9 2.5 query_weight_grad.1
  206.3 2.2 grad_key_value.1.refs_3_
  210.0 5.0 %collective-permute-start.21 = (bf16[272,256]{1,0:T(8,128)(2,1)S(1)}, bf16[272,256]{1,0:T(8,128)(2,1)S(1)}, u32[]{:S(2)}, u32[]{:S(2)}) collective-permute-start(bf16[272,256]{1,0:T(8,128)(2,1)S(1)} %grad_key_value.1.refs_3_), channel_id=1, source_target_pairs={{0,0},{1,4},{4,1},{5,5},{2,2},{3,6},{6,3},{7,7},{8,8},{9,12},{12,9... | collective-permute-start | bytes 417800 | tf_op jit(solution)/shard_map/ppermute | solution.py:416
  215.7 2.2 collective-permute-start.27
  224.0 6.8 %all-to-all-start.4 = ((bf16[16,48,768]{2,1,0:T(8,128)(2,1)}), bf16[16,48,768]{2,1,0:T(8,128)(2,1)}, u32[]{:S(2)}, u32[]{:S(2)}) async-start(bf16[16,48,768]{2,1,0:T(8,128)(2,1)} %copy-done.11), calls=%async_computation.4 | async-start | bytes 2359296 | tf_op jit(solution)/shard_map/all_to_all | solution.py:556
  230.8 4.3 %collective-permute-start.7 = (bf16[256,512]{1,0:T(8,128)(2,1)S(1)}, bf16[256,512]{1,0:T(8,128)(2,1)S(1)}, u32[]{:S(2)}, u32[]{:S(2)}) collective-permute-start(bf16[256,512]{1,0:T(8,128)(2,1)S(1)} %copy-done.30), channel_id=1, source_target_pairs={{0,0},{1,4},{4,1},{5,5},{2,2},{3,6},{6,3},{7,7},{8,8},{9,12},{12,9... | collective-permute-start | bytes 786440 | tf_op jit(solution)/shard_map/ppermute | solution.py:416
  235.2 5.2 %collective-permute-done.7 = bf16[256,512]{1,0:T(8,128)(2,1)S(1)} collective-permute-done((bf16[256,512]{1,0:T(8,128)(2,1)S(1)}, bf16[256,512]{1,0:T(8,128)(2,1)S(1)}, u32[]{:S(2)}, u32[]{:S(2)}) %collective-permute-start.7) | collective-permute-done | bytes 262176 | tf_op jit(solution)/shard_map/ppermute | solution.py:416
  242.5 6.0 %grad_states.1 = bf16[256,5120]{1,0:T(8,128)(2,1)} custom-call(s32[2]{0:T(128)S(1)} %pad_add_fusion.refs_0_.where, bf16[256,512]{1,0:T(8,128)(2,1)S(1)} %collective-permute-done.9.refs_1_.refs_11_, bf16[272,256]{1,0:T(8,128)(2,1)S(1)} %collective-permute-done.21.refs_2_.refs_12_, bf16[2560,512]{1,0:T(8,128)(2,1)S(1)} %bitcast.22, ...), custom_call_target="tpu_custom_call" | custom-call | flops 1000 | bytes 1000 | tf_op jit(solution)/shard_map/grad_states/pallas_call | solution.py:396
  (133 shorter events, 54.4 us)
Async XLA Ops:
  2.5 28.4 %all-to-all-start = ((bf16[64,40,256]{2,1,0:T(8,128)(2,1)}), bf16[64,40,256]{2,1,0:T(8,128)(2,1)}, u32[]{:S(2)}, u32[]{:S(2)}) async-start(bf16[64,40,256]{2,1,0:T(8,128)(2,1)} %broadcast_in_dim.14), calls=%async_computation | async-start | bytes 2621440 | tf_op jit(solution)/shard_map/all_to_all | solution.py:424
  32.6 44.2 %all-to-all-start.1 = ((bf16[64,40,512]{2,1,0:T(8,128)(2,1)}), bf16[64,40,512]{2,1,0:T(8,128)(2,1)S(1)}, u32[]{:S(2)}, u32[]{:S(2)}) async-start(bf16[64,40,512]{2,1,0:T(8,128)(2,1)} %broadcast_in_dim.17), calls=%async_computation.1 | async-start | bytes 5242880 | tf_op jit(solution)/shard_map/all_to_all | solution.py:424
  40.4 5.0 %collective-permute-start = (bf16[2560,256]{1,0:T(8,128)(2,1)}, bf16[2560,256]{1,0:T(8,128)(2,1)S(1)}, u32[]{:S(2)}, u32[]{:S(2)}) collective-permute-start(bf16[2560,256]{1,0:T(8,128)(2,1)} %bitcast.7.refs_2_.refs_5_), channel_id=1, source_target_pairs={{0,1},{1,0},{2,3},{3,2},{4,5},{5,4},{6,7},{7,6},{8,9},{9,8},{10,11... | collective-permute-start | bytes 3932168 | tf_op jit(solution)/shard_map/ppermute | solution.py:420
  50.9 25.8 %collective-permute-start.1 = (bf16[256,256]{1,0:T(8,128)(2,1)S(1)}, bf16[256,256]{1,0:T(8,128)(2,1)S(1)}, u32[]{:S(2)}, u32[]{:S(2)}) collective-permute-start(bf16[256,256]{1,0:T(8,128)(2,1)S(1)} %get-tuple-element.50), channel_id=1, source_target_pairs={{0,0},{1,4},{4,1},{5,5},{2,2},{3,6},{6,3},{7,7},{8,8},{9,12},{12,9... | collective-permute-start | bytes 393224 | tf_op jit(solution)/shard_map/ppermute | solution.py:416
  78.3 17.0 %collective-permute-start.2 = (bf16[2560,512]{1,0:T(8,128)(2,1)S(1)}, bf16[2560,512]{1,0:T(8,128)(2,1)}, u32[]{:S(2)}, u32[]{:S(2)}) collective-permute-start(bf16[2560,512]{1,0:T(8,128)(2,1)S(1)} %bitcast.20), channel_id=1, source_target_pairs={{0,1},{1,0},{2,3},{3,2},{4,5},{5,4},{6,7},{7,6},{8,9},{9,8},{10,11... | collective-permute-start | bytes 7864328 | tf_op jit(solution)/shard_map/ppermute | solution.py:420
  78.3 33.8 %all-to-all-start.2 = ((bf16[16,256,256]{2,1,0:T(8,128)(2,1)}), bf16[16,256,256]{2,1,0:T(8,128)(2,1)}, u32[]{:S(2)}, u32[]{:S(2)}) async-start(bf16[16,256,256]{2,1,0:T(8,128)(2,1)} %broadcast_in_dim.16), calls=%async_computation.2 | async-start | bytes 4194304 | tf_op jit(solution)/shard_map/all_to_all | solution.py:491
  85.3 9.9 %collective-permute-start.3 = (bf16[256,512]{1,0:T(8,128)(2,1)}, bf16[256,512]{1,0:T(8,128)(2,1)S(1)}, u32[]{:S(2)}, u32[]{:S(2)}) collective-permute-start(bf16[256,512]{1,0:T(8,128)(2,1)} %bitcast.33), channel_id=1, source_target_pairs={{0,0},{1,4},{4,1},{5,5},{2,2},{3,6},{6,3},{7,7},{8,8},{9,12},{12,9... | collective-permute-start | bytes 786440 | tf_op jit(solution)/shard_map/ppermute | solution.py:416
  100.3 11.8 %collective-permute-start.5 = (bf16[256,512]{1,0:T(8,128)(2,1)}, bf16[256,512]{1,0:T(8,128)(2,1)S(1)}, u32[]{:S(2)}, u32[]{:S(2)}) collective-permute-start(bf16[256,512]{1,0:T(8,128)(2,1)} %get-tuple-element.58), channel_id=1, source_target_pairs={{0,0},{1,4},{4,1},{5,5},{2,2},{3,6},{6,3},{7,7},{8,8},{9,12},{12,9... | collective-permute-start | bytes 786440 | tf_op jit(solution)/shard_map/ppermute | solution.py:416
  112.1 5.5 %collective-permute-start.6 = (bf16[16,256,256]{2,1,0:T(8,128)(2,1)}, bf16[16,256,256]{2,1,0:T(8,128)(2,1)S(1)}, u32[]{:S(2)}, u32[]{:S(2)}) collective-permute-start(bf16[16,256,256]{2,1,0:T(8,128)(2,1)} %all-to-all-done.2.kv_ref), channel_id=1, source_target_pairs={{0,1},{1,0},{2,3},{3,2},{4,5},{5,4},{6,7},{7,6},{8,9},{9,8},{10,11... | collective-permute-start | bytes 6291464 | tf_op jit(solution)/shard_map/ppermute | solution.py:420
  113.6 37.2 %collective-permute-start.10 = (bf16[2,640,256]{2,1,0:T(8,128)(2,1)}, bf16[2,640,256]{2,1,0:T(8,128)(2,1)S(1)}, u32[]{:S(2)}, u32[]{:S(2)}) collective-permute-start(bf16[2,640,256]{2,1,0:T(8,128)(2,1)} %copy-done.27), channel_id=1, source_target_pairs={{0,6},{2,0},{4,2},{6,4},{1,7},{3,1},{5,3},{7,5},{8,14},{10,8},{12,... | collective-permute-start | bytes 1966088 | tf_op jit(solution)/shard_map/ppermute | solution.py:505
  113.6 37.2 %collective-permute-start.11 = (bf16[2,640,256]{2,1,0:T(8,128)(2,1)}, bf16[2,640,256]{2,1,0:T(8,128)(2,1)S(1)}, u32[]{:S(2)}, u32[]{:S(2)}) collective-permute-start(bf16[2,640,256]{2,1,0:T(8,128)(2,1)} %copy-done.26), channel_id=1, source_target_pairs={{0,4},{2,6},{4,0},{6,2},{1,5},{3,7},{5,1},{7,3},{8,12},{10,14},{12... | collective-permute-start | bytes 1966088 | tf_op jit(solution)/shard_map/ppermute | solution.py:505
  115.6 35.2 %collective-permute-start.12 = (bf16[2,640,256]{2,1,0:T(8,128)(2,1)}, bf16[2,640,256]{2,1,0:T(8,128)(2,1)S(1)}, u32[]{:S(2)}, u32[]{:S(2)}) collective-permute-start(bf16[2,640,256]{2,1,0:T(8,128)(2,1)} %copy-done.25), channel_id=1, source_target_pairs={{0,2},{2,4},{4,6},{6,0},{1,3},{3,5},{5,7},{7,1},{8,10},{10,12},{12... | collective-permute-start | bytes 1966088 | tf_op jit(solution)/shard_map/ppermute | solution.py:505
  153.1 4.2 %collective-permute-start.13 = (bf16[16,256,256]{2,1,0:T(8,128)(2,1)S(1)}, bf16[16,256,256]{2,1,0:T(8,128)(2,1)S(1)}, u32[]{:S(2)}, u32[]{:S(2)}) collective-permute-start(bf16[16,256,256]{2,1,0:T(8,128)(2,1)S(1)} %get-tuple-element.71), channel_id=1, source_target_pairs={{0,1},{1,0},{2,3},{3,2},{4,5},{5,4},{6,7},{7,6},{8,9},{9,8},{10,11... | collective-permute-start | bytes 6291464 | tf_op jit(solution)/shard_map/ppermute | solution.py:420
  159.3 47.1 %all-to-all-start.3 = ((bf16[16,256,256]{2,1,0:T(8,128)(2,1)}), bf16[16,256,256]{2,1,0:T(8,128)(2,1)}, u32[]{:S(2)}, u32[]{:S(2)}) async-start(bf16[16,256,256]{2,1,0:T(8,128)(2,1)} %add_convert_fusion), calls=%async_computation.3 | async-start | bytes 4194304 | tf_op jit(solution)/shard_map/all_to_all | solution.py:525
  166.4 10.5 %collective-permute-start.8 = (bf16[256,640]{1,0:T(8,128)(2,1)}, bf16[256,640]{1,0:T(8,128)(2,1)S(1)}, u32[]{:S(2)}, u32[]{:S(2)}) collective-permute-start(bf16[256,640]{1,0:T(8,128)(2,1)} %copy-done.28), channel_id=1, source_target_pairs={{0,0},{1,4},{4,1},{5,5},{2,2},{3,6},{6,3},{7,7},{8,8},{9,12},{12,9... | collective-permute-start | bytes 983048 | tf_op jit(solution)/shard_map/ppermute | solution.py:416
  179.4 9.5 %collective-permute-start.14 = (bf16[256,512]{1,0:T(8,128)(2,1)}, bf16[256,512]{1,0:T(8,128)(2,1)S(1)}, u32[]{:S(2)}, u32[]{:S(2)}) collective-permute-start(bf16[256,512]{1,0:T(8,128)(2,1)} %get-tuple-element.64.refs_2_), channel_id=1, source_target_pairs={{0,6},{2,0},{4,2},{6,4},{1,7},{3,1},{5,3},{7,5},{8,14},{10,8},{12,... | collective-permute-start | bytes 786440 | tf_op jit(solution)/shard_map/ppermute | solution.py:428
  179.4 14.0 %collective-permute-start.15 = (bf16[256,512]{1,0:T(8,128)(2,1)}, bf16[256,512]{1,0:T(8,128)(2,1)S(1)}, u32[]{:S(2)}, u32[]{:S(2)}) collective-permute-start(bf16[256,512]{1,0:T(8,128)(2,1)} %get-tuple-element.64.refs_2_), channel_id=1, source_target_pairs={{0,4},{2,6},{4,0},{6,2},{1,5},{3,7},{5,1},{7,3},{8,12},{10,14},{12... | collective-permute-start | bytes 786440 | tf_op jit(solution)/shard_map/ppermute | solution.py:428
  184.8 12.6 %collective-permute-start.16 = (bf16[256,512]{1,0:T(8,128)(2,1)}, bf16[256,512]{1,0:T(8,128)(2,1)S(1)}, u32[]{:S(2)}, u32[]{:S(2)}) collective-permute-start(bf16[256,512]{1,0:T(8,128)(2,1)} %get-tuple-element.64.refs_2_), channel_id=1, source_target_pairs={{0,2},{2,4},{4,6},{6,0},{1,3},{3,5},{5,7},{7,1},{8,10},{10,12},{12... | collective-permute-start | bytes 786440 | tf_op jit(solution)/shard_map/ppermute | solution.py:428
  184.8 16.3 %collective-permute-start.17 = (bf16[256,512]{1,0:T(8,128)(2,1)}, bf16[256,512]{1,0:T(8,128)(2,1)S(1)}, u32[]{:S(2)}, u32[]{:S(2)}) collective-permute-start(bf16[256,512]{1,0:T(8,128)(2,1)} %get-tuple-element.64.refs_2_), channel_id=1, source_target_pairs={{0,1},{1,0},{2,3},{3,2},{4,5},{5,4},{6,7},{7,6},{8,9},{9,8},{10,11... | collective-permute-start | bytes 786440 | tf_op jit(solution)/shard_map/ppermute | solution.py:420
  188.9 12.3 %collective-permute-start.18 = (bf16[256,512]{1,0:T(8,128)(2,1)S(1)}, bf16[256,512]{1,0:T(8,128)(2,1)S(1)}, u32[]{:S(2)}, u32[]{:S(2)}) collective-permute-start(bf16[256,512]{1,0:T(8,128)(2,1)S(1)} %collective-permute-done.14.refs_3_), channel_id=1, source_target_pairs={{0,1},{1,0},{2,3},{3,2},{4,5},{5,4},{6,7},{7,6},{8,9},{9,8},{10,11... | collective-permute-start | bytes 786440 | tf_op jit(solution)/shard_map/ppermute | solution.py:420
  193.4 7.8 %collective-permute-start.19 = (bf16[256,512]{1,0:T(8,128)(2,1)S(1)}, bf16[256,512]{1,0:T(8,128)(2,1)S(1)}, u32[]{:S(2)}, u32[]{:S(2)}) collective-permute-start(bf16[256,512]{1,0:T(8,128)(2,1)S(1)} %collective-permute-done.15.refs_4_), channel_id=1, source_target_pairs={{0,1},{1,0},{2,3},{3,2},{4,5},{5,4},{6,7},{7,6},{8,9},{9,8},{10,11... | collective-permute-start | bytes 786440 | tf_op jit(solution)/shard_map/ppermute | solution.py:420
  197.5 3.7 %collective-permute-start.20 = (bf16[256,512]{1,0:T(8,128)(2,1)S(1)}, bf16[256,512]{1,0:T(8,128)(2,1)S(1)}, u32[]{:S(2)}, u32[]{:S(2)}) collective-permute-start(bf16[256,512]{1,0:T(8,128)(2,1)S(1)} %collective-permute-done.16.refs_5_), channel_id=1, source_target_pairs={{0,1},{1,0},{2,3},{3,2},{4,5},{5,4},{6,7},{7,6},{8,9},{9,8},{10,11... | collective-permute-start | bytes 786440 | tf_op jit(solution)/shard_map/ppermute | solution.py:420
  197.9 17.2 %collective-permute-start.9 = (bf16[256,512]{1,0:T(8,128)(2,1)}, bf16[256,512]{1,0:T(8,128)(2,1)S(1)}, u32[]{:S(2)}, u32[]{:S(2)}) collective-permute-start(bf16[256,512]{1,0:T(8,128)(2,1)} %get-tuple-element.64.refs_2_), channel_id=1, source_target_pairs={{0,0},{1,4},{4,1},{5,5},{2,2},{3,6},{6,3},{7,7},{8,8},{9,12},{12,9... | collective-permute-start | bytes 786440 | tf_op jit(solution)/shard_map/ppermute | solution.py:416
  208.5 6.7 %collective-permute-start.22 = (bf16[272,256]{1,0:T(8,128)(2,1)S(1)}, bf16[272,256]{1,0:T(8,128)(2,1)S(1)}, u32[]{:S(2)}, u32[]{:S(2)}) collective-permute-start(bf16[272,256]{1,0:T(8,128)(2,1)S(1)} %grad_key_value.1.refs_3_), channel_id=1, source_target_pairs={{0,6},{2,0},{4,2},{6,4},{1,7},{3,1},{5,3},{7,5},{8,14},{10,8},{12,... | collective-permute-start | bytes 417800 | tf_op jit(solution)/shard_map/ppermute | solution.py:428
  208.6 7.1 %collective-permute-start.23 = (bf16[272,256]{1,0:T(8,128)(2,1)S(1)}, bf16[272,256]{1,0:T(8,128)(2,1)S(1)}, u32[]{:S(2)}, u32[]{:S(2)}) collective-permute-start(bf16[272,256]{1,0:T(8,128)(2,1)S(1)} %grad_key_value.1.refs_3_), channel_id=1, source_target_pairs={{0,4},{2,6},{4,0},{6,2},{1,5},{3,7},{5,1},{7,3},{8,12},{10,14},{12... | collective-permute-start | bytes 417800 | tf_op jit(solution)/shard_map/ppermute | solution.py:428
  209.8 8.4 %collective-permute-start.24 = (bf16[272,256]{1,0:T(8,128)(2,1)S(1)}, bf16[272,256]{1,0:T(8,128)(2,1)S(1)}, u32[]{:S(2)}, u32[]{:S(2)}) collective-permute-start(bf16[272,256]{1,0:T(8,128)(2,1)S(1)} %grad_key_value.1.refs_3_), channel_id=1, source_target_pairs={{0,2},{2,4},{4,6},{6,0},{1,3},{3,5},{5,7},{7,1},{8,10},{10,12},{12... | collective-permute-start | bytes 417800 | tf_op jit(solution)/shard_map/ppermute | solution.py:428
  210.0 10.3 %collective-permute-start.21 = (bf16[272,256]{1,0:T(8,128)(2,1)S(1)}, bf16[272,256]{1,0:T(8,128)(2,1)S(1)}, u32[]{:S(2)}, u32[]{:S(2)}) collective-permute-start(bf16[272,256]{1,0:T(8,128)(2,1)S(1)} %grad_key_value.1.refs_3_), channel_id=1, source_target_pairs={{0,0},{1,4},{4,1},{5,5},{2,2},{3,6},{6,3},{7,7},{8,8},{9,12},{12,9... | collective-permute-start | bytes 417800 | tf_op jit(solution)/shard_map/ppermute | solution.py:416
  215.1 5.3 %collective-permute-start.25 = (bf16[272,256]{1,0:T(8,128)(2,1)S(1)}, bf16[272,256]{1,0:T(8,128)(2,1)S(1)}, u32[]{:S(2)}, u32[]{:S(2)}) collective-permute-start(bf16[272,256]{1,0:T(8,128)(2,1)S(1)} %grad_key_value.1.refs_3_), channel_id=1, source_target_pairs={{0,1},{1,0},{2,3},{3,2},{4,5},{5,4},{6,7},{7,6},{8,9},{9,8},{10,11... | collective-permute-start | bytes 417800 | tf_op jit(solution)/shard_map/ppermute | solution.py:420
  215.2 5.2 %collective-permute-start.26 = (bf16[272,256]{1,0:T(8,128)(2,1)S(1)}, bf16[272,256]{1,0:T(8,128)(2,1)S(1)}, u32[]{:S(2)}, u32[]{:S(2)}) collective-permute-start(bf16[272,256]{1,0:T(8,128)(2,1)S(1)} %collective-permute-done.22.refs_4_), channel_id=1, source_target_pairs={{0,1},{1,0},{2,3},{3,2},{4,5},{5,4},{6,7},{7,6},{8,9},{9,8},{10,11... | collective-permute-start | bytes 417800 | tf_op jit(solution)/shard_map/ppermute | solution.py:420
  215.7 4.7 %collective-permute-start.27 = (bf16[272,256]{1,0:T(8,128)(2,1)S(1)}, bf16[272,256]{1,0:T(8,128)(2,1)S(1)}, u32[]{:S(2)}, u32[]{:S(2)}) collective-permute-start(bf16[272,256]{1,0:T(8,128)(2,1)S(1)} %collective-permute-done.23.refs_5_), channel_id=1, source_target_pairs={{0,1},{1,0},{2,3},{3,2},{4,5},{5,4},{6,7},{7,6},{8,9},{9,8},{10,11... | collective-permute-start | bytes 417800 | tf_op jit(solution)/shard_map/ppermute | solution.py:420
  224.0 24.4 %all-to-all-start.4 = ((bf16[16,48,768]{2,1,0:T(8,128)(2,1)}), bf16[16,48,768]{2,1,0:T(8,128)(2,1)}, u32[]{:S(2)}, u32[]{:S(2)}) async-start(bf16[16,48,768]{2,1,0:T(8,128)(2,1)} %copy-done.11), calls=%async_computation.4 | async-start | bytes 2359296 | tf_op jit(solution)/shard_map/all_to_all | solution.py:556
  230.8 9.6 %collective-permute-start.7 = (bf16[256,512]{1,0:T(8,128)(2,1)S(1)}, bf16[256,512]{1,0:T(8,128)(2,1)S(1)}, u32[]{:S(2)}, u32[]{:S(2)}) collective-permute-start(bf16[256,512]{1,0:T(8,128)(2,1)S(1)} %copy-done.30), channel_id=1, source_target_pairs={{0,0},{1,4},{4,1},{5,5},{2,2},{3,6},{6,3},{7,7},{8,8},{9,12},{12,9... | collective-permute-start | bytes 786440 | tf_op jit(solution)/shard_map/ppermute | solution.py:416
  (36 other events, 180.7 us)

commit v10 on v9

--- a/solution.py
+++ b/solution.py
@@ -82,7 +82,7 @@
         out_ref[1 - core] = other_ref[at]
 
 
-def place_kernel(where, dkv_ref, *refs):
+def place_kernel(where, dkv_ref, raw_ref, *refs):
     blocks, out_ref = refs[:-2], refs[-1]
     for k, block in enumerate(blocks):
         out_ref[lax.rem(where[0] + k, len(blocks))] = block[...]
@@ -108,7 +108,7 @@
 def attention_kernel(
     order, own, q_ref, g_ref, kv_ref, kv_other_ref, ctx_ref, dq_ref, dkv_ref, dkv_other_ref,
     slot_of, ks, vs, kt, vt, acc_kv, qs, gs, qt, gt, acc_o, row_max, row_sum, row_delta, acc_q,
-    sums, sums_other, sems,
+    sums, sems,
 ):
     spans, heads = order.shape[0], q_ref.shape[1] // span
     chunks = spans // per_chunk
@@ -134,10 +134,13 @@
             vs[c, part, :] = both[:, span:]
             kt[c, :, part] = both[:, :span].T
             vt[c, :, part] = both[:, span:].T
+        return carry
+
+    lax.fori_loop(0, chunks, arrange, 0)
+
+    def clear(c, carry):
         acc_kv[c] = jnp.zeros_like(acc_kv[c])
         return carry
-
-    lax.fori_loop(0, chunks, arrange, 0)
 
     first_upper = own[0] > own[1]
     for upper in (True, False):
@@ -179,7 +182,22 @@
             forward(c, False)
             return carry
 
-        lax.fori_loop(0, last, forward_step, 0)
+        def forward_pair(i, carry):
+            c = 2 * i
+            s = [mm(ks[c + j], qt[...]) for j in range(2)]
+            old = row_max[...]
+            new = jnp.maximum(old, jnp.max(jnp.maximum(s[0], s[1]), axis=0, keepdims=True))
+            p = [jnp.exp2(part - new) for part in s]
+            alpha = jnp.exp2(old - new)
+            row_max[...] = new
+            row_sum[...] = row_sum[...] * alpha + jnp.sum(p[0] + p[1], axis=0, keepdims=True)
+            acc_o[...] = (
+                acc_o[...] * alpha + mm(vt[c], p[0].astype(bf16)) + mm(vt[c + 1], p[1].astype(bf16))
+            )
+            return carry
+
+        lax.fori_loop(0, last // 2, forward_pair, 0)
+        lax.fori_loop(last // 2 * 2, last, forward_step, 0)
         forward(last, True)
 
         total = row_sum[...]
@@ -198,16 +216,41 @@
                 p = jnp.where(allowed(c), p, 0.0)
             dp = mm(vs[c], gt[...])
             ds = (p * (dp - row_delta[...])).astype(bf16)
-            acc_kv[c, :, span:] += mm(p.astype(bf16), gs[...])
-            acc_kv[c, :, :span] += mm(ds, qs[...])
+            dv, dk = mm(p.astype(bf16), gs[...]), mm(ds, qs[...])
+            if upper:
+                acc_kv[c, :, span:] = dv
+                acc_kv[c, :, :span] = dk
+            else:
+                acc_kv[c, :, span:] += dv
+                acc_kv[c, :, :span] += dk
             acc_q[...] += mm(kt[c], ds)
 
         def backward_step(c, carry):
             backward(c, False)
             return carry
 
-        lax.fori_loop(0, last, backward_step, 0)
+        def backward_pair(i, carry):
+            c = 2 * i
+            s = [mm(ks[c + j], qt[...]) for j in range(2)]
+            p = [jnp.exp2(part - row_max[...]) for part in s]
+            dp = [mm(vs[c + j], gt[...]) for j in range(2)]
+            ds = [(p[j] * (dp[j] - row_delta[...])).astype(bf16) for j in range(2)]
+            for j in range(2):
+                dv, dk = mm(p[j].astype(bf16), gs[...]), mm(ds[j], qs[...])
+                if upper:
+                    acc_kv[c + j, :, span:] = dv
+                    acc_kv[c + j, :, :span] = dk
+                else:
+                    acc_kv[c + j, :, span:] += dv
+                    acc_kv[c + j, :, :span] += dk
+            acc_q[...] += mm(kt[c], ds[0]) + mm(kt[c + 1], ds[1])
+            return carry
+
+        lax.fori_loop(0, last // 2, backward_pair, 0)
+        lax.fori_loop(last // 2 * 2, last, backward_step, 0)
         backward(last, True)
+        if upper:
+            lax.fori_loop(last + 1, chunks, clear, 0)
         for h in range(heads):
             part = slice(h * span, (h + 1) * span)
             dq_ref[pl.ds(row0, span), part] = acc_q[:, part].T * (span**-0.5)
@@ -217,26 +260,17 @@
             part = slice(j * span, (j + 1) * span)
             slot = slot_of[c * per_chunk + j]
             pair, rows_at = slot // 4, pl.multiple_of(slot % 2 * span, span)
-            mine = (slot // 2) % 2 == core
-            dk = (acc_kv[c, part, :span] * math.log(2.0)).astype(bf16)
-            dv = acc_kv[c, part, span:].astype(bf16)
-
-            @pl.when(mine)
-            def _():
-                sums[pair, pl.ds(rows_at, span), :span] = dk
-                sums[pair, pl.ds(rows_at, span), span:] = dv
-
-            @pl.when(jnp.logical_not(mine))
-            def _():
-                sums_other[pair, pl.ds(rows_at, span), :span] = dk
-                sums_other[pair, pl.ds(rows_at, span), span:] = dv
+            side = jnp.where((slot // 2) % 2 == core, 0, 1)
+            at = pl.ds(rows_at, span)
+            sums[side, pair, at, :span] = (acc_kv[c, part, :span] * math.log(2.0)).astype(bf16)
+            sums[side, pair, at, span:] = acc_kv[c, part, span:].astype(bf16)
 
         return carry
 
     lax.fori_loop(0, chunks, give, 0)
     copies = [
-        pltpu.make_async_copy(sums_other, dkv_other_ref, sems.at[0]),
-        pltpu.make_async_copy(sums, dkv_ref, sems.at[1]),
+        pltpu.make_async_copy(sums.at[1], dkv_other_ref, sems.at[0]),
+        pltpu.make_async_copy(sums.at[0], dkv_ref, sems.at[1]),
     ]
     for copy in copies:
         copy.start()
@@ -276,11 +310,10 @@
             pltpu.VMEM((1, rows), f32),
             pltpu.VMEM((1, rows), f32),
             pltpu.VMEM((span, rows), f32),
-            pltpu.VMEM(kv.shape, bf16),
-            pltpu.VMEM(kv.shape, bf16),
+            pltpu.VMEM((2,) + kv.shape, bf16),
             pltpu.SemaphoreType.DMA((2,)),
         ],
-        compiler_params=pltpu.CompilerParams(vmem_limit_bytes=32 * mib),
+        compiler_params=pltpu.CompilerParams(vmem_limit_bytes=36 * mib),
         cost_estimate=pl.CostEstimate(
             flops=1000, bytes_accessed=1000, transcendentals=0
         ),
@@ -468,10 +501,11 @@
         name="prepare",
         after=(cosine, sine, cos_there, sin_there),
     )
-    kv_mine, w_query, done, own = lax.optimization_barrier((kv_mine, w_query, done, own))
+    q_send = jnp.broadcast_to(w_query[None], (planes * columns, own_rows, q_cols))
+    kv_mine, q_send, done, own = lax.optimization_barrier((kv_mine, q_send, done, own))
     kv_mine = kv_mine.reshape(half, kv_cols)
     kv_theirs = flip(kv_mine)
-    q_mine = to_all(w_query, chips, planes * columns).reshape(half, q_cols)
+    q_mine = lax.all_to_all(q_send, chips, 0, 0).reshape(half, q_cols)
 
     kv16, raw_k = call(
         key_value_kernel,
@@ -513,13 +547,13 @@
             shape(dkv_theirs.shape, bf16),
             shape((columns, 2, half // columns, tok_rows), bf16),
         ),
-        in_specs=[smem, anywhere] + [vmem] * columns,
+        in_specs=[smem, anywhere] + [vmem] * (1 + columns),
         out_specs=(anywhere, vmem),
         input_output_aliases={1: 0},
         compiler_params=pltpu.CompilerParams(vmem_limit_bytes=16 * mib),
         cost_estimate=cheap,
         name="place",
-    )(where, dkv_theirs, turned[0], turned[3], turned[2], turned[1])
+    )(where, dkv_theirs, raw_there, turned[0], turned[3], turned[2], turned[1])
     turned = turned.reshape(2 * columns, half // columns, tok_rows)
     dkv = (dkv_mine.astype(f32) + flip(dkv_theirs).astype(f32)).astype(bf16)
     dkv = lax.all_to_all(dkv, plane, 0, 0)

time: 255 us -> 247 us (0.969)
  waiting for transfers between devices: 70.2 us -> 63.6 us
  local copies, waits for them, and re-layouts: 29.4 us -> 33.4 us
  Pallas kernels: 57.4 us -> 54.1 us
    all_to_all x0 -> x1, starting transfers between devices: none -> 7.85 us  [local(): q_mine = lax.all_to_all(q_send, chips, 0, 0).reshape(half, q_cols)]
    all_to_all x2 -> x1, starting transfers between devices: 18.7 us -> 10.8 us  [to_all(): lax.all_to_all(jnp.broadcast_to(array[None], (count,) + array.shape), axe...]
    ppermute x7, waiting for transfers between devices: 36.9 us -> 30 us  [swap(): return lax.ppermute(array, ('y_hi', 'core'), swapped)]
    unnamed x69 -> x75, local copies, waits for them, and re-layouts: 22.1 us -> 26.1 us
    ppermute x13, starting transfers between devices: 14.5 us -> 10.7 us  [flip(): return lax.ppermute(array, 'core', flipped)]
    pallas_call x1, Pallas kernels: 32.5 us -> 29.2 us  [attention(): pl.pallas_call(attention_kernel, out_shape=(jax.ShapeDtypeStruct((rows_he...]
    all_to_all x2 -> x1, waiting for transfers between devices: 6.53 us -> 7.06 us  [to_all(): lax.all_to_all(jnp.broadcast_to(array[None], (count,) + array.shape), axe...]
  transfers between devices with their start and end apart: 34 -> 34, of which waited for: 14 -> 10; matrix products, arithmetic and copies ran while one was open for 2% -> 2% of each run, Pallas kernels for 21% -> 21%
where the time goes in v10:
time: 247 us; the launch traced here: 243 us
  starting transfers between devices  86.1 us (35%)
  waiting for transfers between devices  63.6 us (26%)
  Pallas kernels  54.1 us (22%)
  local copies, waits for them, and re-layouts  33.4 us (14%)
  other arithmetic  4.4 us (2%)
    ppermute x7, waiting for transfers between devices, swap(): return lax.ppermute(array, ('y_hi', 'core'), swapped)  30 us
    pallas_call x1, Pallas kernels, attention(): pl.pallas_call(attention_kernel, out_shape=(jax.ShapeDtypeStruct((rows_he...  29.2 us
    unnamed x75, local copies, waits for them, and re-layouts  26.1 us
    ppermute x7, starting transfers between devices, swap(): return lax.ppermute(array, ('y_hi', 'core'), swapped)  26 us
    pallas_call x10, Pallas kernels, call(): pl.pallas_call(run, out_shape=shapes, in_specs=[smem if a.dtype == jnp.in...  24.1 us
    all_to_all x1, starting transfers between devices, to_all(): lax.all_to_all(jnp.broadcast_to(array[None], (count,) + array.shape), axe...  10.8 us
    ppermute x13, starting transfers between devices, flip(): return lax.ppermute(array, 'core', flipped)  10.7 us
    ppermute x6, waiting for transfers between devices, ring(): return lax.ppermute(array, column, [(i, (i - step) % 4) for i in range(4)])  9.8 us
  transfers between devices with their start and end apart: 34, of which 10 were waited for; matrix products, arithmetic and copies ran while one was open for 2% of the time, Pallas kernels for 21%

profile of v10, /device:TPU:39, one launch (start us, length us, event | category | flops | bytes accessed | tf_op | source)
XLA Modules:
  0.0 242.7 jit_solution(8085848096679046299)
XLA Ops:
  2.5 10.8 %all-to-all-start = ((bf16[64,40,256]{2,1,0:T(8,128)(2,1)}), bf16[64,40,256]{2,1,0:T(8,128)(2,1)}, u32[]{:S(2)}, u32[]{:S(2)}) async-start(bf16[64,40,256]{2,1,0:T(8,128)(2,1)} %broadcast_in_dim.14), calls=%async_computation | async-start | bytes 2621440 | tf_op jit(solution)/shard_map/all_to_all | solution.py:457
  13.4 3.0 %copy.16 = bf16[5120,256]{1,0:T(8,128)(2,1)S(1)} copy(bf16[5120,256]{0,1:T(8,128)(2,1)} %bitcast.30) | data formatting | bytes 5242880 | tf_op jit(solution)/shard_map/transpose | solution.py:500
  23.9 7.1 %all-to-all-done = bf16[64,40,256]{2,1,0:T(8,128)(2,1)} async-done(((bf16[64,40,256]{2,1,0:T(8,128)(2,1)}), bf16[64,40,256]{2,1,0:T(8,128)(2,1)}, u32[]{:S(2)}, u32[]{:S(2)}) %all-to-all-start) | async-done | bytes 1310752 | tf_op jit(solution)/shard_map/all_to_all | solution.py:457
  32.6 7.9 %all-to-all-start.1 = ((bf16[64,40,512]{2,1,0:T(8,128)(2,1)}), bf16[64,40,512]{2,1,0:T(8,128)(2,1)S(1)}, u32[]{:S(2)}, u32[]{:S(2)}) async-start(bf16[64,40,512]{2,1,0:T(8,128)(2,1)} %broadcast_in_dim.15), calls=%async_computation.1 | async-start | bytes 5242880 | tf_op jit(solution)/shard_map/all_to_all | solution.py:508
  40.4 2.2 collective-permute-start
  42.6 2.9 %collective-permute-done.refs_3_.refs_6_ = bf16[2560,256]{1,0:T(8,128)(2,1)S(1)} collective-permute-done((bf16[2560,256]{1,0:T(8,128)(2,1)}, bf16[2560,256]{1,0:T(8,128)(2,1)S(1)}, u32[]{:S(2)}, u32[]{:S(2)}) %collective-permute-start) | collective-permute-done | bytes 1310752 | tf_op jit(solution)/shard_map/ppermute | solution.py:453
  48.6 2.3 key_value.1
  51.6 4.9 %collective-permute-start.1 = (bf16[256,256]{1,0:T(8,128)(2,1)S(1)}, bf16[256,256]{1,0:T(8,128)(2,1)S(1)}, u32[]{:S(2)}, u32[]{:S(2)}) collective-permute-start(bf16[256,256]{1,0:T(8,128)(2,1)S(1)} %get-tuple-element.50), channel_id=1, source_target_pairs={{0,0},{1,4},{4,1},{5,5},{2,2},{3,6},{6,3},{7,7},{8,8},{9,12},{12,9... | collective-permute-start | bytes 393224 | tf_op jit(solution)/shard_map/ppermute | solution.py:449
  56.4 20.3 %collective-permute-done.1 = bf16[256,256]{1,0:T(8,128)(2,1)S(1)} collective-permute-done((bf16[256,256]{1,0:T(8,128)(2,1)S(1)}, bf16[256,256]{1,0:T(8,128)(2,1)S(1)}, u32[]{:S(2)}, u32[]{:S(2)}) %collective-permute-start.1) | collective-permute-done | bytes 131104 | tf_op jit(solution)/shard_map/ppermute | solution.py:449
  78.3 6.4 %all-to-all-start.2 = ((bf16[16,256,256]{2,1,0:T(8,128)(2,1)}), bf16[16,256,256]{2,1,0:T(8,128)(2,1)}, u32[]{:S(2)}, u32[]{:S(2)}) async-start(bf16[16,256,256]{2,1,0:T(8,128)(2,1)} %broadcast_in_dim.17), calls=%async_computation.2 | async-start | bytes 4194304 | tf_op jit(solution)/shard_map/all_to_all | solution.py:525
  85.3 2.0 collective-permute-start.3
  92.8 2.5 %collective-permute-done.3.refs_8_.g_ref = bf16[256,512]{1,0:T(8,128)(2,1)S(1)} collective-permute-done((bf16[256,512]{1,0:T(8,128)(2,1)}, bf16[256,512]{1,0:T(8,128)(2,1)S(1)}, u32[]{:S(2)}, u32[]{:S(2)}) %collective-permute-start.3) | collective-permute-done | bytes 262176 | tf_op jit(solution)/shard_map/ppermute | solution.py:449
  96.2 4.3 %query.1 = (bf16[256,512]{1,0:T(8,128)(2,1)}, bf16[256,640]{1,0:T(8,128)(2,1)S(1)}) custom-call(bf16[256,2560]{1,0:T(8,128)(2,1)S(1)} %copy-done.7, bf16[256,2560]{1,0:T(8,128)(2,1)S(1)} %copy-done.10, bf16[2560,512]{1,0:T(8,128)(2,1)S(1)} %bitcast.21, bf16[2560,512]{1,0:T(8,128)(2,1)} %collective-permute-done.2.refs_3_.refs_4_, f32[256,128]{1,0:T(8,128)S(1)} %copy-done.23, ...), custom_call_target="tpu_custom_call" | custom-call | flops 1000 | bytes 1000 | tf_op jit(solution)/shard_map/query/pallas_call | solution.py:429
  101.2 2.0 collective-permute-start.5
  103.2 8.9 %all-to-all-done.2.kv_ref = bf16[16,256,256]{2,1,0:T(8,128)(2,1)} async-done(((bf16[16,256,256]{2,1,0:T(8,128)(2,1)}), bf16[16,256,256]{2,1,0:T(8,128)(2,1)}, u32[]{:S(2)}, u32[]{:S(2)}) %all-to-all-start.2) | async-done | bytes 2097184 | tf_op jit(solution)/shard_map/all_to_all | solution.py:525
  114.3 2.0 collective-permute-start.11
  116.3 5.8 %collective-permute-start.8 = (bf16[256,640]{1,0:T(8,128)(2,1)}, bf16[256,640]{1,0:T(8,128)(2,1)S(1)}, u32[]{:S(2)}, u32[]{:S(2)}) collective-permute-start(bf16[256,640]{1,0:T(8,128)(2,1)} %copy-done.31), channel_id=1, source_target_pairs={{0,0},{1,4},{4,1},{5,5},{2,2},{3,6},{6,3},{7,7},{8,8},{9,12},{12,9... | collective-permute-start | bytes 983048 | tf_op jit(solution)/shard_map/ppermute | solution.py:449
  123.1 29.2 %attention.1 = (bf16[256,512]{1,0:T(8,128)(2,1)S(1)}, f32[256,512]{1,0:T(8,128)S(1)}, bf16[16,256,256]{2,1,0:T(8,128)(2,1)S(1)}, bf16[16,256,256]{2,1,0:T(8,128)(2,1)S(1)}) custom-call(s32[64]{0:T(128)S(1)} %copy-done.24, s32[3]{0:T(128)S(1)} %pad_add_fusion.1.own, bf16[256,512]{1,0:T(8,128)(2,1)S(1)} %copy-done.21, ...), custom_call_target="tpu_custom_call" | custom-call | flops 1000 | bytes 1000 | tf_op jit(solution)/shard_map/attention/pallas_call | solution.py:287
  155.3 4.2 %collective-permute-done.13 = bf16[16,256,256]{2,1,0:T(8,128)(2,1)S(1)} collective-permute-done((bf16[16,256,256]{2,1,0:T(8,128)(2,1)S(1)}, bf16[16,256,256]{2,1,0:T(8,128)(2,1)S(1)}, u32[]{:S(2)}, u32[]{:S(2)}) %collective-permute-start.13) | collective-permute-done | bytes 2097184 | tf_op jit(solution)/shard_map/ppermute | solution.py:453
  161.4 7.2 %all-to-all-start.3 = ((bf16[16,256,256]{2,1,0:T(8,128)(2,1)}), bf16[16,256,256]{2,1,0:T(8,128)(2,1)}, u32[]{:S(2)}, u32[]{:S(2)}) async-start(bf16[16,256,256]{2,1,0:T(8,128)(2,1)} %add_convert_fusion), calls=%async_computation.3 | async-start | bytes 4194304 | tf_op jit(solution)/shard_map/all_to_all | solution.py:559
  171.9 2.3 collective-permute-start.14
  175.5 9.8 %collective-permute-done.16.refs_5_ = bf16[256,512]{1,0:T(8,128)(2,1)S(1)} collective-permute-done((bf16[256,512]{1,0:T(8,128)(2,1)}, bf16[256,512]{1,0:T(8,128)(2,1)S(1)}, u32[]{:S(2)}, u32[]{:S(2)}) %collective-permute-start.16) | collective-permute-done | bytes 262176 | tf_op jit(solution)/shard_map/ppermute | solution.py:461
  187.4 3.1 %collective-permute-start.9 = (bf16[256,512]{1,0:T(8,128)(2,1)}, bf16[256,512]{1,0:T(8,128)(2,1)S(1)}, u32[]{:S(2)}, u32[]{:S(2)}) collective-permute-start(bf16[256,512]{1,0:T(8,128)(2,1)} %get-tuple-element.64.refs_2_), channel_id=1, source_target_pairs={{0,0},{1,4},{4,1},{5,5},{2,2},{3,6},{6,3},{7,7},{8,8},{9,12},{12,9... | collective-permute-start | bytes 786440 | tf_op jit(solution)/shard_map/ppermute | solution.py:449
  192.4 2.5 %query_weight_grad.1 = (bf16[640,512]{1,0:T(8,128)(2,1)S(1)}, f32[8,128]{1,0:T(8,128)S(1)}) custom-call(s32[2]{0:T(128)S(1)} %pad_add_fusion.refs_0_.where, bf16[8,640,256]{2,1,0:T(8,128)(2,1)S(1)} %bitcast.23, bf16[256,512]{1,0:T(8,128)(2,1)} %get-tuple-element.64.refs_2_, bf16[256,512]{1,0:T(8,128)(2,1)S(1)} %collective-permute-done.14.refs_3_, ...), custom_call_target="tpu_custom_call" | custom-call | flops 1000 | bytes 1000 | tf_op jit(solution)/shard_map/query_weight_grad/pallas_call | solution.py:429
  195.8 2.2 grad_key_value.1.refs_3_
  200.0 2.4 %collective-permute-start.22 = (bf16[272,256]{1,0:T(8,128)(2,1)S(1)}, bf16[272,256]{1,0:T(8,128)(2,1)S(1)}, u32[]{:S(2)}, u32[]{:S(2)}) collective-permute-start(bf16[272,256]{1,0:T(8,128)(2,1)S(1)} %grad_key_value.1.refs_3_), channel_id=1, source_target_pairs={{0,6},{2,0},{4,2},{6,4},{1,7},{3,1},{5,3},{7,5},{8,14},{10,8},{12,... | collective-permute-start | bytes 417800 | tf_op jit(solution)/shard_map/ppermute | solution.py:461
  203.4 3.8 %collective-permute-start.21 = (bf16[272,256]{1,0:T(8,128)(2,1)S(1)}, bf16[272,256]{1,0:T(8,128)(2,1)S(1)}, u32[]{:S(2)}, u32[]{:S(2)}) collective-permute-start(bf16[272,256]{1,0:T(8,128)(2,1)S(1)} %grad_key_value.1.refs_3_), channel_id=1, source_target_pairs={{0,0},{1,4},{4,1},{5,5},{2,2},{3,6},{6,3},{7,7},{8,8},{9,12},{12,9... | collective-permute-start | bytes 417800 | tf_op jit(solution)/shard_map/ppermute | solution.py:449
  214.9 7.5 %all-to-all-start.4 = ((bf16[16,48,768]{2,1,0:T(8,128)(2,1)}), bf16[16,48,768]{2,1,0:T(8,128)(2,1)}, u32[]{:S(2)}, u32[]{:S(2)}) async-start(bf16[16,48,768]{2,1,0:T(8,128)(2,1)} %copy-done.11), calls=%async_computation.4 | async-start | bytes 2359296 | tf_op jit(solution)/shard_map/all_to_all | solution.py:590
  222.4 4.4 %collective-permute-start.7 = (bf16[256,512]{1,0:T(8,128)(2,1)S(1)}, bf16[256,512]{1,0:T(8,128)(2,1)S(1)}, u32[]{:S(2)}, u32[]{:S(2)}) collective-permute-start(bf16[256,512]{1,0:T(8,128)(2,1)S(1)} %copy-done.33), channel_id=1, source_target_pairs={{0,0},{1,4},{4,1},{5,5},{2,2},{3,6},{6,3},{7,7},{8,8},{9,12},{12,9... | collective-permute-start | bytes 786440 | tf_op jit(solution)/shard_map/ppermute | solution.py:449
  226.7 5.2 %collective-permute-done.7 = bf16[256,512]{1,0:T(8,128)(2,1)S(1)} collective-permute-done((bf16[256,512]{1,0:T(8,128)(2,1)S(1)}, bf16[256,512]{1,0:T(8,128)(2,1)S(1)}, u32[]{:S(2)}, u32[]{:S(2)}) %collective-permute-start.7) | collective-permute-done | bytes 262176 | tf_op jit(solution)/shard_map/ppermute | solution.py:449
  234.0 6.0 %grad_states.1 = bf16[256,5120]{1,0:T(8,128)(2,1)} custom-call(s32[2]{0:T(128)S(1)} %pad_add_fusion.refs_0_.where, bf16[256,512]{1,0:T(8,128)(2,1)S(1)} %collective-permute-done.9.refs_1_.refs_11_, bf16[272,256]{1,0:T(8,128)(2,1)S(1)} %collective-permute-done.21.refs_2_.refs_12_, bf16[2560,512]{1,0:T(8,128)(2,1)S(1)} %bitcast.22, ...), custom_call_target="tpu_custom_call" | custom-call | flops 1000 | bytes 1000 | tf_op jit(solution)/shard_map/grad_states/pallas_call | solution.py:429
  239.9 2.0 finish.1
  (139 shorter events, 54.8 us)
Async XLA Ops:
  2.5 28.4 %all-to-all-start = ((bf16[64,40,256]{2,1,0:T(8,128)(2,1)}), bf16[64,40,256]{2,1,0:T(8,128)(2,1)}, u32[]{:S(2)}, u32[]{:S(2)}) async-start(bf16[64,40,256]{2,1,0:T(8,128)(2,1)} %broadcast_in_dim.14), calls=%async_computation | async-start | bytes 2621440 | tf_op jit(solution)/shard_map/all_to_all | solution.py:457
  32.6 44.2 %all-to-all-start.1 = ((bf16[64,40,512]{2,1,0:T(8,128)(2,1)}), bf16[64,40,512]{2,1,0:T(8,128)(2,1)S(1)}, u32[]{:S(2)}, u32[]{:S(2)}) async-start(bf16[64,40,512]{2,1,0:T(8,128)(2,1)} %broadcast_in_dim.15), calls=%async_computation.1 | async-start | bytes 5242880 | tf_op jit(solution)/shard_map/all_to_all | solution.py:508
  40.4 5.0 %collective-permute-start = (bf16[2560,256]{1,0:T(8,128)(2,1)}, bf16[2560,256]{1,0:T(8,128)(2,1)S(1)}, u32[]{:S(2)}, u32[]{:S(2)}) collective-permute-start(bf16[2560,256]{1,0:T(8,128)(2,1)} %bitcast.7.refs_2_.refs_5_), channel_id=1, source_target_pairs={{0,1},{1,0},{2,3},{3,2},{4,5},{5,4},{6,7},{7,6},{8,9},{9,8},{10,11... | collective-permute-start | bytes 3932168 | tf_op jit(solution)/shard_map/ppermute | solution.py:453
  51.6 25.2 %collective-permute-start.1 = (bf16[256,256]{1,0:T(8,128)(2,1)S(1)}, bf16[256,256]{1,0:T(8,128)(2,1)S(1)}, u32[]{:S(2)}, u32[]{:S(2)}) collective-permute-start(bf16[256,256]{1,0:T(8,128)(2,1)S(1)} %get-tuple-element.50), channel_id=1, source_target_pairs={{0,0},{1,4},{4,1},{5,5},{2,2},{3,6},{6,3},{7,7},{8,8},{9,12},{12,9... | collective-permute-start | bytes 393224 | tf_op jit(solution)/shard_map/ppermute | solution.py:449
  78.3 17.0 %collective-permute-start.2 = (bf16[2560,512]{1,0:T(8,128)(2,1)S(1)}, bf16[2560,512]{1,0:T(8,128)(2,1)}, u32[]{:S(2)}, u32[]{:S(2)}) collective-permute-start(bf16[2560,512]{1,0:T(8,128)(2,1)S(1)} %bitcast.20), channel_id=1, source_target_pairs={{0,1},{1,0},{2,3},{3,2},{4,5},{5,4},{6,7},{7,6},{8,9},{9,8},{10,11... | collective-permute-start | bytes 7864328 | tf_op jit(solution)/shard_map/ppermute | solution.py:453
  78.3 33.8 %all-to-all-start.2 = ((bf16[16,256,256]{2,1,0:T(8,128)(2,1)}), bf16[16,256,256]{2,1,0:T(8,128)(2,1)}, u32[]{:S(2)}, u32[]{:S(2)}) async-start(bf16[16,256,256]{2,1,0:T(8,128)(2,1)} %broadcast_in_dim.17), calls=%async_computation.2 | async-start | bytes 4194304 | tf_op jit(solution)/shard_map/all_to_all | solution.py:525
  84.7 3.5 %collective-permute-start.4 = (bf16[4,640,256]{2,1,0:T(8,128)(2,1)}, bf16[4,640,256]{2,1,0:T(8,128)(2,1)S(1)}, u32[]{:S(2)}, u32[]{:S(2)}) collective-permute-start(bf16[4,640,256]{2,1,0:T(8,128)(2,1)} %copy-done.27), channel_id=1, source_target_pairs={{0,1},{1,0},{2,3},{3,2},{4,5},{5,4},{6,7},{7,6},{8,9},{9,8},{10,11... | collective-permute-start | bytes 3932168 | tf_op jit(solution)/shard_map/ppermute | solution.py:453
  85.3 9.9 %collective-permute-start.3 = (bf16[256,512]{1,0:T(8,128)(2,1)}, bf16[256,512]{1,0:T(8,128)(2,1)S(1)}, u32[]{:S(2)}, u32[]{:S(2)}) collective-permute-start(bf16[256,512]{1,0:T(8,128)(2,1)} %bitcast.33), channel_id=1, source_target_pairs={{0,0},{1,4},{4,1},{5,5},{2,2},{3,6},{6,3},{7,7},{8,8},{9,12},{12,9... | collective-permute-start | bytes 786440 | tf_op jit(solution)/shard_map/ppermute | solution.py:449
  101.2 10.9 %collective-permute-start.5 = (bf16[256,512]{1,0:T(8,128)(2,1)}, bf16[256,512]{1,0:T(8,128)(2,1)S(1)}, u32[]{:S(2)}, u32[]{:S(2)}) collective-permute-start(bf16[256,512]{1,0:T(8,128)(2,1)} %get-tuple-element.58), channel_id=1, source_target_pairs={{0,0},{1,4},{4,1},{5,5},{2,2},{3,6},{6,3},{7,7},{8,8},{9,12},{12,9... | collective-permute-start | bytes 786440 | tf_op jit(solution)/shard_map/ppermute | solution.py:449
  112.8 9.3 %collective-permute-start.6 = (bf16[16,256,256]{2,1,0:T(8,128)(2,1)}, bf16[16,256,256]{2,1,0:T(8,128)(2,1)S(1)}, u32[]{:S(2)}, u32[]{:S(2)}) collective-permute-start(bf16[16,256,256]{2,1,0:T(8,128)(2,1)} %all-to-all-done.2.kv_ref), channel_id=1, source_target_pairs={{0,1},{1,0},{2,3},{3,2},{4,5},{5,4},{6,7},{7,6},{8,9},{9,8},{10,11... | collective-permute-start | bytes 6291464 | tf_op jit(solution)/shard_map/ppermute | solution.py:453
  114.3 38.7 %collective-permute-start.10 = (bf16[2,640,256]{2,1,0:T(8,128)(2,1)}, bf16[2,640,256]{2,1,0:T(8,128)(2,1)S(1)}, u32[]{:S(2)}, u32[]{:S(2)}) collective-permute-start(bf16[2,640,256]{2,1,0:T(8,128)(2,1)} %copy-done.30), channel_id=1, source_target_pairs={{0,6},{2,0},{4,2},{6,4},{1,7},{3,1},{5,3},{7,5},{8,14},{10,8},{12,... | collective-permute-start | bytes 1966088 | tf_op jit(solution)/shard_map/ppermute | solution.py:539
  114.3 38.7 %collective-permute-start.11 = (bf16[2,640,256]{2,1,0:T(8,128)(2,1)}, bf16[2,640,256]{2,1,0:T(8,128)(2,1)S(1)}, u32[]{:S(2)}, u32[]{:S(2)}) collective-permute-start(bf16[2,640,256]{2,1,0:T(8,128)(2,1)} %copy-done.29), channel_id=1, source_target_pairs={{0,4},{2,6},{4,0},{6,2},{1,5},{3,7},{5,1},{7,3},{8,12},{10,14},{12... | collective-permute-start | bytes 1966088 | tf_op jit(solution)/shard_map/ppermute | solution.py:539
  116.3 36.7 %collective-permute-start.12 = (bf16[2,640,256]{2,1,0:T(8,128)(2,1)}, bf16[2,640,256]{2,1,0:T(8,128)(2,1)S(1)}, u32[]{:S(2)}, u32[]{:S(2)}) collective-permute-start(bf16[2,640,256]{2,1,0:T(8,128)(2,1)} %copy-done.28), channel_id=1, source_target_pairs={{0,2},{2,4},{4,6},{6,0},{1,3},{3,5},{5,7},{7,1},{8,10},{10,12},{12... | collective-permute-start | bytes 1966088 | tf_op jit(solution)/shard_map/ppermute | solution.py:539
  116.3 36.7 %collective-permute-start.8 = (bf16[256,640]{1,0:T(8,128)(2,1)}, bf16[256,640]{1,0:T(8,128)(2,1)S(1)}, u32[]{:S(2)}, u32[]{:S(2)}) collective-permute-start(bf16[256,640]{1,0:T(8,128)(2,1)} %copy-done.31), channel_id=1, source_target_pairs={{0,0},{1,4},{4,1},{5,5},{2,2},{3,6},{6,3},{7,7},{8,8},{9,12},{12,9... | collective-permute-start | bytes 983048 | tf_op jit(solution)/shard_map/ppermute | solution.py:449
  155.3 4.2 %collective-permute-start.13 = (bf16[16,256,256]{2,1,0:T(8,128)(2,1)S(1)}, bf16[16,256,256]{2,1,0:T(8,128)(2,1)S(1)}, u32[]{:S(2)}, u32[]{:S(2)}) collective-permute-start(bf16[16,256,256]{2,1,0:T(8,128)(2,1)S(1)} %get-tuple-element.71), channel_id=1, source_target_pairs={{0,1},{1,0},{2,3},{3,2},{4,5},{5,4},{6,7},{7,6},{8,9},{9,8},{10,11... | collective-permute-start | bytes 6291464 | tf_op jit(solution)/shard_map/ppermute | solution.py:453
  161.4 34.4 %all-to-all-start.3 = ((bf16[16,256,256]{2,1,0:T(8,128)(2,1)}), bf16[16,256,256]{2,1,0:T(8,128)(2,1)}, u32[]{:S(2)}, u32[]{:S(2)}) async-start(bf16[16,256,256]{2,1,0:T(8,128)(2,1)} %add_convert_fusion), calls=%async_computation.3 | async-start | bytes 4194304 | tf_op jit(solution)/shard_map/all_to_all | solution.py:559
  171.0 14.3 %collective-permute-start.16 = (bf16[256,512]{1,0:T(8,128)(2,1)}, bf16[256,512]{1,0:T(8,128)(2,1)S(1)}, u32[]{:S(2)}, u32[]{:S(2)}) collective-permute-start(bf16[256,512]{1,0:T(8,128)(2,1)} %get-tuple-element.64.refs_2_), channel_id=1, source_target_pairs={{0,2},{2,4},{4,6},{6,0},{1,3},{3,5},{5,7},{7,1},{8,10},{10,12},{12... | collective-permute-start | bytes 786440 | tf_op jit(solution)/shard_map/ppermute | solution.py:461
  171.8 14.9 %collective-permute-start.15 = (bf16[256,512]{1,0:T(8,128)(2,1)}, bf16[256,512]{1,0:T(8,128)(2,1)S(1)}, u32[]{:S(2)}, u32[]{:S(2)}) collective-permute-start(bf16[256,512]{1,0:T(8,128)(2,1)} %get-tuple-element.64.refs_2_), channel_id=1, source_target_pairs={{0,4},{2,6},{4,0},{6,2},{1,5},{3,7},{5,1},{7,3},{8,12},{10,14},{12... | collective-permute-start | bytes 786440 | tf_op jit(solution)/shard_map/ppermute | solution.py:461
  171.9 14.9 %collective-permute-start.14 = (bf16[256,512]{1,0:T(8,128)(2,1)}, bf16[256,512]{1,0:T(8,128)(2,1)S(1)}, u32[]{:S(2)}, u32[]{:S(2)}) collective-permute-start(bf16[256,512]{1,0:T(8,128)(2,1)} %get-tuple-element.64.refs_2_), channel_id=1, source_target_pairs={{0,6},{2,0},{4,2},{6,4},{1,7},{3,1},{5,3},{7,5},{8,14},{10,8},{12,... | collective-permute-start | bytes 786440 | tf_op jit(solution)/shard_map/ppermute | solution.py:461
  174.2 16.3 %collective-permute-start.17 = (bf16[256,512]{1,0:T(8,128)(2,1)}, bf16[256,512]{1,0:T(8,128)(2,1)S(1)}, u32[]{:S(2)}, u32[]{:S(2)}) collective-permute-start(bf16[256,512]{1,0:T(8,128)(2,1)} %get-tuple-element.64.refs_2_), channel_id=1, source_target_pairs={{0,1},{1,0},{2,3},{3,2},{4,5},{5,4},{6,7},{7,6},{8,9},{9,8},{10,11... | collective-permute-start | bytes 786440 | tf_op jit(solution)/shard_map/ppermute | solution.py:453
  185.3 5.3 %collective-permute-start.20 = (bf16[256,512]{1,0:T(8,128)(2,1)S(1)}, bf16[256,512]{1,0:T(8,128)(2,1)S(1)}, u32[]{:S(2)}, u32[]{:S(2)}) collective-permute-start(bf16[256,512]{1,0:T(8,128)(2,1)S(1)} %collective-permute-done.16.refs_5_), channel_id=1, source_target_pairs={{0,1},{1,0},{2,3},{3,2},{4,5},{5,4},{6,7},{7,6},{8,9},{9,8},{10,11... | collective-permute-start | bytes 786440 | tf_op jit(solution)/shard_map/ppermute | solution.py:453
  186.8 3.8 %collective-permute-start.19 = (bf16[256,512]{1,0:T(8,128)(2,1)S(1)}, bf16[256,512]{1,0:T(8,128)(2,1)S(1)}, u32[]{:S(2)}, u32[]{:S(2)}) collective-permute-start(bf16[256,512]{1,0:T(8,128)(2,1)S(1)} %collective-permute-done.15.refs_4_), channel_id=1, source_target_pairs={{0,1},{1,0},{2,3},{3,2},{4,5},{5,4},{6,7},{7,6},{8,9},{9,8},{10,11... | collective-permute-start | bytes 786440 | tf_op jit(solution)/shard_map/ppermute | solution.py:453
  186.8 3.8 %collective-permute-start.18 = (bf16[256,512]{1,0:T(8,128)(2,1)S(1)}, bf16[256,512]{1,0:T(8,128)(2,1)S(1)}, u32[]{:S(2)}, u32[]{:S(2)}) collective-permute-start(bf16[256,512]{1,0:T(8,128)(2,1)S(1)} %collective-permute-done.14.refs_3_), channel_id=1, source_target_pairs={{0,1},{1,0},{2,3},{3,2},{4,5},{5,4},{6,7},{7,6},{8,9},{9,8},{10,11... | collective-permute-start | bytes 786440 | tf_op jit(solution)/shard_map/ppermute | solution.py:453
  187.4 15.9 %collective-permute-start.9 = (bf16[256,512]{1,0:T(8,128)(2,1)}, bf16[256,512]{1,0:T(8,128)(2,1)S(1)}, u32[]{:S(2)}, u32[]{:S(2)}) collective-permute-start(bf16[256,512]{1,0:T(8,128)(2,1)} %get-tuple-element.64.refs_2_), channel_id=1, source_target_pairs={{0,0},{1,4},{4,1},{5,5},{2,2},{3,6},{6,3},{7,7},{8,8},{9,12},{12,9... | collective-permute-start | bytes 786440 | tf_op jit(solution)/shard_map/ppermute | solution.py:449
  197.9 9.2 %collective-permute-start.24 = (bf16[272,256]{1,0:T(8,128)(2,1)S(1)}, bf16[272,256]{1,0:T(8,128)(2,1)S(1)}, u32[]{:S(2)}, u32[]{:S(2)}) collective-permute-start(bf16[272,256]{1,0:T(8,128)(2,1)S(1)} %grad_key_value.1.refs_3_), channel_id=1, source_target_pairs={{0,2},{2,4},{4,6},{6,0},{1,3},{3,5},{5,7},{7,1},{8,10},{10,12},{12... | collective-permute-start | bytes 417800 | tf_op jit(solution)/shard_map/ppermute | solution.py:461
  199.9 8.8 %collective-permute-start.23 = (bf16[272,256]{1,0:T(8,128)(2,1)S(1)}, bf16[272,256]{1,0:T(8,128)(2,1)S(1)}, u32[]{:S(2)}, u32[]{:S(2)}) collective-permute-start(bf16[272,256]{1,0:T(8,128)(2,1)S(1)} %grad_key_value.1.refs_3_), channel_id=1, source_target_pairs={{0,4},{2,6},{4,0},{6,2},{1,5},{3,7},{5,1},{7,3},{8,12},{10,14},{12... | collective-permute-start | bytes 417800 | tf_op jit(solution)/shard_map/ppermute | solution.py:461
  200.0 8.8 %collective-permute-start.22 = (bf16[272,256]{1,0:T(8,128)(2,1)S(1)}, bf16[272,256]{1,0:T(8,128)(2,1)S(1)}, u32[]{:S(2)}, u32[]{:S(2)}) collective-permute-start(bf16[272,256]{1,0:T(8,128)(2,1)S(1)} %grad_key_value.1.refs_3_), channel_id=1, source_target_pairs={{0,6},{2,0},{4,2},{6,4},{1,7},{3,1},{5,3},{7,5},{8,14},{10,8},{12,... | collective-permute-start | bytes 417800 | tf_op jit(solution)/shard_map/ppermute | solution.py:461
  202.4 6.9 %collective-permute-start.25 = (bf16[272,256]{1,0:T(8,128)(2,1)S(1)}, bf16[272,256]{1,0:T(8,128)(2,1)S(1)}, u32[]{:S(2)}, u32[]{:S(2)}) collective-permute-start(bf16[272,256]{1,0:T(8,128)(2,1)S(1)} %grad_key_value.1.refs_3_), channel_id=1, source_target_pairs={{0,1},{1,0},{2,3},{3,2},{4,5},{5,4},{6,7},{7,6},{8,9},{9,8},{10,11... | collective-permute-start | bytes 417800 | tf_op jit(solution)/shard_map/ppermute | solution.py:453
  203.4 7.9 %collective-permute-start.21 = (bf16[272,256]{1,0:T(8,128)(2,1)S(1)}, bf16[272,256]{1,0:T(8,128)(2,1)S(1)}, u32[]{:S(2)}, u32[]{:S(2)}) collective-permute-start(bf16[272,256]{1,0:T(8,128)(2,1)S(1)} %grad_key_value.1.refs_3_), channel_id=1, source_target_pairs={{0,0},{1,4},{4,1},{5,5},{2,2},{3,6},{6,3},{7,7},{8,8},{9,12},{12,9... | collective-permute-start | bytes 417800 | tf_op jit(solution)/shard_map/ppermute | solution.py:449
  207.2 4.0 %collective-permute-start.28 = (bf16[272,256]{1,0:T(8,128)(2,1)S(1)}, bf16[272,256]{1,0:T(8,128)(2,1)S(1)}, u32[]{:S(2)}, u32[]{:S(2)}) collective-permute-start(bf16[272,256]{1,0:T(8,128)(2,1)S(1)} %collective-permute-done.24.refs_6_), channel_id=1, source_target_pairs={{0,1},{1,0},{2,3},{3,2},{4,5},{5,4},{6,7},{7,6},{8,9},{9,8},{10,11... | collective-permute-start | bytes 417800 | tf_op jit(solution)/shard_map/ppermute | solution.py:453
  214.9 25.0 %all-to-all-start.4 = ((bf16[16,48,768]{2,1,0:T(8,128)(2,1)}), bf16[16,48,768]{2,1,0:T(8,128)(2,1)}, u32[]{:S(2)}, u32[]{:S(2)}) async-start(bf16[16,48,768]{2,1,0:T(8,128)(2,1)} %copy-done.11), calls=%async_computation.4 | async-start | bytes 2359296 | tf_op jit(solution)/shard_map/all_to_all | solution.py:590
  222.4 9.6 %collective-permute-start.7 = (bf16[256,512]{1,0:T(8,128)(2,1)S(1)}, bf16[256,512]{1,0:T(8,128)(2,1)S(1)}, u32[]{:S(2)}, u32[]{:S(2)}) collective-permute-start(bf16[256,512]{1,0:T(8,128)(2,1)S(1)} %copy-done.33), channel_id=1, source_target_pairs={{0,0},{1,4},{4,1},{5,5},{2,2},{3,6},{6,3},{7,7},{8,8},{9,12},{12,9... | collective-permute-start | bytes 786440 | tf_op jit(solution)/shard_map/ppermute | solution.py:449
  (39 other events, 179.3 us)

commit v11 on v10

--- a/solution.py
+++ b/solution.py
@@ -51,10 +51,16 @@
     return inverse * (grad_unit - unit * shrink), grad_normed * unit
 
 
-def prepare_kernel(where, src_ref, toks_ref, toks_theirs_ref, turned_ref, turned_theirs_ref, done_ref):
+def spread_kernel(block_ref, out_ref):
+    for i in range(out_ref.shape[0]):
+        out_ref[i] = block_ref[...]
+
+
+def prepare_kernel(where, src_ref, w_ref, send_ref, toks_ref, toks_theirs_ref, turned_ref, turned_theirs_ref, done_ref):
     planes, columns = src_ref.shape[:2]
     core = where[1]
     done_ref[...] = jnp.zeros_like(done_ref)
+    spread_kernel(w_ref, send_ref)
 
     def piece(plane, y, side):
         return src_ref[plane, y, side].astype(f32)
@@ -83,9 +89,15 @@
 
 
 def place_kernel(where, dkv_ref, raw_ref, *refs):
-    blocks, out_ref = refs[:-2], refs[-1]
-    for k, block in enumerate(blocks):
-        out_ref[lax.rem(where[0] + k, len(blocks))] = block[...]
+    blocks, out_ref, sems = refs[:-3], refs[-2], refs[-1]
+    copies = [
+        pltpu.make_async_copy(block, out_ref.at[lax.rem(where[0] + k, len(blocks))], sems.at[k])
+        for k, block in enumerate(blocks)
+    ]
+    for copy in copies:
+        copy.start()
+    for copy in copies:
+        copy.wait()
 
 
 def key_value_kernel(mine_ref, other_ref, w_ref, w_other_ref, gain_ref, cos_ref, sin_ref, kv_ref, raw_ref):
@@ -371,7 +383,7 @@
 
 
 def weight_grad_kernel(where, turned_ref, query_ref, *rest):
-    blocks, out_ref = rest[:-1], rest[-1]
+    blocks, (out_ref, parts, sems) = rest[:-3], rest[-3:]
     toks = turned_ref.shape[2]
     gains = sum(block[toks:].astype(f32) for block in blocks)
     gain = gains[:8, :span] + gains[:8, span:]
@@ -381,9 +393,14 @@
         [query_ref[...].astype(f32), over_tokens(where, turned_ref, blocks)], axis=1
     )
     own_rows = total.shape[0] // out_ref.shape[0]
+    copies = []
     for i in range(out_ref.shape[0]):
         part = total[i * own_rows : (i + 1) * own_rows]
-        out_ref[i] = jnp.concatenate([part, extra], axis=0).astype(bf16)
+        parts[i] = jnp.concatenate([part, extra], axis=0).astype(bf16)
+        copies.append(pltpu.make_async_copy(parts.at[i], out_ref.at[i], sems.at[i]))
+        copies[-1].start()
+    for copy in copies:
+        copy.wait()
 
 
 def grad_states_kernel(where, gq_ref, gkv_ref, q_ref, q_theirs_ref, kv_ref, kv_theirs_ref, out_ref):
@@ -420,7 +437,7 @@
 cheap = pl.CostEstimate(flops=1000, bytes_accessed=1000, transcendentals=0)
 
 
-def call(kernel, shapes, *args, name, after=(), limit=16, scratch=()):
+def call(kernel, shapes, *args, name, after=(), limit=16, scratch=(), out_spec=vmem):
     count = len(args)
 
     def run(*refs):
@@ -430,7 +447,7 @@
         run,
         out_shape=shapes,
         in_specs=[smem if a.dtype == jnp.int32 else vmem for a in args] + [vmem] * len(after),
-        out_specs=jax.tree.map(lambda _: vmem, shapes),
+        out_specs=jax.tree.map(lambda _: out_spec, shapes),
         scratch_shapes=scratch,
         compiler_params=pltpu.CompilerParams(vmem_limit_bytes=limit * mib),
         cost_estimate=cheap,
@@ -492,16 +509,16 @@
     shape = jax.ShapeDtypeStruct
 
     kv_mine = to_all(jnp.concatenate([w_key, w_value], axis=1), chips, planes * columns)
-    toks_mine, toks_theirs, turned, turned_theirs, done = call(
+    q_send, toks_mine, toks_theirs, turned, turned_theirs, done = call(
         prepare_kernel,
-        (shape((tok_rows, half), bf16),) * 2
+        (shape((planes * columns, own_rows, q_cols), bf16),)
+        + (shape((tok_rows, half), bf16),) * 2
         + (shape((columns, half // columns, tok_rows), bf16),) * 2
         + (shape((8, span), f32),),
-        where, tokens.T.reshape(planes, columns, 2, own_rows, tok_rows),
+        where, tokens.T.reshape(planes, columns, 2, own_rows, tok_rows), w_query,
         name="prepare",
         after=(cosine, sine, cos_there, sin_there),
     )
-    q_send = jnp.broadcast_to(w_query[None], (planes * columns, own_rows, q_cols))
     kv_mine, q_send, done, own = lax.optimization_barrier((kv_mine, q_send, done, own))
     kv_mine = kv_mine.reshape(half, kv_cols)
     kv_theirs = flip(kv_mine)
@@ -514,7 +531,9 @@
         name="key_value",
         after=(done,),
     )
-    kv_send = jnp.broadcast_to(swap(kv16)[None], (planes, tok_rows, kv_cols))
+    kv_send = call(
+        spread_kernel, shape((planes, tok_rows, kv_cols), bf16), swap(kv16), name="spread"
+    )
     *packed, packed_done = call(
         pack_kernel,
         (shape((2, half // columns, tok_rows), bf16),) * columns + (shape((8, span), f32),),
@@ -548,7 +567,8 @@
             shape((columns, 2, half // columns, tok_rows), bf16),
         ),
         in_specs=[smem, anywhere] + [vmem] * (1 + columns),
-        out_specs=(anywhere, vmem),
+        out_specs=(anywhere, anywhere),
+        scratch_shapes=[pltpu.SemaphoreType.DMA((columns,))],
         input_output_aliases={1: 0},
         compiler_params=pltpu.CompilerParams(vmem_limit_bytes=16 * mib),
         cost_estimate=cheap,
@@ -580,12 +600,15 @@
     )
     blocks_kv = around(g_kv)
     g_kv_back = swap(g_kv)
+    all_parts = shape((planes, own_rows + 8, q_cols + kv_cols), bf16)
     parts = call(
         weight_grad_kernel,
-        shape((planes, own_rows + 8, q_cols + kv_cols), bf16),
+        all_parts,
         where, turned, query_parts, *blocks_kv,
         name="weight_grad",
-        after=(g_q_back, g_kv_back),
+        after=(g_q_back,),
+        out_spec=anywhere,
+        scratch=[pltpu.VMEM(all_parts.shape, bf16), pltpu.SemaphoreType.DMA((planes,))],
     )
     parts = lax.all_to_all(parts, plane, 0, 0)
     own_query, own_key, own_value, gain_sum_q, gain_sum_k = call(

time: 247 us -> 247 us (level)
    unnamed x75 -> x81, local copies, waits for them, and re-layouts: 26.1 us -> 29.5 us
    broadcast_in_dim x2 -> x0, local copies, waits for them, and re-layouts: 3.18 us -> none  [the longest x1 1.66 us: local(): jnp.broadcast_to(w_query[None], (planes * columns, own_rows, q_cols))]
    all_to_all x1, waiting for transfers between devices: 0.01 us -> 3.13 us  [local(): dkv = lax.all_to_all(dkv, plane, 0, 0)]
    all_to_all x1, waiting for transfers between devices: 8.87 us -> 5.77 us  [local(): kv_own = lax.all_to_all(kv_send, plane, 0, 0)]
    pallas_call x10 -> x11, Pallas kernels: 24.1 us -> 25 us  [call(): pl.pallas_call(run, out_shape=shapes, in_specs=[smem if a.dtype == jnp.in...]
  transfers between devices with their start and end apart: 34 -> 34, of which waited for: 10 -> 16; matrix products, arithmetic and copies ran while one was open for 2% -> 2% of each run, Pallas kernels for 21% -> 19%
where the time goes in v11:
time: 247 us; the launch traced here: 245 us
  starting transfers between devices  86.5 us (35%)
  waiting for transfers between devices  63.5 us (26%)
  Pallas kernels  55.5 us (22%)
  local copies, waits for them, and re-layouts  33.7 us (14%)
  other arithmetic  4.4 us (2%)
    ppermute x7, waiting for transfers between devices, swap(): return lax.ppermute(array, ('y_hi', 'core'), swapped)  30.7 us
    unnamed x81, local copies, waits for them, and re-layouts  29.5 us
    pallas_call x1, Pallas kernels, attention(): pl.pallas_call(attention_kernel, out_shape=(jax.ShapeDtypeStruct((rows_he...  29 us
    ppermute x7, starting transfers between devices, swap(): return lax.ppermute(array, ('y_hi', 'core'), swapped)  28.4 us
    pallas_call x11, Pallas kernels, call(): pl.pallas_call(run, out_shape=shapes, in_specs=[smem if a.dtype == jnp.in...  25 us
    all_to_all x1, starting transfers between devices, to_all(): lax.all_to_all(jnp.broadcast_to(array[None], (count,) + array.shape), axe...  10.8 us
    ppermute x13, starting transfers between devices, flip(): return lax.ppermute(array, 'core', flipped)  10.3 us
    ppermute x13, waiting for transfers between devices, flip(): return lax.ppermute(array, 'core', flipped)  9.29 us
  transfers between devices with their start and end apart: 34, of which 16 were waited for; matrix products, arithmetic and copies ran while one was open for 2% of the time, Pallas kernels for 19%

profile of v11, /device:TPU:39, one launch (start us, length us, event | category | flops | bytes accessed | tf_op | source)
XLA Modules:
  0.0 244.8 jit_solution(8825915965197405118)
XLA Ops:
  2.5 10.8 %all-to-all-start = ((bf16[64,40,256]{2,1,0:T(8,128)(2,1)}), bf16[64,40,256]{2,1,0:T(8,128)(2,1)}, u32[]{:S(2)}, u32[]{:S(2)}) async-start(bf16[64,40,256]{2,1,0:T(8,128)(2,1)} %broadcast_in_dim.10), calls=%async_computation | async-start | bytes 2621440 | tf_op jit(solution)/shard_map/all_to_all | solution.py:474
  13.4 3.0 %copy.16 = bf16[5120,256]{1,0:T(8,128)(2,1)S(1)} copy(bf16[5120,256]{0,1:T(8,128)(2,1)} %bitcast.30) | data formatting | bytes 5242880 | tf_op jit(solution)/shard_map/transpose | solution.py:518
  25.5 5.4 %all-to-all-done = bf16[64,40,256]{2,1,0:T(8,128)(2,1)} async-done(((bf16[64,40,256]{2,1,0:T(8,128)(2,1)}), bf16[64,40,256]{2,1,0:T(8,128)(2,1)}, u32[]{:S(2)}, u32[]{:S(2)}) %all-to-all-start) | async-done | bytes 1310752 | tf_op jit(solution)/shard_map/all_to_all | solution.py:474
  30.9 7.9 %all-to-all-start.1 = ((bf16[64,40,512]{2,1,0:T(8,128)(2,1)}), bf16[64,40,512]{2,1,0:T(8,128)(2,1)S(1)}, u32[]{:S(2)}, u32[]{:S(2)}) async-start(bf16[64,40,512]{2,1,0:T(8,128)(2,1)} %copy-done.13), calls=%async_computation.1 | async-start | bytes 5242880 | tf_op jit(solution)/shard_map/all_to_all | solution.py:525
  38.8 2.2 collective-permute-start
  41.0 2.9 %collective-permute-done.refs_3_.refs_6_ = bf16[2560,256]{1,0:T(8,128)(2,1)S(1)} collective-permute-done((bf16[2560,256]{1,0:T(8,128)(2,1)}, bf16[2560,256]{1,0:T(8,128)(2,1)S(1)}, u32[]{:S(2)}, u32[]{:S(2)}) %collective-permute-start) | collective-permute-done | bytes 1310752 | tf_op jit(solution)/shard_map/ppermute | solution.py:470
  46.9 2.3 key_value.1
  49.9 4.9 %collective-permute-start.1 = (bf16[256,256]{1,0:T(8,128)(2,1)S(1)}, bf16[256,256]{1,0:T(8,128)(2,1)S(1)}, u32[]{:S(2)}, u32[]{:S(2)}) collective-permute-start(bf16[256,256]{1,0:T(8,128)(2,1)S(1)} %get-tuple-element.52), channel_id=1, source_target_pairs={{0,0},{1,4},{4,1},{5,5},{2,2},{3,6},{6,3},{7,7},{8,8},{9,12},{12,9... | collective-permute-start | bytes 393224 | tf_op jit(solution)/shard_map/ppermute | solution.py:466
  54.8 20.3 %collective-permute-done.1.refs_0_ = bf16[256,256]{1,0:T(8,128)(2,1)S(1)} collective-permute-done((bf16[256,256]{1,0:T(8,128)(2,1)S(1)}, bf16[256,256]{1,0:T(8,128)(2,1)S(1)}, u32[]{:S(2)}, u32[]{:S(2)}) %collective-permute-start.1) | collective-permute-done | bytes 131104 | tf_op jit(solution)/shard_map/ppermute | solution.py:466
  76.6 5.0 %all-to-all-start.2 = ((bf16[16,256,256]{2,1,0:T(8,128)(2,1)}), bf16[16,256,256]{2,1,0:T(8,128)(2,1)}, u32[]{:S(2)}, u32[]{:S(2)}) async-start(bf16[16,256,256]{2,1,0:T(8,128)(2,1)} %copy-done.3), calls=%async_computation.2 | async-start | bytes 4194304 | tf_op jit(solution)/shard_map/all_to_all | solution.py:544
  93.5 4.3 %query.1 = (bf16[256,512]{1,0:T(8,128)(2,1)}, bf16[256,640]{1,0:T(8,128)(2,1)S(1)}) custom-call(bf16[256,2560]{1,0:T(8,128)(2,1)S(1)} %copy-done.8, bf16[256,2560]{1,0:T(8,128)(2,1)S(1)} %copy-done.11, bf16[2560,512]{1,0:T(8,128)(2,1)S(1)} %bitcast.21, bf16[2560,512]{1,0:T(8,128)(2,1)} %collective-permute-done.2.refs_3_.refs_4_, f32[256,128]{1,0:T(8,128)S(1)} %copy-done.26, ...), custom_call_target="tpu_custom_call" | custom-call | flops 1000 | bytes 1000 | tf_op jit(solution)/shard_map/query/pallas_call | solution.py:446
  98.5 2.7 %collective-permute-start.5 = (bf16[256,512]{1,0:T(8,128)(2,1)}, bf16[256,512]{1,0:T(8,128)(2,1)S(1)}, u32[]{:S(2)}, u32[]{:S(2)}) collective-permute-start(bf16[256,512]{1,0:T(8,128)(2,1)} %get-tuple-element.60), channel_id=1, source_target_pairs={{0,0},{1,4},{4,1},{5,5},{2,2},{3,6},{6,3},{7,7},{8,8},{9,12},{12,9... | collective-permute-start | bytes 786440 | tf_op jit(solution)/shard_map/ppermute | solution.py:466
  101.1 5.8 %all-to-all-done.2.kv_ref = bf16[16,256,256]{2,1,0:T(8,128)(2,1)} async-done(((bf16[16,256,256]{2,1,0:T(8,128)(2,1)}), bf16[16,256,256]{2,1,0:T(8,128)(2,1)}, u32[]{:S(2)}, u32[]{:S(2)}) %all-to-all-start.2) | async-done | bytes 2097184 | tf_op jit(solution)/shard_map/all_to_all | solution.py:544
  113.2 5.1 %collective-permute-start.8 = (bf16[256,640]{1,0:T(8,128)(2,1)}, bf16[256,640]{1,0:T(8,128)(2,1)S(1)}, u32[]{:S(2)}, u32[]{:S(2)}) collective-permute-start(bf16[256,640]{1,0:T(8,128)(2,1)} %copy-done.35), channel_id=1, source_target_pairs={{0,0},{1,4},{4,1},{5,5},{2,2},{3,6},{6,3},{7,7},{8,8},{9,12},{12,9... | collective-permute-start | bytes 983048 | tf_op jit(solution)/shard_map/ppermute | solution.py:466
  119.2 29.0 %attention.1 = (bf16[256,512]{1,0:T(8,128)(2,1)S(1)}, f32[256,512]{1,0:T(8,128)S(1)}, bf16[16,256,256]{2,1,0:T(8,128)(2,1)S(1)}, bf16[16,256,256]{2,1,0:T(8,128)(2,1)S(1)}) custom-call(s32[64]{0:T(128)S(1)} %copy-done.28, s32[3]{0:T(128)S(1)} %pad_add_fusion.1.own, bf16[256,512]{1,0:T(8,128)(2,1)S(1)} %copy-done.24, ...), custom_call_target="tpu_custom_call" | custom-call | flops 1000 | bytes 1000 | tf_op jit(solution)/shard_map/attention/pallas_call | solution.py:299
  151.2 4.2 %collective-permute-done.13 = bf16[16,256,256]{2,1,0:T(8,128)(2,1)S(1)} collective-permute-done((bf16[16,256,256]{2,1,0:T(8,128)(2,1)S(1)}, bf16[16,256,256]{2,1,0:T(8,128)(2,1)S(1)}, u32[]{:S(2)}, u32[]{:S(2)}) %collective-permute-start.13) | collective-permute-done | bytes 2097184 | tf_op jit(solution)/shard_map/ppermute | solution.py:470
  157.4 7.4 %all-to-all-start.3 = ((bf16[16,256,256]{2,1,0:T(8,128)(2,1)}), bf16[16,256,256]{2,1,0:T(8,128)(2,1)}, u32[]{:S(2)}, u32[]{:S(2)}) async-start(bf16[16,256,256]{2,1,0:T(8,128)(2,1)} %add_convert_fusion), calls=%async_computation.3 | async-start | bytes 4194304 | tf_op jit(solution)/shard_map/all_to_all | solution.py:579
  168.2 2.2 collective-permute-start.14
  171.7 9.2 %collective-permute-done.16.refs_5_ = bf16[256,512]{1,0:T(8,128)(2,1)S(1)} collective-permute-done((bf16[256,512]{1,0:T(8,128)(2,1)S(1)}, bf16[256,512]{1,0:T(8,128)(2,1)S(1)}, u32[]{:S(2)}, u32[]{:S(2)}) %collective-permute-start.16) | collective-permute-done | bytes 262176 | tf_op jit(solution)/shard_map/ppermute | solution.py:478
  185.8 2.0 query_weight_grad.1
  189.4 3.1 %all-to-all-done.3.refs_1_ = bf16[16,256,256]{2,1,0:T(8,128)(2,1)} async-done(((bf16[16,256,256]{2,1,0:T(8,128)(2,1)}), bf16[16,256,256]{2,1,0:T(8,128)(2,1)}, u32[]{:S(2)}, u32[]{:S(2)}) %all-to-all-start.3) | async-done | bytes 2097184 | tf_op jit(solution)/shard_map/all_to_all | solution.py:579
  192.5 2.2 grad_key_value.1.refs_3_
  195.0 2.4 collective-permute-start.22
  197.4 6.2 %collective-permute-start.9 = (bf16[256,512]{1,0:T(8,128)(2,1)}, bf16[256,512]{1,0:T(8,128)(2,1)S(1)}, u32[]{:S(2)}, u32[]{:S(2)}) collective-permute-start(bf16[256,512]{1,0:T(8,128)(2,1)} %copy-done.22), channel_id=1, source_target_pairs={{0,0},{1,4},{4,1},{5,5},{2,2},{3,6},{6,3},{7,7},{8,8},{9,12},{12,9... | collective-permute-start | bytes 786440 | tf_op jit(solution)/shard_map/ppermute | solution.py:466
  205.9 2.0 collective-permute-done.9.refs_1_.refs_11_
  209.0 3.2 %weight_grad.1 = bf16[16,48,768]{2,1,0:T(8,128)(2,1)S(1)} custom-call(s32[2]{0:T(128)S(1)} %pad_add_fusion.refs_0_.where, bf16[8,640,256]{2,1,0:T(8,128)(2,1)S(1)} %bitcast.24, bf16[640,512]{1,0:T(8,128)(2,1)S(1)} %copy-done.17, bf16[272,256]{1,0:T(8,128)(2,1)S(1)} %grad_key_value.1.refs_3_, bf16[272,256]{1,0:T(8,128)(2,1)S(1)} %collective-permute-done.22.refs_4_, ...), custom_call_target="tpu_custom_call" | custom-call | flops 1000 | bytes 1000 | tf_op jit(solution)/shard_map/weight_grad/pallas_call | solution.py:446
  213.3 7.5 %all-to-all-start.4 = ((bf16[16,48,768]{2,1,0:T(8,128)(2,1)}), bf16[16,48,768]{2,1,0:T(8,128)(2,1)}, u32[]{:S(2)}, u32[]{:S(2)}) async-start(bf16[16,48,768]{2,1,0:T(8,128)(2,1)} %copy-done.12), calls=%async_computation.4 | async-start | bytes 2359296 | tf_op jit(solution)/shard_map/all_to_all | solution.py:613
  220.8 5.7 %collective-permute-start.7 = (bf16[256,512]{1,0:T(8,128)(2,1)S(1)}, bf16[256,512]{1,0:T(8,128)(2,1)S(1)}, u32[]{:S(2)}, u32[]{:S(2)}) collective-permute-start(bf16[256,512]{1,0:T(8,128)(2,1)S(1)} %copy-done.37), channel_id=1, source_target_pairs={{0,0},{1,4},{4,1},{5,5},{2,2},{3,6},{6,3},{7,7},{8,8},{9,12},{12,9... | collective-permute-start | bytes 786440 | tf_op jit(solution)/shard_map/ppermute | solution.py:466
  228.4 2.5 %collective-permute-done.7 = bf16[256,512]{1,0:T(8,128)(2,1)S(1)} collective-permute-done((bf16[256,512]{1,0:T(8,128)(2,1)S(1)}, bf16[256,512]{1,0:T(8,128)(2,1)S(1)}, u32[]{:S(2)}, u32[]{:S(2)}) %collective-permute-start.7) | collective-permute-done | bytes 262176 | tf_op jit(solution)/shard_map/ppermute | solution.py:466
  231.6 3.1 %collective-permute-done.21.refs_2_ = bf16[272,256]{1,0:T(8,128)(2,1)S(1)} collective-permute-done((bf16[272,256]{1,0:T(8,128)(2,1)S(1)}, bf16[272,256]{1,0:T(8,128)(2,1)S(1)}, u32[]{:S(2)}, u32[]{:S(2)}) %collective-permute-start.21) | collective-permute-done | bytes 139296 | tf_op jit(solution)/shard_map/ppermute | solution.py:466
  236.1 5.9 %grad_states.1 = bf16[256,5120]{1,0:T(8,128)(2,1)} custom-call(s32[2]{0:T(128)S(1)} %pad_add_fusion.refs_0_.where, bf16[256,512]{1,0:T(8,128)(2,1)S(1)} %collective-permute-done.9.refs_1_.refs_11_, bf16[272,256]{1,0:T(8,128)(2,1)S(1)} %collective-permute-done.21.refs_2_, bf16[2560,512]{1,0:T(8,128)(2,1)S(1)} %bitcast.22, ...), custom_call_target="tpu_custom_call" | custom-call | flops 1000 | bytes 1000 | tf_op jit(solution)/shard_map/grad_states/pallas_call | solution.py:446
  242.0 2.0 finish.1
  (144 shorter events, 61.4 us)
Async XLA Ops:
  2.5 28.4 %all-to-all-start = ((bf16[64,40,256]{2,1,0:T(8,128)(2,1)}), bf16[64,40,256]{2,1,0:T(8,128)(2,1)}, u32[]{:S(2)}, u32[]{:S(2)}) async-start(bf16[64,40,256]{2,1,0:T(8,128)(2,1)} %broadcast_in_dim.10), calls=%async_computation | async-start | bytes 2621440 | tf_op jit(solution)/shard_map/all_to_all | solution.py:474
  30.9 45.6 %all-to-all-start.1 = ((bf16[64,40,512]{2,1,0:T(8,128)(2,1)}), bf16[64,40,512]{2,1,0:T(8,128)(2,1)S(1)}, u32[]{:S(2)}, u32[]{:S(2)}) async-start(bf16[64,40,512]{2,1,0:T(8,128)(2,1)} %copy-done.13), calls=%async_computation.1 | async-start | bytes 5242880 | tf_op jit(solution)/shard_map/all_to_all | solution.py:525
  38.8 5.0 %collective-permute-start = (bf16[2560,256]{1,0:T(8,128)(2,1)}, bf16[2560,256]{1,0:T(8,128)(2,1)S(1)}, u32[]{:S(2)}, u32[]{:S(2)}) collective-permute-start(bf16[2560,256]{1,0:T(8,128)(2,1)} %bitcast.7.refs_2_.refs_5_), channel_id=1, source_target_pairs={{0,1},{1,0},{2,3},{3,2},{4,5},{5,4},{6,7},{7,6},{8,9},{9,8},{10,11... | collective-permute-start | bytes 3932168 | tf_op jit(solution)/shard_map/ppermute | solution.py:470
  49.9 25.2 %collective-permute-start.1 = (bf16[256,256]{1,0:T(8,128)(2,1)S(1)}, bf16[256,256]{1,0:T(8,128)(2,1)S(1)}, u32[]{:S(2)}, u32[]{:S(2)}) collective-permute-start(bf16[256,256]{1,0:T(8,128)(2,1)S(1)} %get-tuple-element.52), channel_id=1, source_target_pairs={{0,0},{1,4},{4,1},{5,5},{2,2},{3,6},{6,3},{7,7},{8,8},{9,12},{12,9... | collective-permute-start | bytes 393224 | tf_op jit(solution)/shard_map/ppermute | solution.py:466
  76.6 16.0 %collective-permute-start.2 = (bf16[2560,512]{1,0:T(8,128)(2,1)S(1)}, bf16[2560,512]{1,0:T(8,128)(2,1)}, u32[]{:S(2)}, u32[]{:S(2)}) collective-permute-start(bf16[2560,512]{1,0:T(8,128)(2,1)S(1)} %bitcast.20), channel_id=1, source_target_pairs={{0,1},{1,0},{2,3},{3,2},{4,5},{5,4},{6,7},{7,6},{8,9},{9,8},{10,11... | collective-permute-start | bytes 7864328 | tf_op jit(solution)/shard_map/ppermute | solution.py:470
  76.6 30.3 %all-to-all-start.2 = ((bf16[16,256,256]{2,1,0:T(8,128)(2,1)}), bf16[16,256,256]{2,1,0:T(8,128)(2,1)}, u32[]{:S(2)}, u32[]{:S(2)}) async-start(bf16[16,256,256]{2,1,0:T(8,128)(2,1)} %copy-done.3), calls=%async_computation.2 | async-start | bytes 4194304 | tf_op jit(solution)/shard_map/all_to_all | solution.py:544
  81.6 4.0 %collective-permute-start.4 = (bf16[4,640,256]{2,1,0:T(8,128)(2,1)}, bf16[4,640,256]{2,1,0:T(8,128)(2,1)S(1)}, u32[]{:S(2)}, u32[]{:S(2)}) collective-permute-start(bf16[4,640,256]{2,1,0:T(8,128)(2,1)} %copy-done.31), channel_id=1, source_target_pairs={{0,1},{1,0},{2,3},{3,2},{4,5},{5,4},{6,7},{7,6},{8,9},{9,8},{10,11... | collective-permute-start | bytes 3932168 | tf_op jit(solution)/shard_map/ppermute | solution.py:470
  82.8 9.8 %collective-permute-start.3 = (bf16[256,512]{1,0:T(8,128)(2,1)}, bf16[256,512]{1,0:T(8,128)(2,1)S(1)}, u32[]{:S(2)}, u32[]{:S(2)}) collective-permute-start(bf16[256,512]{1,0:T(8,128)(2,1)} %bitcast.33), channel_id=1, source_target_pairs={{0,0},{1,4},{4,1},{5,5},{2,2},{3,6},{6,3},{7,7},{8,8},{9,12},{12,9... | collective-permute-start | bytes 786440 | tf_op jit(solution)/shard_map/ppermute | solution.py:466
  98.5 9.6 %collective-permute-start.5 = (bf16[256,512]{1,0:T(8,128)(2,1)}, bf16[256,512]{1,0:T(8,128)(2,1)S(1)}, u32[]{:S(2)}, u32[]{:S(2)}) collective-permute-start(bf16[256,512]{1,0:T(8,128)(2,1)} %get-tuple-element.60), channel_id=1, source_target_pairs={{0,0},{1,4},{4,1},{5,5},{2,2},{3,6},{6,3},{7,7},{8,8},{9,12},{12,9... | collective-permute-start | bytes 786440 | tf_op jit(solution)/shard_map/ppermute | solution.py:466
  108.8 9.5 %collective-permute-start.6 = (bf16[16,256,256]{2,1,0:T(8,128)(2,1)}, bf16[16,256,256]{2,1,0:T(8,128)(2,1)S(1)}, u32[]{:S(2)}, u32[]{:S(2)}) collective-permute-start(bf16[16,256,256]{2,1,0:T(8,128)(2,1)} %all-to-all-done.2.kv_ref), channel_id=1, source_target_pairs={{0,1},{1,0},{2,3},{3,2},{4,5},{5,4},{6,7},{7,6},{8,9},{9,8},{10,11... | collective-permute-start | bytes 6291464 | tf_op jit(solution)/shard_map/ppermute | solution.py:470
  110.4 37.8 %collective-permute-start.10 = (bf16[2,640,256]{2,1,0:T(8,128)(2,1)}, bf16[2,640,256]{2,1,0:T(8,128)(2,1)S(1)}, u32[]{:S(2)}, u32[]{:S(2)}) collective-permute-start(bf16[2,640,256]{2,1,0:T(8,128)(2,1)} %copy-done.34), channel_id=1, source_target_pairs={{0,6},{2,0},{4,2},{6,4},{1,7},{3,1},{5,3},{7,5},{8,14},{10,8},{12,... | collective-permute-start | bytes 1966088 | tf_op jit(solution)/shard_map/ppermute | solution.py:558
  111.8 36.4 %collective-permute-start.11 = (bf16[2,640,256]{2,1,0:T(8,128)(2,1)}, bf16[2,640,256]{2,1,0:T(8,128)(2,1)S(1)}, u32[]{:S(2)}, u32[]{:S(2)}) collective-permute-start(bf16[2,640,256]{2,1,0:T(8,128)(2,1)} %copy-done.33), channel_id=1, source_target_pairs={{0,4},{2,6},{4,0},{6,2},{1,5},{3,7},{5,1},{7,3},{8,12},{10,14},{12... | collective-permute-start | bytes 1966088 | tf_op jit(solution)/shard_map/ppermute | solution.py:558
  113.2 35.1 %collective-permute-start.12 = (bf16[2,640,256]{2,1,0:T(8,128)(2,1)}, bf16[2,640,256]{2,1,0:T(8,128)(2,1)S(1)}, u32[]{:S(2)}, u32[]{:S(2)}) collective-permute-start(bf16[2,640,256]{2,1,0:T(8,128)(2,1)} %copy-done.32), channel_id=1, source_target_pairs={{0,2},{2,4},{4,6},{6,0},{1,3},{3,5},{5,7},{7,1},{8,10},{10,12},{12... | collective-permute-start | bytes 1966088 | tf_op jit(solution)/shard_map/ppermute | solution.py:558
  113.2 35.1 %collective-permute-start.8 = (bf16[256,640]{1,0:T(8,128)(2,1)}, bf16[256,640]{1,0:T(8,128)(2,1)S(1)}, u32[]{:S(2)}, u32[]{:S(2)}) collective-permute-start(bf16[256,640]{1,0:T(8,128)(2,1)} %copy-done.35), channel_id=1, source_target_pairs={{0,0},{1,4},{4,1},{5,5},{2,2},{3,6},{6,3},{7,7},{8,8},{9,12},{12,9... | collective-permute-start | bytes 983048 | tf_op jit(solution)/shard_map/ppermute | solution.py:466
  151.2 4.2 %collective-permute-start.13 = (bf16[16,256,256]{2,1,0:T(8,128)(2,1)S(1)}, bf16[16,256,256]{2,1,0:T(8,128)(2,1)S(1)}, u32[]{:S(2)}, u32[]{:S(2)}) collective-permute-start(bf16[16,256,256]{2,1,0:T(8,128)(2,1)S(1)} %get-tuple-element.73), channel_id=1, source_target_pairs={{0,1},{1,0},{2,3},{3,2},{4,5},{5,4},{6,7},{7,6},{8,9},{9,8},{10,11... | collective-permute-start | bytes 6291464 | tf_op jit(solution)/shard_map/ppermute | solution.py:470
  157.4 35.1 %all-to-all-start.3 = ((bf16[16,256,256]{2,1,0:T(8,128)(2,1)}), bf16[16,256,256]{2,1,0:T(8,128)(2,1)}, u32[]{:S(2)}, u32[]{:S(2)}) async-start(bf16[16,256,256]{2,1,0:T(8,128)(2,1)} %add_convert_fusion), calls=%async_computation.3 | async-start | bytes 4194304 | tf_op jit(solution)/shard_map/all_to_all | solution.py:579
  166.5 14.5 %collective-permute-start.16 = (bf16[256,512]{1,0:T(8,128)(2,1)S(1)}, bf16[256,512]{1,0:T(8,128)(2,1)S(1)}, u32[]{:S(2)}, u32[]{:S(2)}) collective-permute-start(bf16[256,512]{1,0:T(8,128)(2,1)S(1)} %get-tuple-element.66.refs_2_), channel_id=1, source_target_pairs={{0,2},{2,4},{4,6},{6,0},{1,3},{3,5},{5,7},{7,1},{8,10},{10,12},{12... | collective-permute-start | bytes 786440 | tf_op jit(solution)/shard_map/ppermute | solution.py:478
  167.9 14.2 %collective-permute-start.15 = (bf16[256,512]{1,0:T(8,128)(2,1)S(1)}, bf16[256,512]{1,0:T(8,128)(2,1)S(1)}, u32[]{:S(2)}, u32[]{:S(2)}) collective-permute-start(bf16[256,512]{1,0:T(8,128)(2,1)S(1)} %get-tuple-element.66.refs_2_), channel_id=1, source_target_pairs={{0,4},{2,6},{4,0},{6,2},{1,5},{3,7},{5,1},{7,3},{8,12},{10,14},{12... | collective-permute-start | bytes 786440 | tf_op jit(solution)/shard_map/ppermute | solution.py:478
  168.2 13.9 %collective-permute-start.14 = (bf16[256,512]{1,0:T(8,128)(2,1)S(1)}, bf16[256,512]{1,0:T(8,128)(2,1)S(1)}, u32[]{:S(2)}, u32[]{:S(2)}) collective-permute-start(bf16[256,512]{1,0:T(8,128)(2,1)S(1)} %get-tuple-element.66.refs_2_), channel_id=1, source_target_pairs={{0,6},{2,0},{4,2},{6,4},{1,7},{3,1},{5,3},{7,5},{8,14},{10,8},{12,... | collective-permute-start | bytes 786440 | tf_op jit(solution)/shard_map/ppermute | solution.py:478
  170.4 12.3 %collective-permute-start.17 = (bf16[256,512]{1,0:T(8,128)(2,1)S(1)}, bf16[256,512]{1,0:T(8,128)(2,1)S(1)}, u32[]{:S(2)}, u32[]{:S(2)}) collective-permute-start(bf16[256,512]{1,0:T(8,128)(2,1)S(1)} %get-tuple-element.66.refs_2_), channel_id=1, source_target_pairs={{0,1},{1,0},{2,3},{3,2},{4,5},{5,4},{6,7},{7,6},{8,9},{9,8},{10,11... | collective-permute-start | bytes 786440 | tf_op jit(solution)/shard_map/ppermute | solution.py:470
  180.9 2.3 collective-permute-start.20
  194.7 9.1 %collective-permute-start.24 = (bf16[272,256]{1,0:T(8,128)(2,1)S(1)}, bf16[272,256]{1,0:T(8,128)(2,1)S(1)}, u32[]{:S(2)}, u32[]{:S(2)}) collective-permute-start(bf16[272,256]{1,0:T(8,128)(2,1)S(1)} %grad_key_value.1.refs_3_), channel_id=1, source_target_pairs={{0,2},{2,4},{4,6},{6,0},{1,3},{3,5},{5,7},{7,1},{8,10},{10,12},{12... | collective-permute-start | bytes 417800 | tf_op jit(solution)/shard_map/ppermute | solution.py:478
  194.8 10.2 %collective-permute-start.23 = (bf16[272,256]{1,0:T(8,128)(2,1)S(1)}, bf16[272,256]{1,0:T(8,128)(2,1)S(1)}, u32[]{:S(2)}, u32[]{:S(2)}) collective-permute-start(bf16[272,256]{1,0:T(8,128)(2,1)S(1)} %grad_key_value.1.refs_3_), channel_id=1, source_target_pairs={{0,4},{2,6},{4,0},{6,2},{1,5},{3,7},{5,1},{7,3},{8,12},{10,14},{12... | collective-permute-start | bytes 417800 | tf_op jit(solution)/shard_map/ppermute | solution.py:478
  195.0 10.0 %collective-permute-start.22 = (bf16[272,256]{1,0:T(8,128)(2,1)S(1)}, bf16[272,256]{1,0:T(8,128)(2,1)S(1)}, u32[]{:S(2)}, u32[]{:S(2)}) collective-permute-start(bf16[272,256]{1,0:T(8,128)(2,1)S(1)} %grad_key_value.1.refs_3_), channel_id=1, source_target_pairs={{0,6},{2,0},{4,2},{6,4},{1,7},{3,1},{5,3},{7,5},{8,14},{10,8},{12,... | collective-permute-start | bytes 417800 | tf_op jit(solution)/shard_map/ppermute | solution.py:478
  197.4 10.5 %collective-permute-start.9 = (bf16[256,512]{1,0:T(8,128)(2,1)}, bf16[256,512]{1,0:T(8,128)(2,1)S(1)}, u32[]{:S(2)}, u32[]{:S(2)}) collective-permute-start(bf16[256,512]{1,0:T(8,128)(2,1)} %copy-done.22), channel_id=1, source_target_pairs={{0,0},{1,4},{4,1},{5,5},{2,2},{3,6},{6,3},{7,7},{8,8},{9,12},{12,9... | collective-permute-start | bytes 786440 | tf_op jit(solution)/shard_map/ppermute | solution.py:466
  203.7 4.3 %collective-permute-start.25 = (bf16[272,256]{1,0:T(8,128)(2,1)S(1)}, bf16[272,256]{1,0:T(8,128)(2,1)S(1)}, u32[]{:S(2)}, u32[]{:S(2)}) collective-permute-start(bf16[272,256]{1,0:T(8,128)(2,1)S(1)} %grad_key_value.1.refs_3_), channel_id=1, source_target_pairs={{0,1},{1,0},{2,3},{3,2},{4,5},{5,4},{6,7},{7,6},{8,9},{9,8},{10,11... | collective-permute-start | bytes 417800 | tf_op jit(solution)/shard_map/ppermute | solution.py:470
  203.8 4.2 %collective-permute-start.28 = (bf16[272,256]{1,0:T(8,128)(2,1)S(1)}, bf16[272,256]{1,0:T(8,128)(2,1)S(1)}, u32[]{:S(2)}, u32[]{:S(2)}) collective-permute-start(bf16[272,256]{1,0:T(8,128)(2,1)S(1)} %collective-permute-done.24.refs_6_), channel_id=1, source_target_pairs={{0,1},{1,0},{2,3},{3,2},{4,5},{5,4},{6,7},{7,6},{8,9},{9,8},{10,11... | collective-permute-start | bytes 417800 | tf_op jit(solution)/shard_map/ppermute | solution.py:470
  205.0 2.9 %collective-permute-start.27 = (bf16[272,256]{1,0:T(8,128)(2,1)S(1)}, bf16[272,256]{1,0:T(8,128)(2,1)S(1)}, u32[]{:S(2)}, u32[]{:S(2)}) collective-permute-start(bf16[272,256]{1,0:T(8,128)(2,1)S(1)} %collective-permute-done.23.refs_5_), channel_id=1, source_target_pairs={{0,1},{1,0},{2,3},{3,2},{4,5},{5,4},{6,7},{7,6},{8,9},{9,8},{10,11... | collective-permute-start | bytes 417800 | tf_op jit(solution)/shard_map/ppermute | solution.py:470
  205.0 2.9 %collective-permute-start.26 = (bf16[272,256]{1,0:T(8,128)(2,1)S(1)}, bf16[272,256]{1,0:T(8,128)(2,1)S(1)}, u32[]{:S(2)}, u32[]{:S(2)}) collective-permute-start(bf16[272,256]{1,0:T(8,128)(2,1)S(1)} %collective-permute-done.22.refs_4_), channel_id=1, source_target_pairs={{0,1},{1,0},{2,3},{3,2},{4,5},{5,4},{6,7},{7,6},{8,9},{9,8},{10,11... | collective-permute-start | bytes 417800 | tf_op jit(solution)/shard_map/ppermute | solution.py:470
  213.3 28.7 %all-to-all-start.4 = ((bf16[16,48,768]{2,1,0:T(8,128)(2,1)}), bf16[16,48,768]{2,1,0:T(8,128)(2,1)}, u32[]{:S(2)}, u32[]{:S(2)}) async-start(bf16[16,48,768]{2,1,0:T(8,128)(2,1)} %copy-done.12), calls=%async_computation.4 | async-start | bytes 2359296 | tf_op jit(solution)/shard_map/all_to_all | solution.py:613
  220.8 10.2 %collective-permute-start.7 = (bf16[256,512]{1,0:T(8,128)(2,1)S(1)}, bf16[256,512]{1,0:T(8,128)(2,1)S(1)}, u32[]{:S(2)}, u32[]{:S(2)}) collective-permute-start(bf16[256,512]{1,0:T(8,128)(2,1)S(1)} %copy-done.37), channel_id=1, source_target_pairs={{0,0},{1,4},{4,1},{5,5},{2,2},{3,6},{6,3},{7,7},{8,8},{9,12},{12,9... | collective-permute-start | bytes 786440 | tf_op jit(solution)/shard_map/ppermute | solution.py:466
  226.5 8.3 %collective-permute-start.21 = (bf16[272,256]{1,0:T(8,128)(2,1)S(1)}, bf16[272,256]{1,0:T(8,128)(2,1)S(1)}, u32[]{:S(2)}, u32[]{:S(2)}) collective-permute-start(bf16[272,256]{1,0:T(8,128)(2,1)S(1)} %grad_key_value.1.refs_3_), channel_id=1, source_target_pairs={{0,0},{1,4},{4,1},{5,5},{2,2},{3,6},{6,3},{7,7},{8,8},{9,12},{12,9... | collective-permute-start | bytes 417800 | tf_op jit(solution)/shard_map/ppermute | solution.py:466
  (42 other events, 162.3 us)

commit v12 on v11

--- a/solution.py
+++ b/solution.py
@@ -18,6 +18,7 @@
 smem = pl.BlockSpec(memory_space=pltpu.SMEM)
 vmem = pl.BlockSpec(memory_space=pltpu.VMEM)
 anywhere = pl.BlockSpec(memory_space=pl.ANY)
+hbm = pl.BlockSpec(memory_space=pltpu.HBM)
 
 
 def mm(a, b):
@@ -567,7 +568,7 @@
             shape((columns, 2, half // columns, tok_rows), bf16),
         ),
         in_specs=[smem, anywhere] + [vmem] * (1 + columns),
-        out_specs=(anywhere, anywhere),
+        out_specs=(anywhere, hbm),
         scratch_shapes=[pltpu.SemaphoreType.DMA((columns,))],
         input_output_aliases={1: 0},
         compiler_params=pltpu.CompilerParams(vmem_limit_bytes=16 * mib),
@@ -596,7 +597,7 @@
         shape((tok_rows + 16, kv_cols), bf16),
         raw_there, dkv, gain_k, cos_there, sin_there, gains_q,
         name="grad_key_value",
-        after=(done,),
+        after=(done, g_q_back),
     )
     blocks_kv = around(g_kv)
     g_kv_back = swap(g_kv)
@@ -606,8 +607,7 @@
         all_parts,
         where, turned, query_parts, *blocks_kv,
         name="weight_grad",
-        after=(g_q_back,),
-        out_spec=anywhere,
+        out_spec=hbm,
         scratch=[pltpu.VMEM(all_parts.shape, bf16), pltpu.SemaphoreType.DMA((planes,))],
     )
     parts = lax.all_to_all(parts, plane, 0, 0)

time: 247 us -> 245 us (level)
  waiting for transfers between devices: 63.5 us -> 60.3 us
    ppermute x13, starting transfers between devices: 10.3 us -> 14.6 us  [flip(): return lax.ppermute(array, 'core', flipped)]
    ppermute x7, starting transfers between devices: 28.4 us -> 25 us  [swap(): return lax.ppermute(array, ('y_hi', 'core'), swapped)]
    all_to_all x1, waiting for transfers between devices: 3.13 us -> 0.35 us  [local(): dkv = lax.all_to_all(dkv, plane, 0, 0)]
    unnamed x81 -> x77, local copies, waits for them, and re-layouts: 29.5 us -> 28.8 us
  transfers between devices with their start and end apart: 34 -> 34, of which waited for: 16 -> 17; matrix products, arithmetic and copies ran while one was open for 2% -> 2% of each run, Pallas kernels for 19% -> 19%
where the time goes in v12:
time: 245 us; the launch traced here: 243 us
  starting transfers between devices  88.4 us (36%)
  waiting for transfers between devices  60.3 us (25%)
  Pallas kernels  55.3 us (23%)
  local copies, waits for them, and re-layouts  32.9 us (13%)
  other arithmetic  4.39 us (2%)
    ppermute x7, waiting for transfers between devices, swap(): return lax.ppermute(array, ('y_hi', 'core'), swapped)  29.1 us
    pallas_call x1, Pallas kernels, attention(): pl.pallas_call(attention_kernel, out_shape=(jax.ShapeDtypeStruct((rows_he...  28.9 us
    unnamed x77, local copies, waits for them, and re-layouts  28.8 us
    ppermute x7, starting transfers between devices, swap(): return lax.ppermute(array, ('y_hi', 'core'), swapped)  25 us
    pallas_call x11, Pallas kernels, call(): pl.pallas_call(run, out_shape=shapes, in_specs=[smem if a.dtype == jnp.in...  25 us
    ppermute x13, starting transfers between devices, flip(): return lax.ppermute(array, 'core', flipped)  14.6 us
    all_to_all x1, starting transfers between devices, to_all(): lax.all_to_all(jnp.broadcast_to(array[None], (count,) + array.shape), axe...  10.8 us
    ppermute x6, waiting for transfers between devices, ring(): return lax.ppermute(array, column, [(i, (i - step) % 4) for i in range(4)])  10.7 us
  transfers between devices with their start and end apart: 34, of which 17 were waited for; matrix products, arithmetic and copies ran while one was open for 2% of the time, Pallas kernels for 19%

profile of v12, /device:TPU:39, one launch (start us, length us, event | category | flops | bytes accessed | tf_op | source)
XLA Modules:
  0.0 242.5 jit_solution(7784223476088613721)
XLA Ops:
  2.5 10.8 %all-to-all-start = ((bf16[64,40,256]{2,1,0:T(8,128)(2,1)}), bf16[64,40,256]{2,1,0:T(8,128)(2,1)}, u32[]{:S(2)}, u32[]{:S(2)}) async-start(bf16[64,40,256]{2,1,0:T(8,128)(2,1)} %broadcast_in_dim.10), calls=%async_computation | async-start | bytes 2621440 | tf_op jit(solution)/shard_map/all_to_all | solution.py:475
  13.4 3.0 %copy.16 = bf16[5120,256]{1,0:T(8,128)(2,1)S(1)} copy(bf16[5120,256]{0,1:T(8,128)(2,1)} %bitcast.30) | data formatting | bytes 5242880 | tf_op jit(solution)/shard_map/transpose | solution.py:519
  25.5 5.4 %all-to-all-done = bf16[64,40,256]{2,1,0:T(8,128)(2,1)} async-done(((bf16[64,40,256]{2,1,0:T(8,128)(2,1)}), bf16[64,40,256]{2,1,0:T(8,128)(2,1)}, u32[]{:S(2)}, u32[]{:S(2)}) %all-to-all-start) | async-done | bytes 1310752 | tf_op jit(solution)/shard_map/all_to_all | solution.py:475
  30.9 7.9 %all-to-all-start.1 = ((bf16[64,40,512]{2,1,0:T(8,128)(2,1)}), bf16[64,40,512]{2,1,0:T(8,128)(2,1)S(1)}, u32[]{:S(2)}, u32[]{:S(2)}) async-start(bf16[64,40,512]{2,1,0:T(8,128)(2,1)} %copy-done.13), calls=%async_computation.1 | async-start | bytes 5242880 | tf_op jit(solution)/shard_map/all_to_all | solution.py:526
  38.8 2.2 collective-permute-start
  40.9 2.9 %collective-permute-done.refs_3_.refs_6_ = bf16[2560,256]{1,0:T(8,128)(2,1)S(1)} collective-permute-done((bf16[2560,256]{1,0:T(8,128)(2,1)}, bf16[2560,256]{1,0:T(8,128)(2,1)S(1)}, u32[]{:S(2)}, u32[]{:S(2)}) %collective-permute-start) | collective-permute-done | bytes 1310752 | tf_op jit(solution)/shard_map/ppermute | solution.py:471
  46.9 2.3 key_value.1
  49.9 4.9 %collective-permute-start.1 = (bf16[256,256]{1,0:T(8,128)(2,1)S(1)}, bf16[256,256]{1,0:T(8,128)(2,1)S(1)}, u32[]{:S(2)}, u32[]{:S(2)}) collective-permute-start(bf16[256,256]{1,0:T(8,128)(2,1)S(1)} %get-tuple-element.52), channel_id=1, source_target_pairs={{0,0},{1,4},{4,1},{5,5},{2,2},{3,6},{6,3},{7,7},{8,8},{9,12},{12,9... | collective-permute-start | bytes 393224 | tf_op jit(solution)/shard_map/ppermute | solution.py:467
  54.8 20.3 %collective-permute-done.1.refs_0_ = bf16[256,256]{1,0:T(8,128)(2,1)S(1)} collective-permute-done((bf16[256,256]{1,0:T(8,128)(2,1)S(1)}, bf16[256,256]{1,0:T(8,128)(2,1)S(1)}, u32[]{:S(2)}, u32[]{:S(2)}) %collective-permute-start.1) | collective-permute-done | bytes 131104 | tf_op jit(solution)/shard_map/ppermute | solution.py:467
  76.6 5.0 %all-to-all-start.2 = ((bf16[16,256,256]{2,1,0:T(8,128)(2,1)}), bf16[16,256,256]{2,1,0:T(8,128)(2,1)}, u32[]{:S(2)}, u32[]{:S(2)}) async-start(bf16[16,256,256]{2,1,0:T(8,128)(2,1)} %copy-done.3), calls=%async_computation.2 | async-start | bytes 4194304 | tf_op jit(solution)/shard_map/all_to_all | solution.py:545
  93.5 4.3 %query.1 = (bf16[256,512]{1,0:T(8,128)(2,1)}, bf16[256,640]{1,0:T(8,128)(2,1)S(1)}) custom-call(bf16[256,2560]{1,0:T(8,128)(2,1)S(1)} %copy-done.8, bf16[256,2560]{1,0:T(8,128)(2,1)S(1)} %copy-done.11, bf16[2560,512]{1,0:T(8,128)(2,1)S(1)} %bitcast.21, bf16[2560,512]{1,0:T(8,128)(2,1)} %collective-permute-done.2.refs_3_.refs_4_, f32[256,128]{1,0:T(8,128)S(1)} %copy-done.26, ...), custom_call_target="tpu_custom_call" | custom-call | flops 1000 | bytes 1000 | tf_op jit(solution)/shard_map/query/pallas_call | solution.py:447
  98.4 2.7 %collective-permute-start.5 = (bf16[256,512]{1,0:T(8,128)(2,1)}, bf16[256,512]{1,0:T(8,128)(2,1)S(1)}, u32[]{:S(2)}, u32[]{:S(2)}) collective-permute-start(bf16[256,512]{1,0:T(8,128)(2,1)} %get-tuple-element.60), channel_id=1, source_target_pairs={{0,0},{1,4},{4,1},{5,5},{2,2},{3,6},{6,3},{7,7},{8,8},{9,12},{12,9... | collective-permute-start | bytes 786440 | tf_op jit(solution)/shard_map/ppermute | solution.py:467
  101.1 5.8 %all-to-all-done.2.kv_ref = bf16[16,256,256]{2,1,0:T(8,128)(2,1)} async-done(((bf16[16,256,256]{2,1,0:T(8,128)(2,1)}), bf16[16,256,256]{2,1,0:T(8,128)(2,1)}, u32[]{:S(2)}, u32[]{:S(2)}) %all-to-all-start.2) | async-done | bytes 2097184 | tf_op jit(solution)/shard_map/all_to_all | solution.py:545
  113.1 5.1 %collective-permute-start.8 = (bf16[256,640]{1,0:T(8,128)(2,1)}, bf16[256,640]{1,0:T(8,128)(2,1)S(1)}, u32[]{:S(2)}, u32[]{:S(2)}) collective-permute-start(bf16[256,640]{1,0:T(8,128)(2,1)} %copy-done.35), channel_id=1, source_target_pairs={{0,0},{1,4},{4,1},{5,5},{2,2},{3,6},{6,3},{7,7},{8,8},{9,12},{12,9... | collective-permute-start | bytes 983048 | tf_op jit(solution)/shard_map/ppermute | solution.py:467
  119.2 28.9 %attention.1 = (bf16[256,512]{1,0:T(8,128)(2,1)S(1)}, f32[256,512]{1,0:T(8,128)S(1)}, bf16[16,256,256]{2,1,0:T(8,128)(2,1)S(1)}, bf16[16,256,256]{2,1,0:T(8,128)(2,1)S(1)}) custom-call(s32[64]{0:T(128)S(1)} %copy-done.28, s32[3]{0:T(128)S(1)} %pad_add_fusion.1.own, bf16[256,512]{1,0:T(8,128)(2,1)S(1)} %copy-done.24, ...), custom_call_target="tpu_custom_call" | custom-call | flops 1000 | bytes 1000 | tf_op jit(solution)/shard_map/attention/pallas_call | solution.py:300
  151.1 4.2 %collective-permute-done.13 = bf16[16,256,256]{2,1,0:T(8,128)(2,1)S(1)} collective-permute-done((bf16[16,256,256]{2,1,0:T(8,128)(2,1)S(1)}, bf16[16,256,256]{2,1,0:T(8,128)(2,1)S(1)}, u32[]{:S(2)}, u32[]{:S(2)}) %collective-permute-start.13) | collective-permute-done | bytes 2097184 | tf_op jit(solution)/shard_map/ppermute | solution.py:471
  157.2 7.8 %all-to-all-start.3 = ((bf16[16,256,256]{2,1,0:T(8,128)(2,1)}), bf16[16,256,256]{2,1,0:T(8,128)(2,1)}, u32[]{:S(2)}, u32[]{:S(2)}) async-start(bf16[16,256,256]{2,1,0:T(8,128)(2,1)} %add_convert_fusion), calls=%async_computation.3 | async-start | bytes 4194304 | tf_op jit(solution)/shard_map/all_to_all | solution.py:580
  167.9 2.4 collective-permute-start.14
  171.7 9.5 %collective-permute-done.16.refs_5_ = bf16[256,512]{1,0:T(8,128)(2,1)S(1)} collective-permute-done((bf16[256,512]{1,0:T(8,128)(2,1)S(1)}, bf16[256,512]{1,0:T(8,128)(2,1)S(1)}, u32[]{:S(2)}, u32[]{:S(2)}) %collective-permute-start.16) | collective-permute-done | bytes 262176 | tf_op jit(solution)/shard_map/ppermute | solution.py:479
  183.0 3.5 %collective-permute-start.9 = (bf16[256,512]{1,0:T(8,128)(2,1)S(1)}, bf16[256,512]{1,0:T(8,128)(2,1)S(1)}, u32[]{:S(2)}, u32[]{:S(2)}) collective-permute-start(bf16[256,512]{1,0:T(8,128)(2,1)S(1)} %get-tuple-element.66.refs_2_), channel_id=1, source_target_pairs={{0,0},{1,4},{4,1},{5,5},{2,2},{3,6},{6,3},{7,7},{8,8},{9,12},{12,9... | collective-permute-start | bytes 786440 | tf_op jit(solution)/shard_map/ppermute | solution.py:467
  188.2 2.0 query_weight_grad.1
  192.7 2.2 grad_key_value.1.refs_3_
  195.6 2.5 %collective-permute-start.22 = (bf16[272,256]{1,0:T(8,128)(2,1)S(1)}, bf16[272,256]{1,0:T(8,128)(2,1)S(1)}, u32[]{:S(2)}, u32[]{:S(2)}) collective-permute-start(bf16[272,256]{1,0:T(8,128)(2,1)S(1)} %grad_key_value.1.refs_3_), channel_id=1, source_target_pairs={{0,6},{2,0},{4,2},{6,4},{1,7},{3,1},{5,3},{7,5},{8,14},{10,8},{12,... | collective-permute-start | bytes 417800 | tf_op jit(solution)/shard_map/ppermute | solution.py:479
  201.2 4.1 %collective-permute-start.28 = (bf16[272,256]{1,0:T(8,128)(2,1)S(1)}, bf16[272,256]{1,0:T(8,128)(2,1)S(1)}, u32[]{:S(2)}, u32[]{:S(2)}) collective-permute-start(bf16[272,256]{1,0:T(8,128)(2,1)S(1)} %collective-permute-done.24.refs_6_), channel_id=1, source_target_pairs={{0,1},{1,0},{2,3},{3,2},{4,5},{5,4},{6,7},{7,6},{8,9},{9,8},{10,11... | collective-permute-start | bytes 417800 | tf_op jit(solution)/shard_map/ppermute | solution.py:471
  207.9 3.2 %weight_grad.1 = bf16[16,48,768]{2,1,0:T(8,128)(2,1)S(1)} custom-call(s32[2]{0:T(128)S(1)} %pad_add_fusion.refs_0_.where, bf16[8,640,256]{2,1,0:T(8,128)(2,1)S(1)} %bitcast.24, bf16[640,512]{1,0:T(8,128)(2,1)S(1)} %copy-done.19, bf16[272,256]{1,0:T(8,128)(2,1)S(1)} %grad_key_value.1.refs_3_, bf16[272,256]{1,0:T(8,128)(2,1)S(1)} %collective-permute-done.22.refs_4_, ...), custom_call_target="tpu_custom_call" | custom-call | flops 1000 | bytes 1000 | tf_op jit(solution)/shard_map/weight_grad/pallas_call | solution.py:447
  212.8 7.8 %all-to-all-start.4 = ((bf16[16,48,768]{2,1,0:T(8,128)(2,1)}), bf16[16,48,768]{2,1,0:T(8,128)(2,1)}, u32[]{:S(2)}, u32[]{:S(2)}) async-start(bf16[16,48,768]{2,1,0:T(8,128)(2,1)} %copy-done.12), calls=%async_computation.4 | async-start | bytes 2359296 | tf_op jit(solution)/shard_map/all_to_all | solution.py:613
  220.6 3.4 %collective-permute-start.7 = (bf16[256,512]{1,0:T(8,128)(2,1)S(1)}, bf16[256,512]{1,0:T(8,128)(2,1)S(1)}, u32[]{:S(2)}, u32[]{:S(2)}) collective-permute-start(bf16[256,512]{1,0:T(8,128)(2,1)S(1)} %copy-done.37), channel_id=1, source_target_pairs={{0,0},{1,4},{4,1},{5,5},{2,2},{3,6},{6,3},{7,7},{8,8},{9,12},{12,9... | collective-permute-start | bytes 786440 | tf_op jit(solution)/shard_map/ppermute | solution.py:467
  224.1 3.7 %collective-permute-start.21 = (bf16[272,256]{1,0:T(8,128)(2,1)}, bf16[272,256]{1,0:T(8,128)(2,1)S(1)}, u32[]{:S(2)}, u32[]{:S(2)}) collective-permute-start(bf16[272,256]{1,0:T(8,128)(2,1)} %copy-done.20), channel_id=1, source_target_pairs={{0,0},{1,4},{4,1},{5,5},{2,2},{3,6},{6,3},{7,7},{8,8},{9,12},{12,9... | collective-permute-start | bytes 417800 | tf_op jit(solution)/shard_map/ppermute | solution.py:467
  227.7 2.5 %collective-permute-done.7 = bf16[256,512]{1,0:T(8,128)(2,1)S(1)} collective-permute-done((bf16[256,512]{1,0:T(8,128)(2,1)S(1)}, bf16[256,512]{1,0:T(8,128)(2,1)S(1)}, u32[]{:S(2)}, u32[]{:S(2)}) %collective-permute-start.7) | collective-permute-done | bytes 262176 | tf_op jit(solution)/shard_map/ppermute | solution.py:467
  230.2 2.3 collective-permute-done.21.refs_2_
  233.9 5.9 %grad_states.1 = bf16[256,5120]{1,0:T(8,128)(2,1)} custom-call(s32[2]{0:T(128)S(1)} %pad_add_fusion.refs_0_.where, bf16[256,512]{1,0:T(8,128)(2,1)S(1)} %collective-permute-done.9.refs_7_.refs_1_, bf16[272,256]{1,0:T(8,128)(2,1)S(1)} %collective-permute-done.21.refs_2_, bf16[2560,512]{1,0:T(8,128)(2,1)S(1)} %bitcast.22, ...), custom_call_target="tpu_custom_call" | custom-call | flops 1000 | bytes 1000 | tf_op jit(solution)/shard_map/grad_states/pallas_call | solution.py:447
  239.8 2.0 finish.1
  (140 shorter events, 61.3 us)
Async XLA Ops:
  2.5 28.4 %all-to-all-start = ((bf16[64,40,256]{2,1,0:T(8,128)(2,1)}), bf16[64,40,256]{2,1,0:T(8,128)(2,1)}, u32[]{:S(2)}, u32[]{:S(2)}) async-start(bf16[64,40,256]{2,1,0:T(8,128)(2,1)} %broadcast_in_dim.10), calls=%async_computation | async-start | bytes 2621440 | tf_op jit(solution)/shard_map/all_to_all | solution.py:475
  30.9 45.6 %all-to-all-start.1 = ((bf16[64,40,512]{2,1,0:T(8,128)(2,1)}), bf16[64,40,512]{2,1,0:T(8,128)(2,1)S(1)}, u32[]{:S(2)}, u32[]{:S(2)}) async-start(bf16[64,40,512]{2,1,0:T(8,128)(2,1)} %copy-done.13), calls=%async_computation.1 | async-start | bytes 5242880 | tf_op jit(solution)/shard_map/all_to_all | solution.py:526
  38.8 5.0 %collective-permute-start = (bf16[2560,256]{1,0:T(8,128)(2,1)}, bf16[2560,256]{1,0:T(8,128)(2,1)S(1)}, u32[]{:S(2)}, u32[]{:S(2)}) collective-permute-start(bf16[2560,256]{1,0:T(8,128)(2,1)} %bitcast.7.refs_2_.refs_5_), channel_id=1, source_target_pairs={{0,1},{1,0},{2,3},{3,2},{4,5},{5,4},{6,7},{7,6},{8,9},{9,8},{10,11... | collective-permute-start | bytes 3932168 | tf_op jit(solution)/shard_map/ppermute | solution.py:471
  49.9 25.2 %collective-permute-start.1 = (bf16[256,256]{1,0:T(8,128)(2,1)S(1)}, bf16[256,256]{1,0:T(8,128)(2,1)S(1)}, u32[]{:S(2)}, u32[]{:S(2)}) collective-permute-start(bf16[256,256]{1,0:T(8,128)(2,1)S(1)} %get-tuple-element.52), channel_id=1, source_target_pairs={{0,0},{1,4},{4,1},{5,5},{2,2},{3,6},{6,3},{7,7},{8,8},{9,12},{12,9... | collective-permute-start | bytes 393224 | tf_op jit(solution)/shard_map/ppermute | solution.py:467
  76.6 16.0 %collective-permute-start.2 = (bf16[2560,512]{1,0:T(8,128)(2,1)S(1)}, bf16[2560,512]{1,0:T(8,128)(2,1)}, u32[]{:S(2)}, u32[]{:S(2)}) collective-permute-start(bf16[2560,512]{1,0:T(8,128)(2,1)S(1)} %bitcast.20), channel_id=1, source_target_pairs={{0,1},{1,0},{2,3},{3,2},{4,5},{5,4},{6,7},{7,6},{8,9},{9,8},{10,11... | collective-permute-start | bytes 7864328 | tf_op jit(solution)/shard_map/ppermute | solution.py:471
  76.6 30.3 %all-to-all-start.2 = ((bf16[16,256,256]{2,1,0:T(8,128)(2,1)}), bf16[16,256,256]{2,1,0:T(8,128)(2,1)}, u32[]{:S(2)}, u32[]{:S(2)}) async-start(bf16[16,256,256]{2,1,0:T(8,128)(2,1)} %copy-done.3), calls=%async_computation.2 | async-start | bytes 4194304 | tf_op jit(solution)/shard_map/all_to_all | solution.py:545
  81.6 4.0 %collective-permute-start.4 = (bf16[4,640,256]{2,1,0:T(8,128)(2,1)}, bf16[4,640,256]{2,1,0:T(8,128)(2,1)S(1)}, u32[]{:S(2)}, u32[]{:S(2)}) collective-permute-start(bf16[4,640,256]{2,1,0:T(8,128)(2,1)} %copy-done.31), channel_id=1, source_target_pairs={{0,1},{1,0},{2,3},{3,2},{4,5},{5,4},{6,7},{7,6},{8,9},{9,8},{10,11... | collective-permute-start | bytes 3932168 | tf_op jit(solution)/shard_map/ppermute | solution.py:471
  82.7 9.8 %collective-permute-start.3 = (bf16[256,512]{1,0:T(8,128)(2,1)}, bf16[256,512]{1,0:T(8,128)(2,1)S(1)}, u32[]{:S(2)}, u32[]{:S(2)}) collective-permute-start(bf16[256,512]{1,0:T(8,128)(2,1)} %bitcast.33), channel_id=1, source_target_pairs={{0,0},{1,4},{4,1},{5,5},{2,2},{3,6},{6,3},{7,7},{8,8},{9,12},{12,9... | collective-permute-start | bytes 786440 | tf_op jit(solution)/shard_map/ppermute | solution.py:467
  98.4 9.6 %collective-permute-start.5 = (bf16[256,512]{1,0:T(8,128)(2,1)}, bf16[256,512]{1,0:T(8,128)(2,1)S(1)}, u32[]{:S(2)}, u32[]{:S(2)}) collective-permute-start(bf16[256,512]{1,0:T(8,128)(2,1)} %get-tuple-element.60), channel_id=1, source_target_pairs={{0,0},{1,4},{4,1},{5,5},{2,2},{3,6},{6,3},{7,7},{8,8},{9,12},{12,9... | collective-permute-start | bytes 786440 | tf_op jit(solution)/shard_map/ppermute | solution.py:467
  108.8 9.5 %collective-permute-start.6 = (bf16[16,256,256]{2,1,0:T(8,128)(2,1)}, bf16[16,256,256]{2,1,0:T(8,128)(2,1)S(1)}, u32[]{:S(2)}, u32[]{:S(2)}) collective-permute-start(bf16[16,256,256]{2,1,0:T(8,128)(2,1)} %all-to-all-done.2.kv_ref), channel_id=1, source_target_pairs={{0,1},{1,0},{2,3},{3,2},{4,5},{5,4},{6,7},{7,6},{8,9},{9,8},{10,11... | collective-permute-start | bytes 6291464 | tf_op jit(solution)/shard_map/ppermute | solution.py:471
  110.4 37.7 %collective-permute-start.10 = (bf16[2,640,256]{2,1,0:T(8,128)(2,1)}, bf16[2,640,256]{2,1,0:T(8,128)(2,1)S(1)}, u32[]{:S(2)}, u32[]{:S(2)}) collective-permute-start(bf16[2,640,256]{2,1,0:T(8,128)(2,1)} %copy-done.34), channel_id=1, source_target_pairs={{0,6},{2,0},{4,2},{6,4},{1,7},{3,1},{5,3},{7,5},{8,14},{10,8},{12,... | collective-permute-start | bytes 1966088 | tf_op jit(solution)/shard_map/ppermute | solution.py:559
  111.8 36.3 %collective-permute-start.11 = (bf16[2,640,256]{2,1,0:T(8,128)(2,1)}, bf16[2,640,256]{2,1,0:T(8,128)(2,1)S(1)}, u32[]{:S(2)}, u32[]{:S(2)}) collective-permute-start(bf16[2,640,256]{2,1,0:T(8,128)(2,1)} %copy-done.33), channel_id=1, source_target_pairs={{0,4},{2,6},{4,0},{6,2},{1,5},{3,7},{5,1},{7,3},{8,12},{10,14},{12... | collective-permute-start | bytes 1966088 | tf_op jit(solution)/shard_map/ppermute | solution.py:559
  113.1 35.0 %collective-permute-start.12 = (bf16[2,640,256]{2,1,0:T(8,128)(2,1)}, bf16[2,640,256]{2,1,0:T(8,128)(2,1)S(1)}, u32[]{:S(2)}, u32[]{:S(2)}) collective-permute-start(bf16[2,640,256]{2,1,0:T(8,128)(2,1)} %copy-done.32), channel_id=1, source_target_pairs={{0,2},{2,4},{4,6},{6,0},{1,3},{3,5},{5,7},{7,1},{8,10},{10,12},{12... | collective-permute-start | bytes 1966088 | tf_op jit(solution)/shard_map/ppermute | solution.py:559
  113.1 35.0 %collective-permute-start.8 = (bf16[256,640]{1,0:T(8,128)(2,1)}, bf16[256,640]{1,0:T(8,128)(2,1)S(1)}, u32[]{:S(2)}, u32[]{:S(2)}) collective-permute-start(bf16[256,640]{1,0:T(8,128)(2,1)} %copy-done.35), channel_id=1, source_target_pairs={{0,0},{1,4},{4,1},{5,5},{2,2},{3,6},{6,3},{7,7},{8,8},{9,12},{12,9... | collective-permute-start | bytes 983048 | tf_op jit(solution)/shard_map/ppermute | solution.py:467
  151.1 4.2 %collective-permute-start.13 = (bf16[16,256,256]{2,1,0:T(8,128)(2,1)S(1)}, bf16[16,256,256]{2,1,0:T(8,128)(2,1)S(1)}, u32[]{:S(2)}, u32[]{:S(2)}) collective-permute-start(bf16[16,256,256]{2,1,0:T(8,128)(2,1)S(1)} %get-tuple-element.73), channel_id=1, source_target_pairs={{0,1},{1,0},{2,3},{3,2},{4,5},{5,4},{6,7},{7,6},{8,9},{9,8},{10,11... | collective-permute-start | bytes 6291464 | tf_op jit(solution)/shard_map/ppermute | solution.py:471
  157.2 35.5 %all-to-all-start.3 = ((bf16[16,256,256]{2,1,0:T(8,128)(2,1)}), bf16[16,256,256]{2,1,0:T(8,128)(2,1)}, u32[]{:S(2)}, u32[]{:S(2)}) async-start(bf16[16,256,256]{2,1,0:T(8,128)(2,1)} %add_convert_fusion), calls=%async_computation.3 | async-start | bytes 4194304 | tf_op jit(solution)/shard_map/all_to_all | solution.py:580
  166.7 14.5 %collective-permute-start.16 = (bf16[256,512]{1,0:T(8,128)(2,1)S(1)}, bf16[256,512]{1,0:T(8,128)(2,1)S(1)}, u32[]{:S(2)}, u32[]{:S(2)}) collective-permute-start(bf16[256,512]{1,0:T(8,128)(2,1)S(1)} %get-tuple-element.66.refs_2_), channel_id=1, source_target_pairs={{0,2},{2,4},{4,6},{6,0},{1,3},{3,5},{5,7},{7,1},{8,10},{10,12},{12... | collective-permute-start | bytes 786440 | tf_op jit(solution)/shard_map/ppermute | solution.py:479
  167.8 14.5 %collective-permute-start.15 = (bf16[256,512]{1,0:T(8,128)(2,1)S(1)}, bf16[256,512]{1,0:T(8,128)(2,1)S(1)}, u32[]{:S(2)}, u32[]{:S(2)}) collective-permute-start(bf16[256,512]{1,0:T(8,128)(2,1)S(1)} %get-tuple-element.66.refs_2_), channel_id=1, source_target_pairs={{0,4},{2,6},{4,0},{6,2},{1,5},{3,7},{5,1},{7,3},{8,12},{10,14},{12... | collective-permute-start | bytes 786440 | tf_op jit(solution)/shard_map/ppermute | solution.py:479
  167.9 14.4 %collective-permute-start.14 = (bf16[256,512]{1,0:T(8,128)(2,1)S(1)}, bf16[256,512]{1,0:T(8,128)(2,1)S(1)}, u32[]{:S(2)}, u32[]{:S(2)}) collective-permute-start(bf16[256,512]{1,0:T(8,128)(2,1)S(1)} %get-tuple-element.66.refs_2_), channel_id=1, source_target_pairs={{0,6},{2,0},{4,2},{6,4},{1,7},{3,1},{5,3},{7,5},{8,14},{10,8},{12,... | collective-permute-start | bytes 786440 | tf_op jit(solution)/shard_map/ppermute | solution.py:479
  170.3 16.1 %collective-permute-start.17 = (bf16[256,512]{1,0:T(8,128)(2,1)S(1)}, bf16[256,512]{1,0:T(8,128)(2,1)S(1)}, u32[]{:S(2)}, u32[]{:S(2)}) collective-permute-start(bf16[256,512]{1,0:T(8,128)(2,1)S(1)} %get-tuple-element.66.refs_2_), channel_id=1, source_target_pairs={{0,1},{1,0},{2,3},{3,2},{4,5},{5,4},{6,7},{7,6},{8,9},{9,8},{10,11... | collective-permute-start | bytes 786440 | tf_op jit(solution)/shard_map/ppermute | solution.py:471
  181.2 5.3 %collective-permute-start.20 = (bf16[256,512]{1,0:T(8,128)(2,1)S(1)}, bf16[256,512]{1,0:T(8,128)(2,1)S(1)}, u32[]{:S(2)}, u32[]{:S(2)}) collective-permute-start(bf16[256,512]{1,0:T(8,128)(2,1)S(1)} %collective-permute-done.16.refs_5_), channel_id=1, source_target_pairs={{0,1},{1,0},{2,3},{3,2},{4,5},{5,4},{6,7},{7,6},{8,9},{9,8},{10,11... | collective-permute-start | bytes 786440 | tf_op jit(solution)/shard_map/ppermute | solution.py:471
  182.3 4.1 %collective-permute-start.19 = (bf16[256,512]{1,0:T(8,128)(2,1)S(1)}, bf16[256,512]{1,0:T(8,128)(2,1)S(1)}, u32[]{:S(2)}, u32[]{:S(2)}) collective-permute-start(bf16[256,512]{1,0:T(8,128)(2,1)S(1)} %collective-permute-done.15.refs_4_), channel_id=1, source_target_pairs={{0,1},{1,0},{2,3},{3,2},{4,5},{5,4},{6,7},{7,6},{8,9},{9,8},{10,11... | collective-permute-start | bytes 786440 | tf_op jit(solution)/shard_map/ppermute | solution.py:471
  182.3 4.1 %collective-permute-start.18 = (bf16[256,512]{1,0:T(8,128)(2,1)S(1)}, bf16[256,512]{1,0:T(8,128)(2,1)S(1)}, u32[]{:S(2)}, u32[]{:S(2)}) collective-permute-start(bf16[256,512]{1,0:T(8,128)(2,1)S(1)} %collective-permute-done.14.refs_3_), channel_id=1, source_target_pairs={{0,1},{1,0},{2,3},{3,2},{4,5},{5,4},{6,7},{7,6},{8,9},{9,8},{10,11... | collective-permute-start | bytes 786440 | tf_op jit(solution)/shard_map/ppermute | solution.py:471
  183.0 9.4 %collective-permute-start.9 = (bf16[256,512]{1,0:T(8,128)(2,1)S(1)}, bf16[256,512]{1,0:T(8,128)(2,1)S(1)}, u32[]{:S(2)}, u32[]{:S(2)}) collective-permute-start(bf16[256,512]{1,0:T(8,128)(2,1)S(1)} %get-tuple-element.66.refs_2_), channel_id=1, source_target_pairs={{0,0},{1,4},{4,1},{5,5},{2,2},{3,6},{6,3},{7,7},{8,8},{9,12},{12,9... | collective-permute-start | bytes 786440 | tf_op jit(solution)/shard_map/ppermute | solution.py:467
  194.9 6.3 %collective-permute-start.24 = (bf16[272,256]{1,0:T(8,128)(2,1)S(1)}, bf16[272,256]{1,0:T(8,128)(2,1)S(1)}, u32[]{:S(2)}, u32[]{:S(2)}) collective-permute-start(bf16[272,256]{1,0:T(8,128)(2,1)S(1)} %grad_key_value.1.refs_3_), channel_id=1, source_target_pairs={{0,2},{2,4},{4,6},{6,0},{1,3},{3,5},{5,7},{7,1},{8,10},{10,12},{12... | collective-permute-start | bytes 417800 | tf_op jit(solution)/shard_map/ppermute | solution.py:479
  195.6 9.7 %collective-permute-start.23 = (bf16[272,256]{1,0:T(8,128)(2,1)S(1)}, bf16[272,256]{1,0:T(8,128)(2,1)S(1)}, u32[]{:S(2)}, u32[]{:S(2)}) collective-permute-start(bf16[272,256]{1,0:T(8,128)(2,1)S(1)} %grad_key_value.1.refs_3_), channel_id=1, source_target_pairs={{0,4},{2,6},{4,0},{6,2},{1,5},{3,7},{5,1},{7,3},{8,12},{10,14},{12... | collective-permute-start | bytes 417800 | tf_op jit(solution)/shard_map/ppermute | solution.py:479
  195.6 9.7 %collective-permute-start.22 = (bf16[272,256]{1,0:T(8,128)(2,1)S(1)}, bf16[272,256]{1,0:T(8,128)(2,1)S(1)}, u32[]{:S(2)}, u32[]{:S(2)}) collective-permute-start(bf16[272,256]{1,0:T(8,128)(2,1)S(1)} %grad_key_value.1.refs_3_), channel_id=1, source_target_pairs={{0,6},{2,0},{4,2},{6,4},{1,7},{3,1},{5,3},{7,5},{8,14},{10,8},{12,... | collective-permute-start | bytes 417800 | tf_op jit(solution)/shard_map/ppermute | solution.py:479
  198.1 7.8 %collective-permute-start.25 = (bf16[272,256]{1,0:T(8,128)(2,1)S(1)}, bf16[272,256]{1,0:T(8,128)(2,1)S(1)}, u32[]{:S(2)}, u32[]{:S(2)}) collective-permute-start(bf16[272,256]{1,0:T(8,128)(2,1)S(1)} %grad_key_value.1.refs_3_), channel_id=1, source_target_pairs={{0,1},{1,0},{2,3},{3,2},{4,5},{5,4},{6,7},{7,6},{8,9},{9,8},{10,11... | collective-permute-start | bytes 417800 | tf_op jit(solution)/shard_map/ppermute | solution.py:471
  201.2 5.1 %collective-permute-start.28 = (bf16[272,256]{1,0:T(8,128)(2,1)S(1)}, bf16[272,256]{1,0:T(8,128)(2,1)S(1)}, u32[]{:S(2)}, u32[]{:S(2)}) collective-permute-start(bf16[272,256]{1,0:T(8,128)(2,1)S(1)} %collective-permute-done.24.refs_6_), channel_id=1, source_target_pairs={{0,1},{1,0},{2,3},{3,2},{4,5},{5,4},{6,7},{7,6},{8,9},{9,8},{10,11... | collective-permute-start | bytes 417800 | tf_op jit(solution)/shard_map/ppermute | solution.py:471
  212.8 27.0 %all-to-all-start.4 = ((bf16[16,48,768]{2,1,0:T(8,128)(2,1)}), bf16[16,48,768]{2,1,0:T(8,128)(2,1)}, u32[]{:S(2)}, u32[]{:S(2)}) async-start(bf16[16,48,768]{2,1,0:T(8,128)(2,1)} %copy-done.12), calls=%async_computation.4 | async-start | bytes 2359296 | tf_op jit(solution)/shard_map/all_to_all | solution.py:613
  220.6 9.6 %collective-permute-start.7 = (bf16[256,512]{1,0:T(8,128)(2,1)S(1)}, bf16[256,512]{1,0:T(8,128)(2,1)S(1)}, u32[]{:S(2)}, u32[]{:S(2)}) collective-permute-start(bf16[256,512]{1,0:T(8,128)(2,1)S(1)} %copy-done.37), channel_id=1, source_target_pairs={{0,0},{1,4},{4,1},{5,5},{2,2},{3,6},{6,3},{7,7},{8,8},{9,12},{12,9... | collective-permute-start | bytes 786440 | tf_op jit(solution)/shard_map/ppermute | solution.py:467
  224.1 8.5 %collective-permute-start.21 = (bf16[272,256]{1,0:T(8,128)(2,1)}, bf16[272,256]{1,0:T(8,128)(2,1)S(1)}, u32[]{:S(2)}, u32[]{:S(2)}) collective-permute-start(bf16[272,256]{1,0:T(8,128)(2,1)} %copy-done.20), channel_id=1, source_target_pairs={{0,0},{1,4},{4,1},{5,5},{2,2},{3,6},{6,3},{7,7},{8,8},{9,12},{12,9... | collective-permute-start | bytes 417800 | tf_op jit(solution)/shard_map/ppermute | solution.py:467
  (40 other events, 151.9 us)

commit v13 on v12

--- a/solution.py
+++ b/solution.py
@@ -90,15 +90,9 @@
 
 
 def place_kernel(where, dkv_ref, raw_ref, *refs):
-    blocks, out_ref, sems = refs[:-3], refs[-2], refs[-1]
-    copies = [
-        pltpu.make_async_copy(block, out_ref.at[lax.rem(where[0] + k, len(blocks))], sems.at[k])
-        for k, block in enumerate(blocks)
-    ]
-    for copy in copies:
-        copy.start()
-    for copy in copies:
-        copy.wait()
+    blocks, out_ref = refs[:-2], refs[-1]
+    for k, block in enumerate(blocks):
+        out_ref[lax.rem(where[0] + k, len(blocks))] = block[...]
 
 
 def key_value_kernel(mine_ref, other_ref, w_ref, w_other_ref, gain_ref, cos_ref, sin_ref, kv_ref, raw_ref):
@@ -384,7 +378,7 @@
 
 
 def weight_grad_kernel(where, turned_ref, query_ref, *rest):
-    blocks, (out_ref, parts, sems) = rest[:-3], rest[-3:]
+    blocks, out_ref = rest[:-1], rest[-1]
     toks = turned_ref.shape[2]
     gains = sum(block[toks:].astype(f32) for block in blocks)
     gain = gains[:8, :span] + gains[:8, span:]
@@ -394,14 +388,9 @@
         [query_ref[...].astype(f32), over_tokens(where, turned_ref, blocks)], axis=1
     )
     own_rows = total.shape[0] // out_ref.shape[0]
-    copies = []
     for i in range(out_ref.shape[0]):
         part = total[i * own_rows : (i + 1) * own_rows]
-        parts[i] = jnp.concatenate([part, extra], axis=0).astype(bf16)
-        copies.append(pltpu.make_async_copy(parts.at[i], out_ref.at[i], sems.at[i]))
-        copies[-1].start()
-    for copy in copies:
-        copy.wait()
+        out_ref[i] = jnp.concatenate([part, extra], axis=0).astype(bf16)
 
 
 def grad_states_kernel(where, gq_ref, gkv_ref, q_ref, q_theirs_ref, kv_ref, kv_theirs_ref, out_ref):
@@ -568,8 +557,7 @@
             shape((columns, 2, half // columns, tok_rows), bf16),
         ),
         in_specs=[smem, anywhere] + [vmem] * (1 + columns),
-        out_specs=(anywhere, hbm),
-        scratch_shapes=[pltpu.SemaphoreType.DMA((columns,))],
+        out_specs=(anywhere, vmem),
         input_output_aliases={1: 0},
         compiler_params=pltpu.CompilerParams(vmem_limit_bytes=16 * mib),
         cost_estimate=cheap,
@@ -607,8 +595,6 @@
         all_parts,
         where, turned, query_parts, *blocks_kv,
         name="weight_grad",
-        out_spec=hbm,
-        scratch=[pltpu.VMEM(all_parts.shape, bf16), pltpu.SemaphoreType.DMA((planes,))],
     )
     parts = lax.all_to_all(parts, plane, 0, 0)
     own_query, own_key, own_value, gain_sum_q, gain_sum_k = call(

time: 245 us -> 243 us (level)
  waiting for transfers between devices: 60.3 us -> 64.3 us
  starting transfers between devices: 88.4 us -> 84.9 us
  Pallas kernels: 55.3 us -> 52.6 us
    ppermute x6, waiting for transfers between devices: 10.7 us -> 14.2 us  [ring(): return lax.ppermute(array, column, [(i, (i - step) % 4) for i in range(4)])]
    ppermute x13, starting transfers between devices: 14.6 us -> 12.1 us  [flip(): return lax.ppermute(array, 'core', flipped)]
where the time goes in v13:
time: 243 us; the launch traced here: 240 us
  starting transfers between devices  84.9 us (35%)
  waiting for transfers between devices  64.3 us (26%)
  Pallas kernels  52.6 us (22%)
  local copies, waits for them, and re-layouts  33 us (14%)
  other arithmetic  4.39 us (2%)
    ppermute x7, waiting for transfers between devices, swap(): return lax.ppermute(array, ('y_hi', 'core'), swapped)  29.5 us
    unnamed x77, local copies, waits for them, and re-layouts  28.8 us
    pallas_call x1, Pallas kernels, attention(): pl.pallas_call(attention_kernel, out_shape=(jax.ShapeDtypeStruct((rows_he...  28.6 us
    ppermute x7, starting transfers between devices, swap(): return lax.ppermute(array, ('y_hi', 'core'), swapped)  24.5 us
    pallas_call x11, Pallas kernels, call(): pl.pallas_call(run, out_shape=shapes, in_specs=[smem if a.dtype == jnp.in...  23.3 us
    ppermute x6, waiting for transfers between devices, ring(): return lax.ppermute(array, column, [(i, (i - step) % 4) for i in range(4)])  14.2 us
    ppermute x13, starting transfers between devices, flip(): return lax.ppermute(array, 'core', flipped)  12.1 us
    all_to_all x1, starting transfers between devices, to_all(): lax.all_to_all(jnp.broadcast_to(array[None], (count,) + array.shape), axe...  10.8 us
  transfers between devices with their start and end apart: 34, of which 17 were waited for; matrix products, arithmetic and copies ran while one was open for 2% of the time, Pallas kernels for 19%

profile of v13, /device:TPU:39, one launch (start us, length us, event | category | flops | bytes accessed | tf_op | source)
XLA Modules:
  0.0 240.2 jit_solution(12392312141465435318)
XLA Ops:
  2.5 10.8 %all-to-all-start = ((bf16[64,40,256]{2,1,0:T(8,128)(2,1)}), bf16[64,40,256]{2,1,0:T(8,128)(2,1)}, u32[]{:S(2)}, u32[]{:S(2)}) async-start(bf16[64,40,256]{2,1,0:T(8,128)(2,1)} %broadcast_in_dim.10), calls=%async_computation | async-start | bytes 2621440 | tf_op jit(solution)/shard_map/all_to_all | solution.py:464
  13.4 3.0 %copy.16 = bf16[5120,256]{1,0:T(8,128)(2,1)S(1)} copy(bf16[5120,256]{0,1:T(8,128)(2,1)} %bitcast.30) | data formatting | bytes 5242880 | tf_op jit(solution)/shard_map/transpose | solution.py:508
  25.5 5.4 %all-to-all-done = bf16[64,40,256]{2,1,0:T(8,128)(2,1)} async-done(((bf16[64,40,256]{2,1,0:T(8,128)(2,1)}), bf16[64,40,256]{2,1,0:T(8,128)(2,1)}, u32[]{:S(2)}, u32[]{:S(2)}) %all-to-all-start) | async-done | bytes 1310752 | tf_op jit(solution)/shard_map/all_to_all | solution.py:464
  30.9 7.9 %all-to-all-start.1 = ((bf16[64,40,512]{2,1,0:T(8,128)(2,1)}), bf16[64,40,512]{2,1,0:T(8,128)(2,1)S(1)}, u32[]{:S(2)}, u32[]{:S(2)}) async-start(bf16[64,40,512]{2,1,0:T(8,128)(2,1)} %copy-done.13), calls=%async_computation.1 | async-start | bytes 5242880 | tf_op jit(solution)/shard_map/all_to_all | solution.py:515
  38.8 2.2 collective-permute-start
  40.9 2.9 %collective-permute-done.refs_3_.refs_6_ = bf16[2560,256]{1,0:T(8,128)(2,1)S(1)} collective-permute-done((bf16[2560,256]{1,0:T(8,128)(2,1)}, bf16[2560,256]{1,0:T(8,128)(2,1)S(1)}, u32[]{:S(2)}, u32[]{:S(2)}) %collective-permute-start) | collective-permute-done | bytes 1310752 | tf_op jit(solution)/shard_map/ppermute | solution.py:460
  46.9 2.3 key_value.1
  49.9 4.9 %collective-permute-start.1 = (bf16[256,256]{1,0:T(8,128)(2,1)S(1)}, bf16[256,256]{1,0:T(8,128)(2,1)S(1)}, u32[]{:S(2)}, u32[]{:S(2)}) collective-permute-start(bf16[256,256]{1,0:T(8,128)(2,1)S(1)} %get-tuple-element.52), channel_id=1, source_target_pairs={{0,0},{1,4},{4,1},{5,5},{2,2},{3,6},{6,3},{7,7},{8,8},{9,12},{12,9... | collective-permute-start | bytes 393224 | tf_op jit(solution)/shard_map/ppermute | solution.py:456
  54.8 20.3 %collective-permute-done.1.refs_0_ = bf16[256,256]{1,0:T(8,128)(2,1)S(1)} collective-permute-done((bf16[256,256]{1,0:T(8,128)(2,1)S(1)}, bf16[256,256]{1,0:T(8,128)(2,1)S(1)}, u32[]{:S(2)}, u32[]{:S(2)}) %collective-permute-start.1) | collective-permute-done | bytes 131104 | tf_op jit(solution)/shard_map/ppermute | solution.py:456
  76.6 5.0 %all-to-all-start.2 = ((bf16[16,256,256]{2,1,0:T(8,128)(2,1)}), bf16[16,256,256]{2,1,0:T(8,128)(2,1)}, u32[]{:S(2)}, u32[]{:S(2)}) async-start(bf16[16,256,256]{2,1,0:T(8,128)(2,1)} %copy-done.3), calls=%async_computation.2 | async-start | bytes 4194304 | tf_op jit(solution)/shard_map/all_to_all | solution.py:534
  93.5 4.3 %query.1 = (bf16[256,512]{1,0:T(8,128)(2,1)}, bf16[256,640]{1,0:T(8,128)(2,1)S(1)}) custom-call(bf16[256,2560]{1,0:T(8,128)(2,1)S(1)} %copy-done.8, bf16[256,2560]{1,0:T(8,128)(2,1)S(1)} %copy-done.11, bf16[2560,512]{1,0:T(8,128)(2,1)S(1)} %bitcast.21, bf16[2560,512]{1,0:T(8,128)(2,1)} %collective-permute-done.2.refs_3_.refs_4_, f32[256,128]{1,0:T(8,128)S(1)} %copy-done.26, ...), custom_call_target="tpu_custom_call" | custom-call | flops 1000 | bytes 1000 | tf_op jit(solution)/shard_map/query/pallas_call | solution.py:436
  98.4 2.7 %collective-permute-start.5 = (bf16[256,512]{1,0:T(8,128)(2,1)}, bf16[256,512]{1,0:T(8,128)(2,1)S(1)}, u32[]{:S(2)}, u32[]{:S(2)}) collective-permute-start(bf16[256,512]{1,0:T(8,128)(2,1)} %get-tuple-element.60), channel_id=1, source_target_pairs={{0,0},{1,4},{4,1},{5,5},{2,2},{3,6},{6,3},{7,7},{8,8},{9,12},{12,9... | collective-permute-start | bytes 786440 | tf_op jit(solution)/shard_map/ppermute | solution.py:456
  101.1 5.8 %all-to-all-done.2.kv_ref = bf16[16,256,256]{2,1,0:T(8,128)(2,1)} async-done(((bf16[16,256,256]{2,1,0:T(8,128)(2,1)}), bf16[16,256,256]{2,1,0:T(8,128)(2,1)}, u32[]{:S(2)}, u32[]{:S(2)}) %all-to-all-start.2) | async-done | bytes 2097184 | tf_op jit(solution)/shard_map/all_to_all | solution.py:534
  113.1 5.1 %collective-permute-start.8 = (bf16[256,640]{1,0:T(8,128)(2,1)}, bf16[256,640]{1,0:T(8,128)(2,1)S(1)}, u32[]{:S(2)}, u32[]{:S(2)}) collective-permute-start(bf16[256,640]{1,0:T(8,128)(2,1)} %copy-done.35), channel_id=1, source_target_pairs={{0,0},{1,4},{4,1},{5,5},{2,2},{3,6},{6,3},{7,7},{8,8},{9,12},{12,9... | collective-permute-start | bytes 983048 | tf_op jit(solution)/shard_map/ppermute | solution.py:456
  119.2 28.6 %attention.1 = (bf16[256,512]{1,0:T(8,128)(2,1)S(1)}, f32[256,512]{1,0:T(8,128)S(1)}, bf16[16,256,256]{2,1,0:T(8,128)(2,1)S(1)}, bf16[16,256,256]{2,1,0:T(8,128)(2,1)S(1)}) custom-call(s32[64]{0:T(128)S(1)} %copy-done.28, s32[3]{0:T(128)S(1)} %pad_add_fusion.1.own, bf16[256,512]{1,0:T(8,128)(2,1)S(1)} %copy-done.24, ...), custom_call_target="tpu_custom_call" | custom-call | flops 1000 | bytes 1000 | tf_op jit(solution)/shard_map/attention/pallas_call | solution.py:294
  150.2 4.2 %collective-permute-done.13 = bf16[16,256,256]{2,1,0:T(8,128)(2,1)S(1)} collective-permute-done((bf16[16,256,256]{2,1,0:T(8,128)(2,1)S(1)}, bf16[16,256,256]{2,1,0:T(8,128)(2,1)S(1)}, u32[]{:S(2)}, u32[]{:S(2)}) %collective-permute-start.13) | collective-permute-done | bytes 2097184 | tf_op jit(solution)/shard_map/ppermute | solution.py:460
  154.3 2.0 add_convert_fusion
  156.3 8.3 %all-to-all-start.3 = ((bf16[16,256,256]{2,1,0:T(8,128)(2,1)}), bf16[16,256,256]{2,1,0:T(8,128)(2,1)}, u32[]{:S(2)}, u32[]{:S(2)}) async-start(bf16[16,256,256]{2,1,0:T(8,128)(2,1)} %add_convert_fusion), calls=%async_computation.3 | async-start | bytes 4194304 | tf_op jit(solution)/shard_map/all_to_all | solution.py:568
  167.4 2.0 collective-permute-start.14
  171.0 9.8 %collective-permute-done.16.refs_5_ = bf16[256,512]{1,0:T(8,128)(2,1)S(1)} collective-permute-done((bf16[256,512]{1,0:T(8,128)(2,1)S(1)}, bf16[256,512]{1,0:T(8,128)(2,1)S(1)}, u32[]{:S(2)}, u32[]{:S(2)}) %collective-permute-start.16) | collective-permute-done | bytes 262176 | tf_op jit(solution)/shard_map/ppermute | solution.py:468
  182.5 3.0 %collective-permute-start.9 = (bf16[256,512]{1,0:T(8,128)(2,1)S(1)}, bf16[256,512]{1,0:T(8,128)(2,1)S(1)}, u32[]{:S(2)}, u32[]{:S(2)}) collective-permute-start(bf16[256,512]{1,0:T(8,128)(2,1)S(1)} %get-tuple-element.66.refs_2_), channel_id=1, source_target_pairs={{0,0},{1,4},{4,1},{5,5},{2,2},{3,6},{6,3},{7,7},{8,8},{9,12},{12,9... | collective-permute-start | bytes 786440 | tf_op jit(solution)/shard_map/ppermute | solution.py:456
  187.3 2.0 query_weight_grad.1
  192.3 2.2 grad_key_value.1.refs_3_
  194.7 2.6 %collective-permute-start.22 = (bf16[272,256]{1,0:T(8,128)(2,1)S(1)}, bf16[272,256]{1,0:T(8,128)(2,1)S(1)}, u32[]{:S(2)}, u32[]{:S(2)}) collective-permute-start(bf16[272,256]{1,0:T(8,128)(2,1)S(1)} %grad_key_value.1.refs_3_), channel_id=1, source_target_pairs={{0,6},{2,0},{4,2},{6,4},{1,7},{3,1},{5,3},{7,5},{8,14},{10,8},{12,... | collective-permute-start | bytes 417800 | tf_op jit(solution)/shard_map/ppermute | solution.py:468
  199.1 4.4 %collective-permute-done.24.refs_6_ = bf16[272,256]{1,0:T(8,128)(2,1)S(1)} collective-permute-done((bf16[272,256]{1,0:T(8,128)(2,1)S(1)}, bf16[272,256]{1,0:T(8,128)(2,1)S(1)}, u32[]{:S(2)}, u32[]{:S(2)}) %collective-permute-start.24) | collective-permute-done | bytes 139296 | tf_op jit(solution)/shard_map/ppermute | solution.py:468
  210.7 7.8 %all-to-all-start.4 = ((bf16[16,48,768]{2,1,0:T(8,128)(2,1)}), bf16[16,48,768]{2,1,0:T(8,128)(2,1)}, u32[]{:S(2)}, u32[]{:S(2)}) async-start(bf16[16,48,768]{2,1,0:T(8,128)(2,1)} %copy-done.12), calls=%async_computation.4 | async-start | bytes 2359296 | tf_op jit(solution)/shard_map/all_to_all | solution.py:599
  218.5 3.3 %collective-permute-start.7 = (bf16[256,512]{1,0:T(8,128)(2,1)S(1)}, bf16[256,512]{1,0:T(8,128)(2,1)S(1)}, u32[]{:S(2)}, u32[]{:S(2)}) collective-permute-start(bf16[256,512]{1,0:T(8,128)(2,1)S(1)} %copy-done.37), channel_id=1, source_target_pairs={{0,0},{1,4},{4,1},{5,5},{2,2},{3,6},{6,3},{7,7},{8,8},{9,12},{12,9... | collective-permute-start | bytes 786440 | tf_op jit(solution)/shard_map/ppermute | solution.py:456
  221.8 3.8 %collective-permute-start.21 = (bf16[272,256]{1,0:T(8,128)(2,1)}, bf16[272,256]{1,0:T(8,128)(2,1)S(1)}, u32[]{:S(2)}, u32[]{:S(2)}) collective-permute-start(bf16[272,256]{1,0:T(8,128)(2,1)} %copy-done.20), channel_id=1, source_target_pairs={{0,0},{1,4},{4,1},{5,5},{2,2},{3,6},{6,3},{7,7},{8,8},{9,12},{12,9... | collective-permute-start | bytes 417800 | tf_op jit(solution)/shard_map/ppermute | solution.py:456
  225.6 2.5 %collective-permute-done.7 = bf16[256,512]{1,0:T(8,128)(2,1)S(1)} collective-permute-done((bf16[256,512]{1,0:T(8,128)(2,1)S(1)}, bf16[256,512]{1,0:T(8,128)(2,1)S(1)}, u32[]{:S(2)}, u32[]{:S(2)}) %collective-permute-start.7) | collective-permute-done | bytes 262176 | tf_op jit(solution)/shard_map/ppermute | solution.py:456
  228.1 2.2 collective-permute-done.21.refs_2_
  231.6 5.9 %grad_states.1 = bf16[256,5120]{1,0:T(8,128)(2,1)} custom-call(s32[2]{0:T(128)S(1)} %pad_add_fusion.refs_0_.where, bf16[256,512]{1,0:T(8,128)(2,1)S(1)} %collective-permute-done.9.refs_7_.refs_1_, bf16[272,256]{1,0:T(8,128)(2,1)S(1)} %collective-permute-done.21.refs_2_, bf16[2560,512]{1,0:T(8,128)(2,1)S(1)} %bitcast.22, ...), custom_call_target="tpu_custom_call" | custom-call | flops 1000 | bytes 1000 | tf_op jit(solution)/shard_map/grad_states/pallas_call | solution.py:436
  237.5 2.0 finish.1
  (140 shorter events, 60.3 us)
Async XLA Ops:
  2.5 28.4 %all-to-all-start = ((bf16[64,40,256]{2,1,0:T(8,128)(2,1)}), bf16[64,40,256]{2,1,0:T(8,128)(2,1)}, u32[]{:S(2)}, u32[]{:S(2)}) async-start(bf16[64,40,256]{2,1,0:T(8,128)(2,1)} %broadcast_in_dim.10), calls=%async_computation | async-start | bytes 2621440 | tf_op jit(solution)/shard_map/all_to_all | solution.py:464
  30.9 45.6 %all-to-all-start.1 = ((bf16[64,40,512]{2,1,0:T(8,128)(2,1)}), bf16[64,40,512]{2,1,0:T(8,128)(2,1)S(1)}, u32[]{:S(2)}, u32[]{:S(2)}) async-start(bf16[64,40,512]{2,1,0:T(8,128)(2,1)} %copy-done.13), calls=%async_computation.1 | async-start | bytes 5242880 | tf_op jit(solution)/shard_map/all_to_all | solution.py:515
  38.8 5.0 %collective-permute-start = (bf16[2560,256]{1,0:T(8,128)(2,1)}, bf16[2560,256]{1,0:T(8,128)(2,1)S(1)}, u32[]{:S(2)}, u32[]{:S(2)}) collective-permute-start(bf16[2560,256]{1,0:T(8,128)(2,1)} %bitcast.7.refs_2_.refs_5_), channel_id=1, source_target_pairs={{0,1},{1,0},{2,3},{3,2},{4,5},{5,4},{6,7},{7,6},{8,9},{9,8},{10,11... | collective-permute-start | bytes 3932168 | tf_op jit(solution)/shard_map/ppermute | solution.py:460
  49.9 25.2 %collective-permute-start.1 = (bf16[256,256]{1,0:T(8,128)(2,1)S(1)}, bf16[256,256]{1,0:T(8,128)(2,1)S(1)}, u32[]{:S(2)}, u32[]{:S(2)}) collective-permute-start(bf16[256,256]{1,0:T(8,128)(2,1)S(1)} %get-tuple-element.52), channel_id=1, source_target_pairs={{0,0},{1,4},{4,1},{5,5},{2,2},{3,6},{6,3},{7,7},{8,8},{9,12},{12,9... | collective-permute-start | bytes 393224 | tf_op jit(solution)/shard_map/ppermute | solution.py:456
  76.6 16.0 %collective-permute-start.2 = (bf16[2560,512]{1,0:T(8,128)(2,1)S(1)}, bf16[2560,512]{1,0:T(8,128)(2,1)}, u32[]{:S(2)}, u32[]{:S(2)}) collective-permute-start(bf16[2560,512]{1,0:T(8,128)(2,1)S(1)} %bitcast.20), channel_id=1, source_target_pairs={{0,1},{1,0},{2,3},{3,2},{4,5},{5,4},{6,7},{7,6},{8,9},{9,8},{10,11... | collective-permute-start | bytes 7864328 | tf_op jit(solution)/shard_map/ppermute | solution.py:460
  76.6 30.3 %all-to-all-start.2 = ((bf16[16,256,256]{2,1,0:T(8,128)(2,1)}), bf16[16,256,256]{2,1,0:T(8,128)(2,1)}, u32[]{:S(2)}, u32[]{:S(2)}) async-start(bf16[16,256,256]{2,1,0:T(8,128)(2,1)} %copy-done.3), calls=%async_computation.2 | async-start | bytes 4194304 | tf_op jit(solution)/shard_map/all_to_all | solution.py:534
  81.6 4.0 %collective-permute-start.4 = (bf16[4,640,256]{2,1,0:T(8,128)(2,1)}, bf16[4,640,256]{2,1,0:T(8,128)(2,1)S(1)}, u32[]{:S(2)}, u32[]{:S(2)}) collective-permute-start(bf16[4,640,256]{2,1,0:T(8,128)(2,1)} %copy-done.31), channel_id=1, source_target_pairs={{0,1},{1,0},{2,3},{3,2},{4,5},{5,4},{6,7},{7,6},{8,9},{9,8},{10,11... | collective-permute-start | bytes 3932168 | tf_op jit(solution)/shard_map/ppermute | solution.py:460
  82.7 9.8 %collective-permute-start.3 = (bf16[256,512]{1,0:T(8,128)(2,1)}, bf16[256,512]{1,0:T(8,128)(2,1)S(1)}, u32[]{:S(2)}, u32[]{:S(2)}) collective-permute-start(bf16[256,512]{1,0:T(8,128)(2,1)} %bitcast.33), channel_id=1, source_target_pairs={{0,0},{1,4},{4,1},{5,5},{2,2},{3,6},{6,3},{7,7},{8,8},{9,12},{12,9... | collective-permute-start | bytes 786440 | tf_op jit(solution)/shard_map/ppermute | solution.py:456
  98.4 9.6 %collective-permute-start.5 = (bf16[256,512]{1,0:T(8,128)(2,1)}, bf16[256,512]{1,0:T(8,128)(2,1)S(1)}, u32[]{:S(2)}, u32[]{:S(2)}) collective-permute-start(bf16[256,512]{1,0:T(8,128)(2,1)} %get-tuple-element.60), channel_id=1, source_target_pairs={{0,0},{1,4},{4,1},{5,5},{2,2},{3,6},{6,3},{7,7},{8,8},{9,12},{12,9... | collective-permute-start | bytes 786440 | tf_op jit(solution)/shard_map/ppermute | solution.py:456
  108.8 9.5 %collective-permute-start.6 = (bf16[16,256,256]{2,1,0:T(8,128)(2,1)}, bf16[16,256,256]{2,1,0:T(8,128)(2,1)S(1)}, u32[]{:S(2)}, u32[]{:S(2)}) collective-permute-start(bf16[16,256,256]{2,1,0:T(8,128)(2,1)} %all-to-all-done.2.kv_ref), channel_id=1, source_target_pairs={{0,1},{1,0},{2,3},{3,2},{4,5},{5,4},{6,7},{7,6},{8,9},{9,8},{10,11... | collective-permute-start | bytes 6291464 | tf_op jit(solution)/shard_map/ppermute | solution.py:460
  110.4 37.4 %collective-permute-start.10 = (bf16[2,640,256]{2,1,0:T(8,128)(2,1)}, bf16[2,640,256]{2,1,0:T(8,128)(2,1)S(1)}, u32[]{:S(2)}, u32[]{:S(2)}) collective-permute-start(bf16[2,640,256]{2,1,0:T(8,128)(2,1)} %copy-done.34), channel_id=1, source_target_pairs={{0,6},{2,0},{4,2},{6,4},{1,7},{3,1},{5,3},{7,5},{8,14},{10,8},{12,... | collective-permute-start | bytes 1966088 | tf_op jit(solution)/shard_map/ppermute | solution.py:548
  111.8 36.0 %collective-permute-start.11 = (bf16[2,640,256]{2,1,0:T(8,128)(2,1)}, bf16[2,640,256]{2,1,0:T(8,128)(2,1)S(1)}, u32[]{:S(2)}, u32[]{:S(2)}) collective-permute-start(bf16[2,640,256]{2,1,0:T(8,128)(2,1)} %copy-done.33), channel_id=1, source_target_pairs={{0,4},{2,6},{4,0},{6,2},{1,5},{3,7},{5,1},{7,3},{8,12},{10,14},{12... | collective-permute-start | bytes 1966088 | tf_op jit(solution)/shard_map/ppermute | solution.py:548
  113.1 34.7 %collective-permute-start.12 = (bf16[2,640,256]{2,1,0:T(8,128)(2,1)}, bf16[2,640,256]{2,1,0:T(8,128)(2,1)S(1)}, u32[]{:S(2)}, u32[]{:S(2)}) collective-permute-start(bf16[2,640,256]{2,1,0:T(8,128)(2,1)} %copy-done.32), channel_id=1, source_target_pairs={{0,2},{2,4},{4,6},{6,0},{1,3},{3,5},{5,7},{7,1},{8,10},{10,12},{12... | collective-permute-start | bytes 1966088 | tf_op jit(solution)/shard_map/ppermute | solution.py:548
  113.1 34.7 %collective-permute-start.8 = (bf16[256,640]{1,0:T(8,128)(2,1)}, bf16[256,640]{1,0:T(8,128)(2,1)S(1)}, u32[]{:S(2)}, u32[]{:S(2)}) collective-permute-start(bf16[256,640]{1,0:T(8,128)(2,1)} %copy-done.35), channel_id=1, source_target_pairs={{0,0},{1,4},{4,1},{5,5},{2,2},{3,6},{6,3},{7,7},{8,8},{9,12},{12,9... | collective-permute-start | bytes 983048 | tf_op jit(solution)/shard_map/ppermute | solution.py:456
  150.2 4.2 %collective-permute-start.13 = (bf16[16,256,256]{2,1,0:T(8,128)(2,1)S(1)}, bf16[16,256,256]{2,1,0:T(8,128)(2,1)S(1)}, u32[]{:S(2)}, u32[]{:S(2)}) collective-permute-start(bf16[16,256,256]{2,1,0:T(8,128)(2,1)S(1)} %get-tuple-element.73), channel_id=1, source_target_pairs={{0,1},{1,0},{2,3},{3,2},{4,5},{5,4},{6,7},{7,6},{8,9},{9,8},{10,11... | collective-permute-start | bytes 6291464 | tf_op jit(solution)/shard_map/ppermute | solution.py:460
  156.3 36.0 %all-to-all-start.3 = ((bf16[16,256,256]{2,1,0:T(8,128)(2,1)}), bf16[16,256,256]{2,1,0:T(8,128)(2,1)}, u32[]{:S(2)}, u32[]{:S(2)}) async-start(bf16[16,256,256]{2,1,0:T(8,128)(2,1)} %add_convert_fusion), calls=%async_computation.3 | async-start | bytes 4194304 | tf_op jit(solution)/shard_map/all_to_all | solution.py:568
  166.3 14.5 %collective-permute-start.16 = (bf16[256,512]{1,0:T(8,128)(2,1)S(1)}, bf16[256,512]{1,0:T(8,128)(2,1)S(1)}, u32[]{:S(2)}, u32[]{:S(2)}) collective-permute-start(bf16[256,512]{1,0:T(8,128)(2,1)S(1)} %get-tuple-element.66.refs_2_), channel_id=1, source_target_pairs={{0,2},{2,4},{4,6},{6,0},{1,3},{3,5},{5,7},{7,1},{8,10},{10,12},{12... | collective-permute-start | bytes 786440 | tf_op jit(solution)/shard_map/ppermute | solution.py:468
  166.9 15.0 %collective-permute-start.15 = (bf16[256,512]{1,0:T(8,128)(2,1)S(1)}, bf16[256,512]{1,0:T(8,128)(2,1)S(1)}, u32[]{:S(2)}, u32[]{:S(2)}) collective-permute-start(bf16[256,512]{1,0:T(8,128)(2,1)S(1)} %get-tuple-element.66.refs_2_), channel_id=1, source_target_pairs={{0,4},{2,6},{4,0},{6,2},{1,5},{3,7},{5,1},{7,3},{8,12},{10,14},{12... | collective-permute-start | bytes 786440 | tf_op jit(solution)/shard_map/ppermute | solution.py:468
  167.4 14.6 %collective-permute-start.14 = (bf16[256,512]{1,0:T(8,128)(2,1)S(1)}, bf16[256,512]{1,0:T(8,128)(2,1)S(1)}, u32[]{:S(2)}, u32[]{:S(2)}) collective-permute-start(bf16[256,512]{1,0:T(8,128)(2,1)S(1)} %get-tuple-element.66.refs_2_), channel_id=1, source_target_pairs={{0,6},{2,0},{4,2},{6,4},{1,7},{3,1},{5,3},{7,5},{8,14},{10,8},{12,... | collective-permute-start | bytes 786440 | tf_op jit(solution)/shard_map/ppermute | solution.py:468
  169.4 16.1 %collective-permute-start.17 = (bf16[256,512]{1,0:T(8,128)(2,1)S(1)}, bf16[256,512]{1,0:T(8,128)(2,1)S(1)}, u32[]{:S(2)}, u32[]{:S(2)}) collective-permute-start(bf16[256,512]{1,0:T(8,128)(2,1)S(1)} %get-tuple-element.66.refs_2_), channel_id=1, source_target_pairs={{0,1},{1,0},{2,3},{3,2},{4,5},{5,4},{6,7},{7,6},{8,9},{9,8},{10,11... | collective-permute-start | bytes 786440 | tf_op jit(solution)/shard_map/ppermute | solution.py:460
  180.8 4.8 %collective-permute-start.20 = (bf16[256,512]{1,0:T(8,128)(2,1)S(1)}, bf16[256,512]{1,0:T(8,128)(2,1)S(1)}, u32[]{:S(2)}, u32[]{:S(2)}) collective-permute-start(bf16[256,512]{1,0:T(8,128)(2,1)S(1)} %collective-permute-done.16.refs_5_), channel_id=1, source_target_pairs={{0,1},{1,0},{2,3},{3,2},{4,5},{5,4},{6,7},{7,6},{8,9},{9,8},{10,11... | collective-permute-start | bytes 786440 | tf_op jit(solution)/shard_map/ppermute | solution.py:460
  181.9 3.6 %collective-permute-start.19 = (bf16[256,512]{1,0:T(8,128)(2,1)S(1)}, bf16[256,512]{1,0:T(8,128)(2,1)S(1)}, u32[]{:S(2)}, u32[]{:S(2)}) collective-permute-start(bf16[256,512]{1,0:T(8,128)(2,1)S(1)} %collective-permute-done.15.refs_4_), channel_id=1, source_target_pairs={{0,1},{1,0},{2,3},{3,2},{4,5},{5,4},{6,7},{7,6},{8,9},{9,8},{10,11... | collective-permute-start | bytes 786440 | tf_op jit(solution)/shard_map/ppermute | solution.py:460
  181.9 3.6 %collective-permute-start.18 = (bf16[256,512]{1,0:T(8,128)(2,1)S(1)}, bf16[256,512]{1,0:T(8,128)(2,1)S(1)}, u32[]{:S(2)}, u32[]{:S(2)}) collective-permute-start(bf16[256,512]{1,0:T(8,128)(2,1)S(1)} %collective-permute-done.14.refs_3_), channel_id=1, source_target_pairs={{0,1},{1,0},{2,3},{3,2},{4,5},{5,4},{6,7},{7,6},{8,9},{9,8},{10,11... | collective-permute-start | bytes 786440 | tf_op jit(solution)/shard_map/ppermute | solution.py:460
  182.5 9.4 %collective-permute-start.9 = (bf16[256,512]{1,0:T(8,128)(2,1)S(1)}, bf16[256,512]{1,0:T(8,128)(2,1)S(1)}, u32[]{:S(2)}, u32[]{:S(2)}) collective-permute-start(bf16[256,512]{1,0:T(8,128)(2,1)S(1)} %get-tuple-element.66.refs_2_), channel_id=1, source_target_pairs={{0,0},{1,4},{4,1},{5,5},{2,2},{3,6},{6,3},{7,7},{8,8},{9,12},{12,9... | collective-permute-start | bytes 786440 | tf_op jit(solution)/shard_map/ppermute | solution.py:456
  194.5 9.0 %collective-permute-start.24 = (bf16[272,256]{1,0:T(8,128)(2,1)S(1)}, bf16[272,256]{1,0:T(8,128)(2,1)S(1)}, u32[]{:S(2)}, u32[]{:S(2)}) collective-permute-start(bf16[272,256]{1,0:T(8,128)(2,1)S(1)} %grad_key_value.1.refs_3_), channel_id=1, source_target_pairs={{0,2},{2,4},{4,6},{6,0},{1,3},{3,5},{5,7},{7,1},{8,10},{10,12},{12... | collective-permute-start | bytes 417800 | tf_op jit(solution)/shard_map/ppermute | solution.py:468
  194.7 10.2 %collective-permute-start.23 = (bf16[272,256]{1,0:T(8,128)(2,1)S(1)}, bf16[272,256]{1,0:T(8,128)(2,1)S(1)}, u32[]{:S(2)}, u32[]{:S(2)}) collective-permute-start(bf16[272,256]{1,0:T(8,128)(2,1)S(1)} %grad_key_value.1.refs_3_), channel_id=1, source_target_pairs={{0,4},{2,6},{4,0},{6,2},{1,5},{3,7},{5,1},{7,3},{8,12},{10,14},{12... | collective-permute-start | bytes 417800 | tf_op jit(solution)/shard_map/ppermute | solution.py:468
  194.7 10.2 %collective-permute-start.22 = (bf16[272,256]{1,0:T(8,128)(2,1)S(1)}, bf16[272,256]{1,0:T(8,128)(2,1)S(1)}, u32[]{:S(2)}, u32[]{:S(2)}) collective-permute-start(bf16[272,256]{1,0:T(8,128)(2,1)S(1)} %grad_key_value.1.refs_3_), channel_id=1, source_target_pairs={{0,6},{2,0},{4,2},{6,4},{1,7},{3,1},{5,3},{7,5},{8,14},{10,8},{12,... | collective-permute-start | bytes 417800 | tf_op jit(solution)/shard_map/ppermute | solution.py:468
  197.2 8.2 %collective-permute-start.25 = (bf16[272,256]{1,0:T(8,128)(2,1)S(1)}, bf16[272,256]{1,0:T(8,128)(2,1)S(1)}, u32[]{:S(2)}, u32[]{:S(2)}) collective-permute-start(bf16[272,256]{1,0:T(8,128)(2,1)S(1)} %grad_key_value.1.refs_3_), channel_id=1, source_target_pairs={{0,1},{1,0},{2,3},{3,2},{4,5},{5,4},{6,7},{7,6},{8,9},{9,8},{10,11... | collective-permute-start | bytes 417800 | tf_op jit(solution)/shard_map/ppermute | solution.py:460
  203.5 2.3 collective-permute-start.28
  210.7 26.8 %all-to-all-start.4 = ((bf16[16,48,768]{2,1,0:T(8,128)(2,1)}), bf16[16,48,768]{2,1,0:T(8,128)(2,1)}, u32[]{:S(2)}, u32[]{:S(2)}) async-start(bf16[16,48,768]{2,1,0:T(8,128)(2,1)} %copy-done.12), calls=%async_computation.4 | async-start | bytes 2359296 | tf_op jit(solution)/shard_map/all_to_all | solution.py:599
  218.5 9.6 %collective-permute-start.7 = (bf16[256,512]{1,0:T(8,128)(2,1)S(1)}, bf16[256,512]{1,0:T(8,128)(2,1)S(1)}, u32[]{:S(2)}, u32[]{:S(2)}) collective-permute-start(bf16[256,512]{1,0:T(8,128)(2,1)S(1)} %copy-done.37), channel_id=1, source_target_pairs={{0,0},{1,4},{4,1},{5,5},{2,2},{3,6},{6,3},{7,7},{8,8},{9,12},{12,9... | collective-permute-start | bytes 786440 | tf_op jit(solution)/shard_map/ppermute | solution.py:456
  221.8 8.5 %collective-permute-start.21 = (bf16[272,256]{1,0:T(8,128)(2,1)}, bf16[272,256]{1,0:T(8,128)(2,1)S(1)}, u32[]{:S(2)}, u32[]{:S(2)}) collective-permute-start(bf16[272,256]{1,0:T(8,128)(2,1)} %copy-done.20), channel_id=1, source_target_pairs={{0,0},{1,4},{4,1},{5,5},{2,2},{3,6},{6,3},{7,7},{8,8},{9,12},{12,9... | collective-permute-start | bytes 417800 | tf_op jit(solution)/shard_map/ppermute | solution.py:456
  (40 other events, 150.3 us)
